TPU v7x, 256 devices: a whole 4x4x8 slice. The times are simulated.
256 devices in a mesh: replica: 16 (over x_lo, z), fsdp: 16 (over x_hi, y, core).
Axes of the slice: x: 4 (x_hi: 2, x_lo: 2; x = x_hi * 2 + x_lo), y: 4, z: 8, core: 2. Of those that a mesh axis runs over, the one named last changes fastest.
Arguments:
- token_in: bfloat16 [16, 2048, 8192], P('replica', 'fsdp'), may hold values from -6 to 6
- cotangent: bfloat16 [16, 2048, 512], P('replica', 'fsdp'), may hold values from -6 to 6
- weight: float32 [16, 8192, 512], P('replica', 'fsdp'), may hold values from -4 to 4
- adam_m: float32 [16, 8192, 512], P('replica', 'fsdp'), may hold values from -3 to 3
- adam_v: float32 [16, 8192, 512], P('replica', 'fsdp'), may hold values from 0.05 to 1
- pseudo_grad: float32 [16, 8192, 128], P('replica', 'fsdp'), may hold values from -2 to 2
- momentum: float32 [8192, 128], P('fsdp'), may hold values from -2 to 2
- global_frag: float32 [8192, 128], P('fsdp'), may hold values from -4 to 4
- frag_index: int32 [1], replicated, may hold values from 0 to 3
Outputs:
- values: bfloat16 [16, 2048, 512], P('replica', 'fsdp')
- input_grad: bfloat16 [16, 2048, 8192], P('replica', 'fsdp')
- new_weight: float32 [16, 8192, 512], P('replica', 'fsdp')
- new_m: float32 [16, 8192, 512], P('replica', 'fsdp')
- new_v: float32 [16, 8192, 512], P('replica', 'fsdp')
- new_global: float32 [8192, 128], P('fsdp')
- new_momentum: float32 [8192, 128], P('fsdp')
All inputs are finite; a program needn't handle non-finite values.
Results may differ from a plain program's by a relative error of at most 0.006.
Values may be sent and summed in bfloat16 or wider, within the bound.
No kernel may reach another device: no remote copies, remote signals or barrier semaphores. Data moves between devices by JAX's collectives and lax.ppermute only.
A program may use at most 128 MiB of HBM per device.

v0:
```python
import jax
import jax.numpy as jnp
from jax import lax
from jax.sharding import PartitionSpec as P

D = 8192


beta_first = 0.9
beta_second = 0.95
epsilon = 1e-08
inner_rate = 0.01
decay_rate = 0.1
outer_rate = 0.7
outer_mom = 0.9
mix_share = 0.5


def outer_update(momentum, global_frag, average):
    mom_new = outer_mom * momentum + average
    glob_new = global_frag - outer_rate * (outer_mom * mom_new + average)
    return (mom_new, glob_new)


def body(
    token_in, cotangent, weight, adam_m, adam_v, pseudo_grad, momentum, global_frag, frag_index
):
    scale = D ** (-0.5)
    tokens = token_in[0]
    upstream = cotangent[0]
    master = weight[0]
    replicas = lax.axis_size("replica")
    total = lax.psum(pseudo_grad[0].astype(jnp.bfloat16), "replica").astype(jnp.float32)
    new_momentum, new_global = outer_update(momentum, global_frag, total / replicas)
    weight_bf = master.astype(jnp.bfloat16)
    piece = lax.all_gather(weight_bf, "fsdp", axis=0, tiled=True)
    columns = tokens
    values_acc = jnp.dot(columns, piece, preferred_element_type=jnp.float32)
    block = (
        jnp.einsum("tf,rf->tr", upstream, piece, preferred_element_type=jnp.float32) * scale
    ).astype(jnp.bfloat16)
    values = (values_acc * scale).astype(jnp.bfloat16)
    columns = tokens
    grad = lax.psum_scatter(
        jnp.einsum("tr,tf->rf", columns, upstream, preferred_element_type=jnp.float32) * scale,
        "fsdp",
        scatter_dimension=0,
        tiled=True,
    )
    new_m = beta_first * adam_m[0] + (1.0 - beta_first) * grad
    new_v = beta_second * adam_v[0] + (1.0 - beta_second) * grad * grad
    stepped = master - inner_rate * (new_m / (jnp.sqrt(new_v) + epsilon) + decay_rate * master)
    frag_width = global_frag.shape[1]
    start = frag_index[0] * frag_width
    piece = lax.dynamic_slice_in_dim(stepped, start, frag_width, 1)
    mixed = mix_share * piece + (1.0 - mix_share) * new_global
    new_weight = lax.dynamic_update_slice_in_dim(stepped, mixed, start, 1)
    return (
        values[None],
        block[None],
        new_weight[None],
        new_m[None],
        new_v[None],
        new_global,
        new_momentum,
    )


def solution(mesh):
    in_specs = (
        P("replica", "fsdp", None),
        P("replica", "fsdp", None),
        P("replica", "fsdp", None),
        P("replica", "fsdp", None),
        P("replica", "fsdp", None),
        P("replica", "fsdp", None),
        P("fsdp", None),
        P("fsdp", None),
        P(),
    )
    out_specs = (
        P("replica", "fsdp", None),
        P("replica", "fsdp", None),
        P("replica", "fsdp", None),
        P("replica", "fsdp", None),
        P("replica", "fsdp", None),
        P("fsdp", None),
        P("fsdp", None),
    )
    return jax.shard_map(body, mesh=mesh, in_specs=in_specs, out_specs=out_specs, check_vma=False)
```

profile of v0, /device:TPU:64, one launch (start us, length us, event | category | flops | bytes accessed | tf_op | source)
XLA Modules:
  0.0 264.1 jit_solution(6237533161724754626)
XLA Ops:
  8.0 0.0 copy-start
  8.0 0.0 all-gather.2.cloned.1.call-start
  8.1 2.2 bitcast_convert_fusion
  10.3 0.0 all-gather.2.cloned.1.call-update
  10.3 0.0 reduce-scatter.2.cloned.1.call-start
  10.4 0.0 copy-done
  10.4 9.0 %convolution_multiply_fusion = f32[8192,512]{1,0:T(8,128)} fusion(bf16[1,128,8192]{2,1,0:T(8,128)(2,1)S(1)} %copy-done, bf16[1,128,512]{2,1,0:T(8,128)(2,1)} %param.10), kind=kOutput, calls=%fused_computation | convolution fusion | flops 1077936128 | bytes 19005440 | tf_op jit(solution)/shard_map/tr,tf->rf/dot_general | solution.py:45
  19.4 0.0 copy-start.4
  19.4 0.0 copy-start.2
  19.4 0.0 reduce-scatter.2.cloned.1.call-update
  19.4 0.0 all-reduce.2.cloned.1.call-start
  19.5 0.9 copy-done.4
  20.3 0.7 convert_bitcast_fusion
  21.0 0.0 all-reduce.2.cloned.1.call-update
  21.7 70.8 %all-gather.2.cloned.1.call-done = bf16[8192,512]{1,0:T(8,128)(2,1)} async-done(((bf16[512,512]{1,0:T(8,128)(2,1)}), bf16[8192,512]{1,0:T(8,128)(2,1)}) %all-gather.2.cloned.1.call-update) | async-done | bytes 8388624 | tf_op jit(solution)/shard_map/all_gather | solution.py:36
  92.5 0.0 copy-done.2
  92.5 0.0 copy-start.1
  92.5 7.7 %fusion.1 = bf16[1,128,8192]{2,1,0:T(8,128)(2,1)} fusion(bf16[8192,512]{1,0:T(8,128)(2,1)} %all-gather.2.cloned.1.call-done, bf16[1,128,512]{2,1,0:T(8,128)(2,1)S(1)} %copy-done.2), kind=kOutput, calls=%fused_computation.3 | convolution fusion | flops 1075838976 | bytes 10616832 | tf_op jit(solution)/shard_map/tf,rf->tr/dot_general | solution.py:40
  100.2 0.0 copy-done.1
  100.2 1.9 fusion.11
  102.1 0.0 copy-start.3
  102.1 147.5 %reduce-scatter.2.cloned.1.call-done = f32[512,512]{1,0:T(8,128)} async-done(((f32[8192,512]{1,0:T(8,128)}), f32[512,512]{1,0:T(8,128)}) %reduce-scatter.2.cloned.1.call-update) | async-done | bytes 1048592 | tf_op jit(solution)/shard_map/reduce_scatter | solution.py:44
  249.6 4.2 %fusion.18 = (f32[1,512,512]{2,1,0:T(8,128)}, f32[512,512]{1,0:T(8,128)S(1)}, f32[1,512,512]{2,1,0:T(8,128)}) fusion(f32[512,512]{1,0:T(8,128)} %reduce-scatter.2.cloned.1.call-done, f32[1,512,512]{2,1,0:T(8,128)} %param.13, f32[1,512,512]{2,1,0:T(8,128)} %param.12, f32[1,512,512]{2,1,0:T(8,128)} %param.11), kind=kLoop, calls=%fused_computation.19 | loop fusion | flops 3407872 | bytes 7340032 | tf_op jit(solution)/shard_map/broadcast_in_dim | solution.py:63
  253.8 1.0 copy.17
  254.7 0.0 all-reduce.2.cloned.1.call-done
  254.7 0.0 copy-done.3
  254.7 2.0 bitcast_dynamic-update-slice_fusion
Async XLA Ops:
  8.0 2.4 copy-start
  8.0 84.4 %all-gather.2.cloned.1.call-start = ((), (), s32[]{:S(2)}) async-start(), calls=%async_computation.1 | async-start | bytes 8912896 | tf_op jit(solution)/shard_map/all_gather | solution.py:36
  10.3 239.2 %reduce-scatter.2.cloned.1.call-start = ((), (), s32[]{:S(2)}) async-start(), calls=%async_computation.2 | async-start | bytes 17825792 | tf_op jit(solution)/shard_map/reduce_scatter | solution.py:44
  19.4 0.9 copy-start.4
  19.4 73.1 %copy-start.2 = (bf16[1,128,512]{2,1,0:T(8,128)(2,1)S(1)}, bf16[1,128,512]{2,1,0:T(8,128)(2,1)}, u32[]{:S(2)}) copy-start(bf16[1,128,512]{2,1,0:T(8,128)(2,1)} %param.10) | copy-start | bytes 393220
  19.4 235.3 %all-reduce.2.cloned.1.call-start = ((), (), s32[]{:S(2)}) async-start(), calls=%async_computation.3 | async-start | bytes 262144 | tf_op jit(solution)/shard_map/psum | solution.py:33
  92.5 7.7 %copy-start.1 = (bf16[8192,512]{1,0:T(8,128)(2,1)S(1)}, bf16[8192,512]{1,0:T(8,128)(2,1)}, u32[]{:S(2)}) copy-start(bf16[8192,512]{1,0:T(8,128)(2,1)} %all-gather.2.cloned.1.call-done) | copy-start | bytes 25165828
  102.1 152.7 %copy-start.3 = (f32[512,128]{1,0:T(8,128)S(1)}, f32[512,128]{1,0:T(8,128)}, u32[]{:S(2)}) copy-start(f32[512,128]{1,0:T(8,128)} %param.16) | copy-start | bytes 786436
Sparse Core Ops, SparseCore 0:
  12.2 80.2 all-gather.1
  97.0 152.4 reduce-scatter.1
Sparse Core Ops, SparseCore 1:
  23.1 133.0 all-reduce.1
where the time goes:
time: 265 us; the launch traced here: 264 us
  waiting for transfers between devices  218 us (82%)
  matrix products  18.6 us (7%)
  between operations  16.2 us (6%)
  other arithmetic  9.07 us (3%)
    reduce_scatter x1, waiting for transfers between devices, body(): lax.psum_scatter(jnp.einsum('tr,tf->rf', columns, upstream, preferred_ele...  147 us
    all_gather x1, waiting for transfers between devices, body(): piece = lax.all_gather(weight_bf, 'fsdp', axis=0, tiled=True)  70.8 us
    dot_general x1, matrix products, body(): jnp.einsum('tr,tf->rf', columns, upstream, preferred_element_type=jnp.flo...  9.01 us
    dot_general x1, matrix products, body(): jnp.einsum('tf,rf->tr', upstream, piece, preferred_element_type=jnp.float32)  7.68 us
  transfers between devices with their start and end apart: 3, of which 2 were waited for; matrix products, arithmetic and copies ran while one was open for 9% of the time, Pallas kernels for 0%

commit v1 on v0

--- a/solution.py
+++ b/solution.py
@@ -4,7 +4,6 @@
 from jax.sharding import PartitionSpec as P
 
 D = 8192
-
 
 beta_first = 0.9
 beta_second = 0.95
@@ -14,6 +13,38 @@
 outer_rate = 0.7
 outer_mom = 0.9
 mix_share = 0.5
+
+NY = 4
+
+
+def fsdp_permute(value, target):
+    pairs = []
+    for i in range(16):
+        x, y, c = i // 8, (i // 2) % NY, i % 2
+        x2, y2, c2 = target(x, y, c)
+        pairs.append((i, ((x2 % 2) * NY + y2 % NY) * 2 + c2 % 2))
+    return lax.ppermute(value, "fsdp", pairs)
+
+
+def swap_x(value):
+    return fsdp_permute(value, lambda x, y, c: (x + 1, y, c))
+
+
+def swap_core(value):
+    return fsdp_permute(value, lambda x, y, c: (x, y, c + 1))
+
+
+def shift_y(value, step):
+    return fsdp_permute(value, lambda x, y, c: (x, y + step, c))
+
+
+def replica_sum(value):
+    total = value
+    for bit in (4, 2, 1, 8):
+        sent = total.astype(jnp.bfloat16)
+        other = lax.ppermute(sent, "replica", [(i, i ^ bit) for i in range(16)])
+        total = sent.astype(jnp.float32) + other.astype(jnp.float32)
+    return total
 
 
 def outer_update(momentum, global_frag, average):
@@ -29,24 +60,58 @@
     tokens = token_in[0]
     upstream = cotangent[0]
     master = weight[0]
-    replicas = lax.axis_size("replica")
-    total = lax.psum(pseudo_grad[0].astype(jnp.bfloat16), "replica").astype(jnp.float32)
-    new_momentum, new_global = outer_update(momentum, global_frag, total / replicas)
+    device = lax.axis_index("fsdp")
+    x_hi, y_at, core = device // 8, (device // 2) % NY, device % 2
+    half = D // 2
+
+    up_x = swap_x(upstream)
+    tok_x = swap_x(lax.dynamic_slice_in_dim(tokens, (1 - x_hi) * half, half, 1))
+    tok_o = lax.dynamic_slice_in_dim(tokens, x_hi * half, half, 1)
+
     weight_bf = master.astype(jnp.bfloat16)
-    piece = lax.all_gather(weight_bf, "fsdp", axis=0, tiled=True)
-    columns = tokens
-    values_acc = jnp.dot(columns, piece, preferred_element_type=jnp.float32)
-    block = (
-        jnp.einsum("tf,rf->tr", upstream, piece, preferred_element_type=jnp.float32) * scale
-    ).astype(jnp.bfloat16)
-    values = (values_acc * scale).astype(jnp.bfloat16)
-    columns = tokens
-    grad = lax.psum_scatter(
-        jnp.einsum("tr,tf->rf", columns, upstream, preferred_element_type=jnp.float32) * scale,
-        "fsdp",
-        scatter_dimension=0,
-        tiled=True,
-    )
+    gathered = jnp.zeros((NY, 512, 512), jnp.bfloat16)
+    for step, part in ((0, weight_bf), (1, None), (-1, None), (2, None)):
+        part = shift_y(weight_bf, -step) if part is None else part
+        gathered = lax.dynamic_update_slice_in_dim(gathered, part[None], (y_at + step) % NY, 0)
+    other = swap_core(gathered)
+    rows = jnp.zeros((NY, 2, 512, 512), jnp.bfloat16)
+    rows = lax.dynamic_update_slice_in_dim(rows, gathered[:, None], core, 1)
+    rows = lax.dynamic_update_slice_in_dim(rows, other[:, None], 1 - core, 1)
+    rows = rows.reshape(half, 512)
+
+    def back(up):
+        return (
+            jnp.einsum("tf,rf->tr", up, rows, preferred_element_type=jnp.float32) * scale
+        ).astype(jnp.bfloat16)
+
+    back_x = swap_x(back(up_x))
+    block = jnp.zeros((128, D), jnp.bfloat16)
+    block = lax.dynamic_update_slice_in_dim(block, back(upstream), x_hi * half, 1)
+    block = lax.dynamic_update_slice_in_dim(block, back_x, (1 - x_hi) * half, 1)
+
+    part_x = jnp.dot(tok_x, rows, preferred_element_type=jnp.float32).astype(jnp.bfloat16)
+    part_o = jnp.dot(tok_o, rows, preferred_element_type=jnp.float32)
+    values = ((part_o + swap_x(part_x).astype(jnp.float32)) * scale).astype(jnp.bfloat16)
+
+    tok_2 = jnp.stack([tok_o, tok_x]).reshape(2, 128, NY, 2, 512)
+    up_2 = jnp.stack([upstream, up_x])
+    tok_mine = lax.dynamic_index_in_dim(tok_2, core, 3, False)
+    tok_other = swap_core(lax.dynamic_index_in_dim(tok_2, 1 - core, 3, False))
+    up_other = swap_core(up_2)
+    tok_4 = jnp.concatenate([tok_mine, tok_other]).reshape(512, NY, 512)
+    up_4 = jnp.concatenate([up_2, up_other]).reshape(512, 512)
+
+    def grad_of(step):
+        cols = lax.dynamic_index_in_dim(tok_4, (y_at + step) % NY, 1, False)
+        return jnp.einsum("tr,tf->rf", cols, up_4, preferred_element_type=jnp.float32) * scale
+
+    grad = grad_of(0)
+    for step in (2, 1, -1):
+        grad = grad + shift_y(grad_of(step).astype(jnp.bfloat16), step).astype(jnp.float32)
+
+    total = replica_sum(pseudo_grad[0])
+    new_momentum, new_global = outer_update(momentum, global_frag, total / 16)
+
     new_m = beta_first * adam_m[0] + (1.0 - beta_first) * grad
     new_v = beta_second * adam_v[0] + (1.0 - beta_second) * grad * grad
     stepped = master - inner_rate * (new_m / (jnp.sqrt(new_v) + epsilon) + decay_rate * master)

time: 265 us -> 120 us (0.45)
  waiting for transfers between devices: 218 us -> 25.7 us
  local copies, waits for them, and re-layouts: 1.86 us -> 27.8 us
  starting transfers between devices: 0.12 us -> 25.7 us
  between operations: 16.2 us -> 1.66 us
  other arithmetic: 9.07 us -> 15.9 us
  matrix products: 18.6 us -> 22.4 us
    reduce_scatter x1 -> x0, waiting for transfers between devices: 147 us -> none  [body(): lax.psum_scatter(jnp.einsum('tr,tf->rf', columns, upstream, preferred_ele...]
    all_gather x1 -> x0, waiting for transfers between devices: 70.8 us -> none  [body(): piece = lax.all_gather(weight_bf, 'fsdp', axis=0, tiled=True)]
    ppermute x0 -> x17, starting transfers between devices: none -> 25.7 us  [the longest x13 16.7 us: fsdp_permute(): return lax.ppermute(value, 'fsdp', pairs)]
    ppermute x0 -> x17, waiting for transfers between devices: none -> 25.7 us  [the longest x13 20.4 us: fsdp_permute(): return lax.ppermute(value, 'fsdp', pairs)]
    dynamic_update_slice x0 -> x7, local copies, waits for them, and re-layouts: none -> 8 us  [the longest x3 3.24 us: body(): lax.dynamic_update_slice_in_dim(gathered, part[None], (y_at + step) % NY, 0)]
    dynamic_slice x0 -> x4, local copies, waits for them, and re-layouts: none -> 7.55 us  [the longest x2 3.02 us: body(): tok_x = swap_x(lax.dynamic_slice_in_dim(tokens, (1 - x_hi) * half, half, 1))]
    unnamed x11 -> x38, local copies, waits for them, and re-layouts: 1.86 us -> 7.29 us
    broadcast_in_dim x0 -> x5, local copies, waits for them, and re-layouts: none -> 4.84 us  [the longest x3 2.35 us: body(): block[None]]
  transfers between devices with their start and end apart: 3 -> 17, of which waited for: 2 -> 7; matrix products, arithmetic and copies ran while one was open for 9% -> 47% of each run, Pallas kernels for 0% -> 0%
where the time goes in v1:
time: 120 us; the launch traced here: 119 us
  local copies, waits for them, and re-layouts  27.8 us (23%)
  starting transfers between devices  25.7 us (21%)
  waiting for transfers between devices  25.7 us (21%)
  matrix products  22.4 us (19%)
  other arithmetic  15.9 us (13%)
  between operations  1.66 us (1%)
    ppermute x13, waiting for transfers between devices, fsdp_permute(): return lax.ppermute(value, 'fsdp', pairs)  20.4 us
    ppermute x13, starting transfers between devices, fsdp_permute(): return lax.ppermute(value, 'fsdp', pairs)  16.7 us
    ppermute x4, starting transfers between devices, replica_sum(): other = lax.ppermute(sent, 'replica', [(i, i ^ bit) for i in range(16)])  8.98 us
    dot_general x4, matrix products, grad_of(): jnp.einsum('tr,tf->rf', cols, up_4, preferred_element_type=jnp.float32)  7.9 us
    unnamed x38, local copies, waits for them, and re-layouts  7.29 us
    dot_general x2, matrix products, back(): jnp.einsum('tf,rf->tr', up, rows, preferred_element_type=jnp.float32)  7.03 us
    ppermute x4, waiting for transfers between devices, replica_sum(): other = lax.ppermute(sent, 'replica', [(i, i ^ bit) for i in range(16)])  5.31 us
    dot_general x1, matrix products, body(): jnp.dot(tok_x, rows, preferred_element_type=jnp.float32)  3.92 us
  transfers between devices with their start and end apart: 17, of which 7 were waited for; matrix products, arithmetic and copies ran while one was open for 47% of the time, Pallas kernels for 0%

profile of v1, /device:TPU:64, one launch (start us, length us, event | category | flops | bytes accessed | tf_op | source)
XLA Modules:
  0.0 119.1 jit_solution(13560591119108236275)
XLA Ops:
  0.6 2.1 %bitcast_convert_fusion = bf16[512,512]{1,0:T(8,128)(2,1)} fusion(f32[1,512,512]{2,1,0:T(8,128)} %param.11), kind=kLoop, calls=%fused_computation.36 | loop fusion | flops 262144 | bytes 1572864 | tf_op jit(solution)/shard_map/convert_element_type | solution.py:71
  2.7 3.0 %collective-permute-start = (bf16[512,512]{1,0:T(8,128)(2,1)}, bf16[512,512]{1,0:T(8,128)(2,1)}, u32[]{:S(2)}, u32[]{:S(2)}) collective-permute-start(bf16[512,512]{1,0:T(8,128)(2,1)} %bitcast_convert_fusion), channel_id=1, source_target_pairs={{0,6},{1,7},{2,0},{3,1},{4,2},{5,3},{6,4},{7,5},{8,14},{9,15},{10,... | collective-permute-start | bytes 1572872 | tf_op jit(solution)/shard_map/ppermute | solution.py:26
  5.7 2.2 %collective-permute-start.2 = (bf16[512,512]{1,0:T(8,128)(2,1)}, bf16[512,512]{1,0:T(8,128)(2,1)}, u32[]{:S(2)}, u32[]{:S(2)}) collective-permute-start(bf16[512,512]{1,0:T(8,128)(2,1)} %bitcast_convert_fusion), channel_id=1, source_target_pairs={{0,4},{1,5},{2,6},{3,7},{4,0},{5,1},{6,2},{7,3},{8,12},{9,13},{10,... | collective-permute-start | bytes 1572872 | tf_op jit(solution)/shard_map/ppermute | solution.py:26
  7.9 1.7 %constant_dynamic-slice_fusion = (bf16[1,128,4096]{2,1,0:T(8,128)(2,1)S(1)}, bf16[1,128,4096]{2,1,0:T(8,128)(2,1)S(1)}) fusion(bf16[1,128,8192]{2,1,0:T(8,128)(2,1)} %param.9, s32[]{:T(128)S(6)} %select_n.95, s32[]{:T(128)S(6)} %select_n.81), kind=kLoop, calls=%fused_computation.69 | loop fusion | bytes 4194312 | tf_op jit(solution)/shard_map/dynamic_slice | solution.py:68
  11.0 3.0 %collective-permute-start.4 = (bf16[128,4096]{0,1:T(8,128)(2,1)}, bf16[128,4096]{0,1:T(8,128)(2,1)}, u32[]{:S(2)}, u32[]{:S(2)}) collective-permute-start(bf16[128,4096]{0,1:T(8,128)(2,1)} %bitcast.9), channel_id=1, source_target_pairs={{0,8},{1,9},{2,10},{3,11},{4,12},{5,13},{6,14},{7,15},{8,0},{9,1},... | collective-permute-start | bytes 3145736 | tf_op jit(solution)/shard_map/ppermute | solution.py:26
  14.0 5.5 %collective-permute-start.13 = (bf16[512,128]{1,0:T(8,128)(2,1)S(1)}, bf16[512,128]{1,0:T(8,128)(2,1)S(1)}, u32[]{:S(2)}, u32[]{:S(2)}) collective-permute-start(bf16[512,128]{1,0:T(8,128)(2,1)S(1)} %convert_bitcast_fusion), channel_id=1, source_target_pairs={{0,64},{16,80},{32,96},{48,112},{64,0},{80,16},{96,32},{112,48},{1... | collective-permute-start | bytes 393224 | tf_op jit(solution)/shard_map/ppermute | solution.py:45
  22.4 2.6 %collective-permute-done.13 = bf16[512,128]{1,0:T(8,128)(2,1)S(1)} collective-permute-done((bf16[512,128]{1,0:T(8,128)(2,1)S(1)}, bf16[512,128]{1,0:T(8,128)(2,1)S(1)}, u32[]{:S(2)}, u32[]{:S(2)}) %collective-permute-start.13) | collective-permute-done | bytes 131104 | tf_op jit(solution)/shard_map/ppermute | solution.py:45
  29.5 2.3 %collective-permute-done.1 = bf16[512,512]{1,0:T(8,128)(2,1)} collective-permute-done((bf16[512,512]{1,0:T(8,128)(2,1)}, bf16[512,512]{1,0:T(8,128)(2,1)}, u32[]{:S(2)}, u32[]{:S(2)}) %collective-permute-start.1) | collective-permute-done | bytes 524320 | tf_op jit(solution)/shard_map/ppermute | solution.py:26
  34.2 4.1 %collective-permute-done.4 = bf16[128,4096]{0,1:T(8,128)(2,1)} collective-permute-done((bf16[128,4096]{0,1:T(8,128)(2,1)}, bf16[128,4096]{0,1:T(8,128)(2,1)}, u32[]{:S(2)}, u32[]{:S(2)}) %collective-permute-start.4) | collective-permute-done | bytes 1048608 | tf_op jit(solution)/shard_map/ppermute | solution.py:26
  38.3 2.7 %fusion.15 = (bf16[2,128,4,1,512]{1,4,3,2,0:T(8,128)(2,1)}, bf16[2,128,4,1,512]{1,4,3,2,0:T(8,128)(2,1)}) fusion(s32[]{:T(128)S(6)} %select_n.93, bf16[1,128,4,2,512]{1,4,3,2,0:T(8,128)(2,1)S(1)} %bitcast.95, bf16[1,128,4,2,512]{1,4,3,2,0:T(8,128)(2,1)} %bitcast.18, s32[]{:T(128)S(6)} %select_n.94), kind=kLoop, calls=%fused_computation.31 | loop fusion | flops 1048576 | bytes 4194312 | tf_op jit(solution)/shard_map/stack | solution.py:96
  41.0 2.3 %copy.27 = bf16[2,128,4,1,512]{4,1,3,2,0:T(8,128)(2,1)} copy(bf16[2,128,4,1,512]{1,4,3,2,0:T(8,128)(2,1)} %get-tuple-element.14) | data formatting | bytes 2097152 | tf_op jit(solution)/shard_map/jit(dynamic_index_in_dim)/dynamic_slice | solution.py:99
  44.2 2.0 %collective-permute-start.15 = (bf16[512,128]{1,0:T(8,128)(2,1)S(1)}, bf16[512,128]{1,0:T(8,128)(2,1)}, u32[]{:S(2)}, u32[]{:S(2)}) collective-permute-start(bf16[512,128]{1,0:T(8,128)(2,1)S(1)} %add_convert_fusion.1), channel_id=1, source_target_pairs={{0,16},{16,0},{32,48},{48,32},{64,80},{80,64},{96,112},{112,96},{1... | collective-permute-start | bytes 393224 | tf_op jit(solution)/shard_map/ppermute | solution.py:45
  47.9 2.7 %collective-permute-done.15 = bf16[512,128]{1,0:T(8,128)(2,1)} collective-permute-done((bf16[512,128]{1,0:T(8,128)(2,1)S(1)}, bf16[512,128]{1,0:T(8,128)(2,1)}, u32[]{:S(2)}, u32[]{:S(2)}) %collective-permute-start.15) | collective-permute-done | bytes 131104 | tf_op jit(solution)/shard_map/ppermute | solution.py:45
  50.5 1.6 %add_convert_fusion = bf16[512,128]{1,0:T(8,128)(2,1)} fusion(bf16[512,128]{1,0:T(8,128)(2,1)} %collective-permute-done.15, bf16[512,128]{1,0:T(8,128)(2,1)S(1)} %add_convert_fusion.1), kind=kLoop, calls=%fused_computation.58 | loop fusion | flops 262144 | bytes 393216 | tf_op jit(solution)/shard_map/convert_element_type | solution.py:44
  52.1 1.5 %collective-permute-start.16 = (bf16[512,128]{1,0:T(8,128)(2,1)}, bf16[512,128]{1,0:T(8,128)(2,1)S(1)}, u32[]{:S(2)}, u32[]{:S(2)}) collective-permute-start(bf16[512,128]{1,0:T(8,128)(2,1)} %add_convert_fusion), channel_id=1, source_target_pairs={{0,128},{16,144},{32,160},{48,176},{64,192},{80,208},{96,224},{112... | collective-permute-start | bytes 393224 | tf_op jit(solution)/shard_map/ppermute | solution.py:45
  53.6 1.8 %pad_maximum_fusion.1 = bf16[4,128,512]{2,1,0:T(8,128)(2,1)} fusion(bf16[2,128,512]{2,1,0:T(8,128)(2,1)} %collective-permute-done.9, bf16[1,128,512]{2,1,0:T(8,128)(2,1)S(1)} %bitcast.103, bf16[1,128,512]{2,1,0:T(8,128)(2,1)S(1)} %copy-done.6), kind=kLoop, calls=%fused_computation.39 | loop fusion | flops 524288 | bytes 1048576 | tf_op jit(solution)/shard_map/concatenate | solution.py:102
  55.4 2.3 %broadcast_in_dim.44 = bf16[4,2,512,512]{3,2,1,0:T(8,128)(2,1)} broadcast(bf16[]{:T(256)} %constant.119.clone.1), dimensions={} | broadcast | bytes 4194306 | tf_op jit(solution)/shard_map/broadcast_in_dim | solution.py:77
  57.8 1.4 %bitcast_dynamic-update-slice_fusion = bf16[4,2,512,512]{3,2,1,0:T(8,128)(2,1)} fusion(bf16[4,2,512,512]{3,2,1,0:T(8,128)(2,1)} %broadcast_in_dim.44, s32[]{:T(128)S(6)} %select_n.93, bf16[4,512,512]{2,1,0:T(8,128)(2,1)S(1)} %bitcast_dynamic-update-slice_fusion.2), kind=kLoop, calls=%fused_computation.11 | loop fusion | bytes 4194308 | tf_op jit(solution)/shard_map/dynamic_update_slice | solution.py:78
  59.2 2.3 %copy.26 = bf16[2,128,4,1,512]{4,1,3,2,0:T(8,128)(2,1)} copy(bf16[2,128,4,1,512]{1,4,3,2,0:T(8,128)(2,1)} %get-tuple-element.13) | data formatting | bytes 2097152 | tf_op jit(solution)/shard_map/jit(dynamic_index_in_dim)/dynamic_slice | solution.py:98
  61.5 1.7 %pad_maximum_fusion = bf16[4,128,4,512]{3,1,2,0:T(8,128)(2,1)S(1)} fusion(bf16[2,128,4,512]{3,1,2,0:T(8,128)(2,1)} %collective-permute-done.8, bf16[2,128,4,512]{3,1,2,0:T(8,128)(2,1)} %bitcast.96), kind=kLoop, calls=%fused_computation.10 | loop fusion | flops 1048576 | bytes 4194304 | tf_op jit(solution)/shard_map/concatenate | solution.py:101
  70.0 1.9 %collective-permute-start.10 = (bf16[512,512]{1,0:T(8,128)(2,1)}, bf16[512,512]{1,0:T(8,128)(2,1)}, u32[]{:S(2)}, u32[]{:S(2)}) collective-permute-start(bf16[512,512]{1,0:T(8,128)(2,1)} %fusion.7), channel_id=1, source_target_pairs={{0,4},{1,5},{2,6},{3,7},{4,0},{5,1},{6,2},{7,3},{8,12},{9,13},{10,... | collective-permute-start | bytes 1572872 | tf_op jit(solution)/shard_map/ppermute | solution.py:26
  72.0 3.1 %bitcast_dynamic-update-slice_fusion.1 = bf16[4,2,512,512]{3,2,1,0:T(8,128)(2,1)} fusion(bf16[4,2,512,512]{3,2,1,0:T(8,128)(2,1)} %bitcast_dynamic-update-slice_fusion, s32[]{:T(128)S(6)} %select_n.94, bf16[4,512,512]{2,1,0:T(8,128)(2,1)} %collective-permute-done.3), kind=kLoop, calls=%fused_computation.12 | loop fusion | bytes 4194308 | tf_op jit(solution)/shard_map/dynamic_update_slice | solution.py:79
  75.1 3.9 %convolution_convert_fusion = bf16[128,512]{1,0:T(8,128)(2,1)} fusion(bf16[128,4096]{0,1:T(8,128)(2,1)} %collective-permute-done.4, bf16[4096,512]{1,0:T(8,128)(2,1)} %bitcast.8), kind=kOutput, calls=%fused_computation.26 | convolution fusion | flops 536936448 | bytes 5373952 | tf_op jit(solution)/shard_map/dot_general | solution.py:92
  79.0 3.4 %fusion.3 = bf16[1,128,4096]{1,2,0:T(8,128)(2,1)S(1)} fusion(bf16[4096,512]{1,0:T(8,128)(2,1)} %bitcast.8, bf16[1,128,512]{2,1,0:T(8,128)(2,1)S(1)} %copy-done.6), kind=kOutput, calls=%fused_computation.5 | convolution fusion | flops 537919488 | bytes 5373952 | tf_op jit(solution)/shard_map/tf,rf->tr/dot_general | solution.py:84
  82.4 2.8 %collective-permute-start.5 = (bf16[128,512]{1,0:T(8,128)(2,1)}, bf16[128,512]{1,0:T(8,128)(2,1)S(1)}, u32[]{:S(2)}, u32[]{:S(2)}) collective-permute-start(bf16[128,512]{1,0:T(8,128)(2,1)} %convolution_convert_fusion), channel_id=1, source_target_pairs={{0,8},{1,9},{2,10},{3,11},{4,12},{5,13},{6,14},{7,15},{8,0},{9,1},... | collective-permute-start | bytes 393224 | tf_op jit(solution)/shard_map/ppermute | solution.py:26
  85.8 3.6 %fusion.2 = bf16[128,4096]{0,1:T(8,128)(2,1)S(1)} fusion(bf16[4096,512]{1,0:T(8,128)(2,1)} %bitcast.8, bf16[128,512]{1,0:T(8,128)(2,1)S(1)} %collective-permute-done.6), kind=kOutput, calls=%fused_computation.4 | convolution fusion | flops 537919488 | bytes 5373952 | tf_op jit(solution)/shard_map/tf,rf->tr/dot_general | solution.py:84
  90.3 3.7 %collective-permute-done.11 = bf16[512,512]{1,0:T(8,128)(2,1)} collective-permute-done((bf16[512,512]{1,0:T(8,128)(2,1)}, bf16[512,512]{1,0:T(8,128)(2,1)}, u32[]{:S(2)}, u32[]{:S(2)}) %collective-permute-start.11) | collective-permute-done | bytes 524320 | tf_op jit(solution)/shard_map/ppermute | solution.py:26
  94.0 4.1 %fusion.28 = (f32[1,512,512]{2,1,0:T(8,128)}, f32[512,512]{1,0:T(8,128)S(1)}, f32[1,512,512]{2,1,0:T(8,128)}) fusion(f32[1,512,512]{2,1,0:T(8,128)S(1)} %copy-done.16, f32[1,512,512]{2,1,0:T(8,128)S(1)} %copy-done.17, f32[1,512,512]{2,1,0:T(8,128)S(1)} %copy-done.1, bf16[512,512]{1,0:T(8,128)(2,1)} %collective-permute-done.12, ...), kind=kOutput, calls=%fused_computation.53 | convolution fusion | flops 273678336 | bytes 8912900 | tf_op jit(solution)/shard_map/tr,tf->rf/dot_general | solution.py:106
  99.4 1.8 %bitcast_dynamic-update-slice_fusion.5 = (f32[1,512,512]{2,1,0:T(8,128)S(1)}, f32[512,128]{1,0:T(8,128)}, f32[512,128]{1,0:T(8,128)}) fusion(f32[1,512,512]{2,1,0:T(8,128)S(1)} %copy.38, s32[]{:T(128)S(6)} %select_n.96, f32[512,512]{1,0:T(8,128)S(1)} %get-tuple-element.11, f32[512,128]{1,0:T(8,128)S(1)} %copy-done.13, ...), kind=kLoop, calls=%fused_computation.55 | loop fusion | flops 786432 | bytes 1835012 | tf_op jit(solution)/shard_map/dynamic_update_slice | solution.py:122
  102.2 3.6 %fusion.12 = bf16[1,128,512]{2,1,0:T(8,128)(2,1)} fusion(bf16[4096,512]{1,0:T(8,128)(2,1)} %bitcast.8, bf16[1,128,4096]{2,1,0:T(8,128)(2,1)S(1)} %get-tuple-element.16, bf16[128,512]{1,0:T(8,128)(2,1)S(1)} %collective-permute-done.5), kind=kOutput, calls=%fused_computation.28 | convolution fusion | flops 537133056 | bytes 5505024 | tf_op jit(solution)/shard_map/dot_general | solution.py:93
  105.8 9.0 %collective-permute-done.7 = bf16[128,4096]{0,1:T(8,128)(2,1)S(1)} collective-permute-done((bf16[128,4096]{0,1:T(8,128)(2,1)S(1)}, bf16[128,4096]{0,1:T(8,128)(2,1)S(1)}, u32[]{:S(2)}, u32[]{:S(2)}) %collective-permute-start.7) | collective-permute-done | bytes 1048608 | tf_op jit(solution)/shard_map/ppermute | solution.py:26
  115.8 1.6 %copy.25 = bf16[1,128,4096]{2,1,0:T(8,128)(2,1)S(1)} copy(bf16[1,128,4096]{1,2,0:T(8,128)(2,1)} %bitcast.106) | data formatting | bytes 2097152 | tf_op jit(solution)/shard_map/broadcast_in_dim | solution.py:125
  (76 shorter events, 25.9 us)
Async XLA Ops:
  2.7 25.7 %collective-permute-start = (bf16[512,512]{1,0:T(8,128)(2,1)}, bf16[512,512]{1,0:T(8,128)(2,1)}, u32[]{:S(2)}, u32[]{:S(2)}) collective-permute-start(bf16[512,512]{1,0:T(8,128)(2,1)} %bitcast_convert_fusion), channel_id=1, source_target_pairs={{0,6},{1,7},{2,0},{3,1},{4,2},{5,3},{6,4},{7,5},{8,14},{9,15},{10,... | collective-permute-start | bytes 1572872 | tf_op jit(solution)/shard_map/ppermute | solution.py:26
  5.7 26.1 %collective-permute-start.1 = (bf16[512,512]{1,0:T(8,128)(2,1)}, bf16[512,512]{1,0:T(8,128)(2,1)}, u32[]{:S(2)}, u32[]{:S(2)}) collective-permute-start(bf16[512,512]{1,0:T(8,128)(2,1)} %bitcast_convert_fusion), channel_id=1, source_target_pairs={{0,2},{1,3},{2,4},{3,5},{4,6},{5,7},{6,0},{7,1},{8,10},{9,11},{10,... | collective-permute-start | bytes 1572872 | tf_op jit(solution)/shard_map/ppermute | solution.py:26
  5.7 27.2 %collective-permute-start.2 = (bf16[512,512]{1,0:T(8,128)(2,1)}, bf16[512,512]{1,0:T(8,128)(2,1)}, u32[]{:S(2)}, u32[]{:S(2)}) collective-permute-start(bf16[512,512]{1,0:T(8,128)(2,1)} %bitcast_convert_fusion), channel_id=1, source_target_pairs={{0,4},{1,5},{2,6},{3,7},{4,0},{5,1},{6,2},{7,3},{8,12},{9,13},{10,... | collective-permute-start | bytes 1572872 | tf_op jit(solution)/shard_map/ppermute | solution.py:26
  9.7 4.3 %copy-start.9 = (f32[1,512,128]{2,1,0:T(8,128)S(1)}, f32[1,512,128]{2,1,0:T(8,128)}, u32[]{:S(2)}) copy-start(f32[1,512,128]{2,1,0:T(8,128)} %param.14) | copy-start | bytes 786436
  11.0 27.3 %collective-permute-start.4 = (bf16[128,4096]{0,1:T(8,128)(2,1)}, bf16[128,4096]{0,1:T(8,128)(2,1)}, u32[]{:S(2)}, u32[]{:S(2)}) collective-permute-start(bf16[128,4096]{0,1:T(8,128)(2,1)} %bitcast.9), channel_id=1, source_target_pairs={{0,8},{1,9},{2,10},{3,11},{4,12},{5,13},{6,14},{7,15},{8,0},{9,1},... | collective-permute-start | bytes 3145736 | tf_op jit(solution)/shard_map/ppermute | solution.py:26
  14.0 11.0 %collective-permute-start.13 = (bf16[512,128]{1,0:T(8,128)(2,1)S(1)}, bf16[512,128]{1,0:T(8,128)(2,1)S(1)}, u32[]{:S(2)}, u32[]{:S(2)}) collective-permute-start(bf16[512,128]{1,0:T(8,128)(2,1)S(1)} %convert_bitcast_fusion), channel_id=1, source_target_pairs={{0,64},{16,80},{32,96},{48,112},{64,0},{80,16},{96,32},{112,48},{1... | collective-permute-start | bytes 393224 | tf_op jit(solution)/shard_map/ppermute | solution.py:45
  19.7 6.0 %copy-start.6 = (bf16[1,128,512]{2,1,0:T(8,128)(2,1)S(1)}, bf16[1,128,512]{2,1,0:T(8,128)(2,1)}, u32[]{:S(2)}) copy-start(bf16[1,128,512]{2,1,0:T(8,128)(2,1)} %param.10) | copy-start | bytes 393220
  22.4 15.9 %copy-start = (bf16[1,128,4096]{1,2,0:T(8,128)(2,1)S(1)}, bf16[1,128,4096]{1,2,0:T(8,128)(2,1)}, u32[]{:S(2)}) copy-start(bf16[1,128,4096]{1,2,0:T(8,128)(2,1)} %copy.29) | copy-start | bytes 3145732
  25.7 20.5 %collective-permute-start.6 = (bf16[128,512]{1,0:T(8,128)(2,1)S(1)}, bf16[128,512]{1,0:T(8,128)(2,1)S(1)}, u32[]{:S(2)}, u32[]{:S(2)}) collective-permute-start(bf16[128,512]{1,0:T(8,128)(2,1)S(1)} %bitcast.104), channel_id=1, source_target_pairs={{0,8},{1,9},{2,10},{3,11},{4,12},{5,13},{6,14},{7,15},{8,0},{9,1},... | collective-permute-start | bytes 393224 | tf_op jit(solution)/shard_map/ppermute | solution.py:26
  27.3 13.7 %copy-start.12 = (bf16[512,128]{1,0:T(8,128)(2,1)}, bf16[512,128]{1,0:T(8,128)(2,1)S(1)}, u32[]{:S(2)}) copy-start(bf16[512,128]{1,0:T(8,128)(2,1)S(1)} %add_convert_fusion.2) | copy-start | bytes 393220
  28.5 14.8 %collective-permute-start.14 = (bf16[512,128]{1,0:T(8,128)(2,1)S(1)}, bf16[512,128]{1,0:T(8,128)(2,1)}, u32[]{:S(2)}, u32[]{:S(2)}) collective-permute-start(bf16[512,128]{1,0:T(8,128)(2,1)S(1)} %add_convert_fusion.2), channel_id=1, source_target_pairs={{0,32},{16,48},{32,0},{48,16},{64,96},{80,112},{96,64},{112,80},{1... | collective-permute-start | bytes 393224 | tf_op jit(solution)/shard_map/ppermute | solution.py:45
  34.1 37.9 %collective-permute-start.3 = (bf16[4,512,512]{2,1,0:T(8,128)(2,1)S(1)}, bf16[4,512,512]{2,1,0:T(8,128)(2,1)}, u32[]{:S(2)}, u32[]{:S(2)}) collective-permute-start(bf16[4,512,512]{2,1,0:T(8,128)(2,1)S(1)} %bitcast_dynamic-update-slice_fusion.2), channel_id=1, source_target_pairs={{0,1},{1,0},{2,3},{3,2},{4,5},{5,4},{6,7},{7,6},{8,9},{9,8},{10,11... | collective-permute-start | bytes 6291464 | tf_op jit(solution)/shard_map/ppermute | solution.py:26
  43.2 18.2 %collective-permute-start.8 = (bf16[2,128,4,512]{3,1,2,0:T(8,128)(2,1)}, bf16[2,128,4,512]{3,1,2,0:T(8,128)(2,1)}, u32[]{:S(2)}, u32[]{:S(2)}) collective-permute-start(bf16[2,128,4,512]{3,1,2,0:T(8,128)(2,1)} %bitcast.105), channel_id=1, source_target_pairs={{0,1},{1,0},{2,3},{3,2},{4,5},{5,4},{6,7},{7,6},{8,9},{9,8},{10,11... | collective-permute-start | bytes 3145736 | tf_op jit(solution)/shard_map/ppermute | solution.py:26
  44.2 6.3 %collective-permute-start.15 = (bf16[512,128]{1,0:T(8,128)(2,1)S(1)}, bf16[512,128]{1,0:T(8,128)(2,1)}, u32[]{:S(2)}, u32[]{:S(2)}) collective-permute-start(bf16[512,128]{1,0:T(8,128)(2,1)S(1)} %add_convert_fusion.1), channel_id=1, source_target_pairs={{0,16},{16,0},{32,48},{48,32},{64,80},{80,64},{96,112},{112,96},{1... | collective-permute-start | bytes 393224 | tf_op jit(solution)/shard_map/ppermute | solution.py:45
  47.0 6.6 %collective-permute-start.9 = (bf16[2,128,512]{2,1,0:T(8,128)(2,1)}, bf16[2,128,512]{2,1,0:T(8,128)(2,1)}, u32[]{:S(2)}, u32[]{:S(2)}) collective-permute-start(bf16[2,128,512]{2,1,0:T(8,128)(2,1)} %pad_maximum_fusion.2), channel_id=1, source_target_pairs={{0,1},{1,0},{2,3},{3,2},{4,5},{5,4},{6,7},{7,6},{8,9},{9,8},{10,11... | collective-permute-start | bytes 786440 | tf_op jit(solution)/shard_map/ppermute | solution.py:26
  52.1 46.5 %collective-permute-start.16 = (bf16[512,128]{1,0:T(8,128)(2,1)}, bf16[512,128]{1,0:T(8,128)(2,1)S(1)}, u32[]{:S(2)}, u32[]{:S(2)}) collective-permute-start(bf16[512,128]{1,0:T(8,128)(2,1)} %add_convert_fusion), channel_id=1, source_target_pairs={{0,128},{16,144},{32,160},{48,176},{64,192},{80,208},{96,224},{112... | collective-permute-start | bytes 393224 | tf_op jit(solution)/shard_map/ppermute | solution.py:45
  63.2 1.0 copy-start.10
  63.4 6.7 %copy-start.5 = (bf16[4,128,4,512]{3,1,0,2:T(8,128)(2,1)}, bf16[4,128,4,512]{3,1,0,2:T(8,128)(2,1)S(1)}, u32[]{:S(2)}) copy-start(bf16[4,128,4,512]{3,1,0,2:T(8,128)(2,1)S(1)} %copy.28) | copy-start | bytes 6291460
  65.5 23.9 %collective-permute-start.12 = (bf16[512,512]{1,0:T(8,128)(2,1)}, bf16[512,512]{1,0:T(8,128)(2,1)}, u32[]{:S(2)}, u32[]{:S(2)}) collective-permute-start(bf16[512,512]{1,0:T(8,128)(2,1)} %fusion.9), channel_id=1, source_target_pairs={{0,6},{1,7},{2,0},{3,1},{4,2},{5,3},{6,4},{7,5},{8,14},{9,15},{10,... | collective-permute-start | bytes 1572872 | tf_op jit(solution)/shard_map/ppermute | solution.py:26
  68.1 25.9 %collective-permute-start.11 = (bf16[512,512]{1,0:T(8,128)(2,1)}, bf16[512,512]{1,0:T(8,128)(2,1)}, u32[]{:S(2)}, u32[]{:S(2)}) collective-permute-start(bf16[512,512]{1,0:T(8,128)(2,1)} %fusion.8), channel_id=1, source_target_pairs={{0,2},{1,3},{2,4},{3,5},{4,6},{5,7},{6,0},{7,1},{8,10},{9,11},{10,... | collective-permute-start | bytes 1572872 | tf_op jit(solution)/shard_map/ppermute | solution.py:26
  70.0 24.0 %collective-permute-start.10 = (bf16[512,512]{1,0:T(8,128)(2,1)}, bf16[512,512]{1,0:T(8,128)(2,1)}, u32[]{:S(2)}, u32[]{:S(2)}) collective-permute-start(bf16[512,512]{1,0:T(8,128)(2,1)} %fusion.7), channel_id=1, source_target_pairs={{0,4},{1,5},{2,6},{3,7},{4,0},{5,1},{6,2},{7,3},{8,12},{9,13},{10,... | collective-permute-start | bytes 1572872 | tf_op jit(solution)/shard_map/ppermute | solution.py:26
  82.4 19.7 %collective-permute-start.5 = (bf16[128,512]{1,0:T(8,128)(2,1)}, bf16[128,512]{1,0:T(8,128)(2,1)S(1)}, u32[]{:S(2)}, u32[]{:S(2)}) collective-permute-start(bf16[128,512]{1,0:T(8,128)(2,1)} %convolution_convert_fusion), channel_id=1, source_target_pairs={{0,8},{1,9},{2,10},{3,11},{4,12},{5,13},{6,14},{7,15},{8,0},{9,1},... | collective-permute-start | bytes 393224 | tf_op jit(solution)/shard_map/ppermute | solution.py:26
  85.8 8.2 %copy-start.1 = (f32[1,512,512]{2,1,0:T(8,128)S(1)}, f32[1,512,512]{2,1,0:T(8,128)}, u32[]{:S(2)}) copy-start(f32[1,512,512]{2,1,0:T(8,128)} %param.11) | copy-start | bytes 3145732
  85.8 8.2 %copy-start.11 = (bf16[4,128,512]{2,1,0:T(8,128)(2,1)S(1)}, bf16[4,128,512]{2,1,0:T(8,128)(2,1)}, u32[]{:S(2)}) copy-start(bf16[4,128,512]{2,1,0:T(8,128)(2,1)} %pad_maximum_fusion.1) | copy-start | bytes 1572868
  85.8 8.2 %copy-start.16 = (f32[1,512,512]{2,1,0:T(8,128)S(1)}, f32[1,512,512]{2,1,0:T(8,128)}, u32[]{:S(2)}) copy-start(f32[1,512,512]{2,1,0:T(8,128)} %param.13) | copy-start | bytes 3145732
  85.8 8.2 %copy-start.17 = (f32[1,512,512]{2,1,0:T(8,128)S(1)}, f32[1,512,512]{2,1,0:T(8,128)}, u32[]{:S(2)}) copy-start(f32[1,512,512]{2,1,0:T(8,128)} %param.12) | copy-start | bytes 3145732
  89.4 25.4 %collective-permute-start.7 = (bf16[128,4096]{0,1:T(8,128)(2,1)S(1)}, bf16[128,4096]{0,1:T(8,128)(2,1)S(1)}, u32[]{:S(2)}, u32[]{:S(2)}) collective-permute-start(bf16[128,4096]{0,1:T(8,128)(2,1)S(1)} %fusion.2), channel_id=1, source_target_pairs={{0,8},{1,9},{2,10},{3,11},{4,12},{5,13},{6,14},{7,15},{8,0},{9,1},... | collective-permute-start | bytes 3145736 | tf_op jit(solution)/shard_map/ppermute | solution.py:26
  98.4 1.0 copy-start.14
  98.5 16.3 %copy-start.2 = (bf16[1,128,8192]{2,1,0:T(8,128)(2,1)}, bf16[1,128,8192]{2,1,0:T(8,128)(2,1)S(1)}, u32[]{:S(2)}) copy-start(bf16[1,128,8192]{2,1,0:T(8,128)(2,1)S(1)} %constant_dynamic-update-slice_fusion.1) | copy-start | bytes 6291460
  101.2 1.0 copy-start.8
  115.8 1.9 %copy-start.3 = (bf16[1,128,8192]{2,1,0:T(8,128)(2,1)S(1)}, bf16[1,128,8192]{2,1,0:T(8,128)(2,1)}, u32[]{:S(2)}) copy-start(bf16[1,128,8192]{2,1,0:T(8,128)(2,1)} %copy-done.2) | copy-start | bytes 6291460
  117.8 1.3 %copy-start.4 = (bf16[1,128,8192]{2,1,0:T(8,128)(2,1)}, bf16[1,128,8192]{2,1,0:T(8,128)(2,1)S(1)}, u32[]{:S(2)}) copy-start(bf16[1,128,8192]{2,1,0:T(8,128)(2,1)S(1)} %constant_dynamic-update-slice_fusion) | copy-start | bytes 6291460
  (3 other events, 2.6 us)

commit v2 on v0

v2 whole, which is shorter than its diff:
```python
import functools

import jax
import jax.numpy as jnp
from jax import lax
from jax.experimental import pallas as pl
from jax.experimental.pallas import tpu as pltpu
from jax.sharding import PartitionSpec as P

D = 8192
SCALE = D ** (-0.5)

beta_first = 0.9
beta_second = 0.95
epsilon = 1e-08
inner_rate = 0.01
decay_rate = 0.1
outer_rate = 0.7
outer_mom = 0.9
mix_share = 0.5

NY = 4
TOK = 128
ROWS = 512
F = 512
PIECE = NY * ROWS
VMEM = pltpu.CompilerParams(vmem_limit_bytes=40 * 1024 * 1024)


def fsdp_permute(value, target):
    pairs = []
    for i in range(16):
        x, y, c = i // 8, (i // 2) % NY, i % 2
        x2, y2, c2 = target(x, y, c)
        pairs.append((i, ((x2 % 2) * NY + y2 % NY) * 2 + c2 % 2))
    return lax.ppermute(value, "fsdp", pairs)


def swap_x(value):
    return fsdp_permute(value, lambda x, y, c: (x + 1, y, c))


def swap_core(value):
    return fsdp_permute(value, lambda x, y, c: (x, y, c + 1))


def shift_y(value, step):
    return fsdp_permute(value, lambda x, y, c: (x, y + step, c))


def replica_step(total, bit):
    sent = total.astype(jnp.bfloat16)
    other = lax.ppermute(sent, "replica", [(i, i ^ bit) for i in range(16)])
    return sent.astype(jnp.float32) + other.astype(jnp.float32)


def after(value, *others):
    return lax.optimization_barrier((value, *others))[0]


def outer_update(momentum, global_frag, average):
    mom_new = outer_mom * momentum + average
    glob_new = global_frag - outer_rate * (outer_mom * mom_new + average)
    return (mom_new, glob_new)


def shape(rows, cols, dtype=jnp.bfloat16):
    return jax.ShapeDtypeStruct((rows, cols), dtype)


SMALL = pl.CostEstimate(flops=1, bytes_accessed=1, transcendentals=0)


def here():
    device = lax.axis_index("fsdp")
    return device // (2 * NY), lax.rem(device // 2, NY), lax.rem(device, 2)


def column(x, y, c):
    return pl.ds(pl.multiple_of(((x * NY + y) * 2 + c) * ROWS, ROWS), ROWS)


def pieces_of(tokens, wanted):
    def kernel(source, *refs):
        targets, sems = refs[:-1], refs[-1]
        x, _, c = here()
        copies = []
        for i, ((dx, dc), target) in enumerate(zip(wanted, targets, strict=True)):
            for k in range(NY):
                copies.append(
                    pltpu.make_async_copy(
                        source.at[:, column(1 - x if dx else x, k, 1 - c if dc else c)],
                        target.at[:, pl.ds(k * ROWS, ROWS)],
                        sems.at[i * NY + k],
                    )
                )
        for copy in copies:
            copy.start()
        for copy in copies:
            copy.wait()

    return pl.pallas_call(
        kernel,
        in_specs=[pl.BlockSpec(memory_space=pltpu.HBM)],
        out_specs=[pl.BlockSpec(memory_space=pltpu.VMEM)] * len(wanted),
        out_shape=[shape(TOK, PIECE) for _ in wanted],
        scratch_shapes=[pltpu.SemaphoreType.DMA((NY * len(wanted),))],
        cost_estimate=SMALL,
        compiler_params=VMEM,
        name="pieces",
    )(tokens)


def input_grad_pieces(up, blocks):
    def kernel(up_ref, w0, w1, w2, w3, *outs):
        up = up_ref[...]
        for step, w in enumerate((w0, w1, w2, w3)):
            at = pl.multiple_of(lax.rem(here()[1] + step, NY) * ROWS, ROWS)
            grad = lax.dot_general(
                up, w[...], (((1,), (1,)), ((), ())), preferred_element_type=jnp.float32
            )
            grad = (grad * SCALE).astype(jnp.bfloat16)
            for k, out in enumerate(outs):
                out[:, pl.ds(at, ROWS)] = grad[k * TOK : (k + 1) * TOK]

    return pl.pallas_call(
        kernel,
        in_specs=[pl.BlockSpec(memory_space=pltpu.VMEM)] * 5,
        out_specs=[pl.BlockSpec(memory_space=pltpu.VMEM)] * 4,
        out_shape=[shape(TOK, PIECE)] * 4,
        cost_estimate=SMALL,
        compiler_params=VMEM,
        name="input_grad",
    )(up, *blocks)


def weight_grad_blocks(toks, up):
    def kernel(t0, t1, t2, t3, up_ref, g0, g1, g2, g3):
        up = up_ref[...]
        for step, out in ((2, g2), (1, g1), (3, g3), (0, g0)):
            at = pl.multiple_of(lax.rem(here()[1] + step, NY) * ROWS, ROWS)
            tok = jnp.concatenate([t[:, pl.ds(at, ROWS)] for t in (t0, t1, t2, t3)], axis=0)
            grad = lax.dot_general(
                tok, up, (((0,), (0,)), ((), ())), preferred_element_type=jnp.float32
            )
            out[...] = (grad * SCALE).astype(out.dtype)

    return pl.pallas_call(
        kernel,
        in_specs=[pl.BlockSpec(memory_space=pltpu.VMEM)] * 5,
        out_specs=[pl.BlockSpec(memory_space=pltpu.VMEM)] * 4,
        out_shape=[shape(ROWS, F, jnp.float32)] + [shape(ROWS, F)] * 3,
        cost_estimate=SMALL,
        compiler_params=VMEM,
        name="weight_grad",
    )(*toks, up)


def value_parts(toks, blocks):
    def kernel(t0, t1, t2, t3, w0, w1, w2, w3, own, far, core):
        total = jnp.zeros((4 * TOK, F), jnp.float32)
        for step, w in enumerate((w0, w1, w2, w3)):
            at = pl.multiple_of(lax.rem(here()[1] + step, NY) * ROWS, ROWS)
            tok = jnp.concatenate([t[:, pl.ds(at, ROWS)] for t in (t0, t1, t2, t3)], axis=0)
            total += jnp.dot(tok, w[...], preferred_element_type=jnp.float32)
        own[...] = total[:TOK]
        far[...] = total[TOK : 2 * TOK]
        core[...] = total[2 * TOK :]

    return pl.pallas_call(
        kernel,
        in_specs=[pl.BlockSpec(memory_space=pltpu.VMEM)] * 8,
        out_specs=[pl.BlockSpec(memory_space=pltpu.VMEM)] * 3,
        out_shape=[shape(TOK, F, jnp.float32)] * 2 + [shape(2 * TOK, F, jnp.float32)],
        cost_estimate=SMALL,
        compiler_params=VMEM,
        name="values",
    )(*toks, *blocks)


def assemble(block, parts, wanted):
    def kernel(*refs):
        sources, target, sems = refs[: len(wanted)], refs[-2], refs[-1]
        x, _, c = here()
        copies = []
        for i, ((dx, dc), source) in enumerate(zip(wanted, sources, strict=True)):
            for k in range(NY):
                copies.append(
                    pltpu.make_async_copy(
                        source.at[:, pl.ds(k * ROWS, ROWS)],
                        target.at[:, column(1 - x if dx else x, k, 1 - c if dc else c)],
                        sems.at[i * NY + k],
                    )
                )
        for copy in copies:
            copy.start()
        for copy in copies:
            copy.wait()

    ins = [pl.BlockSpec(memory_space=pltpu.VMEM)] * len(wanted)
    args, alias = list(parts), {}
    if block is not None:
        ins.append(pl.BlockSpec(memory_space=pltpu.HBM))
        args.append(block)
        alias = {len(wanted): 0}
    return pl.pallas_call(
        kernel,
        in_specs=ins,
        out_specs=pl.BlockSpec(memory_space=pltpu.HBM),
        out_shape=shape(TOK, D),
        scratch_shapes=[pltpu.SemaphoreType.DMA((NY * len(wanted),))],
        input_output_aliases=alias,
        cost_estimate=SMALL,
        compiler_params=VMEM,
        name="assemble",
    )(*args)


STRIP = 64


def adam(frag_index, grads, adam_m, adam_v, master, new_global):
    def kernel(frag, g0, g1, g2, g3, m, v, w, glob, hbm_w, hbm_m, hbm_v, new_w, new_m, new_v, sems):
        at = pl.ds(pl.multiple_of(frag[0] * 128, 128), 128)
        copies = []
        for k in range(ROWS // STRIP):
            rows = pl.ds(k * STRIP, STRIP)
            grad = g0[rows, :] + g1[rows, :].astype(jnp.float32)
            grad = grad + g2[rows, :].astype(jnp.float32)
            grad = grad + g3[rows, :].astype(jnp.float32)
            mom = beta_first * m[rows, :] + (1.0 - beta_first) * grad
            var = beta_second * v[rows, :] + (1.0 - beta_second) * grad * grad
            new_m[rows, :] = mom
            new_v[rows, :] = var
            old = w[rows, :]
            new_w[rows, :] = old - inner_rate * (
                mom / (jnp.sqrt(var) + epsilon) + decay_rate * old
            )
            new_w[rows, at] = mix_share * new_w[rows, at] + (1.0 - mix_share) * glob[rows, :]
            for i, (source, target) in enumerate(
                ((new_w, hbm_w), (new_m, hbm_m), (new_v, hbm_v))
            ):
                copy = pltpu.make_async_copy(source.at[rows], target.at[rows], sems.at[i, k])
                copy.start()
                copies.append(copy)
        for copy in copies:
            copy.wait()

    return pl.pallas_call(
        kernel,
        in_specs=[pl.BlockSpec(memory_space=pltpu.SMEM)]
        + [pl.BlockSpec(memory_space=pltpu.VMEM)] * 8,
        out_specs=[pl.BlockSpec(memory_space=pltpu.HBM)] * 3,
        out_shape=[shape(ROWS, F, jnp.float32)] * 3,
        scratch_shapes=[pltpu.VMEM((ROWS, F), jnp.float32)] * 3
        + [pltpu.SemaphoreType.DMA((3, ROWS // STRIP))],
        cost_estimate=SMALL,
        compiler_params=VMEM,
        name="adam",
    )(frag_index, *grads, adam_m, adam_v, master, new_global)


def body(
    token_in, cotangent, weight, adam_m, adam_v, pseudo_grad, momentum, global_frag, frag_index
):
    tokens = token_in[0]
    up_own = cotangent[0]
    master = weight[0]

    (send_far,) = pieces_of(tokens, ((1, 1),))
    far = swap_x(send_far)
    up_x = swap_x(up_own)
    weight_bf = master.astype(jnp.bfloat16)
    block_1 = shift_y(weight_bf, -1)
    block_3 = shift_y(weight_bf, 1)
    total = replica_step(pseudo_grad[0], 8)
    tok_own, send_core, send_x = pieces_of(after(tokens, send_far), ((0, 0), (0, 1), (1, 0)))
    up_2 = jnp.concatenate([up_own, up_x])
    up_4 = jnp.concatenate([up_2, swap_core(after(up_2, total))])
    tok_core = swap_core(after(send_core, up_4))
    tok_x = swap_x(after(send_x, total))
    total = replica_step(total, 1)
    tok_far = swap_core(far)
    block_2 = shift_y(after(weight_bf, block_1, block_3), 2)
    total = replica_step(total, 2)
    total = replica_step(total, 4)
    new_momentum, new_global = outer_update(momentum, global_frag, total / 16)
    toks = (tok_own, tok_x, tok_core, tok_far)
    blocks = (weight_bf, block_1, block_2, block_3)

    ig_own, ig_x, ig_core, ig_far = input_grad_pieces(up_4, blocks)
    back_far = swap_core(ig_far)
    back_x = swap_x(ig_x)
    back_core = swap_core(ig_core)
    back_other = swap_x(back_far)

    g0, g1, g2, g3 = weight_grad_blocks(toks, after(up_4, new_global))
    r2 = shift_y(g2, 2)
    r1 = shift_y(after(g1, r2), 1)
    r3 = shift_y(after(g3, r2), -1)

    val_own, val_x, val_core = value_parts(toks, blocks)
    val_back = swap_core(val_core)
    val_far = swap_x((val_x + val_back[TOK:]).astype(jnp.bfloat16))
    values = val_own + val_back[:TOK] + val_far.astype(jnp.float32)
    values = (values * SCALE).astype(jnp.bfloat16)

    block = assemble(None, (ig_own, back_core), ((0, 0), (0, 1)))
    new_weight, new_m, new_v = adam(
        frag_index, (g0, r1, r2, r3), adam_m[0], adam_v[0], master, new_global
    )
    block = assemble(block, (back_x, back_other), ((1, 0), (1, 1)))
    return (
        values[None],
        block[None],
        new_weight[None],
        new_m[None],
        new_v[None],
        new_global,
        new_momentum,
    )


def solution(mesh):
    in_specs = (
        P("replica", "fsdp", None),
        P("replica", "fsdp", None),
        P("replica", "fsdp", None),
        P("replica", "fsdp", None),
        P("replica", "fsdp", None),
        P("replica", "fsdp", None),
        P("fsdp", None),
        P("fsdp", None),
        P(),
    )
    out_specs = (
        P("replica", "fsdp", None),
        P("replica", "fsdp", None),
        P("replica", "fsdp", None),
        P("replica", "fsdp", None),
        P("replica", "fsdp", None),
        P("fsdp", None),
        P("fsdp", None),
    )
    return jax.shard_map(body, mesh=mesh, in_specs=in_specs, out_specs=out_specs, check_vma=False)
```

time: 265 us -> 85.4 us (0.32)
  waiting for transfers between devices: 218 us -> 35.5 us
  starting transfers between devices: 0.12 us -> 31.9 us
  matrix products: 18.6 us -> 0 us
  between operations: 16.2 us -> 1.68 us
  Pallas kernels: 0 us -> 8.53 us
  other arithmetic: 9.07 us -> 3.96 us
    reduce_scatter x1 -> x0, waiting for transfers between devices: 147 us -> none  [body(): lax.psum_scatter(jnp.einsum('tr,tf->rf', columns, upstream, preferred_ele...]
    all_gather x1 -> x0, waiting for transfers between devices: 70.8 us -> none  [body(): piece = lax.all_gather(weight_bf, 'fsdp', axis=0, tiled=True)]
    ppermute x0 -> x22, waiting for transfers between devices: none -> 35.5 us  [the longest x18 25.2 us: fsdp_permute(): return lax.ppermute(value, 'fsdp', pairs)]
    ppermute x0 -> x22, starting transfers between devices: none -> 31.9 us  [the longest x18 22.8 us: fsdp_permute(): return lax.ppermute(value, 'fsdp', pairs)]
    dot_general x3 -> x0, matrix products: 18.6 us -> none  [the longest x1 9.01 us: body(): jnp.einsum('tr,tf->rf', columns, upstream, preferred_element_type=jnp.flo...]
    pallas_call x0 -> x8, Pallas kernels: none -> 8.53 us  [the longest x2 2.09 us: assemble(): pl.pallas_call(kernel, in_specs=ins, out_specs=pl.BlockSpec(memory_space=...]
    broadcast_in_dim x1, other arithmetic: 4.21 us -> 0.72 us  [body(): values[None]]
  transfers between devices with their start and end apart: 3 -> 22, of which waited for: 2 -> 6; matrix products, arithmetic and copies ran while one was open for 9% -> 4% of each run, Pallas kernels for 0% -> 8%
where the time goes in v2:
time: 85.4 us; the launch traced here: 84.3 us
  waiting for transfers between devices  35.5 us (42%)
  starting transfers between devices  31.9 us (37%)
  Pallas kernels  8.53 us (10%)
  other arithmetic  3.96 us (5%)
  local copies, waits for them, and re-layouts  2.75 us (3%)
  between operations  1.68 us (2%)
    ppermute x18, waiting for transfers between devices, fsdp_permute(): return lax.ppermute(value, 'fsdp', pairs)  25.2 us
    ppermute x18, starting transfers between devices, fsdp_permute(): return lax.ppermute(value, 'fsdp', pairs)  22.8 us
    ppermute x4, waiting for transfers between devices, replica_step(): other = lax.ppermute(sent, 'replica', [(i, i ^ bit) for i in range(16)])  10.3 us
    ppermute x4, starting transfers between devices, replica_step(): other = lax.ppermute(sent, 'replica', [(i, i ^ bit) for i in range(16)])  9.15 us
    unnamed x18, local copies, waits for them, and re-layouts  2.75 us
    pallas_call x2, Pallas kernels, assemble(): pl.pallas_call(kernel, in_specs=ins, out_specs=pl.BlockSpec(memory_space=...  2.09 us
    pallas_call x1, Pallas kernels, adam(): pl.pallas_call(kernel, in_specs=[pl.BlockSpec(memory_space=pltpu.SMEM)] +...  2.08 us
  transfers between devices with their start and end apart: 22, of which 6 were waited for; matrix products, arithmetic and copies ran while one was open for 4% of the time, Pallas kernels for 8%

profile of v2, /device:TPU:64, one launch (start us, length us, event | category | flops | bytes accessed | tf_op | source)
XLA Modules:
  0.0 84.3 jit_solution(2568161881305983187)
XLA Ops:
  0.6 1.0 %convert_bitcast_fusion = bf16[512,128]{1,0:T(8,128)(2,1)S(1)} fusion(f32[1,512,128]{2,1,0:T(8,128)} %param.14), kind=kLoop, calls=%fused_computation.15 | loop fusion | flops 65536 | bytes 393216 | tf_op jit(solution)/shard_map/convert_element_type | solution.py:52
  1.6 1.6 %collective-permute-start = (bf16[512,128]{1,0:T(8,128)(2,1)S(1)}, bf16[512,128]{1,0:T(8,128)(2,1)S(1)}, u32[]{:S(2)}, u32[]{:S(2)}) collective-permute-start(bf16[512,128]{1,0:T(8,128)(2,1)S(1)} %convert_bitcast_fusion), channel_id=1, source_target_pairs={{0,128},{16,144},{32,160},{48,176},{64,192},{80,208},{96,224},{112... | collective-permute-start | bytes 393224 | tf_op jit(solution)/shard_map/ppermute | solution.py:53
  3.2 1.3 %bitcast_convert_fusion.w0 = bf16[512,512]{1,0:T(8,128)(2,1)S(1)} fusion(f32[1,512,512]{2,1,0:T(8,128)} %param.11), kind=kLoop, calls=%fused_computation.16 | loop fusion | flops 262144 | bytes 1572864 | tf_op jit(solution)/shard_map/convert_element_type | solution.py:273
  4.5 3.1 %collective-permute-start.7 = (bf16[512,512]{1,0:T(8,128)(2,1)S(1)}, bf16[512,512]{1,0:T(8,128)(2,1)S(1)}, u32[]{:S(2)}, u32[]{:S(2)}) collective-permute-start(bf16[512,512]{1,0:T(8,128)(2,1)S(1)} %bitcast_convert_fusion.w0), channel_id=1, source_target_pairs={{0,6},{1,7},{2,0},{3,1},{4,2},{5,3},{6,4},{7,5},{8,14},{9,15},{10,... | collective-permute-start | bytes 1572872 | tf_op jit(solution)/shard_map/ppermute | solution.py:36
  7.6 2.7 %collective-permute-start.2 = (bf16[128,512]{1,0:T(8,128)(2,1)}, bf16[128,512]{1,0:T(8,128)(2,1)S(1)}, u32[]{:S(2)}, u32[]{:S(2)}) collective-permute-start(bf16[128,512]{1,0:T(8,128)(2,1)} %bitcast.24), channel_id=1, source_target_pairs={{0,8},{1,9},{2,10},{3,11},{4,12},{5,13},{6,14},{7,15},{8,0},{9,1},... | collective-permute-start | bytes 393224 | tf_op jit(solution)/shard_map/ppermute | solution.py:36
  10.3 1.6 %copy-done = bf16[1,128,8192]{2,1,0:T(8,128)(2,1)S(1)} copy-done((bf16[1,128,8192]{2,1,0:T(8,128)(2,1)S(1)}, bf16[1,128,8192]{2,1,0:T(8,128)(2,1)}, u32[]{:S(2)}) %copy-start) | copy-done | bytes 2097176
  12.0 0.9 %collective-permute-start.5 = (bf16[128,2048]{1,0:T(8,128)(2,1)S(1)}, bf16[128,2048]{1,0:T(8,128)(2,1)S(1)}, u32[]{:S(2)}, u32[]{:S(2)}) collective-permute-start(bf16[128,2048]{1,0:T(8,128)(2,1)S(1)} %pieces.2), channel_id=1, source_target_pairs={{0,8},{1,9},{2,10},{3,11},{4,12},{5,13},{6,14},{7,15},{8,0},{9,1},... | collective-permute-start | bytes 1572872 | tf_op jit(solution)/shard_map/ppermute | solution.py:36
  13.0 2.0 %collective-permute-start.16 = (bf16[512,128]{1,0:T(8,128)(2,1)S(1)}, bf16[512,128]{1,0:T(8,128)(2,1)S(1)}, u32[]{:S(2)}, u32[]{:S(2)}) collective-permute-start(bf16[512,128]{1,0:T(8,128)(2,1)S(1)} %fusion.5), channel_id=1, source_target_pairs={{0,16},{16,0},{32,48},{48,32},{64,80},{80,64},{96,112},{112,96},{1... | collective-permute-start | bytes 393224 | tf_op jit(solution)/shard_map/ppermute | solution.py:53
  15.1 2.9 %collective-permute-done.16 = bf16[512,128]{1,0:T(8,128)(2,1)S(1)} collective-permute-done((bf16[512,128]{1,0:T(8,128)(2,1)S(1)}, bf16[512,128]{1,0:T(8,128)(2,1)S(1)}, u32[]{:S(2)}, u32[]{:S(2)}) %collective-permute-start.16) | collective-permute-done | bytes 131104 | tf_op jit(solution)/shard_map/ppermute | solution.py:53
  18.6 2.8 %collective-permute-start.1 = (bf16[128,2048]{1,0:T(8,128)(2,1)S(1)}, bf16[128,2048]{1,0:T(8,128)(2,1)S(1)}, u32[]{:S(2)}, u32[]{:S(2)}) collective-permute-start(bf16[128,2048]{1,0:T(8,128)(2,1)S(1)} %get-tuple-element.35), channel_id=1, source_target_pairs={{0,8},{1,9},{2,10},{3,11},{4,12},{5,13},{6,14},{7,15},{8,0},{9,1},... | collective-permute-start | bytes 1572872 | tf_op jit(solution)/shard_map/ppermute | solution.py:36
  21.9 1.9 %collective-permute-start.9 = (bf16[512,512]{1,0:T(8,128)(2,1)S(1)}, bf16[512,512]{1,0:T(8,128)(2,1)S(1)}, u32[]{:S(2)}, u32[]{:S(2)}) collective-permute-start(bf16[512,512]{1,0:T(8,128)(2,1)S(1)} %bitcast_convert_fusion.w0), channel_id=1, source_target_pairs={{0,4},{1,5},{2,6},{3,7},{4,0},{5,1},{6,2},{7,3},{8,12},{9,13},{10,... | collective-permute-start | bytes 1572872 | tf_op jit(solution)/shard_map/ppermute | solution.py:36
  23.9 4.6 %collective-permute-done.5 = bf16[128,2048]{1,0:T(8,128)(2,1)S(1)} collective-permute-done((bf16[128,2048]{1,0:T(8,128)(2,1)S(1)}, bf16[128,2048]{1,0:T(8,128)(2,1)S(1)}, u32[]{:S(2)}, u32[]{:S(2)}) %collective-permute-start.5) | collective-permute-done | bytes 524320 | tf_op jit(solution)/shard_map/ppermute | solution.py:36
  28.6 5.5 %collective-permute-start.18 = (bf16[512,128]{1,0:T(8,128)(2,1)S(1)}, bf16[512,128]{1,0:T(8,128)(2,1)S(1)}, u32[]{:S(2)}, u32[]{:S(2)}) collective-permute-start(bf16[512,128]{1,0:T(8,128)(2,1)S(1)} %add_convert_fusion), channel_id=1, source_target_pairs={{0,64},{16,80},{32,96},{48,112},{64,0},{80,16},{96,32},{112,48},{1... | collective-permute-start | bytes 393224 | tf_op jit(solution)/shard_map/ppermute | solution.py:53
  34.0 7.4 %collective-permute-done.18 = bf16[512,128]{1,0:T(8,128)(2,1)S(1)} collective-permute-done((bf16[512,128]{1,0:T(8,128)(2,1)S(1)}, bf16[512,128]{1,0:T(8,128)(2,1)S(1)}, u32[]{:S(2)}, u32[]{:S(2)}) %collective-permute-start.18) | collective-permute-done | bytes 131104 | tf_op jit(solution)/shard_map/ppermute | solution.py:53
  41.4 0.8 multiply_subtract_fusion
  42.2 1.3 %weight_grad.1 = (f32[512,512]{1,0:T(8,128)S(1)}, bf16[512,512]{1,0:T(8,128)(2,1)S(1)}, bf16[512,512]{1,0:T(8,128)(2,1)S(1)}, bf16[512,512]{1,0:T(8,128)(2,1)S(1)}) custom-call(bf16[128,2048]{1,0:T(8,128)(2,1)S(1)} %get-tuple-element.33.t0, bf16[128,2048]{1,0:T(8,128)(2,1)S(1)} %collective-permute-done.1.t1, ...), custom_call_target="tpu_custom_call" | custom-call | flops 1 | bytes 1 | tf_op jit(solution)/shard_map/weight_grad/pallas_call | solution.py:148
  43.5 2.3 %collective-permute-start.19 = (bf16[512,512]{1,0:T(8,128)(2,1)S(1)}, bf16[512,512]{1,0:T(8,128)(2,1)S(1)}, u32[]{:S(2)}, u32[]{:S(2)}) collective-permute-start(bf16[512,512]{1,0:T(8,128)(2,1)S(1)} %get-tuple-element.50), channel_id=1, source_target_pairs={{0,4},{1,5},{2,6},{3,7},{4,0},{5,1},{6,2},{7,3},{8,12},{9,13},{10,... | collective-permute-start | bytes 1572872 | tf_op jit(solution)/shard_map/ppermute | solution.py:36
  45.8 1.2 %values.1 = (f32[128,512]{1,0:T(8,128)S(1)}, f32[128,512]{1,0:T(8,128)S(1)}, f32[256,512]{1,0:T(8,128)S(1)}) custom-call(bf16[128,2048]{1,0:T(8,128)(2,1)S(1)} %get-tuple-element.33.t0, bf16[128,2048]{1,0:T(8,128)(2,1)S(1)} %collective-permute-done.1.t1, bf16[128,2048]{1,0:T(8,128)(2,1)S(1)} %collective-permute-done.4.t2, ...), custom_call_target="tpu_custom_call" | custom-call | flops 1 | bytes 1 | tf_op jit(solution)/shard_map/values/pallas_call | solution.py:170
  47.2 1.3 %input_grad.1 = (bf16[128,2048]{1,0:T(8,128)(2,1)S(1)}, bf16[128,2048]{1,0:T(8,128)(2,1)S(1)}, bf16[128,2048]{1,0:T(8,128)(2,1)S(1)}, bf16[128,2048]{1,0:T(8,128)(2,1)S(1)}) custom-call(bf16[512,512]{1,0:T(8,128)(2,1)S(1)} %pad_maximum_fusion.up_ref, bf16[512,512]{1,0:T(8,128)(2,1)S(1)} %bitcast_convert_fusion.w0, ...), custom_call_target="tpu_custom_call" | custom-call | flops 1 | bytes 1 | tf_op jit(solution)/shard_map/input_grad/pallas_call | solution.py:126
  48.5 0.8 collective-permute-start.13
  49.3 1.0 %collective-permute-start.12 = (bf16[128,2048]{1,0:T(8,128)(2,1)S(1)}, bf16[128,2048]{1,0:T(8,128)(2,1)S(1)}, u32[]{:S(2)}, u32[]{:S(2)}) collective-permute-start(bf16[128,2048]{1,0:T(8,128)(2,1)S(1)} %get-tuple-element.43), channel_id=1, source_target_pairs={{0,8},{1,9},{2,10},{3,11},{4,12},{5,13},{6,14},{7,15},{8,0},{9,1},... | collective-permute-start | bytes 1572872 | tf_op jit(solution)/shard_map/ppermute | solution.py:36
  50.3 8.2 %collective-permute-done.19.g2 = bf16[512,512]{1,0:T(8,128)(2,1)S(1)} collective-permute-done((bf16[512,512]{1,0:T(8,128)(2,1)S(1)}, bf16[512,512]{1,0:T(8,128)(2,1)S(1)}, u32[]{:S(2)}, u32[]{:S(2)}) %collective-permute-start.19) | collective-permute-done | bytes 524320 | tf_op jit(solution)/shard_map/ppermute | solution.py:36
  58.5 0.8 %collective-permute-start.20 = (bf16[512,512]{1,0:T(8,128)(2,1)S(1)}, bf16[512,512]{1,0:T(8,128)(2,1)S(1)}, u32[]{:S(2)}, u32[]{:S(2)}) collective-permute-start(bf16[512,512]{1,0:T(8,128)(2,1)S(1)} %get-tuple-element.51), channel_id=1, source_target_pairs={{0,2},{1,3},{2,4},{3,5},{4,6},{5,7},{6,0},{7,1},{8,10},{9,11},{10,... | collective-permute-start | bytes 1572872 | tf_op jit(solution)/shard_map/ppermute | solution.py:36
  59.4 2.4 %collective-permute-start.21 = (bf16[512,512]{1,0:T(8,128)(2,1)S(1)}, bf16[512,512]{1,0:T(8,128)(2,1)S(1)}, u32[]{:S(2)}, u32[]{:S(2)}) collective-permute-start(bf16[512,512]{1,0:T(8,128)(2,1)S(1)} %get-tuple-element.53), channel_id=1, source_target_pairs={{0,6},{1,7},{2,0},{3,1},{4,2},{5,3},{6,4},{7,5},{8,14},{9,15},{10,... | collective-permute-start | bytes 1572872 | tf_op jit(solution)/shard_map/ppermute | solution.py:36
  61.8 1.0 %collective-permute-start.14 = (bf16[128,2048]{1,0:T(8,128)(2,1)S(1)}, bf16[128,2048]{1,0:T(8,128)(2,1)S(1)}, u32[]{:S(2)}, u32[]{:S(2)}) collective-permute-start(bf16[128,2048]{1,0:T(8,128)(2,1)S(1)} %collective-permute-done.13), channel_id=1, source_target_pairs={{0,8},{1,9},{2,10},{3,11},{4,12},{5,13},{6,14},{7,15},{8,0},{9,1},... | collective-permute-start | bytes 1572872 | tf_op jit(solution)/shard_map/ppermute | solution.py:36
  62.8 2.6 %collective-permute-start.11 = (bf16[128,512]{1,0:T(8,128)(2,1)S(1)}, bf16[128,512]{1,0:T(8,128)(2,1)S(1)}, u32[]{:S(2)}, u32[]{:S(2)}) collective-permute-start(bf16[128,512]{1,0:T(8,128)(2,1)S(1)} %fusion), channel_id=1, source_target_pairs={{0,8},{1,9},{2,10},{3,11},{4,12},{5,13},{6,14},{7,15},{8,0},{9,1},... | collective-permute-start | bytes 393224 | tf_op jit(solution)/shard_map/ppermute | solution.py:36
  66.1 1.0 %assemble.2.refs_2_ = bf16[128,8192]{1,0:T(8,128)(2,1)} custom-call(bf16[128,2048]{1,0:T(8,128)(2,1)S(1)} %get-tuple-element.45.refs_0_, bf16[128,2048]{1,0:T(8,128)(2,1)S(1)} %collective-permute-done.15.refs_1_), custom_call_target="tpu_custom_call" | custom-call | flops 1 | bytes 1 | tf_op jit(solution)/shard_map/assemble/pallas_call | solution.py:206
  67.2 12.0 %collective-permute-done.11 = bf16[128,512]{1,0:T(8,128)(2,1)S(1)} collective-permute-done((bf16[128,512]{1,0:T(8,128)(2,1)S(1)}, bf16[128,512]{1,0:T(8,128)(2,1)S(1)}, u32[]{:S(2)}, u32[]{:S(2)}) %collective-permute-start.11) | collective-permute-done | bytes 131104 | tf_op jit(solution)/shard_map/ppermute | solution.py:36
  79.1 0.7 fusion.4
  79.9 1.0 %assemble.3 = bf16[128,8192]{1,0:T(8,128)(2,1)} custom-call(bf16[128,2048]{1,0:T(8,128)(2,1)S(1)} %collective-permute-done.12.refs_0_, bf16[128,2048]{1,0:T(8,128)(2,1)S(1)} %collective-permute-done.14.refs_1_, bf16[128,8192]{1,0:T(8,128)(2,1)} %assemble.2.refs_2_), custom_call_target="tpu_custom_call", output_to_operand_aliasing={{}: (2, {})} | custom-call | flops 1 | bytes 1 | tf_op jit(solution)/shard_map/assemble/pallas_call | solution.py:206
  81.0 0.5 copy-done.1
  82.1 2.1 %adam.1 = (f32[512,512]{1,0:T(8,128)}, f32[512,512]{1,0:T(8,128)}, f32[512,512]{1,0:T(8,128)}) custom-call(s32[1]{0:T(128)S(6)} %copy.18.frag, f32[512,512]{1,0:T(8,128)S(1)} %get-tuple-element.48.g0, bf16[512,512]{1,0:T(8,128)(2,1)S(1)} %collective-permute-done.20.g1, bf16[512,512]{1,0:T(8,128)(2,1)S(1)} %collective-permute-done.19.g2, ...), custom_call_target="tpu_custom_call" | custom-call | flops 1 | bytes 1 | tf_op jit(solution)/shard_map/adam/pallas_call | solution.py:249
  (48 shorter events, 2.2 us)
Async XLA Ops:
  1.6 11.3 %copy-start.5 = (f32[1,512,128]{2,1,0:T(8,128)S(1)}, f32[1,512,128]{2,1,0:T(8,128)}, u32[]{:S(2)}) copy-start(f32[1,512,128]{2,1,0:T(8,128)} %param.14) | copy-start | bytes 786436
  1.6 13.4 %copy-start.6 = (bf16[1,128,512]{2,1,0:T(8,128)(2,1)S(1)}, bf16[1,128,512]{2,1,0:T(8,128)(2,1)}, u32[]{:S(2)}) copy-start(bf16[1,128,512]{2,1,0:T(8,128)(2,1)} %param.10) | copy-start | bytes 393220
  1.6 11.3 %collective-permute-start = (bf16[512,128]{1,0:T(8,128)(2,1)S(1)}, bf16[512,128]{1,0:T(8,128)(2,1)S(1)}, u32[]{:S(2)}, u32[]{:S(2)}) collective-permute-start(bf16[512,128]{1,0:T(8,128)(2,1)S(1)} %convert_bitcast_fusion), channel_id=1, source_target_pairs={{0,128},{16,144},{32,160},{48,176},{64,192},{80,208},{96,224},{112... | collective-permute-start | bytes 393224 | tf_op jit(solution)/shard_map/ppermute | solution.py:53
  4.5 16.9 %collective-permute-start.7 = (bf16[512,512]{1,0:T(8,128)(2,1)S(1)}, bf16[512,512]{1,0:T(8,128)(2,1)S(1)}, u32[]{:S(2)}, u32[]{:S(2)}) collective-permute-start(bf16[512,512]{1,0:T(8,128)(2,1)S(1)} %bitcast_convert_fusion.w0), channel_id=1, source_target_pairs={{0,6},{1,7},{2,0},{3,1},{4,2},{5,3},{6,4},{7,5},{8,14},{9,15},{10,... | collective-permute-start | bytes 1572872 | tf_op jit(solution)/shard_map/ppermute | solution.py:36
  7.6 14.3 %collective-permute-start.8 = (bf16[512,512]{1,0:T(8,128)(2,1)S(1)}, bf16[512,512]{1,0:T(8,128)(2,1)S(1)}, u32[]{:S(2)}, u32[]{:S(2)}) collective-permute-start(bf16[512,512]{1,0:T(8,128)(2,1)S(1)} %bitcast_convert_fusion.w0), channel_id=1, source_target_pairs={{0,2},{1,3},{2,4},{3,5},{4,6},{5,7},{6,0},{7,1},{8,10},{9,11},{10,... | collective-permute-start | bytes 1572872 | tf_op jit(solution)/shard_map/ppermute | solution.py:36
  7.6 7.4 %collective-permute-start.2 = (bf16[128,512]{1,0:T(8,128)(2,1)}, bf16[128,512]{1,0:T(8,128)(2,1)S(1)}, u32[]{:S(2)}, u32[]{:S(2)}) collective-permute-start(bf16[128,512]{1,0:T(8,128)(2,1)} %bitcast.24), channel_id=1, source_target_pairs={{0,8},{1,9},{2,10},{3,11},{4,12},{5,13},{6,14},{7,15},{8,0},{9,1},... | collective-permute-start | bytes 393224 | tf_op jit(solution)/shard_map/ppermute | solution.py:36
  10.3 1.6 %copy-start = (bf16[1,128,8192]{2,1,0:T(8,128)(2,1)S(1)}, bf16[1,128,8192]{2,1,0:T(8,128)(2,1)}, u32[]{:S(2)}) copy-start(bf16[1,128,8192]{2,1,0:T(8,128)(2,1)} %param.9) | copy-start | bytes 6291460
  12.0 16.5 %collective-permute-start.5 = (bf16[128,2048]{1,0:T(8,128)(2,1)S(1)}, bf16[128,2048]{1,0:T(8,128)(2,1)S(1)}, u32[]{:S(2)}, u32[]{:S(2)}) collective-permute-start(bf16[128,2048]{1,0:T(8,128)(2,1)S(1)} %pieces.2), channel_id=1, source_target_pairs={{0,8},{1,9},{2,10},{3,11},{4,12},{5,13},{6,14},{7,15},{8,0},{9,1},... | collective-permute-start | bytes 1572872 | tf_op jit(solution)/shard_map/ppermute | solution.py:36
  13.0 5.1 %collective-permute-start.16 = (bf16[512,128]{1,0:T(8,128)(2,1)S(1)}, bf16[512,128]{1,0:T(8,128)(2,1)S(1)}, u32[]{:S(2)}, u32[]{:S(2)}) collective-permute-start(bf16[512,128]{1,0:T(8,128)(2,1)S(1)} %fusion.5), channel_id=1, source_target_pairs={{0,16},{16,0},{32,48},{48,32},{64,80},{80,64},{96,112},{112,96},{1... | collective-permute-start | bytes 393224 | tf_op jit(solution)/shard_map/ppermute | solution.py:53
  15.0 26.4 %copy-start.7 = (f32[512,128]{1,0:T(8,128)S(1)}, f32[512,128]{1,0:T(8,128)}, u32[]{:S(2)}) copy-start(f32[512,128]{1,0:T(8,128)} %param.16) | copy-start | bytes 786436
  15.0 26.4 %copy-start.8 = (f32[512,128]{1,0:T(8,128)S(1)}, f32[512,128]{1,0:T(8,128)}, u32[]{:S(2)}) copy-start(f32[512,128]{1,0:T(8,128)} %param.15) | copy-start | bytes 786436
  15.0 3.5 %collective-permute-start.3 = (bf16[256,512]{1,0:T(8,128)(2,1)S(1)}, bf16[256,512]{1,0:T(8,128)(2,1)S(1)}, u32[]{:S(2)}, u32[]{:S(2)}) collective-permute-start(bf16[256,512]{1,0:T(8,128)(2,1)S(1)} %pad_maximum_fusion.1), channel_id=1, source_target_pairs={{0,1},{1,0},{2,3},{3,2},{4,5},{5,4},{6,7},{7,6},{8,9},{9,8},{10,11... | collective-permute-start | bytes 786440 | tf_op jit(solution)/shard_map/ppermute | solution.py:36
  18.1 10.4 %collective-permute-start.17 = (bf16[512,128]{1,0:T(8,128)(2,1)S(1)}, bf16[512,128]{1,0:T(8,128)(2,1)S(1)}, u32[]{:S(2)}, u32[]{:S(2)}) collective-permute-start(bf16[512,128]{1,0:T(8,128)(2,1)S(1)} %add_convert_fusion.1), channel_id=1, source_target_pairs={{0,32},{16,48},{32,0},{48,16},{64,96},{80,112},{96,64},{112,80},{1... | collective-permute-start | bytes 393224 | tf_op jit(solution)/shard_map/ppermute | solution.py:53
  18.6 23.6 %collective-permute-start.1 = (bf16[128,2048]{1,0:T(8,128)(2,1)S(1)}, bf16[128,2048]{1,0:T(8,128)(2,1)S(1)}, u32[]{:S(2)}, u32[]{:S(2)}) collective-permute-start(bf16[128,2048]{1,0:T(8,128)(2,1)S(1)} %get-tuple-element.35), channel_id=1, source_target_pairs={{0,8},{1,9},{2,10},{3,11},{4,12},{5,13},{6,14},{7,15},{8,0},{9,1},... | collective-permute-start | bytes 1572872 | tf_op jit(solution)/shard_map/ppermute | solution.py:36
  21.5 20.8 %collective-permute-start.4 = (bf16[128,2048]{1,0:T(8,128)(2,1)S(1)}, bf16[128,2048]{1,0:T(8,128)(2,1)S(1)}, u32[]{:S(2)}, u32[]{:S(2)}) collective-permute-start(bf16[128,2048]{1,0:T(8,128)(2,1)S(1)} %get-tuple-element.38), channel_id=1, source_target_pairs={{0,1},{1,0},{2,3},{3,2},{4,5},{5,4},{6,7},{7,6},{8,9},{9,8},{10,11... | collective-permute-start | bytes 1572872 | tf_op jit(solution)/shard_map/ppermute | solution.py:36
  21.9 23.9 %collective-permute-start.9 = (bf16[512,512]{1,0:T(8,128)(2,1)S(1)}, bf16[512,512]{1,0:T(8,128)(2,1)S(1)}, u32[]{:S(2)}, u32[]{:S(2)}) collective-permute-start(bf16[512,512]{1,0:T(8,128)(2,1)S(1)} %bitcast_convert_fusion.w0), channel_id=1, source_target_pairs={{0,4},{1,5},{2,6},{3,7},{4,0},{5,1},{6,2},{7,3},{8,12},{9,13},{10,... | collective-permute-start | bytes 1572872 | tf_op jit(solution)/shard_map/ppermute | solution.py:36
  28.5 13.7 %collective-permute-start.6 = (bf16[128,2048]{1,0:T(8,128)(2,1)S(1)}, bf16[128,2048]{1,0:T(8,128)(2,1)S(1)}, u32[]{:S(2)}, u32[]{:S(2)}) collective-permute-start(bf16[128,2048]{1,0:T(8,128)(2,1)S(1)} %collective-permute-done.5), channel_id=1, source_target_pairs={{0,1},{1,0},{2,3},{3,2},{4,5},{5,4},{6,7},{7,6},{8,9},{9,8},{10,11... | collective-permute-start | bytes 1572872 | tf_op jit(solution)/shard_map/ppermute | solution.py:36
  28.6 12.9 %collective-permute-start.18 = (bf16[512,128]{1,0:T(8,128)(2,1)S(1)}, bf16[512,128]{1,0:T(8,128)(2,1)S(1)}, u32[]{:S(2)}, u32[]{:S(2)}) collective-permute-start(bf16[512,128]{1,0:T(8,128)(2,1)S(1)} %add_convert_fusion), channel_id=1, source_target_pairs={{0,64},{16,80},{32,96},{48,112},{64,0},{80,16},{96,32},{112,48},{1... | collective-permute-start | bytes 393224 | tf_op jit(solution)/shard_map/ppermute | solution.py:53
  42.2 38.8 %copy-start.2 = (f32[512,128]{1,0:T(8,128)}, f32[512,128]{1,0:T(8,128)S(1)}, u32[]{:S(2)}) copy-start(f32[512,128]{1,0:T(8,128)S(1)} %get-tuple-element.57.glob) | copy-start | bytes 786436
  43.5 15.0 %collective-permute-start.19 = (bf16[512,512]{1,0:T(8,128)(2,1)S(1)}, bf16[512,512]{1,0:T(8,128)(2,1)S(1)}, u32[]{:S(2)}, u32[]{:S(2)}) collective-permute-start(bf16[512,512]{1,0:T(8,128)(2,1)S(1)} %get-tuple-element.50), channel_id=1, source_target_pairs={{0,4},{1,5},{2,6},{3,7},{4,0},{5,1},{6,2},{7,3},{8,12},{9,13},{10,... | collective-permute-start | bytes 1572872 | tf_op jit(solution)/shard_map/ppermute | solution.py:36
  47.1 12.3 %collective-permute-start.10 = (f32[256,512]{1,0:T(8,128)S(1)}, f32[256,512]{1,0:T(8,128)S(1)}, u32[]{:S(2)}, u32[]{:S(2)}) collective-permute-start(f32[256,512]{1,0:T(8,128)S(1)} %get-tuple-element.41), channel_id=1, source_target_pairs={{0,1},{1,0},{2,3},{3,2},{4,5},{5,4},{6,7},{7,6},{8,9},{9,8},{10,11... | collective-permute-start | bytes 1572872 | tf_op jit(solution)/shard_map/ppermute | solution.py:36
  48.5 13.3 %collective-permute-start.13 = (bf16[128,2048]{1,0:T(8,128)(2,1)S(1)}, bf16[128,2048]{1,0:T(8,128)(2,1)S(1)}, u32[]{:S(2)}, u32[]{:S(2)}) collective-permute-start(bf16[128,2048]{1,0:T(8,128)(2,1)S(1)} %get-tuple-element.44), channel_id=1, source_target_pairs={{0,1},{1,0},{2,3},{3,2},{4,5},{5,4},{6,7},{7,6},{8,9},{9,8},{10,11... | collective-permute-start | bytes 1572872 | tf_op jit(solution)/shard_map/ppermute | solution.py:36
  49.2 13.6 %collective-permute-start.15 = (bf16[128,2048]{1,0:T(8,128)(2,1)S(1)}, bf16[128,2048]{1,0:T(8,128)(2,1)S(1)}, u32[]{:S(2)}, u32[]{:S(2)}) collective-permute-start(bf16[128,2048]{1,0:T(8,128)(2,1)S(1)} %get-tuple-element.46), channel_id=1, source_target_pairs={{0,1},{1,0},{2,3},{3,2},{4,5},{5,4},{6,7},{7,6},{8,9},{9,8},{10,11... | collective-permute-start | bytes 1572872 | tf_op jit(solution)/shard_map/ppermute | solution.py:36
  49.3 30.5 %collective-permute-start.12 = (bf16[128,2048]{1,0:T(8,128)(2,1)S(1)}, bf16[128,2048]{1,0:T(8,128)(2,1)S(1)}, u32[]{:S(2)}, u32[]{:S(2)}) collective-permute-start(bf16[128,2048]{1,0:T(8,128)(2,1)S(1)} %get-tuple-element.43), channel_id=1, source_target_pairs={{0,8},{1,9},{2,10},{3,11},{4,12},{5,13},{6,14},{7,15},{8,0},{9,1},... | collective-permute-start | bytes 1572872 | tf_op jit(solution)/shard_map/ppermute | solution.py:36
  58.5 22.4 %collective-permute-start.20 = (bf16[512,512]{1,0:T(8,128)(2,1)S(1)}, bf16[512,512]{1,0:T(8,128)(2,1)S(1)}, u32[]{:S(2)}, u32[]{:S(2)}) collective-permute-start(bf16[512,512]{1,0:T(8,128)(2,1)S(1)} %get-tuple-element.51), channel_id=1, source_target_pairs={{0,2},{1,3},{2,4},{3,5},{4,6},{5,7},{6,0},{7,1},{8,10},{9,11},{10,... | collective-permute-start | bytes 1572872 | tf_op jit(solution)/shard_map/ppermute | solution.py:36
  59.4 21.6 %collective-permute-start.21 = (bf16[512,512]{1,0:T(8,128)(2,1)S(1)}, bf16[512,512]{1,0:T(8,128)(2,1)S(1)}, u32[]{:S(2)}, u32[]{:S(2)}) collective-permute-start(bf16[512,512]{1,0:T(8,128)(2,1)S(1)} %get-tuple-element.53), channel_id=1, source_target_pairs={{0,6},{1,7},{2,0},{3,1},{4,2},{5,3},{6,4},{7,5},{8,14},{9,15},{10,... | collective-permute-start | bytes 1572872 | tf_op jit(solution)/shard_map/ppermute | solution.py:36
  61.8 18.1 %collective-permute-start.14 = (bf16[128,2048]{1,0:T(8,128)(2,1)S(1)}, bf16[128,2048]{1,0:T(8,128)(2,1)S(1)}, u32[]{:S(2)}, u32[]{:S(2)}) collective-permute-start(bf16[128,2048]{1,0:T(8,128)(2,1)S(1)} %collective-permute-done.13), channel_id=1, source_target_pairs={{0,8},{1,9},{2,10},{3,11},{4,12},{5,13},{6,14},{7,15},{8,0},{9,1},... | collective-permute-start | bytes 1572872 | tf_op jit(solution)/shard_map/ppermute | solution.py:36
  62.8 16.3 %collective-permute-start.11 = (bf16[128,512]{1,0:T(8,128)(2,1)S(1)}, bf16[128,512]{1,0:T(8,128)(2,1)S(1)}, u32[]{:S(2)}, u32[]{:S(2)}) collective-permute-start(bf16[128,512]{1,0:T(8,128)(2,1)S(1)} %fusion), channel_id=1, source_target_pairs={{0,8},{1,9},{2,10},{3,11},{4,12},{5,13},{6,14},{7,15},{8,0},{9,1},... | collective-permute-start | bytes 393224 | tf_op jit(solution)/shard_map/ppermute | solution.py:36
  79.9 1.6 %copy-start.1 = (f32[1,512,512]{2,1,0:T(8,128)S(1)}, f32[1,512,512]{2,1,0:T(8,128)}, u32[]{:S(2)}) copy-start(f32[1,512,512]{2,1,0:T(8,128)} %param.11) | copy-start | bytes 3145732
  79.9 1.9 %copy-start.3 = (f32[1,512,512]{2,1,0:T(8,128)S(1)}, f32[1,512,512]{2,1,0:T(8,128)}, u32[]{:S(2)}) copy-start(f32[1,512,512]{2,1,0:T(8,128)} %param.12) | copy-start | bytes 3145732
  79.9 2.2 %copy-start.4 = (f32[1,512,512]{2,1,0:T(8,128)S(1)}, f32[1,512,512]{2,1,0:T(8,128)}, u32[]{:S(2)}) copy-start(f32[1,512,512]{2,1,0:T(8,128)} %param.13) | copy-start | bytes 3145732

commit v3 on v2

v3 whole, which is shorter than its diff:
```python
import functools

import jax
import jax.numpy as jnp
from jax import lax
from jax.experimental import pallas as pl
from jax.experimental.pallas import tpu as pltpu
from jax.sharding import PartitionSpec as P

D = 8192
SCALE = D ** (-0.5)

beta_first = 0.9
beta_second = 0.95
epsilon = 1e-08
inner_rate = 0.01
decay_rate = 0.1
outer_rate = 0.7
outer_mom = 0.9
mix_share = 0.5

NY = 4
TOK = 128
ROWS = 512
F = 512
PIECE = NY * ROWS
HALF = ROWS // 2
VMEM = pltpu.CompilerParams(vmem_limit_bytes=40 * 1024 * 1024)


def fsdp_permute(value, target):
    pairs = []
    for i in range(16):
        x, y, c = i // 8, (i // 2) % NY, i % 2
        x2, y2, c2 = target(x, y, c)
        pairs.append((i, ((x2 % 2) * NY + y2 % NY) * 2 + c2 % 2))
    return lax.ppermute(value, "fsdp", pairs)


def swap_x(value):
    return fsdp_permute(value, lambda x, y, c: (x + 1, y, c))


def swap_core(value):
    return fsdp_permute(value, lambda x, y, c: (x, y, c + 1))


def shift_y(value, step):
    return fsdp_permute(value, lambda x, y, c: (x, y + step, c))


def replica_step(total, partner):
    sent = total.astype(jnp.bfloat16)
    other = lax.ppermute(sent, "replica", [(i, partner(i)) for i in range(16)])
    return sent.astype(jnp.float32) + other.astype(jnp.float32)


def after(value, *others):
    return lax.optimization_barrier((value, *others))[0]


def outer_update(momentum, global_frag, average):
    mom_new = outer_mom * momentum + average
    glob_new = global_frag - outer_rate * (outer_mom * mom_new + average)
    return (mom_new, glob_new)


def shape(rows, cols, dtype=jnp.bfloat16):
    return jax.ShapeDtypeStruct((rows, cols), dtype)


SMALL = pl.CostEstimate(flops=1, bytes_accessed=1, transcendentals=0)


def here():
    device = lax.axis_index("fsdp")
    return device // (2 * NY), lax.rem(device // 2, NY), lax.rem(device, 2)


def column(x, y, c):
    return pl.ds(pl.multiple_of(((x * NY + y) * 2 + c) * ROWS, ROWS), ROWS)


def pieces_of(tokens, up, wanted):
    groups = [(i, g) for i, stack in enumerate(wanted) for g in stack]

    def kernel(source, up_ref, *refs):
        targets, sems = refs[:-1], refs[-1]
        x, _, c = here()
        copies, filled = [], [0] * len(wanted)
        for n, (i, (dx, dc, start, size, with_up)) in enumerate(groups):
            rows, into = pl.ds(start, size), pl.ds(filled[i], size)
            filled[i] += size
            moves = [
                (
                    source.at[rows, column(1 - x if dx else x, k, 1 - c if dc else c)],
                    targets[i].at[into, pl.ds(k * ROWS, ROWS)],
                )
                for k in range(NY)
            ]
            if with_up:
                moves.append((up_ref.at[rows], targets[i].at[into, pl.ds(PIECE, F)]))
            for k, (here_from, here_to) in enumerate(moves):
                copies.append(pltpu.make_async_copy(here_from, here_to, sems.at[n, k]))
        for copy in copies:
            copy.start()
        for copy in copies:
            copy.wait()

    return pl.pallas_call(
        kernel,
        in_specs=[pl.BlockSpec(memory_space=pltpu.VMEM), pl.BlockSpec(memory_space=pltpu.HBM)],
        out_specs=[pl.BlockSpec(memory_space=pltpu.VMEM)] * len(wanted),
        out_shape=[
            shape(sum(g[3] for g in stack), PIECE + F * stack[0][4]) for stack in wanted
        ],
        scratch_shapes=[pltpu.SemaphoreType.DMA((len(groups), NY + 1))],
        cost_estimate=SMALL,
        compiler_params=VMEM,
        name="pieces",
    )(tokens, up)


def places(blocks):
    y = here()[1]
    for (step, start), block in zip(((0, 0), (1, 0), (3, 0), (2, 0), (2, HALF)), blocks, strict=True):
        at = pl.multiple_of(lax.rem(y + step, NY) * ROWS + start, HALF)
        yield pl.ds(at, block.shape[0]), block


def input_grad(ups, blocks):
    def kernel(u0, u1, u2, *refs):
        own, far_x, core, far = refs[5:]
        up = jnp.concatenate([u0[...], u1[:, PIECE:], u2[...]], axis=0)
        for at, block in places(refs[:5]):
            grad = lax.dot_general(
                up, block[...], (((1,), (1,)), ((), ())), preferred_element_type=jnp.float32
            )
            grad = (grad * SCALE).astype(jnp.bfloat16)
            own[:, at] = grad[:TOK]
            far_x[:, at] = grad[TOK : 2 * TOK]
            core[:, at] = grad[2 * TOK : 3 * TOK]
            far[:, at] = grad[3 * TOK :]

    return pl.pallas_call(
        kernel,
        in_specs=[pl.BlockSpec(memory_space=pltpu.VMEM)] * 8,
        out_specs=[pl.BlockSpec(memory_space=pltpu.VMEM)] * 4,
        out_shape=[shape(TOK, PIECE)] * 4,
        cost_estimate=SMALL,
        compiler_params=VMEM,
        name="input_grad",
    )(*ups, *blocks)


def value_parts(toks, blocks):
    def kernel(t0, t1, t2, t3, *refs):
        own, far, pair = refs[5:]
        total = jnp.zeros((4 * TOK, F), jnp.float32)
        for at, block in places(refs[:5]):
            tok = jnp.concatenate([t0[:, at], t1[:, at], t2[:, at], t3[:, at]], axis=0)
            total += jnp.dot(tok, block[...], preferred_element_type=jnp.float32)
        own[...] = total[:TOK]
        far[...] = total[TOK : 2 * TOK]
        pair[...] = total[2 * TOK :]

    return pl.pallas_call(
        kernel,
        in_specs=[pl.BlockSpec(memory_space=pltpu.VMEM)] * 9,
        out_specs=[pl.BlockSpec(memory_space=pltpu.VMEM)] * 3,
        out_shape=[shape(TOK, F, jnp.float32)] * 2 + [shape(2 * TOK, F, jnp.float32)],
        cost_estimate=SMALL,
        compiler_params=VMEM,
        name="values",
    )(*toks, *blocks)


def weight_grad_blocks(toks, ups):
    def kernel(t0, t1, t2, t3, u0, u2, g0, g1, g3, up_half, down_half):
        up = jnp.concatenate([u0[...], t1[:, PIECE:], u2[...]], axis=0)
        y = here()[1]
        for step in (2, 1, 3, 0):
            at = pl.ds(pl.multiple_of(lax.rem(y + step, NY) * ROWS, ROWS), ROWS)
            tok = jnp.concatenate([t0[:, at], t1[:, at], t2[:, at], t3[:, at]], axis=0)
            grad = SCALE * lax.dot_general(
                tok, up, (((0,), (0,)), ((), ())), preferred_element_type=jnp.float32
            )
            if step == 2:
                up_half[...] = grad[:HALF].astype(jnp.bfloat16)
                down_half[...] = grad[HALF:].astype(jnp.bfloat16)
            else:
                {0: g0, 1: g1, 3: g3}[step][...] = grad

    return pl.pallas_call(
        kernel,
        in_specs=[pl.BlockSpec(memory_space=pltpu.VMEM)] * 6,
        out_specs=[pl.BlockSpec(memory_space=pltpu.VMEM)] * 5,
        out_shape=[shape(ROWS, F, jnp.float32)] * 3 + [shape(HALF, F)] * 2,
        cost_estimate=SMALL,
        compiler_params=VMEM,
        name="weight_grad",
    )(*toks, *ups)


def relay(g1, g3, from_below, from_above):
    def kernel(g1, g3, from_below, from_above, s1, s3):
        s1[:HALF] = (g1[:HALF] + from_below[...].astype(jnp.float32)).astype(jnp.bfloat16)
        s1[HALF:] = g1[HALF:].astype(jnp.bfloat16)
        s3[:HALF] = g3[:HALF].astype(jnp.bfloat16)
        s3[HALF:] = (g3[HALF:] + from_above[...].astype(jnp.float32)).astype(jnp.bfloat16)

    return pl.pallas_call(
        kernel,
        in_specs=[pl.BlockSpec(memory_space=pltpu.VMEM)] * 4,
        out_specs=[pl.BlockSpec(memory_space=pltpu.VMEM)] * 2,
        out_shape=[shape(ROWS, F)] * 2,
        cost_estimate=SMALL,
        compiler_params=VMEM,
        name="relay",
    )(g1, g3, from_below, from_above)


def assemble(block, parts, wanted):
    n = len(wanted)
    groups = [(i, j, g) for i, stack in enumerate(wanted) for j, g in enumerate(stack)]

    def kernel(*refs):
        target, sems = refs[-2:]
        x, _, c = here()
        copies = []
        for m, (i, j, (dx, dc)) in enumerate(groups):
            for k in range(NY):
                copies.append(
                    pltpu.make_async_copy(
                        refs[i].at[pl.ds(j * TOK, TOK), pl.ds(k * ROWS, ROWS)],
                        target.at[:, column(1 - x if dx else x, k, 1 - c if dc else c)],
                        sems.at[m * NY + k],
                    )
                )
        for copy in copies:
            copy.start()
        for copy in copies:
            copy.wait()

    args = list(parts)
    ins = [pl.BlockSpec(memory_space=pltpu.VMEM)] * n
    alias = {}
    if block is not None:
        alias = {n: 0}
        ins.append(pl.BlockSpec(memory_space=pltpu.HBM))
        args.append(block)
    return pl.pallas_call(
        kernel,
        in_specs=ins,
        out_specs=pl.BlockSpec(memory_space=pltpu.HBM),
        out_shape=shape(TOK, D),
        scratch_shapes=[pltpu.SemaphoreType.DMA((NY * len(groups),))],
        input_output_aliases=alias,
        cost_estimate=SMALL,
        compiler_params=VMEM,
        name="assemble",
    )(*args)


STRIP = 64


def adam(frag_index, grads, adam_m, adam_v, master, new_global):
    def kernel(frag, g0, g1, g3, m, v, w, glob, hbm_w, hbm_m, hbm_v, new_w, new_m, new_v, sems):
        at = pl.ds(pl.multiple_of(frag[0] * 128, 128), 128)
        copies = []
        for k in range(ROWS // STRIP):
            rows = pl.ds(k * STRIP, STRIP)
            grad = g0[rows, :] + g1[rows, :].astype(jnp.float32)
            grad = grad + g3[rows, :].astype(jnp.float32)
            mom = beta_first * m[rows, :] + (1.0 - beta_first) * grad
            var = beta_second * v[rows, :] + (1.0 - beta_second) * grad * grad
            new_m[rows, :] = mom
            new_v[rows, :] = var
            old = w[rows, :]
            new_w[rows, :] = old - inner_rate * (
                mom / (jnp.sqrt(var) + epsilon) + decay_rate * old
            )
            new_w[rows, at] = mix_share * new_w[rows, at] + (1.0 - mix_share) * glob[rows, :]
            for i, (source, target) in enumerate(
                ((new_w, hbm_w), (new_m, hbm_m), (new_v, hbm_v))
            ):
                copy = pltpu.make_async_copy(source.at[rows], target.at[rows], sems.at[i, k])
                copy.start()
                copies.append(copy)
        for copy in copies:
            copy.wait()

    return pl.pallas_call(
        kernel,
        in_specs=[pl.BlockSpec(memory_space=pltpu.SMEM)]
        + [pl.BlockSpec(memory_space=pltpu.VMEM)] * 7,
        out_specs=[pl.BlockSpec(memory_space=pltpu.HBM)] * 3,
        out_shape=[shape(ROWS, F, jnp.float32)] * 3,
        scratch_shapes=[pltpu.VMEM((ROWS, F), jnp.float32)] * 3
        + [pltpu.SemaphoreType.DMA((3, ROWS // STRIP))],
        cost_estimate=SMALL,
        compiler_params=VMEM,
        name="adam",
    )(frag_index, *grads, adam_m, adam_v, master, new_global)


def body(
    token_in, cotangent, weight, adam_m, adam_v, pseudo_grad, momentum, global_frag, frag_index
):
    tokens = token_in[0]
    up_own = cotangent[0]
    master = weight[0]

    send_x, send_far = pieces_of(tokens, up_own, [((1, 0, 0, TOK, 1),), ((1, 1, 0, TOK, 0),)])
    tok_x = swap_x(send_x)
    for_core = swap_x(send_far)
    weight_bf = after(master.astype(jnp.bfloat16), send_x)
    block_1 = shift_y(weight_bf, -1)
    block_3 = shift_y(weight_bf, 1)
    tok_own, send_core = pieces_of(
        after(tokens, send_x), up_own, [((0, 0, 0, TOK, 0),), ((0, 1, 0, TOK, 0),)]
    )
    tok_core = swap_core(send_core)
    up_pair = swap_core(jnp.concatenate([up_own, tok_x[:, PIECE:]]))
    block_2a = shift_y(block_1[:HALF], -1)
    block_2b = shift_y(block_3[HALF:], 1)
    blocks = (weight_bf, block_1, block_3, block_2a, block_2b)

    total = replica_step(after(pseudo_grad[0].astype(jnp.bfloat16), tok_core), lambda i: i ^ 6)
    up_ready, total = lax.optimization_barrier((up_own, total))

    ig_own, ig_x, ig_core, ig_far = input_grad((up_ready, tok_x, up_pair), blocks)
    back_x = swap_x(ig_x)
    back_far = swap_core(ig_far)
    back_other = swap_x(back_far)
    back_core = swap_core(ig_core)

    tok_far = swap_core(after(for_core, ig_own))
    toks = (tok_own, tok_x, tok_core, tok_far)
    g0, g1, g3, up_half, down_half = weight_grad_blocks(toks, (after(up_own, back_far), up_pair))
    s1, s3 = relay(after(g1, back_x), g3, shift_y(up_half, 1), shift_y(down_half, -1))
    r1 = shift_y(s1, 1)
    r3 = shift_y(s3, -1)

    total = replica_step(after(total, back_far), lambda i: i ^ 1)
    block_0 = after(weight_bf, g0, back_core)
    val_own, val_x, val_pair = value_parts(toks, (block_0, *blocks[1:]))
    val_back = swap_core(val_pair)
    total = replica_step(after(total, val_back), lambda i: i ^ 2)
    total = replica_step(after(total, s1), lambda i: i ^ 8)
    new_momentum, new_global = outer_update(momentum, global_frag, total / 16)

    val_far = swap_x((val_x + val_back[TOK:]).astype(jnp.bfloat16))
    values = val_own + val_back[:TOK] + val_far.astype(jnp.float32)
    values = (values * SCALE).astype(jnp.bfloat16)

    block = assemble(None, (ig_own, back_core, back_x), [((0, 0),), ((0, 1),), ((1, 0),)])
    new_weight, new_m, new_v = adam(
        frag_index, (g0, r1, r3), adam_m[0], adam_v[0], master, new_global
    )
    block = assemble(block, (after(back_other, new_weight),), [((1, 1),)])
    return (
        values[None],
        block[None],
        new_weight[None],
        new_m[None],
        new_v[None],
        new_global,
        new_momentum,
    )


def solution(mesh):
    in_specs = (
        P("replica", "fsdp", None),
        P("replica", "fsdp", None),
        P("replica", "fsdp", None),
        P("replica", "fsdp", None),
        P("replica", "fsdp", None),
        P("replica", "fsdp", None),
        P("fsdp", None),
        P("fsdp", None),
        P(),
    )
    out_specs = (
        P("replica", "fsdp", None),
        P("replica", "fsdp", None),
        P("replica", "fsdp", None),
        P("replica", "fsdp", None),
        P("replica", "fsdp", None),
        P("fsdp", None),
        P("fsdp", None),
    )
    return jax.shard_map(body, mesh=mesh, in_specs=in_specs, out_specs=out_specs, check_vma=False)
```

time: 85.4 us -> 76.3 us (0.89); the launches traced: 84.3 us -> 76.2 us
  waiting for transfers between devices: 35.5 us -> 30.9 us
  other arithmetic: 3.96 us -> 1.76 us
  starting transfers between devices: 31.9 us -> 30.5 us
    ppermute x4, waiting for transfers between devices: 10.3 us -> 2.82 us  [replica_step(): other = lax.ppermute(sent, 'replica', [(i, partner(i)) for i in range(16)])]
    ppermute x18 -> x19, waiting for transfers between devices: 25.2 us -> 28.1 us  [fsdp_permute(): return lax.ppermute(value, 'fsdp', pairs)]
    convert_element_type x5 -> x2, other arithmetic: 2.36 us -> 0.08 us  [the longest x1 0.07 us: body(): weight_bf = after(master.astype(jnp.bfloat16), send_x)]
    ppermute x4, starting transfers between devices: 9.15 us -> 8.21 us  [replica_step(): other = lax.ppermute(sent, 'replica', [(i, partner(i)) for i in range(16)])]
    ppermute x18 -> x19, starting transfers between devices: 22.8 us -> 22.3 us  [fsdp_permute(): return lax.ppermute(value, 'fsdp', pairs)]
    unnamed x18 -> x20, local copies, waits for them, and re-layouts: 2.75 us -> 2.53 us
    pallas_call x3 -> x4, Pallas kernels: 1.81 us -> 1.97 us  [the longest x1 1.29 us: input_grad(): pl.pallas_call(kernel, in_specs=[pl.BlockSpec(memory_space=pltpu.VMEM)] *...]
  transfers between devices with their start and end apart: 22 -> 23, of which waited for: 6 -> 8; matrix products, arithmetic and copies ran while one was open for 4% -> 2% of each run, Pallas kernels for 8% -> 10%
where the time goes in v3:
time: 76.3 us; the launch traced here: 76.2 us
  waiting for transfers between devices  30.9 us (40%)
  starting transfers between devices  30.5 us (40%)
  Pallas kernels  8.6 us (11%)
  local copies, waits for them, and re-layouts  2.58 us (3%)
  between operations  1.78 us (2%)
  other arithmetic  1.76 us (2%)
    ppermute x19, waiting for transfers between devices, fsdp_permute(): return lax.ppermute(value, 'fsdp', pairs)  28.1 us
    ppermute x19, starting transfers between devices, fsdp_permute(): return lax.ppermute(value, 'fsdp', pairs)  22.3 us
    ppermute x4, starting transfers between devices, replica_step(): other = lax.ppermute(sent, 'replica', [(i, partner(i)) for i in range(16)])  8.21 us
    ppermute x4, waiting for transfers between devices, replica_step(): other = lax.ppermute(sent, 'replica', [(i, partner(i)) for i in range(16)])  2.82 us
    unnamed x20, local copies, waits for them, and re-layouts  2.53 us
    pallas_call x2, Pallas kernels, assemble(): pl.pallas_call(kernel, in_specs=ins, out_specs=pl.BlockSpec(memory_space=...  2.07 us
    pallas_call x1, Pallas kernels, adam(): pl.pallas_call(kernel, in_specs=[pl.BlockSpec(memory_space=pltpu.SMEM)] +...  2.01 us
  transfers between devices with their start and end apart: 23, of which 8 were waited for; matrix products, arithmetic and copies ran while one was open for 2% of the time, Pallas kernels for 10%

profile of v3, /device:TPU:64, one launch (start us, length us, event | category | flops | bytes accessed | tf_op | source)
XLA Modules:
  0.0 76.2 jit_solution(6968591131164801846)
XLA Ops:
  0.6 1.6 %copy-done = bf16[1,128,8192]{2,1,0:T(8,128)(2,1)S(1)} copy-done((bf16[1,128,8192]{2,1,0:T(8,128)(2,1)S(1)}, bf16[1,128,8192]{2,1,0:T(8,128)(2,1)}, u32[]{:S(2)}) %copy-start) | copy-done | bytes 2097176
  2.2 0.9 %copy-done.2 = bf16[1,128,512]{2,1,0:T(8,128)(2,1)S(1)} copy-done((bf16[1,128,512]{2,1,0:T(8,128)(2,1)S(1)}, bf16[1,128,512]{2,1,0:T(8,128)(2,1)}, u32[]{:S(2)}) %copy-start.2) | copy-done | bytes 131096
  3.4 3.1 %collective-permute-start = (bf16[128,2560]{1,0:T(8,128)(2,1)S(1)}, bf16[128,2560]{1,0:T(8,128)(2,1)S(1)}, u32[]{:S(2)}, u32[]{:S(2)}) collective-permute-start(bf16[128,2560]{1,0:T(8,128)(2,1)S(1)} %get-tuple-element.41), channel_id=1, source_target_pairs={{0,8},{1,9},{2,10},{3,11},{4,12},{5,13},{6,14},{7,15},{8,0},{9,1},... | collective-permute-start | bytes 1966088 | tf_op jit(solution)/shard_map/ppermute | solution.py:37
  7.0 3.1 %collective-permute-start.5 = (bf16[512,512]{1,0:T(8,128)(2,1)S(1)}, bf16[512,512]{1,0:T(8,128)(2,1)S(1)}, u32[]{:S(2)}, u32[]{:S(2)}) collective-permute-start(bf16[512,512]{1,0:T(8,128)(2,1)S(1)} %bitcast_convert_fusion.refs_0_), channel_id=1, source_target_pairs={{0,6},{1,7},{2,0},{3,1},{4,2},{5,3},{6,4},{7,5},{8,14},{9,15},{10,... | collective-permute-start | bytes 1572872 | tf_op jit(solution)/shard_map/ppermute | solution.py:37
  10.1 0.5 collective-permute-start.2
  10.6 4.6 %collective-permute-start.3 = (bf16[512,128]{1,0:T(8,128)(2,1)S(1)}, bf16[512,128]{1,0:T(8,128)(2,1)S(1)}, u32[]{:S(2)}, u32[]{:S(2)}) collective-permute-start(bf16[512,128]{1,0:T(8,128)(2,1)S(1)} %convert_bitcast_fusion), channel_id=1, source_target_pairs={{0,96},{16,112},{32,64},{48,80},{64,32},{80,48},{96,0},{112,16},{1... | collective-permute-start | bytes 393224 | tf_op jit(solution)/shard_map/ppermute | solution.py:54
  15.2 6.7 %collective-permute-done.5.refs_1_ = bf16[512,512]{1,0:T(8,128)(2,1)S(1)} collective-permute-done((bf16[512,512]{1,0:T(8,128)(2,1)S(1)}, bf16[512,512]{1,0:T(8,128)(2,1)S(1)}, u32[]{:S(2)}, u32[]{:S(2)}) %collective-permute-start.5) | collective-permute-done | bytes 524320 | tf_op jit(solution)/shard_map/ppermute | solution.py:37
  22.0 3.8 %collective-permute-start.7 = (bf16[256,512]{1,0:T(8,128)(2,1)S(1)}, bf16[256,512]{1,0:T(8,128)(2,1)S(1)}, u32[]{:S(2)}, u32[]{:S(2)}) collective-permute-start(bf16[256,512]{1,0:T(8,128)(2,1)S(1)} %slice.21), channel_id=1, source_target_pairs={{0,6},{1,7},{2,0},{3,1},{4,2},{5,3},{6,4},{7,5},{8,14},{9,15},{10,... | collective-permute-start | bytes 786440 | tf_op jit(solution)/shard_map/ppermute | solution.py:37
  26.1 5.1 %collective-permute-done.7.refs_3_ = bf16[256,512]{1,0:T(8,128)(2,1)S(1)} collective-permute-done((bf16[256,512]{1,0:T(8,128)(2,1)S(1)}, bf16[256,512]{1,0:T(8,128)(2,1)S(1)}, u32[]{:S(2)}, u32[]{:S(2)}) %collective-permute-start.7) | collective-permute-done | bytes 262176 | tf_op jit(solution)/shard_map/ppermute | solution.py:37
  31.2 3.5 %collective-permute-done.8.refs_4_ = bf16[256,512]{1,0:T(8,128)(2,1)S(1)} collective-permute-done((bf16[256,512]{1,0:T(8,128)(2,1)S(1)}, bf16[256,512]{1,0:T(8,128)(2,1)S(1)}, u32[]{:S(2)}, u32[]{:S(2)}) %collective-permute-start.8) | collective-permute-done | bytes 262176 | tf_op jit(solution)/shard_map/ppermute | solution.py:37
  34.7 1.3 %input_grad.1 = (bf16[128,2048]{1,0:T(8,128)(2,1)S(1)}, bf16[128,2048]{1,0:T(8,128)(2,1)S(1)}, bf16[128,2048]{1,0:T(8,128)(2,1)S(1)}, bf16[128,2048]{1,0:T(8,128)(2,1)S(1)}) custom-call(bf16[128,512]{1,0:T(8,128)(2,1)S(1)} %bitcast.20, bf16[128,2560]{1,0:T(8,128)(2,1)S(1)} %collective-permute-done.u1.t1, bf16[256,512]{1,0:T(8,128)(2,1)S(1)} %collective-permute-done.4.u2, ...), custom_call_target="tpu_custom_call" | custom-call | flops 1 | bytes 1 | tf_op jit(solution)/shard_map/input_grad/pallas_call | solution.py:145
  36.1 0.5 collective-permute-start.9
  36.7 0.5 collective-permute-start.15
  37.2 0.8 %collective-permute-done.10 = bf16[128,2048]{1,0:T(8,128)(2,1)S(1)} collective-permute-done((bf16[128,2048]{1,0:T(8,128)(2,1)S(1)}, bf16[128,2048]{1,0:T(8,128)(2,1)S(1)}, u32[]{:S(2)}, u32[]{:S(2)}) %collective-permute-start.10) | collective-permute-done | bytes 524320 | tf_op jit(solution)/shard_map/ppermute | solution.py:37
  38.0 0.7 collective-permute-done.9.t3
  38.7 1.3 %weight_grad.1 = (f32[512,512]{1,0:T(8,128)S(1)}, f32[512,512]{1,0:T(8,128)S(1)}, f32[512,512]{1,0:T(8,128)S(1)}, bf16[256,512]{1,0:T(8,128)(2,1)S(1)}, bf16[256,512]{1,0:T(8,128)(2,1)S(1)}) custom-call(bf16[128,2048]{1,0:T(8,128)(2,1)S(1)} %get-tuple-element.43.t0, bf16[128,2560]{1,0:T(8,128)(2,1)S(1)} %collective-permute-done.u1.t1, ...), custom_call_target="tpu_custom_call" | custom-call | flops 1 | bytes 1 | tf_op jit(solution)/shard_map/weight_grad/pallas_call | solution.py:194
  40.1 1.2 %values.1 = (f32[128,512]{1,0:T(8,128)S(1)}, f32[128,512]{1,0:T(8,128)S(1)}, f32[256,512]{1,0:T(8,128)S(1)}) custom-call(bf16[128,2048]{1,0:T(8,128)(2,1)S(1)} %get-tuple-element.43.t0, bf16[128,2560]{1,0:T(8,128)(2,1)S(1)} %collective-permute-done.u1.t1, bf16[128,2048]{1,0:T(8,128)(2,1)S(1)} %collective-permute-done.1.t2, ...), custom_call_target="tpu_custom_call" | custom-call | flops 1 | bytes 1 | tf_op jit(solution)/shard_map/values/pallas_call | solution.py:167
  41.5 2.1 %collective-permute-start.20 = (bf16[512,128]{1,0:T(8,128)(2,1)S(1)}, bf16[512,128]{1,0:T(8,128)(2,1)S(1)}, u32[]{:S(2)}, u32[]{:S(2)}) collective-permute-start(bf16[512,128]{1,0:T(8,128)(2,1)S(1)} %convert_add_fusion.2), channel_id=1, source_target_pairs={{0,16},{16,0},{32,48},{48,32},{64,80},{80,64},{96,112},{112,96},{1... | collective-permute-start | bytes 393224 | tf_op jit(solution)/shard_map/ppermute | solution.py:54
  43.6 3.2 %collective-permute-start.17 = (bf16[256,512]{1,0:T(8,128)(2,1)S(1)}, bf16[256,512]{1,0:T(8,128)(2,1)S(1)}, u32[]{:S(2)}, u32[]{:S(2)}) collective-permute-start(bf16[256,512]{1,0:T(8,128)(2,1)S(1)} %get-tuple-element.64), channel_id=1, source_target_pairs={{0,6},{1,7},{2,0},{3,1},{4,2},{5,3},{6,4},{7,5},{8,14},{9,15},{10,... | collective-permute-start | bytes 786440 | tf_op jit(solution)/shard_map/ppermute | solution.py:37
  47.5 5.0 %collective-permute-done.15.refs_2_ = bf16[128,2048]{1,0:T(8,128)(2,1)S(1)} collective-permute-done((bf16[128,2048]{1,0:T(8,128)(2,1)S(1)}, bf16[128,2048]{1,0:T(8,128)(2,1)S(1)}, u32[]{:S(2)}, u32[]{:S(2)}) %collective-permute-start.15) | collective-permute-done | bytes 524320 | tf_op jit(solution)/shard_map/ppermute | solution.py:37
  52.4 0.5 collective-permute-start.14
  53.0 1.2 %assemble.2.refs_1_ = bf16[128,8192]{1,0:T(8,128)(2,1)} custom-call(bf16[128,2048]{1,0:T(8,128)(2,1)S(1)} %get-tuple-element.49.refs_0_, bf16[128,2048]{1,0:T(8,128)(2,1)S(1)} %collective-permute-done.11.refs_1_, bf16[128,2048]{1,0:T(8,128)(2,1)S(1)} %collective-permute-done.15.refs_2_), custom_call_target="tpu_custom_call" | custom-call | flops 1 | bytes 1 | tf_op jit(solution)/shard_map/assemble/pallas_call | solution.py:252
  54.5 0.3 collective-permute-start.18
  54.8 3.0 %collective-permute-start.19 = (bf16[512,512]{1,0:T(8,128)(2,1)S(1)}, bf16[512,512]{1,0:T(8,128)(2,1)S(1)}, u32[]{:S(2)}, u32[]{:S(2)}) collective-permute-start(bf16[512,512]{1,0:T(8,128)(2,1)S(1)} %get-tuple-element.66), channel_id=1, source_target_pairs={{0,6},{1,7},{2,0},{3,1},{4,2},{5,3},{6,4},{7,5},{8,14},{9,15},{10,... | collective-permute-start | bytes 1572872 | tf_op jit(solution)/shard_map/ppermute | solution.py:37
  57.8 3.1 %collective-permute-start.13 = (bf16[128,512]{1,0:T(8,128)(2,1)S(1)}, bf16[128,512]{1,0:T(8,128)(2,1)S(1)}, u32[]{:S(2)}, u32[]{:S(2)}) collective-permute-start(bf16[128,512]{1,0:T(8,128)(2,1)S(1)} %fusion), channel_id=1, source_target_pairs={{0,8},{1,9},{2,10},{3,11},{4,12},{5,13},{6,14},{7,15},{8,0},{9,1},... | collective-permute-start | bytes 393224 | tf_op jit(solution)/shard_map/ppermute | solution.py:37
  60.9 2.8 %collective-permute-done.21 = bf16[512,128]{1,0:T(8,128)(2,1)S(1)} collective-permute-done((bf16[512,128]{1,0:T(8,128)(2,1)S(1)}, bf16[512,128]{1,0:T(8,128)(2,1)S(1)}, u32[]{:S(2)}, u32[]{:S(2)}) %collective-permute-start.21) | collective-permute-done | bytes 131104 | tf_op jit(solution)/shard_map/ppermute | solution.py:54
  63.8 1.6 %collective-permute-start.22 = (bf16[512,128]{1,0:T(8,128)(2,1)S(1)}, bf16[512,128]{1,0:T(8,128)(2,1)S(1)}, u32[]{:S(2)}, u32[]{:S(2)}) collective-permute-start(bf16[512,128]{1,0:T(8,128)(2,1)S(1)} %convert_add_fusion), channel_id=1, source_target_pairs={{0,128},{16,144},{32,160},{48,176},{64,192},{80,208},{96,224},{112... | collective-permute-start | bytes 393224 | tf_op jit(solution)/shard_map/ppermute | solution.py:54
  65.4 6.2 %collective-permute-done.13 = bf16[128,512]{1,0:T(8,128)(2,1)S(1)} collective-permute-done((bf16[128,512]{1,0:T(8,128)(2,1)S(1)}, bf16[128,512]{1,0:T(8,128)(2,1)S(1)}, u32[]{:S(2)}, u32[]{:S(2)}) %collective-permute-start.13) | collective-permute-done | bytes 131104 | tf_op jit(solution)/shard_map/ppermute | solution.py:37
  71.6 0.7 fusion.4
  72.3 0.8 %multiply_subtract_fusion = (f32[512,128]{1,0:T(8,128)S(1)}, f32[512,128]{1,0:T(8,128)}) fusion(f32[512,128]{1,0:T(8,128)S(1)} %copy-done.7, bf16[512,128]{1,0:T(8,128)(2,1)S(1)} %collective-permute-done.22, bf16[512,128]{1,0:T(8,128)(2,1)S(1)} %convert_add_fusion, f32[512,128]{1,0:T(8,128)S(1)} %copy-done.8), kind=kLoop, calls=%fused_computation.7 | loop fusion | flops 655360 | bytes 1310720 | tf_op jit(solution)/shard_map/sub | solution.py:64
  73.1 2.0 %adam.1 = (f32[512,512]{1,0:T(8,128)}, f32[512,512]{1,0:T(8,128)}, f32[512,512]{1,0:T(8,128)}) custom-call(s32[1]{0:T(128)S(6)} %copy.18.frag, f32[512,512]{1,0:T(8,128)S(1)} %get-tuple-element.53.g0, bf16[512,512]{1,0:T(8,128)(2,1)S(1)} %collective-permute-done.18.g1, bf16[512,512]{1,0:T(8,128)(2,1)S(1)} %collective-permute-done.19.g3, ...), custom_call_target="tpu_custom_call" | custom-call | flops 1 | bytes 1 | tf_op jit(solution)/shard_map/adam/pallas_call | solution.py:294
  75.2 0.8 %assemble.3 = bf16[128,8192]{1,0:T(8,128)(2,1)} custom-call(bf16[128,2048]{1,0:T(8,128)(2,1)S(1)} %collective-permute-done.14.refs_0_, bf16[128,8192]{1,0:T(8,128)(2,1)} %assemble.2.refs_1_), custom_call_target="tpu_custom_call", output_to_operand_aliasing={{}: (1, {})} | custom-call | flops 1 | bytes 1 | tf_op jit(solution)/shard_map/assemble/pallas_call | solution.py:252
  (55 shorter events, 1.8 us)
Async XLA Ops:
  0.6 1.6 %copy-start = (bf16[1,128,8192]{2,1,0:T(8,128)(2,1)S(1)}, bf16[1,128,8192]{2,1,0:T(8,128)(2,1)}, u32[]{:S(2)}) copy-start(bf16[1,128,8192]{2,1,0:T(8,128)(2,1)} %param.9) | copy-start | bytes 6291460
  3.1 3.8 %copy-start.1 = (f32[1,512,512]{2,1,0:T(8,128)S(1)}, f32[1,512,512]{2,1,0:T(8,128)}, u32[]{:S(2)}) copy-start(f32[1,512,512]{2,1,0:T(8,128)} %param.11) | copy-start | bytes 3145732
  3.4 7.2 %copy-start.9 = (f32[1,512,128]{2,1,0:T(8,128)S(1)}, f32[1,512,128]{2,1,0:T(8,128)}, u32[]{:S(2)}) copy-start(f32[1,512,128]{2,1,0:T(8,128)} %param.14) | copy-start | bytes 786436
  3.4 22.4 %collective-permute-start = (bf16[128,2560]{1,0:T(8,128)(2,1)S(1)}, bf16[128,2560]{1,0:T(8,128)(2,1)S(1)}, u32[]{:S(2)}, u32[]{:S(2)}) collective-permute-start(bf16[128,2560]{1,0:T(8,128)(2,1)S(1)} %get-tuple-element.41), channel_id=1, source_target_pairs={{0,8},{1,9},{2,10},{3,11},{4,12},{5,13},{6,14},{7,15},{8,0},{9,1},... | collective-permute-start | bytes 1966088 | tf_op jit(solution)/shard_map/ppermute | solution.py:37
  6.8 27.9 %copy-start.3 = (bf16[1,128,512]{2,1,0:T(8,128)(2,1)S(1)}, bf16[1,128,512]{2,1,0:T(8,128)(2,1)}, u32[]{:S(2)}) copy-start(bf16[1,128,512]{2,1,0:T(8,128)(2,1)} %param.10) | copy-start | bytes 393220
  6.8 3.8 %collective-permute-start.1 = (bf16[128,2048]{1,0:T(8,128)(2,1)S(1)}, bf16[128,2048]{1,0:T(8,128)(2,1)S(1)}, u32[]{:S(2)}, u32[]{:S(2)}) collective-permute-start(bf16[128,2048]{1,0:T(8,128)(2,1)S(1)} %get-tuple-element.44), channel_id=1, source_target_pairs={{0,1},{1,0},{2,3},{3,2},{4,5},{5,4},{6,7},{7,6},{8,9},{9,8},{10,11... | collective-permute-start | bytes 1572872 | tf_op jit(solution)/shard_map/ppermute | solution.py:37
  7.0 14.9 %collective-permute-start.5 = (bf16[512,512]{1,0:T(8,128)(2,1)S(1)}, bf16[512,512]{1,0:T(8,128)(2,1)S(1)}, u32[]{:S(2)}, u32[]{:S(2)}) collective-permute-start(bf16[512,512]{1,0:T(8,128)(2,1)S(1)} %bitcast_convert_fusion.refs_0_), channel_id=1, source_target_pairs={{0,6},{1,7},{2,0},{3,1},{4,2},{5,3},{6,4},{7,5},{8,14},{9,15},{10,... | collective-permute-start | bytes 1572872 | tf_op jit(solution)/shard_map/ppermute | solution.py:37
  10.1 15.6 %collective-permute-start.6 = (bf16[512,512]{1,0:T(8,128)(2,1)S(1)}, bf16[512,512]{1,0:T(8,128)(2,1)S(1)}, u32[]{:S(2)}, u32[]{:S(2)}) collective-permute-start(bf16[512,512]{1,0:T(8,128)(2,1)S(1)} %bitcast_convert_fusion.refs_0_), channel_id=1, source_target_pairs={{0,2},{1,3},{2,4},{3,5},{4,6},{5,7},{6,0},{7,1},{8,10},{9,11},{10,... | collective-permute-start | bytes 1572872 | tf_op jit(solution)/shard_map/ppermute | solution.py:37
  10.1 26.0 %collective-permute-start.2 = (bf16[128,2048]{1,0:T(8,128)(2,1)S(1)}, bf16[128,2048]{1,0:T(8,128)(2,1)S(1)}, u32[]{:S(2)}, u32[]{:S(2)}) collective-permute-start(bf16[128,2048]{1,0:T(8,128)(2,1)S(1)} %get-tuple-element.45), channel_id=1, source_target_pairs={{0,8},{1,9},{2,10},{3,11},{4,12},{5,13},{6,14},{7,15},{8,0},{9,1},... | collective-permute-start | bytes 1572872 | tf_op jit(solution)/shard_map/ppermute | solution.py:37
  10.6 15.4 %collective-permute-start.3 = (bf16[512,128]{1,0:T(8,128)(2,1)S(1)}, bf16[512,128]{1,0:T(8,128)(2,1)S(1)}, u32[]{:S(2)}, u32[]{:S(2)}) collective-permute-start(bf16[512,128]{1,0:T(8,128)(2,1)S(1)} %convert_bitcast_fusion), channel_id=1, source_target_pairs={{0,96},{16,112},{32,64},{48,80},{64,32},{80,48},{96,0},{112,16},{1... | collective-permute-start | bytes 393224 | tf_op jit(solution)/shard_map/ppermute | solution.py:54
  22.0 9.2 %collective-permute-start.7 = (bf16[256,512]{1,0:T(8,128)(2,1)S(1)}, bf16[256,512]{1,0:T(8,128)(2,1)S(1)}, u32[]{:S(2)}, u32[]{:S(2)}) collective-permute-start(bf16[256,512]{1,0:T(8,128)(2,1)S(1)} %slice.21), channel_id=1, source_target_pairs={{0,6},{1,7},{2,0},{3,1},{4,2},{5,3},{6,4},{7,5},{8,14},{9,15},{10,... | collective-permute-start | bytes 786440 | tf_op jit(solution)/shard_map/ppermute | solution.py:37
  25.8 8.9 %collective-permute-start.8 = (bf16[256,512]{1,0:T(8,128)(2,1)S(1)}, bf16[256,512]{1,0:T(8,128)(2,1)S(1)}, u32[]{:S(2)}, u32[]{:S(2)}) collective-permute-start(bf16[256,512]{1,0:T(8,128)(2,1)S(1)} %slice.22), channel_id=1, source_target_pairs={{0,2},{1,3},{2,4},{3,5},{4,6},{5,7},{6,0},{7,1},{8,10},{9,11},{10,... | collective-permute-start | bytes 786440 | tf_op jit(solution)/shard_map/ppermute | solution.py:37
  25.9 8.8 %collective-permute-start.4 = (bf16[256,512]{1,0:T(8,128)(2,1)S(1)}, bf16[256,512]{1,0:T(8,128)(2,1)S(1)}, u32[]{:S(2)}, u32[]{:S(2)}) collective-permute-start(bf16[256,512]{1,0:T(8,128)(2,1)S(1)} %pad_maximum_fusion), channel_id=1, source_target_pairs={{0,1},{1,0},{2,3},{3,2},{4,5},{5,4},{6,7},{7,6},{8,9},{9,8},{10,11... | collective-permute-start | bytes 786440 | tf_op jit(solution)/shard_map/ppermute | solution.py:37
  36.0 2.0 %collective-permute-start.10 = (bf16[128,2048]{1,0:T(8,128)(2,1)S(1)}, bf16[128,2048]{1,0:T(8,128)(2,1)S(1)}, u32[]{:S(2)}, u32[]{:S(2)}) collective-permute-start(bf16[128,2048]{1,0:T(8,128)(2,1)S(1)} %get-tuple-element.51), channel_id=1, source_target_pairs={{0,1},{1,0},{2,3},{3,2},{4,5},{5,4},{6,7},{7,6},{8,9},{9,8},{10,11... | collective-permute-start | bytes 1572872 | tf_op jit(solution)/shard_map/ppermute | solution.py:37
  36.1 2.6 %collective-permute-start.9 = (bf16[128,2048]{1,0:T(8,128)(2,1)S(1)}, bf16[128,2048]{1,0:T(8,128)(2,1)S(1)}, u32[]{:S(2)}, u32[]{:S(2)}) collective-permute-start(bf16[128,2048]{1,0:T(8,128)(2,1)S(1)} %collective-permute-done.2), channel_id=1, source_target_pairs={{0,1},{1,0},{2,3},{3,2},{4,5},{5,4},{6,7},{7,6},{8,9},{9,8},{10,11... | collective-permute-start | bytes 1572872 | tf_op jit(solution)/shard_map/ppermute | solution.py:37
  36.6 3.5 %collective-permute-start.11 = (bf16[128,2048]{1,0:T(8,128)(2,1)S(1)}, bf16[128,2048]{1,0:T(8,128)(2,1)S(1)}, u32[]{:S(2)}, u32[]{:S(2)}) collective-permute-start(bf16[128,2048]{1,0:T(8,128)(2,1)S(1)} %get-tuple-element.54), channel_id=1, source_target_pairs={{0,1},{1,0},{2,3},{3,2},{4,5},{5,4},{6,7},{7,6},{8,9},{9,8},{10,11... | collective-permute-start | bytes 1572872 | tf_op jit(solution)/shard_map/ppermute | solution.py:37
  36.7 15.8 %collective-permute-start.15 = (bf16[128,2048]{1,0:T(8,128)(2,1)S(1)}, bf16[128,2048]{1,0:T(8,128)(2,1)S(1)}, u32[]{:S(2)}, u32[]{:S(2)}) collective-permute-start(bf16[128,2048]{1,0:T(8,128)(2,1)S(1)} %get-tuple-element.60), channel_id=1, source_target_pairs={{0,8},{1,9},{2,10},{3,11},{4,12},{5,13},{6,14},{7,15},{8,0},{9,1},... | collective-permute-start | bytes 1572872 | tf_op jit(solution)/shard_map/ppermute | solution.py:37
  41.3 16.5 %collective-permute-start.12 = (f32[256,512]{1,0:T(8,128)S(1)}, f32[256,512]{1,0:T(8,128)S(1)}, u32[]{:S(2)}, u32[]{:S(2)}) collective-permute-start(f32[256,512]{1,0:T(8,128)S(1)} %get-tuple-element.57), channel_id=1, source_target_pairs={{0,1},{1,0},{2,3},{3,2},{4,5},{5,4},{6,7},{7,6},{8,9},{9,8},{10,11... | collective-permute-start | bytes 1572872 | tf_op jit(solution)/shard_map/ppermute | solution.py:37
  41.5 12.7 %collective-permute-start.20 = (bf16[512,128]{1,0:T(8,128)(2,1)S(1)}, bf16[512,128]{1,0:T(8,128)(2,1)S(1)}, u32[]{:S(2)}, u32[]{:S(2)}) collective-permute-start(bf16[512,128]{1,0:T(8,128)(2,1)S(1)} %convert_add_fusion.2), channel_id=1, source_target_pairs={{0,16},{16,0},{32,48},{48,32},{64,80},{80,64},{96,112},{112,96},{1... | collective-permute-start | bytes 393224 | tf_op jit(solution)/shard_map/ppermute | solution.py:54
  43.6 10.7 %collective-permute-start.16 = (bf16[256,512]{1,0:T(8,128)(2,1)S(1)}, bf16[256,512]{1,0:T(8,128)(2,1)S(1)}, u32[]{:S(2)}, u32[]{:S(2)}) collective-permute-start(bf16[256,512]{1,0:T(8,128)(2,1)S(1)} %get-tuple-element.63), channel_id=1, source_target_pairs={{0,2},{1,3},{2,4},{3,5},{4,6},{5,7},{6,0},{7,1},{8,10},{9,11},{10,... | collective-permute-start | bytes 786440 | tf_op jit(solution)/shard_map/ppermute | solution.py:37
  43.6 10.7 %collective-permute-start.17 = (bf16[256,512]{1,0:T(8,128)(2,1)S(1)}, bf16[256,512]{1,0:T(8,128)(2,1)S(1)}, u32[]{:S(2)}, u32[]{:S(2)}) collective-permute-start(bf16[256,512]{1,0:T(8,128)(2,1)S(1)} %get-tuple-element.64), channel_id=1, source_target_pairs={{0,6},{1,7},{2,0},{3,1},{4,2},{5,3},{6,4},{7,5},{8,14},{9,15},{10,... | collective-permute-start | bytes 786440 | tf_op jit(solution)/shard_map/ppermute | solution.py:37
  52.4 22.7 %collective-permute-start.14 = (bf16[128,2048]{1,0:T(8,128)(2,1)S(1)}, bf16[128,2048]{1,0:T(8,128)(2,1)S(1)}, u32[]{:S(2)}, u32[]{:S(2)}) collective-permute-start(bf16[128,2048]{1,0:T(8,128)(2,1)S(1)} %collective-permute-done.10), channel_id=1, source_target_pairs={{0,8},{1,9},{2,10},{3,11},{4,12},{5,13},{6,14},{7,15},{8,0},{9,1},... | collective-permute-start | bytes 1572872 | tf_op jit(solution)/shard_map/ppermute | solution.py:37
  54.3 18.1 %copy-start.7 = (f32[512,128]{1,0:T(8,128)S(1)}, f32[512,128]{1,0:T(8,128)}, u32[]{:S(2)}) copy-start(f32[512,128]{1,0:T(8,128)} %param.16) | copy-start | bytes 786436
  54.3 18.0 %copy-start.8 = (f32[512,128]{1,0:T(8,128)S(1)}, f32[512,128]{1,0:T(8,128)}, u32[]{:S(2)}) copy-start(f32[512,128]{1,0:T(8,128)} %param.15) | copy-start | bytes 786436
  54.4 18.7 %copy-start.5 = (f32[1,512,512]{2,1,0:T(8,128)S(1)}, f32[1,512,512]{2,1,0:T(8,128)}, u32[]{:S(2)}) copy-start(f32[1,512,512]{2,1,0:T(8,128)} %param.12) | copy-start | bytes 3145732
  54.5 18.7 %copy-start.6 = (f32[1,512,512]{2,1,0:T(8,128)S(1)}, f32[1,512,512]{2,1,0:T(8,128)}, u32[]{:S(2)}) copy-start(f32[1,512,512]{2,1,0:T(8,128)} %param.13) | copy-start | bytes 3145732
  54.5 18.7 %collective-permute-start.18 = (bf16[512,512]{1,0:T(8,128)(2,1)S(1)}, bf16[512,512]{1,0:T(8,128)(2,1)S(1)}, u32[]{:S(2)}, u32[]{:S(2)}) collective-permute-start(bf16[512,512]{1,0:T(8,128)(2,1)S(1)} %get-tuple-element.65), channel_id=1, source_target_pairs={{0,2},{1,3},{2,4},{3,5},{4,6},{5,7},{6,0},{7,1},{8,10},{9,11},{10,... | collective-permute-start | bytes 1572872 | tf_op jit(solution)/shard_map/ppermute | solution.py:37
  54.8 18.4 %collective-permute-start.19 = (bf16[512,512]{1,0:T(8,128)(2,1)S(1)}, bf16[512,512]{1,0:T(8,128)(2,1)S(1)}, u32[]{:S(2)}, u32[]{:S(2)}) collective-permute-start(bf16[512,512]{1,0:T(8,128)(2,1)S(1)} %get-tuple-element.66), channel_id=1, source_target_pairs={{0,6},{1,7},{2,0},{3,1},{4,2},{5,3},{6,4},{7,5},{8,14},{9,15},{10,... | collective-permute-start | bytes 1572872 | tf_op jit(solution)/shard_map/ppermute | solution.py:37
  57.8 6.0 %collective-permute-start.21 = (bf16[512,128]{1,0:T(8,128)(2,1)S(1)}, bf16[512,128]{1,0:T(8,128)(2,1)S(1)}, u32[]{:S(2)}, u32[]{:S(2)}) collective-permute-start(bf16[512,128]{1,0:T(8,128)(2,1)S(1)} %convert_add_fusion.1), channel_id=1, source_target_pairs={{0,32},{16,48},{32,0},{48,16},{64,96},{80,112},{96,64},{112,80},{1... | collective-permute-start | bytes 393224 | tf_op jit(solution)/shard_map/ppermute | solution.py:54
  57.8 13.8 %collective-permute-start.13 = (bf16[128,512]{1,0:T(8,128)(2,1)S(1)}, bf16[128,512]{1,0:T(8,128)(2,1)S(1)}, u32[]{:S(2)}, u32[]{:S(2)}) collective-permute-start(bf16[128,512]{1,0:T(8,128)(2,1)S(1)} %fusion), channel_id=1, source_target_pairs={{0,8},{1,9},{2,10},{3,11},{4,12},{5,13},{6,14},{7,15},{8,0},{9,1},... | collective-permute-start | bytes 393224 | tf_op jit(solution)/shard_map/ppermute | solution.py:37
  63.8 8.5 %collective-permute-start.22 = (bf16[512,128]{1,0:T(8,128)(2,1)S(1)}, bf16[512,128]{1,0:T(8,128)(2,1)S(1)}, u32[]{:S(2)}, u32[]{:S(2)}) collective-permute-start(bf16[512,128]{1,0:T(8,128)(2,1)S(1)} %convert_add_fusion), channel_id=1, source_target_pairs={{0,128},{16,144},{32,160},{48,176},{64,192},{80,208},{96,224},{112... | collective-permute-start | bytes 393224 | tf_op jit(solution)/shard_map/ppermute | solution.py:54
  73.1 2.1 %copy-start.4 = (f32[512,128]{1,0:T(8,128)}, f32[512,128]{1,0:T(8,128)S(1)}, u32[]{:S(2)}) copy-start(f32[512,128]{1,0:T(8,128)S(1)} %get-tuple-element.75.glob) | copy-start | bytes 786436
  (1 other events, 0.9 us)

commit v4 on v3

--- a/solution.py
+++ b/solution.py
@@ -25,6 +25,8 @@
 F = 512
 PIECE = NY * ROWS
 HALF = ROWS // 2
+FIRST = 96
+LATER = 320
 VMEM = pltpu.CompilerParams(vmem_limit_bytes=40 * 1024 * 1024)
 
 
@@ -130,17 +132,14 @@
 
 def input_grad(ups, blocks):
     def kernel(u0, u1, u2, *refs):
-        own, far_x, core, far = refs[5:]
-        up = jnp.concatenate([u0[...], u1[:, PIECE:], u2[...]], axis=0)
+        up = jnp.concatenate([u0[...], u1[...], u2[...]], axis=0)
         for at, block in places(refs[:5]):
             grad = lax.dot_general(
                 up, block[...], (((1,), (1,)), ((), ())), preferred_element_type=jnp.float32
             )
             grad = (grad * SCALE).astype(jnp.bfloat16)
-            own[:, at] = grad[:TOK]
-            far_x[:, at] = grad[TOK : 2 * TOK]
-            core[:, at] = grad[2 * TOK : 3 * TOK]
-            far[:, at] = grad[3 * TOK :]
+            for k, out in enumerate(refs[5:]):
+                out[:, at] = grad[k * TOK : (k + 1) * TOK]
 
     return pl.pallas_call(
         kernel,
@@ -162,99 +161,158 @@
             total += jnp.dot(tok, block[...], preferred_element_type=jnp.float32)
         own[...] = total[:TOK]
         far[...] = total[TOK : 2 * TOK]
-        pair[...] = total[2 * TOK :]
+        pair[...] = total[2 * TOK :].astype(jnp.bfloat16)
 
     return pl.pallas_call(
         kernel,
         in_specs=[pl.BlockSpec(memory_space=pltpu.VMEM)] * 9,
         out_specs=[pl.BlockSpec(memory_space=pltpu.VMEM)] * 3,
-        out_shape=[shape(TOK, F, jnp.float32)] * 2 + [shape(2 * TOK, F, jnp.float32)],
+        out_shape=[shape(TOK, F, jnp.float32)] * 2 + [shape(2 * TOK, F)],
         cost_estimate=SMALL,
         compiler_params=VMEM,
         name="values",
     )(*toks, *blocks)
 
 
-def weight_grad_blocks(toks, ups):
-    def kernel(t0, t1, t2, t3, u0, u2, g0, g1, g3, up_half, down_half):
-        up = jnp.concatenate([u0[...], t1[:, PIECE:], u2[...]], axis=0)
+def split(passed):
+    def kernel(passed, out):
+        out[...] = passed[:FIRST]
+
+    return pl.pallas_call(
+        kernel,
+        in_specs=[pl.BlockSpec(memory_space=pltpu.VMEM)],
+        out_specs=pl.BlockSpec(memory_space=pltpu.VMEM),
+        out_shape=shape(FIRST, PIECE),
+        cost_estimate=SMALL,
+        compiler_params=VMEM,
+        name="split",
+    )(passed)
+
+
+def pack(passed, val_back, val_x):
+    rest = TOK - FIRST
+
+    def kernel(passed, val_back, val_x, out):
+        out[:rest] = passed[FIRST:]
+        total = val_x[...] + val_back[TOK:].astype(jnp.float32)
+        for k in range(NY):
+            rows = slice(k * rest, (k + 1) * rest)
+            out[rest:, k * F : (k + 1) * F] = total[rows].astype(jnp.bfloat16)
+
+    return pl.pallas_call(
+        kernel,
+        in_specs=[pl.BlockSpec(memory_space=pltpu.VMEM)] * 3,
+        out_specs=pl.BlockSpec(memory_space=pltpu.VMEM),
+        out_shape=shape(2 * rest, PIECE),
+        cost_estimate=SMALL,
+        compiler_params=VMEM,
+        name="pack",
+    )(passed, val_back, val_x)
+
+
+def weight_grad(toks, ups):
+    def kernel(t0, t1, t2, t3, u0, u1, u2, own, to_above, to_below, keep_above, keep_below):
+        up = jnp.concatenate([u0[...], u1[...], u2[...]], axis=0)
         y = here()[1]
-        for step in (2, 1, 3, 0):
+
+        def block(step):
             at = pl.ds(pl.multiple_of(lax.rem(y + step, NY) * ROWS, ROWS), ROWS)
             tok = jnp.concatenate([t0[:, at], t1[:, at], t2[:, at], t3[:, at]], axis=0)
-            grad = SCALE * lax.dot_general(
+            return SCALE * lax.dot_general(
                 tok, up, (((0,), (0,)), ((), ())), preferred_element_type=jnp.float32
             )
-            if step == 2:
-                up_half[...] = grad[:HALF].astype(jnp.bfloat16)
-                down_half[...] = grad[HALF:].astype(jnp.bfloat16)
-            else:
-                {0: g0, 1: g1, 3: g3}[step][...] = grad
-
-    return pl.pallas_call(
-        kernel,
-        in_specs=[pl.BlockSpec(memory_space=pltpu.VMEM)] * 6,
+
+        grad = block(2)
+        to_above[:HALF] = grad[:HALF].astype(jnp.bfloat16)
+        to_below[:HALF] = grad[HALF:].astype(jnp.bfloat16)
+        grad = block(1)
+        keep_above[...] = grad[:LATER]
+        to_above[HALF:] = grad[LATER:].astype(jnp.bfloat16)
+        grad = block(3)
+        to_below[HALF:] = grad[: ROWS - LATER].astype(jnp.bfloat16)
+        keep_below[...] = grad[ROWS - LATER :]
+        own[...] = block(0)
+
+    return pl.pallas_call(
+        kernel,
+        in_specs=[pl.BlockSpec(memory_space=pltpu.VMEM)] * 7,
         out_specs=[pl.BlockSpec(memory_space=pltpu.VMEM)] * 5,
-        out_shape=[shape(ROWS, F, jnp.float32)] * 3 + [shape(HALF, F)] * 2,
+        out_shape=[shape(ROWS, F, jnp.float32)]
+        + [shape(HALF + ROWS - LATER, F)] * 2
+        + [shape(LATER, F, jnp.float32)] * 2,
         cost_estimate=SMALL,
         compiler_params=VMEM,
         name="weight_grad",
     )(*toks, *ups)
 
 
-def relay(g1, g3, from_below, from_above):
-    def kernel(g1, g3, from_below, from_above, s1, s3):
-        s1[:HALF] = (g1[:HALF] + from_below[...].astype(jnp.float32)).astype(jnp.bfloat16)
-        s1[HALF:] = g1[HALF:].astype(jnp.bfloat16)
-        s3[:HALF] = g3[:HALF].astype(jnp.bfloat16)
-        s3[HALF:] = (g3[HALF:] + from_above[...].astype(jnp.float32)).astype(jnp.bfloat16)
+def relay(keep_above, keep_below, from_below, from_above):
+    def kernel(keep_above, keep_below, from_below, from_above, to_above, to_below):
+        more = LATER - HALF
+        came = from_below[:HALF].astype(jnp.float32)
+        to_above[:HALF] = (keep_above[:HALF] + came).astype(jnp.bfloat16)
+        to_above[HALF:] = keep_above[HALF:].astype(jnp.bfloat16)
+        came = from_above[:HALF].astype(jnp.float32)
+        to_below[:more] = keep_below[:more].astype(jnp.bfloat16)
+        to_below[more:] = (keep_below[more:] + came).astype(jnp.bfloat16)
 
     return pl.pallas_call(
         kernel,
         in_specs=[pl.BlockSpec(memory_space=pltpu.VMEM)] * 4,
         out_specs=[pl.BlockSpec(memory_space=pltpu.VMEM)] * 2,
-        out_shape=[shape(ROWS, F)] * 2,
+        out_shape=[shape(LATER, F)] * 2,
         cost_estimate=SMALL,
         compiler_params=VMEM,
         name="relay",
-    )(g1, g3, from_below, from_above)
-
-
-def assemble(block, parts, wanted):
+    )(keep_above, keep_below, from_below, from_above)
+
+
+def assemble(block, parts, wanted, vals=()):
     n = len(wanted)
-    groups = [(i, j, g) for i, stack in enumerate(wanted) for j, g in enumerate(stack)]
 
     def kernel(*refs):
-        target, sems = refs[-2:]
+        target, sems = refs[-3 if vals else -2], refs[-1]
         x, _, c = here()
         copies = []
-        for m, (i, j, (dx, dc)) in enumerate(groups):
+        for i, (dx, dc, start, size) in enumerate(wanted):
             for k in range(NY):
+                place = column(1 - x if dx else x, k, 1 - c if dc else c)
                 copies.append(
                     pltpu.make_async_copy(
-                        refs[i].at[pl.ds(j * TOK, TOK), pl.ds(k * ROWS, ROWS)],
-                        target.at[:, column(1 - x if dx else x, k, 1 - c if dc else c)],
-                        sems.at[m * NY + k],
+                        refs[i].at[pl.ds(0, size), pl.ds(k * ROWS, ROWS)],
+                        target.at[pl.ds(start, size), place],
+                        sems.at[i * NY + k],
                     )
                 )
         for copy in copies:
             copy.start()
+        if vals:
+            own, pair = refs[n : n + 2]
+            rest = TOK - FIRST
+            total = own[...] + pair[:TOK].astype(jnp.float32)
+            for k in range(NY):
+                rows = slice(k * rest, (k + 1) * rest)
+                came = refs[n - 1][rest:, k * F : (k + 1) * F].astype(jnp.float32)
+                refs[-2][rows] = ((total[rows] + came) * SCALE).astype(jnp.bfloat16)
         for copy in copies:
             copy.wait()
 
-    args = list(parts)
-    ins = [pl.BlockSpec(memory_space=pltpu.VMEM)] * n
-    alias = {}
+    args = [*parts, *vals]
+    ins = [pl.BlockSpec(memory_space=pltpu.VMEM)] * len(args)
+    outs, shapes, alias = [pl.BlockSpec(memory_space=pltpu.HBM)], [shape(TOK, D)], {}
+    if vals:
+        outs.append(pl.BlockSpec(memory_space=pltpu.VMEM))
+        shapes.append(shape(TOK, F))
     if block is not None:
-        alias = {n: 0}
+        alias = {len(args): 0}
         ins.append(pl.BlockSpec(memory_space=pltpu.HBM))
         args.append(block)
     return pl.pallas_call(
         kernel,
         in_specs=ins,
-        out_specs=pl.BlockSpec(memory_space=pltpu.HBM),
-        out_shape=shape(TOK, D),
-        scratch_shapes=[pltpu.SemaphoreType.DMA((NY * len(groups),))],
+        out_specs=outs if vals else outs[0],
+        out_shape=shapes if vals else shapes[0],
+        scratch_shapes=[pltpu.SemaphoreType.DMA((NY * n,))],
         input_output_aliases=alias,
         cost_estimate=SMALL,
         compiler_params=VMEM,
@@ -266,13 +324,22 @@
 
 
 def adam(frag_index, grads, adam_m, adam_v, master, new_global):
-    def kernel(frag, g0, g1, g3, m, v, w, glob, hbm_w, hbm_m, hbm_v, new_w, new_m, new_v, sems):
+    def kernel(frag, g0, from_above, r1, from_below, r3, m, v, w, glob, hbm_w, hbm_m, hbm_v, new_w, new_m, new_v, sems):
         at = pl.ds(pl.multiple_of(frag[0] * 128, 128), 128)
         copies = []
         for k in range(ROWS // STRIP):
             rows = pl.ds(k * STRIP, STRIP)
-            grad = g0[rows, :] + g1[rows, :].astype(jnp.float32)
-            grad = grad + g3[rows, :].astype(jnp.float32)
+            top = k * STRIP
+            if top < LATER:
+                grad = g0[rows, :] + r1[rows, :].astype(jnp.float32)
+            else:
+                came = from_below[pl.ds(HALF + top - LATER, STRIP), :]
+                grad = g0[rows, :] + came.astype(jnp.float32)
+            if top < ROWS - LATER:
+                grad = grad + from_above[pl.ds(HALF + top, STRIP), :].astype(jnp.float32)
+            else:
+                came = r3[pl.ds(top - (ROWS - LATER), STRIP), :]
+                grad = grad + came.astype(jnp.float32)
             mom = beta_first * m[rows, :] + (1.0 - beta_first) * grad
             var = beta_second * v[rows, :] + (1.0 - beta_second) * grad * grad
             new_m[rows, :] = mom
@@ -294,7 +361,7 @@
     return pl.pallas_call(
         kernel,
         in_specs=[pl.BlockSpec(memory_space=pltpu.SMEM)]
-        + [pl.BlockSpec(memory_space=pltpu.VMEM)] * 7,
+        + [pl.BlockSpec(memory_space=pltpu.VMEM)] * 9,
         out_specs=[pl.BlockSpec(memory_space=pltpu.HBM)] * 3,
         out_shape=[shape(ROWS, F, jnp.float32)] * 3,
         scratch_shapes=[pltpu.VMEM((ROWS, F), jnp.float32)] * 3
@@ -314,7 +381,8 @@
 
     send_x, send_far = pieces_of(tokens, up_own, [((1, 0, 0, TOK, 1),), ((1, 1, 0, TOK, 0),)])
     tok_x = swap_x(send_x)
-    for_core = swap_x(send_far)
+    for_far = swap_core(send_far)
+    tok_far = swap_x(for_far)
     weight_bf = after(master.astype(jnp.bfloat16), send_x)
     block_1 = shift_y(weight_bf, -1)
     block_3 = shift_y(weight_bf, 1)
@@ -322,44 +390,47 @@
         after(tokens, send_x), up_own, [((0, 0, 0, TOK, 0),), ((0, 1, 0, TOK, 0),)]
     )
     tok_core = swap_core(send_core)
-    up_pair = swap_core(jnp.concatenate([up_own, tok_x[:, PIECE:]]))
+    up_x = tok_x[:, PIECE:]
+    up_pair = swap_core(jnp.concatenate([up_own, up_x]))
     block_2a = shift_y(block_1[:HALF], -1)
     block_2b = shift_y(block_3[HALF:], 1)
     blocks = (weight_bf, block_1, block_3, block_2a, block_2b)
 
-    total = replica_step(after(pseudo_grad[0].astype(jnp.bfloat16), tok_core), lambda i: i ^ 6)
+    total = replica_step(after(pseudo_grad[0].astype(jnp.bfloat16), tok_core, for_far), lambda i: i ^ 6)
+    total = replica_step(total, lambda i: i ^ 1)
     up_ready, total = lax.optimization_barrier((up_own, total))
-
-    ig_own, ig_x, ig_core, ig_far = input_grad((up_ready, tok_x, up_pair), blocks)
+    toks = (tok_own, tok_x, tok_core, tok_far)
+    g0, to_above, to_below, keep_above, keep_below = weight_grad(toks, (up_ready, up_x, up_pair))
+    from_below, from_above = shift_y(to_above, 1), shift_y(to_below, -1)
+
+    ig_own, ig_x, ig_core, ig_far = input_grad((after(up_ready, g0), up_x, up_pair), blocks)
     back_x = swap_x(ig_x)
     back_far = swap_core(ig_far)
-    back_other = swap_x(back_far)
     back_core = swap_core(ig_core)
-
-    tok_far = swap_core(after(for_core, ig_own))
-    toks = (tok_own, tok_x, tok_core, tok_far)
-    g0, g1, g3, up_half, down_half = weight_grad_blocks(toks, (after(up_own, back_far), up_pair))
-    s1, s3 = relay(after(g1, back_x), g3, shift_y(up_half, 1), shift_y(down_half, -1))
+    other_a = swap_x(split(back_far))
+
+    val_own, val_x, val_pair = value_parts(toks, (after(weight_bf, g0), *blocks[1:]))
+    val_back = swap_core(val_pair)
+    other_b = swap_x(after(pack(back_far, val_back, val_x), other_a))
+    total = replica_step(after(total, back_core), lambda i: i ^ 2)
+
+    s1, s3 = relay(after(keep_above, back_x), keep_below, from_below, from_above)
     r1 = shift_y(s1, 1)
     r3 = shift_y(s3, -1)
 
-    total = replica_step(after(total, back_far), lambda i: i ^ 1)
-    block_0 = after(weight_bf, g0, back_core)
-    val_own, val_x, val_pair = value_parts(toks, (block_0, *blocks[1:]))
-    val_back = swap_core(val_pair)
-    total = replica_step(after(total, val_back), lambda i: i ^ 2)
     total = replica_step(after(total, s1), lambda i: i ^ 8)
     new_momentum, new_global = outer_update(momentum, global_frag, total / 16)
 
-    val_far = swap_x((val_x + val_back[TOK:]).astype(jnp.bfloat16))
-    values = val_own + val_back[:TOK] + val_far.astype(jnp.float32)
-    values = (values * SCALE).astype(jnp.bfloat16)
-
-    block = assemble(None, (ig_own, back_core, back_x), [((0, 0),), ((0, 1),), ((1, 0),)])
+    block = assemble(
+        None, (ig_own, back_core, back_x), ((0, 0, 0, TOK), (0, 1, 0, TOK), (1, 0, 0, TOK))
+    )
     new_weight, new_m, new_v = adam(
-        frag_index, (g0, r1, r3), adam_m[0], adam_v[0], master, new_global
-    )
-    block = assemble(block, (after(back_other, new_weight),), [((1, 1),)])
+        frag_index, (g0, from_above, r1, from_below, r3), adam_m[0], adam_v[0], master, new_global
+    )
+    other_b = after(other_b, new_weight)
+    block, values = assemble(
+        block, (other_a, other_b), ((1, 1, 0, FIRST), (1, 1, FIRST, TOK - FIRST)), (val_own, val_back)
+    )
     return (
         values[None],
         block[None],

time: 76.3 us -> 72.9 us (0.955)
  waiting for transfers between devices: 30.9 us -> 28.7 us
  starting transfers between devices: 30.5 us -> 29.2 us
    ppermute x19, waiting for transfers between devices: 28.1 us -> 23.3 us  [fsdp_permute(): return lax.ppermute(value, 'fsdp', pairs)]
    ppermute x4, starting transfers between devices: 8.21 us -> 5.62 us  [replica_step(): other = lax.ppermute(sent, 'replica', [(i, partner(i)) for i in range(16)])]
    ppermute x4, waiting for transfers between devices: 2.82 us -> 5.38 us  [replica_step(): other = lax.ppermute(sent, 'replica', [(i, partner(i)) for i in range(16)])]
    ppermute x19, starting transfers between devices: 22.3 us -> 23.6 us  [fsdp_permute(): return lax.ppermute(value, 'fsdp', pairs)]
    pallas_call x3 -> x5, Pallas kernels: 3.38 us -> 4.14 us  [the longest x2 2.77 us: assemble(): pl.pallas_call(kernel, in_specs=ins, out_specs=outs if vals else outs[0],...]
  transfers between devices with their start and end apart: 23 -> 23, of which waited for: 8 -> 7; matrix products, arithmetic and copies ran while one was open for 2% -> 1% of each run, Pallas kernels for 10% -> 9%
where the time goes in v4:
time: 72.9 us; the launch traced here: 72.7 us
  starting transfers between devices  29.2 us (40%)
  waiting for transfers between devices  28.7 us (39%)
  Pallas kernels  9.35 us (13%)
  local copies, waits for them, and re-layouts  2.58 us (4%)
  between operations  1.77 us (2%)
  other arithmetic  1.01 us (1%)
    ppermute x19, starting transfers between devices, fsdp_permute(): return lax.ppermute(value, 'fsdp', pairs)  23.6 us
    ppermute x19, waiting for transfers between devices, fsdp_permute(): return lax.ppermute(value, 'fsdp', pairs)  23.3 us
    ppermute x4, starting transfers between devices, replica_step(): other = lax.ppermute(sent, 'replica', [(i, partner(i)) for i in range(16)])  5.62 us
    ppermute x4, waiting for transfers between devices, replica_step(): other = lax.ppermute(sent, 'replica', [(i, partner(i)) for i in range(16)])  5.38 us
    pallas_call x2, Pallas kernels, assemble(): pl.pallas_call(kernel, in_specs=ins, out_specs=outs if vals else outs[0],...  2.77 us
    unnamed x20, local copies, waits for them, and re-layouts  2.53 us
    pallas_call x1, Pallas kernels, adam(): pl.pallas_call(kernel, in_specs=[pl.BlockSpec(memory_space=pltpu.SMEM)] +...  2.02 us
  transfers between devices with their start and end apart: 23, of which 7 were waited for; matrix products, arithmetic and copies ran while one was open for 1% of the time, Pallas kernels for 9%

profile of v4, /device:TPU:64, one launch (start us, length us, event | category | flops | bytes accessed | tf_op | source)
XLA Modules:
  0.0 72.7 jit_solution(5215387790813551606)
XLA Ops:
  0.6 1.6 %copy-done = bf16[1,128,8192]{2,1,0:T(8,128)(2,1)S(1)} copy-done((bf16[1,128,8192]{2,1,0:T(8,128)(2,1)S(1)}, bf16[1,128,8192]{2,1,0:T(8,128)(2,1)}, u32[]{:S(2)}) %copy-start) | copy-done | bytes 2097176
  2.2 0.9 %copy-done.2 = bf16[1,128,512]{2,1,0:T(8,128)(2,1)S(1)} copy-done((bf16[1,128,512]{2,1,0:T(8,128)(2,1)S(1)}, bf16[1,128,512]{2,1,0:T(8,128)(2,1)}, u32[]{:S(2)}) %copy-start.2) | copy-done | bytes 131096
  3.8 0.6 collective-permute-start
  4.4 3.0 %collective-permute-start.4 = (bf16[128,2560]{1,0:T(8,128)(2,1)S(1)}, bf16[128,2560]{1,0:T(8,128)(2,1)S(1)}, u32[]{:S(2)}, u32[]{:S(2)}) collective-permute-start(bf16[128,2560]{1,0:T(8,128)(2,1)S(1)} %get-tuple-element.42), channel_id=1, source_target_pairs={{0,8},{1,9},{2,10},{3,11},{4,12},{5,13},{6,14},{7,15},{8,0},{9,1},... | collective-permute-start | bytes 1966088 | tf_op jit(solution)/shard_map/ppermute | solution.py:39
  7.5 1.7 %collective-permute-start.8 = (bf16[512,512]{1,0:T(8,128)(2,1)S(1)}, bf16[512,512]{1,0:T(8,128)(2,1)S(1)}, u32[]{:S(2)}, u32[]{:S(2)}) collective-permute-start(bf16[512,512]{1,0:T(8,128)(2,1)S(1)} %bitcast_convert_fusion.refs_0_), channel_id=1, source_target_pairs={{0,2},{1,3},{2,4},{3,5},{4,6},{5,7},{6,0},{7,1},{8,10},{9,11},{10,... | collective-permute-start | bytes 1572872 | tf_op jit(solution)/shard_map/ppermute | solution.py:39
  9.1 1.7 %collective-permute-start.7 = (bf16[512,512]{1,0:T(8,128)(2,1)S(1)}, bf16[512,512]{1,0:T(8,128)(2,1)S(1)}, u32[]{:S(2)}, u32[]{:S(2)}) collective-permute-start(bf16[512,512]{1,0:T(8,128)(2,1)S(1)} %bitcast_convert_fusion.refs_0_), channel_id=1, source_target_pairs={{0,6},{1,7},{2,0},{3,1},{4,2},{5,3},{6,4},{7,5},{8,14},{9,15},{10,... | collective-permute-start | bytes 1572872 | tf_op jit(solution)/shard_map/ppermute | solution.py:39
  10.8 4.6 %collective-permute-start.2 = (bf16[512,128]{1,0:T(8,128)(2,1)S(1)}, bf16[512,128]{1,0:T(8,128)(2,1)S(1)}, u32[]{:S(2)}, u32[]{:S(2)}) collective-permute-start(bf16[512,128]{1,0:T(8,128)(2,1)S(1)} %convert_bitcast_fusion), channel_id=1, source_target_pairs={{0,96},{16,112},{32,64},{48,80},{64,32},{80,48},{96,0},{112,16},{1... | collective-permute-start | bytes 393224 | tf_op jit(solution)/shard_map/ppermute | solution.py:56
  15.4 0.5 collective-permute-start.5
  15.9 5.4 %collective-permute-done.2 = bf16[512,128]{1,0:T(8,128)(2,1)S(1)} collective-permute-done((bf16[512,128]{1,0:T(8,128)(2,1)S(1)}, bf16[512,128]{1,0:T(8,128)(2,1)S(1)}, u32[]{:S(2)}, u32[]{:S(2)}) %collective-permute-start.2) | collective-permute-done | bytes 131104 | tf_op jit(solution)/shard_map/ppermute | solution.py:56
  21.7 1.8 %collective-permute-done.4.t1 = bf16[128,2560]{1,0:T(8,128)(2,1)S(1)} collective-permute-done((bf16[128,2560]{1,0:T(8,128)(2,1)S(1)}, bf16[128,2560]{1,0:T(8,128)(2,1)S(1)}, u32[]{:S(2)}, u32[]{:S(2)}) %collective-permute-start.4) | collective-permute-done | bytes 655392 | tf_op jit(solution)/shard_map/ppermute | solution.py:39
  23.7 1.7 %collective-permute-start.10 = (bf16[256,512]{1,0:T(8,128)(2,1)S(1)}, bf16[256,512]{1,0:T(8,128)(2,1)S(1)}, u32[]{:S(2)}, u32[]{:S(2)}) collective-permute-start(bf16[256,512]{1,0:T(8,128)(2,1)S(1)} %slice.14), channel_id=1, source_target_pairs={{0,2},{1,3},{2,4},{3,5},{4,6},{5,7},{6,0},{7,1},{8,10},{9,11},{10,... | collective-permute-start | bytes 786440 | tf_op jit(solution)/shard_map/ppermute | solution.py:39
  25.3 1.7 %collective-permute-start.9 = (bf16[256,512]{1,0:T(8,128)(2,1)S(1)}, bf16[256,512]{1,0:T(8,128)(2,1)S(1)}, u32[]{:S(2)}, u32[]{:S(2)}) collective-permute-start(bf16[256,512]{1,0:T(8,128)(2,1)S(1)} %slice.13), channel_id=1, source_target_pairs={{0,6},{1,7},{2,0},{3,1},{4,2},{5,3},{6,4},{7,5},{8,14},{9,15},{10,... | collective-permute-start | bytes 786440 | tf_op jit(solution)/shard_map/ppermute | solution.py:39
  27.1 6.7 %collective-permute-done.5.t3 = bf16[128,2048]{1,0:T(8,128)(2,1)S(1)} collective-permute-done((bf16[128,2048]{1,0:T(8,128)(2,1)S(1)}, bf16[128,2048]{1,0:T(8,128)(2,1)S(1)}, u32[]{:S(2)}, u32[]{:S(2)}) %collective-permute-start.5) | collective-permute-done | bytes 524320 | tf_op jit(solution)/shard_map/ppermute | solution.py:39
  33.9 1.3 %weight_grad.1 = (f32[512,512]{1,0:T(8,128)S(1)}, bf16[448,512]{1,0:T(8,128)(2,1)S(1)}, bf16[448,512]{1,0:T(8,128)(2,1)S(1)}, f32[320,512]{1,0:T(8,128)S(1)}, f32[320,512]{1,0:T(8,128)S(1)}) custom-call(bf16[128,2048]{1,0:T(8,128)(2,1)S(1)} %get-tuple-element.48.t0, bf16[128,2560]{1,0:T(8,128)(2,1)S(1)} %collective-permute-done.4.t1, ...), custom_call_target="tpu_custom_call" | custom-call | flops 1 | bytes 1 | tf_op jit(solution)/shard_map/weight_grad/pallas_call | solution.py:236
  35.2 1.3 %input_grad.1 = (bf16[128,2048]{1,0:T(8,128)(2,1)S(1)}, bf16[128,2048]{1,0:T(8,128)(2,1)S(1)}, bf16[128,2048]{1,0:T(8,128)(2,1)S(1)}, bf16[128,2048]{1,0:T(8,128)(2,1)S(1)}) custom-call(bf16[128,512]{1,0:T(8,128)(2,1)S(1)} %bitcast.20, bf16[128,512]{1,0:T(8,128)(2,1)S(1)} %slice.12.u1, bf16[256,512]{1,0:T(8,128)(2,1)S(1)} %collective-permute-done.6.u2, ...), custom_call_target="tpu_custom_call" | custom-call | flops 1 | bytes 1 | tf_op jit(solution)/shard_map/input_grad/pallas_call | solution.py:144
  36.6 0.5 collective-permute-start.11
  37.1 3.0 %collective-permute-start.16 = (bf16[128,2048]{1,0:T(8,128)(2,1)S(1)}, bf16[128,2048]{1,0:T(8,128)(2,1)S(1)}, u32[]{:S(2)}, u32[]{:S(2)}) collective-permute-start(bf16[128,2048]{1,0:T(8,128)(2,1)S(1)} %get-tuple-element.59), channel_id=1, source_target_pairs={{0,8},{1,9},{2,10},{3,11},{4,12},{5,13},{6,14},{7,15},{8,0},{9,1},... | collective-permute-start | bytes 1572872 | tf_op jit(solution)/shard_map/ppermute | solution.py:39
  40.1 3.0 %collective-permute-start.15 = (bf16[448,512]{1,0:T(8,128)(2,1)S(1)}, bf16[448,512]{1,0:T(8,128)(2,1)S(1)}, u32[]{:S(2)}, u32[]{:S(2)}) collective-permute-start(bf16[448,512]{1,0:T(8,128)(2,1)S(1)} %get-tuple-element.57), channel_id=1, source_target_pairs={{0,6},{1,7},{2,0},{3,1},{4,2},{5,3},{6,4},{7,5},{8,14},{9,15},{10,... | collective-permute-start | bytes 1376264 | tf_op jit(solution)/shard_map/ppermute | solution.py:39
  43.2 1.0 %collective-permute-start.12 = (bf16[96,2048]{1,0:T(8,128)(2,1)S(1)}, bf16[96,2048]{1,0:T(8,128)(2,1)S(1)}, u32[]{:S(2)}, u32[]{:S(2)}) collective-permute-start(bf16[96,2048]{1,0:T(8,128)(2,1)S(1)} %split.1), channel_id=1, source_target_pairs={{0,8},{1,9},{2,10},{3,11},{4,12},{5,13},{6,14},{7,15},{8,0},{9,1},... | collective-permute-start | bytes 1179656 | tf_op jit(solution)/shard_map/ppermute | solution.py:39
  44.2 1.2 %values.1 = (f32[128,512]{1,0:T(8,128)S(1)}, f32[128,512]{1,0:T(8,128)S(1)}, bf16[256,512]{1,0:T(8,128)(2,1)S(1)}) custom-call(bf16[128,2048]{1,0:T(8,128)(2,1)S(1)} %get-tuple-element.48.t0, bf16[128,2560]{1,0:T(8,128)(2,1)S(1)} %collective-permute-done.4.t1, bf16[128,2048]{1,0:T(8,128)(2,1)S(1)} %collective-permute-done.t2, ...), custom_call_target="tpu_custom_call" | custom-call | flops 1 | bytes 1 | tf_op jit(solution)/shard_map/values/pallas_call | solution.py:166
  45.4 8.0 %collective-permute-done.16.refs_2_ = bf16[128,2048]{1,0:T(8,128)(2,1)S(1)} collective-permute-done((bf16[128,2048]{1,0:T(8,128)(2,1)S(1)}, bf16[128,2048]{1,0:T(8,128)(2,1)S(1)}, u32[]{:S(2)}, u32[]{:S(2)}) %collective-permute-start.16) | collective-permute-done | bytes 524320 | tf_op jit(solution)/shard_map/ppermute | solution.py:39
  53.4 2.9 %collective-permute-done.17.from_below = bf16[448,512]{1,0:T(8,128)(2,1)S(1)} collective-permute-done((bf16[448,512]{1,0:T(8,128)(2,1)S(1)}, bf16[448,512]{1,0:T(8,128)(2,1)S(1)}, u32[]{:S(2)}, u32[]{:S(2)}) %collective-permute-start.17) | collective-permute-done | bytes 458784 | tf_op jit(solution)/shard_map/ppermute | solution.py:39
  56.5 0.7 collective-permute-start.22
  57.2 1.0 %collective-permute-start.19 = (bf16[320,512]{1,0:T(8,128)(2,1)S(1)}, bf16[320,512]{1,0:T(8,128)(2,1)S(1)}, u32[]{:S(2)}, u32[]{:S(2)}) collective-permute-start(bf16[320,512]{1,0:T(8,128)(2,1)S(1)} %get-tuple-element.64), channel_id=1, source_target_pairs={{0,6},{1,7},{2,0},{3,1},{4,2},{5,3},{6,4},{7,5},{8,14},{9,15},{10,... | collective-permute-start | bytes 983048 | tf_op jit(solution)/shard_map/ppermute | solution.py:39
  58.2 1.0 %collective-permute-start.18 = (bf16[320,512]{1,0:T(8,128)(2,1)S(1)}, bf16[320,512]{1,0:T(8,128)(2,1)S(1)}, u32[]{:S(2)}, u32[]{:S(2)}) collective-permute-start(bf16[320,512]{1,0:T(8,128)(2,1)S(1)} %get-tuple-element.63), channel_id=1, source_target_pairs={{0,2},{1,3},{2,4},{3,5},{4,6},{5,7},{6,0},{7,1},{8,10},{9,11},{10,... | collective-permute-start | bytes 983048 | tf_op jit(solution)/shard_map/ppermute | solution.py:39
  59.3 2.6 %collective-permute-done.12.refs_0_ = bf16[96,2048]{1,0:T(8,128)(2,1)S(1)} collective-permute-done((bf16[96,2048]{1,0:T(8,128)(2,1)S(1)}, bf16[96,2048]{1,0:T(8,128)(2,1)S(1)}, u32[]{:S(2)}, u32[]{:S(2)}) %collective-permute-start.12) | collective-permute-done | bytes 393248 | tf_op jit(solution)/shard_map/ppermute | solution.py:39
  61.8 3.0 %collective-permute-start.14 = (bf16[64,2048]{1,0:T(8,128)(2,1)S(1)}, bf16[64,2048]{1,0:T(8,128)(2,1)S(1)}, u32[]{:S(2)}, u32[]{:S(2)}) collective-permute-start(bf16[64,2048]{1,0:T(8,128)(2,1)S(1)} %pack.1), channel_id=1, source_target_pairs={{0,8},{1,9},{2,10},{3,11},{4,12},{5,13},{6,14},{7,15},{8,0},{9,1},... | collective-permute-start | bytes 786440 | tf_op jit(solution)/shard_map/ppermute | solution.py:39
  65.5 1.2 %assemble.2.refs_4_ = bf16[128,8192]{1,0:T(8,128)(2,1)} custom-call(bf16[128,2048]{1,0:T(8,128)(2,1)S(1)} %get-tuple-element.72.refs_0_, bf16[128,2048]{1,0:T(8,128)(2,1)S(1)} %collective-permute-done.20.refs_1_, bf16[128,2048]{1,0:T(8,128)(2,1)S(1)} %collective-permute-done.16.refs_2_), custom_call_target="tpu_custom_call" | custom-call | flops 1 | bytes 1 | tf_op jit(solution)/shard_map/assemble/pallas_call | solution.py:310
  66.8 0.8 %multiply_subtract_fusion = (f32[512,128]{1,0:T(8,128)S(1)}, f32[512,128]{1,0:T(8,128)}) fusion(f32[512,128]{1,0:T(8,128)S(1)} %copy-done.7, bf16[512,128]{1,0:T(8,128)(2,1)S(1)} %collective-permute-done.22, bf16[512,128]{1,0:T(8,128)(2,1)S(1)} %convert_add_fusion, f32[512,128]{1,0:T(8,128)S(1)} %copy-done.8), kind=kLoop, calls=%fused_computation.1 | loop fusion | flops 655360 | bytes 1310720 | tf_op jit(solution)/shard_map/sub | solution.py:66
  67.6 1.3 %collective-permute-done.18.r1 = bf16[320,512]{1,0:T(8,128)(2,1)S(1)} collective-permute-done((bf16[320,512]{1,0:T(8,128)(2,1)S(1)}, bf16[320,512]{1,0:T(8,128)(2,1)S(1)}, u32[]{:S(2)}, u32[]{:S(2)}) %collective-permute-start.18) | collective-permute-done | bytes 327712 | tf_op jit(solution)/shard_map/ppermute | solution.py:39
  68.9 2.0 %adam.1 = (f32[512,512]{1,0:T(8,128)}, f32[512,512]{1,0:T(8,128)}, f32[512,512]{1,0:T(8,128)}) custom-call(s32[1]{0:T(128)S(6)} %copy.18.frag, f32[512,512]{1,0:T(8,128)S(1)} %get-tuple-element.49.g0, bf16[448,512]{1,0:T(8,128)(2,1)S(1)} %collective-permute-done.15.from_above, bf16[320,512]{1,0:T(8,128)(2,1)S(1)} %collective-permute-done.18.r1, ...), custom_call_target="tpu_custom_call" | custom-call | flops 1 | bytes 1 | tf_op jit(solution)/shard_map/adam/pallas_call | solution.py:361
  71.0 1.5 %assemble.3 = (bf16[128,8192]{1,0:T(8,128)(2,1)}, bf16[128,512]{1,0:T(8,128)(2,1)}) custom-call(bf16[96,2048]{1,0:T(8,128)(2,1)S(1)} %collective-permute-done.12.refs_0_, bf16[64,2048]{1,0:T(8,128)(2,1)S(1)} %collective-permute-done.14.refs_1_, f32[128,512]{1,0:T(8,128)S(1)} %get-tuple-element.71.refs_2_, ...), custom_call_target="tpu_custom_call", output_to_operand_aliasing={{0}: (4, {})} | custom-call | flops 1 | bytes 1 | tf_op jit(solution)/shard_map/assemble/pallas_call | solution.py:310
  (55 shorter events, 1.7 us)
Async XLA Ops:
  0.6 1.6 %copy-start = (bf16[1,128,8192]{2,1,0:T(8,128)(2,1)S(1)}, bf16[1,128,8192]{2,1,0:T(8,128)(2,1)}, u32[]{:S(2)}) copy-start(bf16[1,128,8192]{2,1,0:T(8,128)(2,1)} %param.9) | copy-start | bytes 6291460
  3.1 4.3 %copy-start.1 = (f32[1,512,512]{2,1,0:T(8,128)S(1)}, f32[1,512,512]{2,1,0:T(8,128)}, u32[]{:S(2)}) copy-start(f32[1,512,512]{2,1,0:T(8,128)} %param.11) | copy-start | bytes 3145732
  3.4 7.4 %copy-start.9 = (f32[1,512,128]{2,1,0:T(8,128)S(1)}, f32[1,512,128]{2,1,0:T(8,128)}, u32[]{:S(2)}) copy-start(f32[1,512,128]{2,1,0:T(8,128)} %param.14) | copy-start | bytes 786436
  3.4 7.4 %collective-permute-start.1 = (bf16[128,2048]{1,0:T(8,128)(2,1)S(1)}, bf16[128,2048]{1,0:T(8,128)(2,1)S(1)}, u32[]{:S(2)}, u32[]{:S(2)}) collective-permute-start(bf16[128,2048]{1,0:T(8,128)(2,1)S(1)} %get-tuple-element.45), channel_id=1, source_target_pairs={{0,1},{1,0},{2,3},{3,2},{4,5},{5,4},{6,7},{7,6},{8,9},{9,8},{10,11... | collective-permute-start | bytes 1572872 | tf_op jit(solution)/shard_map/ppermute | solution.py:39
  3.8 30.0 %copy-start.3 = (bf16[1,128,512]{2,1,0:T(8,128)(2,1)S(1)}, bf16[1,128,512]{2,1,0:T(8,128)(2,1)}, u32[]{:S(2)}) copy-start(bf16[1,128,512]{2,1,0:T(8,128)(2,1)} %param.10) | copy-start | bytes 393220
  3.8 7.0 %collective-permute-start = (bf16[128,2048]{1,0:T(8,128)(2,1)S(1)}, bf16[128,2048]{1,0:T(8,128)(2,1)S(1)}, u32[]{:S(2)}, u32[]{:S(2)}) collective-permute-start(bf16[128,2048]{1,0:T(8,128)(2,1)S(1)} %get-tuple-element.44), channel_id=1, source_target_pairs={{0,1},{1,0},{2,3},{3,2},{4,5},{5,4},{6,7},{7,6},{8,9},{9,8},{10,11... | collective-permute-start | bytes 1572872 | tf_op jit(solution)/shard_map/ppermute | solution.py:39
  4.4 19.1 %collective-permute-start.4 = (bf16[128,2560]{1,0:T(8,128)(2,1)S(1)}, bf16[128,2560]{1,0:T(8,128)(2,1)S(1)}, u32[]{:S(2)}, u32[]{:S(2)}) collective-permute-start(bf16[128,2560]{1,0:T(8,128)(2,1)S(1)} %get-tuple-element.42), channel_id=1, source_target_pairs={{0,8},{1,9},{2,10},{3,11},{4,12},{5,13},{6,14},{7,15},{8,0},{9,1},... | collective-permute-start | bytes 1966088 | tf_op jit(solution)/shard_map/ppermute | solution.py:39
  7.5 16.1 %collective-permute-start.8 = (bf16[512,512]{1,0:T(8,128)(2,1)S(1)}, bf16[512,512]{1,0:T(8,128)(2,1)S(1)}, u32[]{:S(2)}, u32[]{:S(2)}) collective-permute-start(bf16[512,512]{1,0:T(8,128)(2,1)S(1)} %bitcast_convert_fusion.refs_0_), channel_id=1, source_target_pairs={{0,2},{1,3},{2,4},{3,5},{4,6},{5,7},{6,0},{7,1},{8,10},{9,11},{10,... | collective-permute-start | bytes 1572872 | tf_op jit(solution)/shard_map/ppermute | solution.py:39
  9.1 16.2 %collective-permute-start.7 = (bf16[512,512]{1,0:T(8,128)(2,1)S(1)}, bf16[512,512]{1,0:T(8,128)(2,1)S(1)}, u32[]{:S(2)}, u32[]{:S(2)}) collective-permute-start(bf16[512,512]{1,0:T(8,128)(2,1)S(1)} %bitcast_convert_fusion.refs_0_), channel_id=1, source_target_pairs={{0,6},{1,7},{2,0},{3,1},{4,2},{5,3},{6,4},{7,5},{8,14},{9,15},{10,... | collective-permute-start | bytes 1572872 | tf_op jit(solution)/shard_map/ppermute | solution.py:39
  10.8 10.4 %collective-permute-start.2 = (bf16[512,128]{1,0:T(8,128)(2,1)S(1)}, bf16[512,128]{1,0:T(8,128)(2,1)S(1)}, u32[]{:S(2)}, u32[]{:S(2)}) collective-permute-start(bf16[512,128]{1,0:T(8,128)(2,1)S(1)} %convert_bitcast_fusion), channel_id=1, source_target_pairs={{0,96},{16,112},{32,64},{48,80},{64,32},{80,48},{96,0},{112,16},{1... | collective-permute-start | bytes 393224 | tf_op jit(solution)/shard_map/ppermute | solution.py:56
  15.4 18.5 %collective-permute-start.5 = (bf16[128,2048]{1,0:T(8,128)(2,1)S(1)}, bf16[128,2048]{1,0:T(8,128)(2,1)S(1)}, u32[]{:S(2)}, u32[]{:S(2)}) collective-permute-start(bf16[128,2048]{1,0:T(8,128)(2,1)S(1)} %collective-permute-done.1), channel_id=1, source_target_pairs={{0,8},{1,9},{2,10},{3,11},{4,12},{5,13},{6,14},{7,15},{8,0},{9,1},... | collective-permute-start | bytes 1572872 | tf_op jit(solution)/shard_map/ppermute | solution.py:39
  21.3 5.7 %collective-permute-start.3 = (bf16[512,128]{1,0:T(8,128)(2,1)S(1)}, bf16[512,128]{1,0:T(8,128)(2,1)S(1)}, u32[]{:S(2)}, u32[]{:S(2)}) collective-permute-start(bf16[512,128]{1,0:T(8,128)(2,1)S(1)} %add_convert_fusion), channel_id=1, source_target_pairs={{0,16},{16,0},{32,48},{48,32},{64,80},{80,64},{96,112},{112,96},{1... | collective-permute-start | bytes 393224 | tf_op jit(solution)/shard_map/ppermute | solution.py:56
  23.5 3.6 %collective-permute-start.6 = (bf16[256,512]{1,0:T(8,128)(2,1)S(1)}, bf16[256,512]{1,0:T(8,128)(2,1)S(1)}, u32[]{:S(2)}, u32[]{:S(2)}) collective-permute-start(bf16[256,512]{1,0:T(8,128)(2,1)S(1)} %pad_maximum_fusion), channel_id=1, source_target_pairs={{0,1},{1,0},{2,3},{3,2},{4,5},{5,4},{6,7},{7,6},{8,9},{9,8},{10,11... | collective-permute-start | bytes 786440 | tf_op jit(solution)/shard_map/ppermute | solution.py:39
  23.7 11.5 %collective-permute-start.10 = (bf16[256,512]{1,0:T(8,128)(2,1)S(1)}, bf16[256,512]{1,0:T(8,128)(2,1)S(1)}, u32[]{:S(2)}, u32[]{:S(2)}) collective-permute-start(bf16[256,512]{1,0:T(8,128)(2,1)S(1)} %slice.14), channel_id=1, source_target_pairs={{0,2},{1,3},{2,4},{3,5},{4,6},{5,7},{6,0},{7,1},{8,10},{9,11},{10,... | collective-permute-start | bytes 786440 | tf_op jit(solution)/shard_map/ppermute | solution.py:39
  25.3 9.9 %collective-permute-start.9 = (bf16[256,512]{1,0:T(8,128)(2,1)S(1)}, bf16[256,512]{1,0:T(8,128)(2,1)S(1)}, u32[]{:S(2)}, u32[]{:S(2)}) collective-permute-start(bf16[256,512]{1,0:T(8,128)(2,1)S(1)} %slice.13), channel_id=1, source_target_pairs={{0,6},{1,7},{2,0},{3,1},{4,2},{5,3},{6,4},{7,5},{8,14},{9,15},{10,... | collective-permute-start | bytes 786440 | tf_op jit(solution)/shard_map/ppermute | solution.py:39
  36.5 6.6 %collective-permute-start.20 = (bf16[128,2048]{1,0:T(8,128)(2,1)S(1)}, bf16[128,2048]{1,0:T(8,128)(2,1)S(1)}, u32[]{:S(2)}, u32[]{:S(2)}) collective-permute-start(bf16[128,2048]{1,0:T(8,128)(2,1)S(1)} %get-tuple-element.66), channel_id=1, source_target_pairs={{0,1},{1,0},{2,3},{3,2},{4,5},{5,4},{6,7},{7,6},{8,9},{9,8},{10,11... | collective-permute-start | bytes 1572872 | tf_op jit(solution)/shard_map/ppermute | solution.py:39
  36.6 6.6 %collective-permute-start.11 = (bf16[128,2048]{1,0:T(8,128)(2,1)S(1)}, bf16[128,2048]{1,0:T(8,128)(2,1)S(1)}, u32[]{:S(2)}, u32[]{:S(2)}) collective-permute-start(bf16[128,2048]{1,0:T(8,128)(2,1)S(1)} %get-tuple-element.52), channel_id=1, source_target_pairs={{0,1},{1,0},{2,3},{3,2},{4,5},{5,4},{6,7},{7,6},{8,9},{9,8},{10,11... | collective-permute-start | bytes 1572872 | tf_op jit(solution)/shard_map/ppermute | solution.py:39
  37.1 16.3 %collective-permute-start.16 = (bf16[128,2048]{1,0:T(8,128)(2,1)S(1)}, bf16[128,2048]{1,0:T(8,128)(2,1)S(1)}, u32[]{:S(2)}, u32[]{:S(2)}) collective-permute-start(bf16[128,2048]{1,0:T(8,128)(2,1)S(1)} %get-tuple-element.59), channel_id=1, source_target_pairs={{0,8},{1,9},{2,10},{3,11},{4,12},{5,13},{6,14},{7,15},{8,0},{9,1},... | collective-permute-start | bytes 1572872 | tf_op jit(solution)/shard_map/ppermute | solution.py:39
  40.1 13.3 %collective-permute-start.15 = (bf16[448,512]{1,0:T(8,128)(2,1)S(1)}, bf16[448,512]{1,0:T(8,128)(2,1)S(1)}, u32[]{:S(2)}, u32[]{:S(2)}) collective-permute-start(bf16[448,512]{1,0:T(8,128)(2,1)S(1)} %get-tuple-element.57), channel_id=1, source_target_pairs={{0,6},{1,7},{2,0},{3,1},{4,2},{5,3},{6,4},{7,5},{8,14},{9,15},{10,... | collective-permute-start | bytes 1376264 | tf_op jit(solution)/shard_map/ppermute | solution.py:39
  43.1 13.2 %collective-permute-start.17 = (bf16[448,512]{1,0:T(8,128)(2,1)S(1)}, bf16[448,512]{1,0:T(8,128)(2,1)S(1)}, u32[]{:S(2)}, u32[]{:S(2)}) collective-permute-start(bf16[448,512]{1,0:T(8,128)(2,1)S(1)} %get-tuple-element.62), channel_id=1, source_target_pairs={{0,2},{1,3},{2,4},{3,5},{4,6},{5,7},{6,0},{7,1},{8,10},{9,11},{10,... | collective-permute-start | bytes 1376264 | tf_op jit(solution)/shard_map/ppermute | solution.py:39
  43.2 13.3 %collective-permute-start.21 = (bf16[512,128]{1,0:T(8,128)(2,1)S(1)}, bf16[512,128]{1,0:T(8,128)(2,1)S(1)}, u32[]{:S(2)}, u32[]{:S(2)}) collective-permute-start(bf16[512,128]{1,0:T(8,128)(2,1)S(1)} %convert_add_fusion.1), channel_id=1, source_target_pairs={{0,32},{16,48},{32,0},{48,16},{64,96},{80,112},{96,64},{112,80},{1... | collective-permute-start | bytes 393224 | tf_op jit(solution)/shard_map/ppermute | solution.py:56
  43.2 18.6 %collective-permute-start.12 = (bf16[96,2048]{1,0:T(8,128)(2,1)S(1)}, bf16[96,2048]{1,0:T(8,128)(2,1)S(1)}, u32[]{:S(2)}, u32[]{:S(2)}) collective-permute-start(bf16[96,2048]{1,0:T(8,128)(2,1)S(1)} %split.1), channel_id=1, source_target_pairs={{0,8},{1,9},{2,10},{3,11},{4,12},{5,13},{6,14},{7,15},{8,0},{9,1},... | collective-permute-start | bytes 1179656 | tf_op jit(solution)/shard_map/ppermute | solution.py:39
  53.4 5.8 %collective-permute-start.13 = (bf16[256,512]{1,0:T(8,128)(2,1)S(1)}, bf16[256,512]{1,0:T(8,128)(2,1)S(1)}, u32[]{:S(2)}, u32[]{:S(2)}) collective-permute-start(bf16[256,512]{1,0:T(8,128)(2,1)S(1)} %get-tuple-element.54), channel_id=1, source_target_pairs={{0,1},{1,0},{2,3},{3,2},{4,5},{5,4},{6,7},{7,6},{8,9},{9,8},{10,11... | collective-permute-start | bytes 786440 | tf_op jit(solution)/shard_map/ppermute | solution.py:39
  56.5 10.3 %collective-permute-start.22 = (bf16[512,128]{1,0:T(8,128)(2,1)S(1)}, bf16[512,128]{1,0:T(8,128)(2,1)S(1)}, u32[]{:S(2)}, u32[]{:S(2)}) collective-permute-start(bf16[512,128]{1,0:T(8,128)(2,1)S(1)} %convert_add_fusion), channel_id=1, source_target_pairs={{0,128},{16,144},{32,160},{48,176},{64,192},{80,208},{96,224},{112... | collective-permute-start | bytes 393224 | tf_op jit(solution)/shard_map/ppermute | solution.py:56
  57.2 10.4 %collective-permute-start.19 = (bf16[320,512]{1,0:T(8,128)(2,1)S(1)}, bf16[320,512]{1,0:T(8,128)(2,1)S(1)}, u32[]{:S(2)}, u32[]{:S(2)}) collective-permute-start(bf16[320,512]{1,0:T(8,128)(2,1)S(1)} %get-tuple-element.64), channel_id=1, source_target_pairs={{0,6},{1,7},{2,0},{3,1},{4,2},{5,3},{6,4},{7,5},{8,14},{9,15},{10,... | collective-permute-start | bytes 983048 | tf_op jit(solution)/shard_map/ppermute | solution.py:39
  58.2 10.8 %collective-permute-start.18 = (bf16[320,512]{1,0:T(8,128)(2,1)S(1)}, bf16[320,512]{1,0:T(8,128)(2,1)S(1)}, u32[]{:S(2)}, u32[]{:S(2)}) collective-permute-start(bf16[320,512]{1,0:T(8,128)(2,1)S(1)} %get-tuple-element.63), channel_id=1, source_target_pairs={{0,2},{1,3},{2,4},{3,5},{4,6},{5,7},{6,0},{7,1},{8,10},{9,11},{10,... | collective-permute-start | bytes 983048 | tf_op jit(solution)/shard_map/ppermute | solution.py:39
  59.2 7.5 %copy-start.7 = (f32[512,128]{1,0:T(8,128)S(1)}, f32[512,128]{1,0:T(8,128)}, u32[]{:S(2)}) copy-start(f32[512,128]{1,0:T(8,128)} %param.16) | copy-start | bytes 786436
  59.2 7.5 %copy-start.8 = (f32[512,128]{1,0:T(8,128)S(1)}, f32[512,128]{1,0:T(8,128)}, u32[]{:S(2)}) copy-start(f32[512,128]{1,0:T(8,128)} %param.15) | copy-start | bytes 786436
  61.8 9.2 %collective-permute-start.14 = (bf16[64,2048]{1,0:T(8,128)(2,1)S(1)}, bf16[64,2048]{1,0:T(8,128)(2,1)S(1)}, u32[]{:S(2)}, u32[]{:S(2)}) collective-permute-start(bf16[64,2048]{1,0:T(8,128)(2,1)S(1)} %pack.1), channel_id=1, source_target_pairs={{0,8},{1,9},{2,10},{3,11},{4,12},{5,13},{6,14},{7,15},{8,0},{9,1},... | collective-permute-start | bytes 786440 | tf_op jit(solution)/shard_map/ppermute | solution.py:39
  65.5 3.4 %copy-start.5 = (f32[1,512,512]{2,1,0:T(8,128)S(1)}, f32[1,512,512]{2,1,0:T(8,128)}, u32[]{:S(2)}) copy-start(f32[1,512,512]{2,1,0:T(8,128)} %param.12) | copy-start | bytes 3145732
  65.5 3.4 %copy-start.6 = (f32[1,512,512]{2,1,0:T(8,128)S(1)}, f32[1,512,512]{2,1,0:T(8,128)}, u32[]{:S(2)}) copy-start(f32[1,512,512]{2,1,0:T(8,128)} %param.13) | copy-start | bytes 3145732
  67.6 3.4 %copy-start.4 = (f32[512,128]{1,0:T(8,128)}, f32[512,128]{1,0:T(8,128)S(1)}, u32[]{:S(2)}) copy-start(f32[512,128]{1,0:T(8,128)S(1)} %get-tuple-element.77.glob) | copy-start | bytes 786436
  (1 other events, 0.9 us)

commit v5 on v4

--- a/solution.py
+++ b/solution.py
@@ -383,7 +383,7 @@
     tok_x = swap_x(send_x)
     for_far = swap_core(send_far)
     tok_far = swap_x(for_far)
-    weight_bf = after(master.astype(jnp.bfloat16), send_x)
+    weight_bf = after(master.astype(jnp.bfloat16), for_far)
     block_1 = shift_y(weight_bf, -1)
     block_3 = shift_y(weight_bf, 1)
     tok_own, send_core = pieces_of(
@@ -400,14 +400,16 @@
     total = replica_step(total, lambda i: i ^ 1)
     up_ready, total = lax.optimization_barrier((up_own, total))
     toks = (tok_own, tok_x, tok_core, tok_far)
-    g0, to_above, to_below, keep_above, keep_below = weight_grad(toks, (up_ready, up_x, up_pair))
-    from_below, from_above = shift_y(to_above, 1), shift_y(to_below, -1)
-
-    ig_own, ig_x, ig_core, ig_far = input_grad((after(up_ready, g0), up_x, up_pair), blocks)
+    ig_own, ig_x, ig_core, ig_far = input_grad((up_ready, up_x, up_pair), blocks)
     back_x = swap_x(ig_x)
     back_far = swap_core(ig_far)
     back_core = swap_core(ig_core)
     other_a = swap_x(split(back_far))
+
+    g0, to_above, to_below, keep_above, keep_below = weight_grad(
+        toks, (after(up_own, ig_own), up_x, up_pair)
+    )
+    from_below, from_above = shift_y(to_above, 1), shift_y(to_below, -1)
 
     val_own, val_x, val_pair = value_parts(toks, (after(weight_bf, g0), *blocks[1:]))
     val_back = swap_core(val_pair)

time: 72.9 us -> 73.1 us (level)
  transfers between devices with their start and end apart: 23 -> 23, of which waited for: 7 -> 9; matrix products, arithmetic and copies ran while one was open for 1% -> 1% of each run, Pallas kernels for 9% -> 10%
where the time goes in v5:
time: 73.1 us; the launch traced here: 72.9 us
  starting transfers between devices  29.4 us (40%)
  waiting for transfers between devices  28.8 us (39%)
  Pallas kernels  9.36 us (13%)
  local copies, waits for them, and re-layouts  2.58 us (4%)
  between operations  1.78 us (2%)
  other arithmetic  1.01 us (1%)
    ppermute x19, starting transfers between devices, fsdp_permute(): return lax.ppermute(value, 'fsdp', pairs)  23.8 us
    ppermute x19, waiting for transfers between devices, fsdp_permute(): return lax.ppermute(value, 'fsdp', pairs)  23.7 us
    ppermute x4, starting transfers between devices, replica_step(): other = lax.ppermute(sent, 'replica', [(i, partner(i)) for i in range(16)])  5.61 us
    ppermute x4, waiting for transfers between devices, replica_step(): other = lax.ppermute(sent, 'replica', [(i, partner(i)) for i in range(16)])  5.15 us
    pallas_call x2, Pallas kernels, assemble(): pl.pallas_call(kernel, in_specs=ins, out_specs=outs if vals else outs[0],...  2.76 us
    unnamed x20, local copies, waits for them, and re-layouts  2.53 us
    pallas_call x1, Pallas kernels, adam(): pl.pallas_call(kernel, in_specs=[pl.BlockSpec(memory_space=pltpu.SMEM)] +...  2.04 us
  transfers between devices with their start and end apart: 23, of which 9 were waited for; matrix products, arithmetic and copies ran while one was open for 1% of the time, Pallas kernels for 10%

profile of v5, /device:TPU:64, one launch (start us, length us, event | category | flops | bytes accessed | tf_op | source)
XLA Modules:
  0.0 72.9 jit_solution(15480657353097916723)
XLA Ops:
  0.6 1.6 %copy-done = bf16[1,128,8192]{2,1,0:T(8,128)(2,1)S(1)} copy-done((bf16[1,128,8192]{2,1,0:T(8,128)(2,1)S(1)}, bf16[1,128,8192]{2,1,0:T(8,128)(2,1)}, u32[]{:S(2)}) %copy-start) | copy-done | bytes 2097176
  2.2 0.9 %copy-done.2 = bf16[1,128,512]{2,1,0:T(8,128)(2,1)S(1)} copy-done((bf16[1,128,512]{2,1,0:T(8,128)(2,1)S(1)}, bf16[1,128,512]{2,1,0:T(8,128)(2,1)}, u32[]{:S(2)}) %copy-start.2) | copy-done | bytes 131096
  3.5 0.3 pieces.3
  3.8 0.6 collective-permute-start
  4.4 3.0 %collective-permute-start.4 = (bf16[128,2560]{1,0:T(8,128)(2,1)S(1)}, bf16[128,2560]{1,0:T(8,128)(2,1)S(1)}, u32[]{:S(2)}, u32[]{:S(2)}) collective-permute-start(bf16[128,2560]{1,0:T(8,128)(2,1)S(1)} %get-tuple-element.42), channel_id=1, source_target_pairs={{0,8},{1,9},{2,10},{3,11},{4,12},{5,13},{6,14},{7,15},{8,0},{9,1},... | collective-permute-start | bytes 1966088 | tf_op jit(solution)/shard_map/ppermute | solution.py:39
  7.5 3.1 %collective-permute-start.6 = (bf16[512,512]{1,0:T(8,128)(2,1)S(1)}, bf16[512,512]{1,0:T(8,128)(2,1)S(1)}, u32[]{:S(2)}, u32[]{:S(2)}) collective-permute-start(bf16[512,512]{1,0:T(8,128)(2,1)S(1)} %bitcast_convert_fusion.refs_0_), channel_id=1, source_target_pairs={{0,6},{1,7},{2,0},{3,1},{4,2},{5,3},{6,4},{7,5},{8,14},{9,15},{10,... | collective-permute-start | bytes 1572872 | tf_op jit(solution)/shard_map/ppermute | solution.py:39
  10.6 4.6 %collective-permute-start.2 = (bf16[512,128]{1,0:T(8,128)(2,1)S(1)}, bf16[512,128]{1,0:T(8,128)(2,1)S(1)}, u32[]{:S(2)}, u32[]{:S(2)}) collective-permute-start(bf16[512,128]{1,0:T(8,128)(2,1)S(1)} %convert_bitcast_fusion), channel_id=1, source_target_pairs={{0,96},{16,112},{32,64},{48,80},{64,32},{80,48},{96,0},{112,16},{1... | collective-permute-start | bytes 393224 | tf_op jit(solution)/shard_map/ppermute | solution.py:56
  15.2 0.9 %collective-permute-start.12 = (bf16[128,2048]{1,0:T(8,128)(2,1)S(1)}, bf16[128,2048]{1,0:T(8,128)(2,1)S(1)}, u32[]{:S(2)}, u32[]{:S(2)}) collective-permute-start(bf16[128,2048]{1,0:T(8,128)(2,1)S(1)} %collective-permute-done.1), channel_id=1, source_target_pairs={{0,8},{1,9},{2,10},{3,11},{4,12},{5,13},{6,14},{7,15},{8,0},{9,1},... | collective-permute-start | bytes 1572872 | tf_op jit(solution)/shard_map/ppermute | solution.py:39
  16.1 5.1 %collective-permute-done.2 = bf16[512,128]{1,0:T(8,128)(2,1)S(1)} collective-permute-done((bf16[512,128]{1,0:T(8,128)(2,1)S(1)}, bf16[512,128]{1,0:T(8,128)(2,1)S(1)}, u32[]{:S(2)}, u32[]{:S(2)}) %collective-permute-start.2) | collective-permute-done | bytes 131104 | tf_op jit(solution)/shard_map/ppermute | solution.py:56
  21.3 0.4 collective-permute-start.3
  21.6 1.9 %collective-permute-done.4.t1 = bf16[128,2560]{1,0:T(8,128)(2,1)S(1)} collective-permute-done((bf16[128,2560]{1,0:T(8,128)(2,1)S(1)}, bf16[128,2560]{1,0:T(8,128)(2,1)S(1)}, u32[]{:S(2)}, u32[]{:S(2)}) %collective-permute-start.4) | collective-permute-done | bytes 655392 | tf_op jit(solution)/shard_map/ppermute | solution.py:39
  23.7 3.1 %collective-permute-start.8 = (bf16[256,512]{1,0:T(8,128)(2,1)S(1)}, bf16[256,512]{1,0:T(8,128)(2,1)S(1)}, u32[]{:S(2)}, u32[]{:S(2)}) collective-permute-start(bf16[256,512]{1,0:T(8,128)(2,1)S(1)} %slice.13), channel_id=1, source_target_pairs={{0,6},{1,7},{2,0},{3,1},{4,2},{5,3},{6,4},{7,5},{8,14},{9,15},{10,... | collective-permute-start | bytes 786440 | tf_op jit(solution)/shard_map/ppermute | solution.py:39
  26.9 6.0 %collective-permute-done.8.refs_3_ = bf16[256,512]{1,0:T(8,128)(2,1)S(1)} collective-permute-done((bf16[256,512]{1,0:T(8,128)(2,1)S(1)}, bf16[256,512]{1,0:T(8,128)(2,1)S(1)}, u32[]{:S(2)}, u32[]{:S(2)}) %collective-permute-start.8) | collective-permute-done | bytes 262176 | tf_op jit(solution)/shard_map/ppermute | solution.py:39
  33.0 3.5 %collective-permute-done.9.refs_4_ = bf16[256,512]{1,0:T(8,128)(2,1)S(1)} collective-permute-done((bf16[256,512]{1,0:T(8,128)(2,1)S(1)}, bf16[256,512]{1,0:T(8,128)(2,1)S(1)}, u32[]{:S(2)}, u32[]{:S(2)}) %collective-permute-start.9) | collective-permute-done | bytes 262176 | tf_op jit(solution)/shard_map/ppermute | solution.py:39
  36.5 1.3 %input_grad.1 = (bf16[128,2048]{1,0:T(8,128)(2,1)S(1)}, bf16[128,2048]{1,0:T(8,128)(2,1)S(1)}, bf16[128,2048]{1,0:T(8,128)(2,1)S(1)}, bf16[128,2048]{1,0:T(8,128)(2,1)S(1)}) custom-call(bf16[128,512]{1,0:T(8,128)(2,1)S(1)} %bitcast.19, bf16[128,512]{1,0:T(8,128)(2,1)S(1)} %slice.12.u1, bf16[256,512]{1,0:T(8,128)(2,1)S(1)} %collective-permute-done.5.u2, ...), custom_call_target="tpu_custom_call" | custom-call | flops 1 | bytes 1 | tf_op jit(solution)/shard_map/input_grad/pallas_call | solution.py:144
  37.9 0.5 collective-permute-start.10
  38.4 3.0 %collective-permute-start.16 = (bf16[128,2048]{1,0:T(8,128)(2,1)S(1)}, bf16[128,2048]{1,0:T(8,128)(2,1)S(1)}, u32[]{:S(2)}, u32[]{:S(2)}) collective-permute-start(bf16[128,2048]{1,0:T(8,128)(2,1)S(1)} %get-tuple-element.60), channel_id=1, source_target_pairs={{0,8},{1,9},{2,10},{3,11},{4,12},{5,13},{6,14},{7,15},{8,0},{9,1},... | collective-permute-start | bytes 1572872 | tf_op jit(solution)/shard_map/ppermute | solution.py:39
  41.4 1.3 %weight_grad.1 = (f32[512,512]{1,0:T(8,128)S(1)}, bf16[448,512]{1,0:T(8,128)(2,1)S(1)}, bf16[448,512]{1,0:T(8,128)(2,1)S(1)}, f32[320,512]{1,0:T(8,128)S(1)}, f32[320,512]{1,0:T(8,128)S(1)}) custom-call(bf16[128,2048]{1,0:T(8,128)(2,1)S(1)} %get-tuple-element.50.t0, bf16[128,2560]{1,0:T(8,128)(2,1)S(1)} %collective-permute-done.4.t1, ...), custom_call_target="tpu_custom_call" | custom-call | flops 1 | bytes 1 | tf_op jit(solution)/shard_map/weight_grad/pallas_call | solution.py:236
  43.0 1.8 %collective-permute-start.17 = (bf16[448,512]{1,0:T(8,128)(2,1)S(1)}, bf16[448,512]{1,0:T(8,128)(2,1)S(1)}, u32[]{:S(2)}, u32[]{:S(2)}) collective-permute-start(bf16[448,512]{1,0:T(8,128)(2,1)S(1)} %get-tuple-element.63), channel_id=1, source_target_pairs={{0,2},{1,3},{2,4},{3,5},{4,6},{5,7},{6,0},{7,1},{8,10},{9,11},{10,... | collective-permute-start | bytes 1376264 | tf_op jit(solution)/shard_map/ppermute | solution.py:39
  44.9 0.9 %collective-permute-start.11 = (bf16[96,2048]{1,0:T(8,128)(2,1)S(1)}, bf16[96,2048]{1,0:T(8,128)(2,1)S(1)}, u32[]{:S(2)}, u32[]{:S(2)}) collective-permute-start(bf16[96,2048]{1,0:T(8,128)(2,1)S(1)} %split.1), channel_id=1, source_target_pairs={{0,8},{1,9},{2,10},{3,11},{4,12},{5,13},{6,14},{7,15},{8,0},{9,1},... | collective-permute-start | bytes 1179656 | tf_op jit(solution)/shard_map/ppermute | solution.py:39
  45.7 1.2 %values.1 = (f32[128,512]{1,0:T(8,128)S(1)}, f32[128,512]{1,0:T(8,128)S(1)}, bf16[256,512]{1,0:T(8,128)(2,1)S(1)}) custom-call(bf16[128,2048]{1,0:T(8,128)(2,1)S(1)} %get-tuple-element.50.t0, bf16[128,2560]{1,0:T(8,128)(2,1)S(1)} %collective-permute-done.4.t1, bf16[128,2048]{1,0:T(8,128)(2,1)S(1)} %collective-permute-done.t2, ...), custom_call_target="tpu_custom_call" | custom-call | flops 1 | bytes 1 | tf_op jit(solution)/shard_map/values/pallas_call | solution.py:166
  47.0 7.7 %collective-permute-done.16.refs_2_ = bf16[128,2048]{1,0:T(8,128)(2,1)S(1)} collective-permute-done((bf16[128,2048]{1,0:T(8,128)(2,1)S(1)}, bf16[128,2048]{1,0:T(8,128)(2,1)S(1)}, u32[]{:S(2)}, u32[]{:S(2)}) %collective-permute-start.16) | collective-permute-done | bytes 524320 | tf_op jit(solution)/shard_map/ppermute | solution.py:39
  54.7 0.4 collective-permute-done.15.from_above
  55.0 1.5 %collective-permute-done.17.from_below = bf16[448,512]{1,0:T(8,128)(2,1)S(1)} collective-permute-done((bf16[448,512]{1,0:T(8,128)(2,1)S(1)}, bf16[448,512]{1,0:T(8,128)(2,1)S(1)}, u32[]{:S(2)}, u32[]{:S(2)}) %collective-permute-start.17) | collective-permute-done | bytes 458784 | tf_op jit(solution)/shard_map/ppermute | solution.py:39
  56.7 0.7 collective-permute-start.22
  57.6 3.0 %collective-permute-start.19 = (bf16[320,512]{1,0:T(8,128)(2,1)S(1)}, bf16[320,512]{1,0:T(8,128)(2,1)S(1)}, u32[]{:S(2)}, u32[]{:S(2)}) collective-permute-start(bf16[320,512]{1,0:T(8,128)(2,1)S(1)} %get-tuple-element.65), channel_id=1, source_target_pairs={{0,6},{1,7},{2,0},{3,1},{4,2},{5,3},{6,4},{7,5},{8,14},{9,15},{10,... | collective-permute-start | bytes 983048 | tf_op jit(solution)/shard_map/ppermute | solution.py:39
  60.7 2.4 %collective-permute-done.11.refs_0_ = bf16[96,2048]{1,0:T(8,128)(2,1)S(1)} collective-permute-done((bf16[96,2048]{1,0:T(8,128)(2,1)S(1)}, bf16[96,2048]{1,0:T(8,128)(2,1)S(1)}, u32[]{:S(2)}, u32[]{:S(2)}) %collective-permute-start.11) | collective-permute-done | bytes 393248 | tf_op jit(solution)/shard_map/ppermute | solution.py:39
  63.1 3.0 %collective-permute-start.14 = (bf16[64,2048]{1,0:T(8,128)(2,1)S(1)}, bf16[64,2048]{1,0:T(8,128)(2,1)S(1)}, u32[]{:S(2)}, u32[]{:S(2)}) collective-permute-start(bf16[64,2048]{1,0:T(8,128)(2,1)S(1)} %pack.1), channel_id=1, source_target_pairs={{0,8},{1,9},{2,10},{3,11},{4,12},{5,13},{6,14},{7,15},{8,0},{9,1},... | collective-permute-start | bytes 786440 | tf_op jit(solution)/shard_map/ppermute | solution.py:39
  66.8 1.2 %assemble.2.refs_4_ = bf16[128,8192]{1,0:T(8,128)(2,1)} custom-call(bf16[128,2048]{1,0:T(8,128)(2,1)S(1)} %get-tuple-element.51.refs_0_, bf16[128,2048]{1,0:T(8,128)(2,1)S(1)} %collective-permute-done.20.refs_1_, bf16[128,2048]{1,0:T(8,128)(2,1)S(1)} %collective-permute-done.16.refs_2_), custom_call_target="tpu_custom_call" | custom-call | flops 1 | bytes 1 | tf_op jit(solution)/shard_map/assemble/pallas_call | solution.py:310
  68.1 0.8 %multiply_subtract_fusion = (f32[512,128]{1,0:T(8,128)S(1)}, f32[512,128]{1,0:T(8,128)}) fusion(f32[512,128]{1,0:T(8,128)S(1)} %copy-done.7, bf16[512,128]{1,0:T(8,128)(2,1)S(1)} %collective-permute-done.22, bf16[512,128]{1,0:T(8,128)(2,1)S(1)} %convert_add_fusion, f32[512,128]{1,0:T(8,128)S(1)} %copy-done.8), kind=kLoop, calls=%fused_computation.1 | loop fusion | flops 655360 | bytes 1310720 | tf_op jit(solution)/shard_map/sub | solution.py:66
  68.9 2.0 %adam.1 = (f32[512,512]{1,0:T(8,128)}, f32[512,512]{1,0:T(8,128)}, f32[512,512]{1,0:T(8,128)}) custom-call(s32[1]{0:T(128)S(6)} %copy.18.frag, f32[512,512]{1,0:T(8,128)S(1)} %get-tuple-element.53.g0, bf16[448,512]{1,0:T(8,128)(2,1)S(1)} %collective-permute-done.15.from_above, bf16[320,512]{1,0:T(8,128)(2,1)S(1)} %collective-permute-done.18.r1, ...), custom_call_target="tpu_custom_call" | custom-call | flops 1 | bytes 1 | tf_op jit(solution)/shard_map/adam/pallas_call | solution.py:361
  71.2 1.5 %assemble.3 = (bf16[128,8192]{1,0:T(8,128)(2,1)}, bf16[128,512]{1,0:T(8,128)(2,1)}) custom-call(bf16[96,2048]{1,0:T(8,128)(2,1)S(1)} %collective-permute-done.11.refs_0_, bf16[64,2048]{1,0:T(8,128)(2,1)S(1)} %collective-permute-done.14.refs_1_, f32[128,512]{1,0:T(8,128)S(1)} %get-tuple-element.72.refs_2_, ...), custom_call_target="tpu_custom_call", output_to_operand_aliasing={{0}: (4, {})} | custom-call | flops 1 | bytes 1 | tf_op jit(solution)/shard_map/assemble/pallas_call | solution.py:310
  (55 shorter events, 1.9 us)
Async XLA Ops:
  0.6 1.6 %copy-start = (bf16[1,128,8192]{2,1,0:T(8,128)(2,1)S(1)}, bf16[1,128,8192]{2,1,0:T(8,128)(2,1)}, u32[]{:S(2)}) copy-start(bf16[1,128,8192]{2,1,0:T(8,128)(2,1)} %param.9) | copy-start | bytes 6291460
  3.1 4.3 %copy-start.1 = (f32[1,512,512]{2,1,0:T(8,128)S(1)}, f32[1,512,512]{2,1,0:T(8,128)}, u32[]{:S(2)}) copy-start(f32[1,512,512]{2,1,0:T(8,128)} %param.11) | copy-start | bytes 3145732
  3.4 7.2 %copy-start.9 = (f32[1,512,128]{2,1,0:T(8,128)S(1)}, f32[1,512,128]{2,1,0:T(8,128)}, u32[]{:S(2)}) copy-start(f32[1,512,128]{2,1,0:T(8,128)} %param.14) | copy-start | bytes 786436
  3.4 4.1 %collective-permute-start.1 = (bf16[128,2048]{1,0:T(8,128)(2,1)S(1)}, bf16[128,2048]{1,0:T(8,128)(2,1)S(1)}, u32[]{:S(2)}, u32[]{:S(2)}) collective-permute-start(bf16[128,2048]{1,0:T(8,128)(2,1)S(1)} %get-tuple-element.45), channel_id=1, source_target_pairs={{0,1},{1,0},{2,3},{3,2},{4,5},{5,4},{6,7},{7,6},{8,9},{9,8},{10,11... | collective-permute-start | bytes 1572872 | tf_op jit(solution)/shard_map/ppermute | solution.py:39
  3.8 32.7 %copy-start.3 = (bf16[1,128,512]{2,1,0:T(8,128)(2,1)S(1)}, bf16[1,128,512]{2,1,0:T(8,128)(2,1)}, u32[]{:S(2)}) copy-start(bf16[1,128,512]{2,1,0:T(8,128)(2,1)} %param.10) | copy-start | bytes 393220
  3.8 6.8 %collective-permute-start = (bf16[128,2048]{1,0:T(8,128)(2,1)S(1)}, bf16[128,2048]{1,0:T(8,128)(2,1)S(1)}, u32[]{:S(2)}, u32[]{:S(2)}) collective-permute-start(bf16[128,2048]{1,0:T(8,128)(2,1)S(1)} %get-tuple-element.44), channel_id=1, source_target_pairs={{0,1},{1,0},{2,3},{3,2},{4,5},{5,4},{6,7},{7,6},{8,9},{9,8},{10,11... | collective-permute-start | bytes 1572872 | tf_op jit(solution)/shard_map/ppermute | solution.py:39
  4.4 19.1 %collective-permute-start.4 = (bf16[128,2560]{1,0:T(8,128)(2,1)S(1)}, bf16[128,2560]{1,0:T(8,128)(2,1)S(1)}, u32[]{:S(2)}, u32[]{:S(2)}) collective-permute-start(bf16[128,2560]{1,0:T(8,128)(2,1)S(1)} %get-tuple-element.42), channel_id=1, source_target_pairs={{0,8},{1,9},{2,10},{3,11},{4,12},{5,13},{6,14},{7,15},{8,0},{9,1},... | collective-permute-start | bytes 1966088 | tf_op jit(solution)/shard_map/ppermute | solution.py:39
  7.5 16.1 %collective-permute-start.6 = (bf16[512,512]{1,0:T(8,128)(2,1)S(1)}, bf16[512,512]{1,0:T(8,128)(2,1)S(1)}, u32[]{:S(2)}, u32[]{:S(2)}) collective-permute-start(bf16[512,512]{1,0:T(8,128)(2,1)S(1)} %bitcast_convert_fusion.refs_0_), channel_id=1, source_target_pairs={{0,6},{1,7},{2,0},{3,1},{4,2},{5,3},{6,4},{7,5},{8,14},{9,15},{10,... | collective-permute-start | bytes 1572872 | tf_op jit(solution)/shard_map/ppermute | solution.py:39
  10.6 16.2 %collective-permute-start.7 = (bf16[512,512]{1,0:T(8,128)(2,1)S(1)}, bf16[512,512]{1,0:T(8,128)(2,1)S(1)}, u32[]{:S(2)}, u32[]{:S(2)}) collective-permute-start(bf16[512,512]{1,0:T(8,128)(2,1)S(1)} %bitcast_convert_fusion.refs_0_), channel_id=1, source_target_pairs={{0,2},{1,3},{2,4},{3,5},{4,6},{5,7},{6,0},{7,1},{8,10},{9,11},{10,... | collective-permute-start | bytes 1572872 | tf_op jit(solution)/shard_map/ppermute | solution.py:39
  10.6 10.6 %collective-permute-start.2 = (bf16[512,128]{1,0:T(8,128)(2,1)S(1)}, bf16[512,128]{1,0:T(8,128)(2,1)S(1)}, u32[]{:S(2)}, u32[]{:S(2)}) collective-permute-start(bf16[512,128]{1,0:T(8,128)(2,1)S(1)} %convert_bitcast_fusion), channel_id=1, source_target_pairs={{0,96},{16,112},{32,64},{48,80},{64,32},{80,48},{96,0},{112,16},{1... | collective-permute-start | bytes 393224 | tf_op jit(solution)/shard_map/ppermute | solution.py:56
  15.2 26.2 %collective-permute-start.12 = (bf16[128,2048]{1,0:T(8,128)(2,1)S(1)}, bf16[128,2048]{1,0:T(8,128)(2,1)S(1)}, u32[]{:S(2)}, u32[]{:S(2)}) collective-permute-start(bf16[128,2048]{1,0:T(8,128)(2,1)S(1)} %collective-permute-done.1), channel_id=1, source_target_pairs={{0,8},{1,9},{2,10},{3,11},{4,12},{5,13},{6,14},{7,15},{8,0},{9,1},... | collective-permute-start | bytes 1572872 | tf_op jit(solution)/shard_map/ppermute | solution.py:39
  21.3 5.6 %collective-permute-start.3 = (bf16[512,128]{1,0:T(8,128)(2,1)S(1)}, bf16[512,128]{1,0:T(8,128)(2,1)S(1)}, u32[]{:S(2)}, u32[]{:S(2)}) collective-permute-start(bf16[512,128]{1,0:T(8,128)(2,1)S(1)} %add_convert_fusion), channel_id=1, source_target_pairs={{0,16},{16,0},{32,48},{48,32},{64,80},{80,64},{96,112},{112,96},{1... | collective-permute-start | bytes 393224 | tf_op jit(solution)/shard_map/ppermute | solution.py:56
  23.5 3.4 %collective-permute-start.5 = (bf16[256,512]{1,0:T(8,128)(2,1)S(1)}, bf16[256,512]{1,0:T(8,128)(2,1)S(1)}, u32[]{:S(2)}, u32[]{:S(2)}) collective-permute-start(bf16[256,512]{1,0:T(8,128)(2,1)S(1)} %pad_maximum_fusion), channel_id=1, source_target_pairs={{0,1},{1,0},{2,3},{3,2},{4,5},{5,4},{6,7},{7,6},{8,9},{9,8},{10,11... | collective-permute-start | bytes 786440 | tf_op jit(solution)/shard_map/ppermute | solution.py:39
  23.7 9.3 %collective-permute-start.8 = (bf16[256,512]{1,0:T(8,128)(2,1)S(1)}, bf16[256,512]{1,0:T(8,128)(2,1)S(1)}, u32[]{:S(2)}, u32[]{:S(2)}) collective-permute-start(bf16[256,512]{1,0:T(8,128)(2,1)S(1)} %slice.13), channel_id=1, source_target_pairs={{0,6},{1,7},{2,0},{3,1},{4,2},{5,3},{6,4},{7,5},{8,14},{9,15},{10,... | collective-permute-start | bytes 786440 | tf_op jit(solution)/shard_map/ppermute | solution.py:39
  26.8 9.7 %collective-permute-start.9 = (bf16[256,512]{1,0:T(8,128)(2,1)S(1)}, bf16[256,512]{1,0:T(8,128)(2,1)S(1)}, u32[]{:S(2)}, u32[]{:S(2)}) collective-permute-start(bf16[256,512]{1,0:T(8,128)(2,1)S(1)} %slice.14), channel_id=1, source_target_pairs={{0,2},{1,3},{2,4},{3,5},{4,6},{5,7},{6,0},{7,1},{8,10},{9,11},{10,... | collective-permute-start | bytes 786440 | tf_op jit(solution)/shard_map/ppermute | solution.py:39
  37.8 7.1 %collective-permute-start.20 = (bf16[128,2048]{1,0:T(8,128)(2,1)S(1)}, bf16[128,2048]{1,0:T(8,128)(2,1)S(1)}, u32[]{:S(2)}, u32[]{:S(2)}) collective-permute-start(bf16[128,2048]{1,0:T(8,128)(2,1)S(1)} %get-tuple-element.67), channel_id=1, source_target_pairs={{0,1},{1,0},{2,3},{3,2},{4,5},{5,4},{6,7},{7,6},{8,9},{9,8},{10,11... | collective-permute-start | bytes 1572872 | tf_op jit(solution)/shard_map/ppermute | solution.py:39
  37.9 7.0 %collective-permute-start.10 = (bf16[128,2048]{1,0:T(8,128)(2,1)S(1)}, bf16[128,2048]{1,0:T(8,128)(2,1)S(1)}, u32[]{:S(2)}, u32[]{:S(2)}) collective-permute-start(bf16[128,2048]{1,0:T(8,128)(2,1)S(1)} %get-tuple-element.49), channel_id=1, source_target_pairs={{0,1},{1,0},{2,3},{3,2},{4,5},{5,4},{6,7},{7,6},{8,9},{9,8},{10,11... | collective-permute-start | bytes 1572872 | tf_op jit(solution)/shard_map/ppermute | solution.py:39
  38.4 16.3 %collective-permute-start.16 = (bf16[128,2048]{1,0:T(8,128)(2,1)S(1)}, bf16[128,2048]{1,0:T(8,128)(2,1)S(1)}, u32[]{:S(2)}, u32[]{:S(2)}) collective-permute-start(bf16[128,2048]{1,0:T(8,128)(2,1)S(1)} %get-tuple-element.60), channel_id=1, source_target_pairs={{0,8},{1,9},{2,10},{3,11},{4,12},{5,13},{6,14},{7,15},{8,0},{9,1},... | collective-permute-start | bytes 1572872 | tf_op jit(solution)/shard_map/ppermute | solution.py:39
  42.7 12.3 %collective-permute-start.15 = (bf16[448,512]{1,0:T(8,128)(2,1)S(1)}, bf16[448,512]{1,0:T(8,128)(2,1)S(1)}, u32[]{:S(2)}, u32[]{:S(2)}) collective-permute-start(bf16[448,512]{1,0:T(8,128)(2,1)S(1)} %get-tuple-element.58), channel_id=1, source_target_pairs={{0,6},{1,7},{2,0},{3,1},{4,2},{5,3},{6,4},{7,5},{8,14},{9,15},{10,... | collective-permute-start | bytes 1376264 | tf_op jit(solution)/shard_map/ppermute | solution.py:39
  43.0 13.5 %collective-permute-start.17 = (bf16[448,512]{1,0:T(8,128)(2,1)S(1)}, bf16[448,512]{1,0:T(8,128)(2,1)S(1)}, u32[]{:S(2)}, u32[]{:S(2)}) collective-permute-start(bf16[448,512]{1,0:T(8,128)(2,1)S(1)} %get-tuple-element.63), channel_id=1, source_target_pairs={{0,2},{1,3},{2,4},{3,5},{4,6},{5,7},{6,0},{7,1},{8,10},{9,11},{10,... | collective-permute-start | bytes 1376264 | tf_op jit(solution)/shard_map/ppermute | solution.py:39
  44.8 11.8 %collective-permute-start.21 = (bf16[512,128]{1,0:T(8,128)(2,1)S(1)}, bf16[512,128]{1,0:T(8,128)(2,1)S(1)}, u32[]{:S(2)}, u32[]{:S(2)}) collective-permute-start(bf16[512,128]{1,0:T(8,128)(2,1)S(1)} %convert_add_fusion.1), channel_id=1, source_target_pairs={{0,32},{16,48},{32,0},{48,16},{64,96},{80,112},{96,64},{112,80},{1... | collective-permute-start | bytes 393224 | tf_op jit(solution)/shard_map/ppermute | solution.py:56
  44.9 18.2 %collective-permute-start.11 = (bf16[96,2048]{1,0:T(8,128)(2,1)S(1)}, bf16[96,2048]{1,0:T(8,128)(2,1)S(1)}, u32[]{:S(2)}, u32[]{:S(2)}) collective-permute-start(bf16[96,2048]{1,0:T(8,128)(2,1)S(1)} %split.1), channel_id=1, source_target_pairs={{0,8},{1,9},{2,10},{3,11},{4,12},{5,13},{6,14},{7,15},{8,0},{9,1},... | collective-permute-start | bytes 1179656 | tf_op jit(solution)/shard_map/ppermute | solution.py:39
  54.7 5.9 %collective-permute-start.13 = (bf16[256,512]{1,0:T(8,128)(2,1)S(1)}, bf16[256,512]{1,0:T(8,128)(2,1)S(1)}, u32[]{:S(2)}, u32[]{:S(2)}) collective-permute-start(bf16[256,512]{1,0:T(8,128)(2,1)S(1)} %get-tuple-element.55), channel_id=1, source_target_pairs={{0,1},{1,0},{2,3},{3,2},{4,5},{5,4},{6,7},{7,6},{8,9},{9,8},{10,11... | collective-permute-start | bytes 786440 | tf_op jit(solution)/shard_map/ppermute | solution.py:39
  56.7 11.4 %collective-permute-start.22 = (bf16[512,128]{1,0:T(8,128)(2,1)S(1)}, bf16[512,128]{1,0:T(8,128)(2,1)S(1)}, u32[]{:S(2)}, u32[]{:S(2)}) collective-permute-start(bf16[512,128]{1,0:T(8,128)(2,1)S(1)} %convert_add_fusion), channel_id=1, source_target_pairs={{0,128},{16,144},{32,160},{48,176},{64,192},{80,208},{96,224},{112... | collective-permute-start | bytes 393224 | tf_op jit(solution)/shard_map/ppermute | solution.py:56
  57.4 11.5 %collective-permute-start.18 = (bf16[320,512]{1,0:T(8,128)(2,1)S(1)}, bf16[320,512]{1,0:T(8,128)(2,1)S(1)}, u32[]{:S(2)}, u32[]{:S(2)}) collective-permute-start(bf16[320,512]{1,0:T(8,128)(2,1)S(1)} %get-tuple-element.64), channel_id=1, source_target_pairs={{0,2},{1,3},{2,4},{3,5},{4,6},{5,7},{6,0},{7,1},{8,10},{9,11},{10,... | collective-permute-start | bytes 983048 | tf_op jit(solution)/shard_map/ppermute | solution.py:39
  57.6 11.2 %collective-permute-start.19 = (bf16[320,512]{1,0:T(8,128)(2,1)S(1)}, bf16[320,512]{1,0:T(8,128)(2,1)S(1)}, u32[]{:S(2)}, u32[]{:S(2)}) collective-permute-start(bf16[320,512]{1,0:T(8,128)(2,1)S(1)} %get-tuple-element.65), channel_id=1, source_target_pairs={{0,6},{1,7},{2,0},{3,1},{4,2},{5,3},{6,4},{7,5},{8,14},{9,15},{10,... | collective-permute-start | bytes 983048 | tf_op jit(solution)/shard_map/ppermute | solution.py:39
  60.6 7.4 %copy-start.7 = (f32[512,128]{1,0:T(8,128)S(1)}, f32[512,128]{1,0:T(8,128)}, u32[]{:S(2)}) copy-start(f32[512,128]{1,0:T(8,128)} %param.16) | copy-start | bytes 786436
  60.6 7.4 %copy-start.8 = (f32[512,128]{1,0:T(8,128)S(1)}, f32[512,128]{1,0:T(8,128)}, u32[]{:S(2)}) copy-start(f32[512,128]{1,0:T(8,128)} %param.15) | copy-start | bytes 786436
  63.1 8.1 %collective-permute-start.14 = (bf16[64,2048]{1,0:T(8,128)(2,1)S(1)}, bf16[64,2048]{1,0:T(8,128)(2,1)S(1)}, u32[]{:S(2)}, u32[]{:S(2)}) collective-permute-start(bf16[64,2048]{1,0:T(8,128)(2,1)S(1)} %pack.1), channel_id=1, source_target_pairs={{0,8},{1,9},{2,10},{3,11},{4,12},{5,13},{6,14},{7,15},{8,0},{9,1},... | collective-permute-start | bytes 786440 | tf_op jit(solution)/shard_map/ppermute | solution.py:39
  66.8 2.1 %copy-start.5 = (f32[1,512,512]{2,1,0:T(8,128)S(1)}, f32[1,512,512]{2,1,0:T(8,128)}, u32[]{:S(2)}) copy-start(f32[1,512,512]{2,1,0:T(8,128)} %param.12) | copy-start | bytes 3145732
  66.8 2.1 %copy-start.6 = (f32[1,512,512]{2,1,0:T(8,128)S(1)}, f32[1,512,512]{2,1,0:T(8,128)}, u32[]{:S(2)}) copy-start(f32[1,512,512]{2,1,0:T(8,128)} %param.13) | copy-start | bytes 3145732
  68.9 2.1 %copy-start.4 = (f32[512,128]{1,0:T(8,128)}, f32[512,128]{1,0:T(8,128)S(1)}, u32[]{:S(2)}) copy-start(f32[512,128]{1,0:T(8,128)S(1)} %get-tuple-element.77.glob) | copy-start | bytes 786436
  (1 other events, 0.9 us)

commit v6 on v4

--- a/solution.py
+++ b/solution.py
@@ -271,7 +271,7 @@
     n = len(wanted)
 
     def kernel(*refs):
-        target, sems = refs[-3 if vals else -2], refs[-1]
+        *_, target, sems = refs if not vals else (refs[-4], refs[-1])
         x, _, c = here()
         copies = []
         for i, (dx, dc, start, size) in enumerate(wanted):
@@ -294,6 +294,8 @@
                 rows = slice(k * rest, (k + 1) * rest)
                 came = refs[n - 1][rest:, k * F : (k + 1) * F].astype(jnp.float32)
                 refs[-2][rows] = ((total[rows] + came) * SCALE).astype(jnp.bfloat16)
+            copies.append(pltpu.make_async_copy(refs[-2], refs[-3], sems.at[NY * n]))
+            copies[-1].start()
         for copy in copies:
             copy.wait()
 
@@ -301,7 +303,7 @@
     ins = [pl.BlockSpec(memory_space=pltpu.VMEM)] * len(args)
     outs, shapes, alias = [pl.BlockSpec(memory_space=pltpu.HBM)], [shape(TOK, D)], {}
     if vals:
-        outs.append(pl.BlockSpec(memory_space=pltpu.VMEM))
+        outs.append(pl.BlockSpec(memory_space=pltpu.HBM))
         shapes.append(shape(TOK, F))
     if block is not None:
         alias = {len(args): 0}
@@ -312,7 +314,8 @@
         in_specs=ins,
         out_specs=outs if vals else outs[0],
         out_shape=shapes if vals else shapes[0],
-        scratch_shapes=[pltpu.SemaphoreType.DMA((NY * n,))],
+        scratch_shapes=[pltpu.VMEM((TOK, F), jnp.bfloat16)] * bool(vals)
+        + [pltpu.SemaphoreType.DMA((NY * n + 1,))],
         input_output_aliases=alias,
         cost_estimate=SMALL,
         compiler_params=VMEM,
@@ -422,14 +425,15 @@
     new_momentum, new_global = outer_update(momentum, global_frag, total / 16)
 
     block = assemble(
-        None, (ig_own, back_core, back_x), ((0, 0, 0, TOK), (0, 1, 0, TOK), (1, 0, 0, TOK))
+        None,
+        (ig_own, back_core, back_x, other_a),
+        ((0, 0, 0, TOK), (0, 1, 0, TOK), (1, 0, 0, TOK), (1, 1, 0, FIRST)),
     )
     new_weight, new_m, new_v = adam(
-        frag_index, (g0, from_above, r1, from_below, r3), adam_m[0], adam_v[0], master, new_global
-    )
-    other_b = after(other_b, new_weight)
+        frag_index, (g0, from_above, r1, from_below, r3), adam_m[0], adam_v[0], master, after(new_global, block)
+    )
     block, values = assemble(
-        block, (other_a, other_b), ((1, 1, 0, FIRST), (1, 1, FIRST, TOK - FIRST)), (val_own, val_back)
+        block, (after(other_b, new_weight),), ((1, 1, FIRST, TOK - FIRST),), (val_own, val_back)
     )
     return (
         values[None],

time: 72.9 us -> 72.2 us (level)
  no operation moved by 1% of the time
where the time goes in v6:
time: 72.2 us; the launch traced here: 71.9 us
  starting transfers between devices  29.2 us (40%)
  waiting for transfers between devices  28.6 us (40%)
  Pallas kernels  8.74 us (12%)
  local copies, waits for them, and re-layouts  2.57 us (4%)
  between operations  1.76 us (2%)
  other arithmetic  1.01 us (1%)
    ppermute x19, starting transfers between devices, fsdp_permute(): return lax.ppermute(value, 'fsdp', pairs)  23.6 us
    ppermute x19, waiting for transfers between devices, fsdp_permute(): return lax.ppermute(value, 'fsdp', pairs)  23.2 us
    ppermute x4, starting transfers between devices, replica_step(): other = lax.ppermute(sent, 'replica', [(i, partner(i)) for i in range(16)])  5.62 us
    ppermute x4, waiting for transfers between devices, replica_step(): other = lax.ppermute(sent, 'replica', [(i, partner(i)) for i in range(16)])  5.38 us
    unnamed x20, local copies, waits for them, and re-layouts  2.53 us
    pallas_call x2, Pallas kernels, assemble(): pl.pallas_call(kernel, in_specs=ins, out_specs=outs if vals else outs[0],...  2.16 us
    pallas_call x1, Pallas kernels, adam(): pl.pallas_call(kernel, in_specs=[pl.BlockSpec(memory_space=pltpu.SMEM)] +...  2.02 us
  transfers between devices with their start and end apart: 23, of which 7 were waited for; matrix products, arithmetic and copies ran while one was open for 1% of the time, Pallas kernels for 9%

profile of v6, /device:TPU:64, one launch (start us, length us, event | category | flops | bytes accessed | tf_op | source)
XLA Modules:
  0.0 71.9 jit_solution(318576566603689997)
XLA Ops:
  0.6 1.6 %copy-done = bf16[1,128,8192]{2,1,0:T(8,128)(2,1)S(1)} copy-done((bf16[1,128,8192]{2,1,0:T(8,128)(2,1)S(1)}, bf16[1,128,8192]{2,1,0:T(8,128)(2,1)}, u32[]{:S(2)}) %copy-start) | copy-done | bytes 2097176
  2.2 0.9 %copy-done.2 = bf16[1,128,512]{2,1,0:T(8,128)(2,1)S(1)} copy-done((bf16[1,128,512]{2,1,0:T(8,128)(2,1)S(1)}, bf16[1,128,512]{2,1,0:T(8,128)(2,1)}, u32[]{:S(2)}) %copy-start.2) | copy-done | bytes 131096
  3.8 0.6 collective-permute-start
  4.4 3.0 %collective-permute-start.4 = (bf16[128,2560]{1,0:T(8,128)(2,1)S(1)}, bf16[128,2560]{1,0:T(8,128)(2,1)S(1)}, u32[]{:S(2)}, u32[]{:S(2)}) collective-permute-start(bf16[128,2560]{1,0:T(8,128)(2,1)S(1)} %get-tuple-element.43), channel_id=1, source_target_pairs={{0,8},{1,9},{2,10},{3,11},{4,12},{5,13},{6,14},{7,15},{8,0},{9,1},... | collective-permute-start | bytes 1966088 | tf_op jit(solution)/shard_map/ppermute | solution.py:39
  7.5 1.7 %collective-permute-start.8 = (bf16[512,512]{1,0:T(8,128)(2,1)S(1)}, bf16[512,512]{1,0:T(8,128)(2,1)S(1)}, u32[]{:S(2)}, u32[]{:S(2)}) collective-permute-start(bf16[512,512]{1,0:T(8,128)(2,1)S(1)} %bitcast_convert_fusion.refs_0_), channel_id=1, source_target_pairs={{0,2},{1,3},{2,4},{3,5},{4,6},{5,7},{6,0},{7,1},{8,10},{9,11},{10,... | collective-permute-start | bytes 1572872 | tf_op jit(solution)/shard_map/ppermute | solution.py:39
  9.1 1.7 %collective-permute-start.7 = (bf16[512,512]{1,0:T(8,128)(2,1)S(1)}, bf16[512,512]{1,0:T(8,128)(2,1)S(1)}, u32[]{:S(2)}, u32[]{:S(2)}) collective-permute-start(bf16[512,512]{1,0:T(8,128)(2,1)S(1)} %bitcast_convert_fusion.refs_0_), channel_id=1, source_target_pairs={{0,6},{1,7},{2,0},{3,1},{4,2},{5,3},{6,4},{7,5},{8,14},{9,15},{10,... | collective-permute-start | bytes 1572872 | tf_op jit(solution)/shard_map/ppermute | solution.py:39
  10.8 4.6 %collective-permute-start.2 = (bf16[512,128]{1,0:T(8,128)(2,1)S(1)}, bf16[512,128]{1,0:T(8,128)(2,1)S(1)}, u32[]{:S(2)}, u32[]{:S(2)}) collective-permute-start(bf16[512,128]{1,0:T(8,128)(2,1)S(1)} %convert_bitcast_fusion), channel_id=1, source_target_pairs={{0,96},{16,112},{32,64},{48,80},{64,32},{80,48},{96,0},{112,16},{1... | collective-permute-start | bytes 393224 | tf_op jit(solution)/shard_map/ppermute | solution.py:56
  15.4 0.5 collective-permute-start.5
  15.9 5.4 %collective-permute-done.2 = bf16[512,128]{1,0:T(8,128)(2,1)S(1)} collective-permute-done((bf16[512,128]{1,0:T(8,128)(2,1)S(1)}, bf16[512,128]{1,0:T(8,128)(2,1)S(1)}, u32[]{:S(2)}, u32[]{:S(2)}) %collective-permute-start.2) | collective-permute-done | bytes 131104 | tf_op jit(solution)/shard_map/ppermute | solution.py:56
  21.7 1.8 %collective-permute-done.4.t1 = bf16[128,2560]{1,0:T(8,128)(2,1)S(1)} collective-permute-done((bf16[128,2560]{1,0:T(8,128)(2,1)S(1)}, bf16[128,2560]{1,0:T(8,128)(2,1)S(1)}, u32[]{:S(2)}, u32[]{:S(2)}) %collective-permute-start.4) | collective-permute-done | bytes 655392 | tf_op jit(solution)/shard_map/ppermute | solution.py:39
  23.7 1.7 %collective-permute-start.10 = (bf16[256,512]{1,0:T(8,128)(2,1)S(1)}, bf16[256,512]{1,0:T(8,128)(2,1)S(1)}, u32[]{:S(2)}, u32[]{:S(2)}) collective-permute-start(bf16[256,512]{1,0:T(8,128)(2,1)S(1)} %slice.14), channel_id=1, source_target_pairs={{0,2},{1,3},{2,4},{3,5},{4,6},{5,7},{6,0},{7,1},{8,10},{9,11},{10,... | collective-permute-start | bytes 786440 | tf_op jit(solution)/shard_map/ppermute | solution.py:39
  25.3 1.7 %collective-permute-start.9 = (bf16[256,512]{1,0:T(8,128)(2,1)S(1)}, bf16[256,512]{1,0:T(8,128)(2,1)S(1)}, u32[]{:S(2)}, u32[]{:S(2)}) collective-permute-start(bf16[256,512]{1,0:T(8,128)(2,1)S(1)} %slice.13), channel_id=1, source_target_pairs={{0,6},{1,7},{2,0},{3,1},{4,2},{5,3},{6,4},{7,5},{8,14},{9,15},{10,... | collective-permute-start | bytes 786440 | tf_op jit(solution)/shard_map/ppermute | solution.py:39
  27.1 6.7 %collective-permute-done.5.t3 = bf16[128,2048]{1,0:T(8,128)(2,1)S(1)} collective-permute-done((bf16[128,2048]{1,0:T(8,128)(2,1)S(1)}, bf16[128,2048]{1,0:T(8,128)(2,1)S(1)}, u32[]{:S(2)}, u32[]{:S(2)}) %collective-permute-start.5) | collective-permute-done | bytes 524320 | tf_op jit(solution)/shard_map/ppermute | solution.py:39
  33.9 1.3 %weight_grad.1 = (f32[512,512]{1,0:T(8,128)S(1)}, bf16[448,512]{1,0:T(8,128)(2,1)S(1)}, bf16[448,512]{1,0:T(8,128)(2,1)S(1)}, f32[320,512]{1,0:T(8,128)S(1)}, f32[320,512]{1,0:T(8,128)S(1)}) custom-call(bf16[128,2048]{1,0:T(8,128)(2,1)S(1)} %get-tuple-element.49.t0, bf16[128,2560]{1,0:T(8,128)(2,1)S(1)} %collective-permute-done.4.t1, ...), custom_call_target="tpu_custom_call" | custom-call | flops 1 | bytes 1 | tf_op jit(solution)/shard_map/weight_grad/pallas_call | solution.py:236
  35.2 1.3 %input_grad.1 = (bf16[128,2048]{1,0:T(8,128)(2,1)S(1)}, bf16[128,2048]{1,0:T(8,128)(2,1)S(1)}, bf16[128,2048]{1,0:T(8,128)(2,1)S(1)}, bf16[128,2048]{1,0:T(8,128)(2,1)S(1)}) custom-call(bf16[128,512]{1,0:T(8,128)(2,1)S(1)} %bitcast.20, bf16[128,512]{1,0:T(8,128)(2,1)S(1)} %slice.12.u1, bf16[256,512]{1,0:T(8,128)(2,1)S(1)} %collective-permute-done.6.u2, ...), custom_call_target="tpu_custom_call" | custom-call | flops 1 | bytes 1 | tf_op jit(solution)/shard_map/input_grad/pallas_call | solution.py:144
  36.6 0.5 collective-permute-start.11
  37.1 3.0 %collective-permute-start.16 = (bf16[128,2048]{1,0:T(8,128)(2,1)S(1)}, bf16[128,2048]{1,0:T(8,128)(2,1)S(1)}, u32[]{:S(2)}, u32[]{:S(2)}) collective-permute-start(bf16[128,2048]{1,0:T(8,128)(2,1)S(1)} %get-tuple-element.60), channel_id=1, source_target_pairs={{0,8},{1,9},{2,10},{3,11},{4,12},{5,13},{6,14},{7,15},{8,0},{9,1},... | collective-permute-start | bytes 1572872 | tf_op jit(solution)/shard_map/ppermute | solution.py:39
  40.1 3.0 %collective-permute-start.15 = (bf16[448,512]{1,0:T(8,128)(2,1)S(1)}, bf16[448,512]{1,0:T(8,128)(2,1)S(1)}, u32[]{:S(2)}, u32[]{:S(2)}) collective-permute-start(bf16[448,512]{1,0:T(8,128)(2,1)S(1)} %get-tuple-element.58), channel_id=1, source_target_pairs={{0,6},{1,7},{2,0},{3,1},{4,2},{5,3},{6,4},{7,5},{8,14},{9,15},{10,... | collective-permute-start | bytes 1376264 | tf_op jit(solution)/shard_map/ppermute | solution.py:39
  43.2 1.0 %collective-permute-start.13 = (bf16[96,2048]{1,0:T(8,128)(2,1)S(1)}, bf16[96,2048]{1,0:T(8,128)(2,1)S(1)}, u32[]{:S(2)}, u32[]{:S(2)}) collective-permute-start(bf16[96,2048]{1,0:T(8,128)(2,1)S(1)} %split.1), channel_id=1, source_target_pairs={{0,8},{1,9},{2,10},{3,11},{4,12},{5,13},{6,14},{7,15},{8,0},{9,1},... | collective-permute-start | bytes 1179656 | tf_op jit(solution)/shard_map/ppermute | solution.py:39
  44.2 1.2 %values.1 = (f32[128,512]{1,0:T(8,128)S(1)}, f32[128,512]{1,0:T(8,128)S(1)}, bf16[256,512]{1,0:T(8,128)(2,1)S(1)}) custom-call(bf16[128,2048]{1,0:T(8,128)(2,1)S(1)} %get-tuple-element.49.t0, bf16[128,2560]{1,0:T(8,128)(2,1)S(1)} %collective-permute-done.4.t1, bf16[128,2048]{1,0:T(8,128)(2,1)S(1)} %collective-permute-done.t2, ...), custom_call_target="tpu_custom_call" | custom-call | flops 1 | bytes 1 | tf_op jit(solution)/shard_map/values/pallas_call | solution.py:166
  45.4 7.9 %collective-permute-done.16.refs_2_ = bf16[128,2048]{1,0:T(8,128)(2,1)S(1)} collective-permute-done((bf16[128,2048]{1,0:T(8,128)(2,1)S(1)}, bf16[128,2048]{1,0:T(8,128)(2,1)S(1)}, u32[]{:S(2)}, u32[]{:S(2)}) %collective-permute-start.16) | collective-permute-done | bytes 524320 | tf_op jit(solution)/shard_map/ppermute | solution.py:39
  53.4 2.9 %collective-permute-done.17.from_below = bf16[448,512]{1,0:T(8,128)(2,1)S(1)} collective-permute-done((bf16[448,512]{1,0:T(8,128)(2,1)S(1)}, bf16[448,512]{1,0:T(8,128)(2,1)S(1)}, u32[]{:S(2)}, u32[]{:S(2)}) %collective-permute-start.17) | collective-permute-done | bytes 458784 | tf_op jit(solution)/shard_map/ppermute | solution.py:39
  56.5 0.7 collective-permute-start.22
  57.2 1.0 %collective-permute-start.19 = (bf16[320,512]{1,0:T(8,128)(2,1)S(1)}, bf16[320,512]{1,0:T(8,128)(2,1)S(1)}, u32[]{:S(2)}, u32[]{:S(2)}) collective-permute-start(bf16[320,512]{1,0:T(8,128)(2,1)S(1)} %get-tuple-element.65), channel_id=1, source_target_pairs={{0,6},{1,7},{2,0},{3,1},{4,2},{5,3},{6,4},{7,5},{8,14},{9,15},{10,... | collective-permute-start | bytes 983048 | tf_op jit(solution)/shard_map/ppermute | solution.py:39
  58.2 1.0 %collective-permute-start.18 = (bf16[320,512]{1,0:T(8,128)(2,1)S(1)}, bf16[320,512]{1,0:T(8,128)(2,1)S(1)}, u32[]{:S(2)}, u32[]{:S(2)}) collective-permute-start(bf16[320,512]{1,0:T(8,128)(2,1)S(1)} %get-tuple-element.64), channel_id=1, source_target_pairs={{0,2},{1,3},{2,4},{3,5},{4,6},{5,7},{6,0},{7,1},{8,10},{9,11},{10,... | collective-permute-start | bytes 983048 | tf_op jit(solution)/shard_map/ppermute | solution.py:39
  59.2 2.6 %collective-permute-done.13.refs_3_ = bf16[96,2048]{1,0:T(8,128)(2,1)S(1)} collective-permute-done((bf16[96,2048]{1,0:T(8,128)(2,1)S(1)}, bf16[96,2048]{1,0:T(8,128)(2,1)S(1)}, u32[]{:S(2)}, u32[]{:S(2)}) %collective-permute-start.13) | collective-permute-done | bytes 393248 | tf_op jit(solution)/shard_map/ppermute | solution.py:39
  61.8 3.0 %collective-permute-start.14 = (bf16[64,2048]{1,0:T(8,128)(2,1)S(1)}, bf16[64,2048]{1,0:T(8,128)(2,1)S(1)}, u32[]{:S(2)}, u32[]{:S(2)}) collective-permute-start(bf16[64,2048]{1,0:T(8,128)(2,1)S(1)} %pack.1), channel_id=1, source_target_pairs={{0,8},{1,9},{2,10},{3,11},{4,12},{5,13},{6,14},{7,15},{8,0},{9,1},... | collective-permute-start | bytes 786440 | tf_op jit(solution)/shard_map/ppermute | solution.py:39
  65.5 0.8 %multiply_subtract_fusion = (f32[512,128]{1,0:T(8,128)S(1)}, f32[512,128]{1,0:T(8,128)}) fusion(f32[512,128]{1,0:T(8,128)S(1)} %copy-done.7, bf16[512,128]{1,0:T(8,128)(2,1)S(1)} %collective-permute-done.22, bf16[512,128]{1,0:T(8,128)(2,1)S(1)} %convert_add_fusion, f32[512,128]{1,0:T(8,128)S(1)} %copy-done.8), kind=kLoop, calls=%fused_computation.1 | loop fusion | flops 655360 | bytes 1310720 | tf_op jit(solution)/shard_map/sub | solution.py:66
  66.3 1.4 %assemble.2.refs_3_ = bf16[128,8192]{1,0:T(8,128)(2,1)} custom-call(bf16[128,2048]{1,0:T(8,128)(2,1)S(1)} %get-tuple-element.70.refs_0_, bf16[128,2048]{1,0:T(8,128)(2,1)S(1)} %collective-permute-done.20.refs_1_, bf16[128,2048]{1,0:T(8,128)(2,1)S(1)} %collective-permute-done.16.refs_2_, bf16[96,2048]{1,0:T(8,128)(2,1)S(1)} %collective-permute-done.13.refs_3_), custom_call_target="tpu_custom_call" | custom-call | flops 1 | bytes 1 | tf_op jit(solution)/shard_map/assemble/pallas_call | solution.py:312
  67.7 1.2 %collective-permute-done.18.r1 = bf16[320,512]{1,0:T(8,128)(2,1)S(1)} collective-permute-done((bf16[320,512]{1,0:T(8,128)(2,1)S(1)}, bf16[320,512]{1,0:T(8,128)(2,1)S(1)}, u32[]{:S(2)}, u32[]{:S(2)}) %collective-permute-start.18) | collective-permute-done | bytes 327712 | tf_op jit(solution)/shard_map/ppermute | solution.py:39
  68.9 2.0 %adam.1 = (f32[512,512]{1,0:T(8,128)}, f32[512,512]{1,0:T(8,128)}, f32[512,512]{1,0:T(8,128)}) custom-call(s32[1]{0:T(128)S(6)} %copy.18.frag, f32[512,512]{1,0:T(8,128)S(1)} %get-tuple-element.50.g0, bf16[448,512]{1,0:T(8,128)(2,1)S(1)} %collective-permute-done.15.from_above, bf16[320,512]{1,0:T(8,128)(2,1)S(1)} %collective-permute-done.18.r1, ...), custom_call_target="tpu_custom_call" | custom-call | flops 1 | bytes 1 | tf_op jit(solution)/shard_map/adam/pallas_call | solution.py:364
  71.0 0.8 %assemble.3 = (bf16[128,8192]{1,0:T(8,128)(2,1)}, bf16[128,512]{1,0:T(8,128)(2,1)}) custom-call(bf16[64,2048]{1,0:T(8,128)(2,1)S(1)} %collective-permute-done.14.refs_0_, f32[128,512]{1,0:T(8,128)S(1)} %get-tuple-element.74.refs_1_, bf16[256,512]{1,0:T(8,128)(2,1)S(1)} %collective-permute-done.12.val_back.refs_2_, ...), custom_call_target="tpu_custom_call", output_to_operand_aliasing={{0}: (3, {})} | custom-call | flops 1 | bytes 1 | tf_op jit(solution)/shard_map/assemble/pallas_call | solution.py:312
  (55 shorter events, 1.7 us)
Async XLA Ops:
  0.6 1.6 %copy-start = (bf16[1,128,8192]{2,1,0:T(8,128)(2,1)S(1)}, bf16[1,128,8192]{2,1,0:T(8,128)(2,1)}, u32[]{:S(2)}) copy-start(bf16[1,128,8192]{2,1,0:T(8,128)(2,1)} %param.9) | copy-start | bytes 6291460
  3.1 4.3 %copy-start.1 = (f32[1,512,512]{2,1,0:T(8,128)S(1)}, f32[1,512,512]{2,1,0:T(8,128)}, u32[]{:S(2)}) copy-start(f32[1,512,512]{2,1,0:T(8,128)} %param.11) | copy-start | bytes 3145732
  3.4 7.4 %copy-start.9 = (f32[1,512,128]{2,1,0:T(8,128)S(1)}, f32[1,512,128]{2,1,0:T(8,128)}, u32[]{:S(2)}) copy-start(f32[1,512,128]{2,1,0:T(8,128)} %param.14) | copy-start | bytes 786436
  3.4 7.4 %collective-permute-start.1 = (bf16[128,2048]{1,0:T(8,128)(2,1)S(1)}, bf16[128,2048]{1,0:T(8,128)(2,1)S(1)}, u32[]{:S(2)}, u32[]{:S(2)}) collective-permute-start(bf16[128,2048]{1,0:T(8,128)(2,1)S(1)} %get-tuple-element.46), channel_id=1, source_target_pairs={{0,1},{1,0},{2,3},{3,2},{4,5},{5,4},{6,7},{7,6},{8,9},{9,8},{10,11... | collective-permute-start | bytes 1572872 | tf_op jit(solution)/shard_map/ppermute | solution.py:39
  3.8 30.0 %copy-start.3 = (bf16[1,128,512]{2,1,0:T(8,128)(2,1)S(1)}, bf16[1,128,512]{2,1,0:T(8,128)(2,1)}, u32[]{:S(2)}) copy-start(bf16[1,128,512]{2,1,0:T(8,128)(2,1)} %param.10) | copy-start | bytes 393220
  3.8 7.0 %collective-permute-start = (bf16[128,2048]{1,0:T(8,128)(2,1)S(1)}, bf16[128,2048]{1,0:T(8,128)(2,1)S(1)}, u32[]{:S(2)}, u32[]{:S(2)}) collective-permute-start(bf16[128,2048]{1,0:T(8,128)(2,1)S(1)} %get-tuple-element.45), channel_id=1, source_target_pairs={{0,1},{1,0},{2,3},{3,2},{4,5},{5,4},{6,7},{7,6},{8,9},{9,8},{10,11... | collective-permute-start | bytes 1572872 | tf_op jit(solution)/shard_map/ppermute | solution.py:39
  4.4 19.1 %collective-permute-start.4 = (bf16[128,2560]{1,0:T(8,128)(2,1)S(1)}, bf16[128,2560]{1,0:T(8,128)(2,1)S(1)}, u32[]{:S(2)}, u32[]{:S(2)}) collective-permute-start(bf16[128,2560]{1,0:T(8,128)(2,1)S(1)} %get-tuple-element.43), channel_id=1, source_target_pairs={{0,8},{1,9},{2,10},{3,11},{4,12},{5,13},{6,14},{7,15},{8,0},{9,1},... | collective-permute-start | bytes 1966088 | tf_op jit(solution)/shard_map/ppermute | solution.py:39
  7.5 16.1 %collective-permute-start.8 = (bf16[512,512]{1,0:T(8,128)(2,1)S(1)}, bf16[512,512]{1,0:T(8,128)(2,1)S(1)}, u32[]{:S(2)}, u32[]{:S(2)}) collective-permute-start(bf16[512,512]{1,0:T(8,128)(2,1)S(1)} %bitcast_convert_fusion.refs_0_), channel_id=1, source_target_pairs={{0,2},{1,3},{2,4},{3,5},{4,6},{5,7},{6,0},{7,1},{8,10},{9,11},{10,... | collective-permute-start | bytes 1572872 | tf_op jit(solution)/shard_map/ppermute | solution.py:39
  9.1 16.2 %collective-permute-start.7 = (bf16[512,512]{1,0:T(8,128)(2,1)S(1)}, bf16[512,512]{1,0:T(8,128)(2,1)S(1)}, u32[]{:S(2)}, u32[]{:S(2)}) collective-permute-start(bf16[512,512]{1,0:T(8,128)(2,1)S(1)} %bitcast_convert_fusion.refs_0_), channel_id=1, source_target_pairs={{0,6},{1,7},{2,0},{3,1},{4,2},{5,3},{6,4},{7,5},{8,14},{9,15},{10,... | collective-permute-start | bytes 1572872 | tf_op jit(solution)/shard_map/ppermute | solution.py:39
  10.8 10.4 %collective-permute-start.2 = (bf16[512,128]{1,0:T(8,128)(2,1)S(1)}, bf16[512,128]{1,0:T(8,128)(2,1)S(1)}, u32[]{:S(2)}, u32[]{:S(2)}) collective-permute-start(bf16[512,128]{1,0:T(8,128)(2,1)S(1)} %convert_bitcast_fusion), channel_id=1, source_target_pairs={{0,96},{16,112},{32,64},{48,80},{64,32},{80,48},{96,0},{112,16},{1... | collective-permute-start | bytes 393224 | tf_op jit(solution)/shard_map/ppermute | solution.py:56
  15.4 18.5 %collective-permute-start.5 = (bf16[128,2048]{1,0:T(8,128)(2,1)S(1)}, bf16[128,2048]{1,0:T(8,128)(2,1)S(1)}, u32[]{:S(2)}, u32[]{:S(2)}) collective-permute-start(bf16[128,2048]{1,0:T(8,128)(2,1)S(1)} %collective-permute-done.1), channel_id=1, source_target_pairs={{0,8},{1,9},{2,10},{3,11},{4,12},{5,13},{6,14},{7,15},{8,0},{9,1},... | collective-permute-start | bytes 1572872 | tf_op jit(solution)/shard_map/ppermute | solution.py:39
  21.3 5.7 %collective-permute-start.3 = (bf16[512,128]{1,0:T(8,128)(2,1)S(1)}, bf16[512,128]{1,0:T(8,128)(2,1)S(1)}, u32[]{:S(2)}, u32[]{:S(2)}) collective-permute-start(bf16[512,128]{1,0:T(8,128)(2,1)S(1)} %add_convert_fusion), channel_id=1, source_target_pairs={{0,16},{16,0},{32,48},{48,32},{64,80},{80,64},{96,112},{112,96},{1... | collective-permute-start | bytes 393224 | tf_op jit(solution)/shard_map/ppermute | solution.py:56
  23.5 3.6 %collective-permute-start.6 = (bf16[256,512]{1,0:T(8,128)(2,1)S(1)}, bf16[256,512]{1,0:T(8,128)(2,1)S(1)}, u32[]{:S(2)}, u32[]{:S(2)}) collective-permute-start(bf16[256,512]{1,0:T(8,128)(2,1)S(1)} %pad_maximum_fusion), channel_id=1, source_target_pairs={{0,1},{1,0},{2,3},{3,2},{4,5},{5,4},{6,7},{7,6},{8,9},{9,8},{10,11... | collective-permute-start | bytes 786440 | tf_op jit(solution)/shard_map/ppermute | solution.py:39
  23.7 11.5 %collective-permute-start.10 = (bf16[256,512]{1,0:T(8,128)(2,1)S(1)}, bf16[256,512]{1,0:T(8,128)(2,1)S(1)}, u32[]{:S(2)}, u32[]{:S(2)}) collective-permute-start(bf16[256,512]{1,0:T(8,128)(2,1)S(1)} %slice.14), channel_id=1, source_target_pairs={{0,2},{1,3},{2,4},{3,5},{4,6},{5,7},{6,0},{7,1},{8,10},{9,11},{10,... | collective-permute-start | bytes 786440 | tf_op jit(solution)/shard_map/ppermute | solution.py:39
  25.3 9.9 %collective-permute-start.9 = (bf16[256,512]{1,0:T(8,128)(2,1)S(1)}, bf16[256,512]{1,0:T(8,128)(2,1)S(1)}, u32[]{:S(2)}, u32[]{:S(2)}) collective-permute-start(bf16[256,512]{1,0:T(8,128)(2,1)S(1)} %slice.13), channel_id=1, source_target_pairs={{0,6},{1,7},{2,0},{3,1},{4,2},{5,3},{6,4},{7,5},{8,14},{9,15},{10,... | collective-permute-start | bytes 786440 | tf_op jit(solution)/shard_map/ppermute | solution.py:39
  36.5 6.6 %collective-permute-start.20 = (bf16[128,2048]{1,0:T(8,128)(2,1)S(1)}, bf16[128,2048]{1,0:T(8,128)(2,1)S(1)}, u32[]{:S(2)}, u32[]{:S(2)}) collective-permute-start(bf16[128,2048]{1,0:T(8,128)(2,1)S(1)} %get-tuple-element.67), channel_id=1, source_target_pairs={{0,1},{1,0},{2,3},{3,2},{4,5},{5,4},{6,7},{7,6},{8,9},{9,8},{10,11... | collective-permute-start | bytes 1572872 | tf_op jit(solution)/shard_map/ppermute | solution.py:39
  36.6 6.6 %collective-permute-start.11 = (bf16[128,2048]{1,0:T(8,128)(2,1)S(1)}, bf16[128,2048]{1,0:T(8,128)(2,1)S(1)}, u32[]{:S(2)}, u32[]{:S(2)}) collective-permute-start(bf16[128,2048]{1,0:T(8,128)(2,1)S(1)} %get-tuple-element.53), channel_id=1, source_target_pairs={{0,1},{1,0},{2,3},{3,2},{4,5},{5,4},{6,7},{7,6},{8,9},{9,8},{10,11... | collective-permute-start | bytes 1572872 | tf_op jit(solution)/shard_map/ppermute | solution.py:39
  37.1 16.3 %collective-permute-start.16 = (bf16[128,2048]{1,0:T(8,128)(2,1)S(1)}, bf16[128,2048]{1,0:T(8,128)(2,1)S(1)}, u32[]{:S(2)}, u32[]{:S(2)}) collective-permute-start(bf16[128,2048]{1,0:T(8,128)(2,1)S(1)} %get-tuple-element.60), channel_id=1, source_target_pairs={{0,8},{1,9},{2,10},{3,11},{4,12},{5,13},{6,14},{7,15},{8,0},{9,1},... | collective-permute-start | bytes 1572872 | tf_op jit(solution)/shard_map/ppermute | solution.py:39
  40.1 13.3 %collective-permute-start.15 = (bf16[448,512]{1,0:T(8,128)(2,1)S(1)}, bf16[448,512]{1,0:T(8,128)(2,1)S(1)}, u32[]{:S(2)}, u32[]{:S(2)}) collective-permute-start(bf16[448,512]{1,0:T(8,128)(2,1)S(1)} %get-tuple-element.58), channel_id=1, source_target_pairs={{0,6},{1,7},{2,0},{3,1},{4,2},{5,3},{6,4},{7,5},{8,14},{9,15},{10,... | collective-permute-start | bytes 1376264 | tf_op jit(solution)/shard_map/ppermute | solution.py:39
  43.1 13.2 %collective-permute-start.17 = (bf16[448,512]{1,0:T(8,128)(2,1)S(1)}, bf16[448,512]{1,0:T(8,128)(2,1)S(1)}, u32[]{:S(2)}, u32[]{:S(2)}) collective-permute-start(bf16[448,512]{1,0:T(8,128)(2,1)S(1)} %get-tuple-element.63), channel_id=1, source_target_pairs={{0,2},{1,3},{2,4},{3,5},{4,6},{5,7},{6,0},{7,1},{8,10},{9,11},{10,... | collective-permute-start | bytes 1376264 | tf_op jit(solution)/shard_map/ppermute | solution.py:39
  43.2 13.3 %collective-permute-start.21 = (bf16[512,128]{1,0:T(8,128)(2,1)S(1)}, bf16[512,128]{1,0:T(8,128)(2,1)S(1)}, u32[]{:S(2)}, u32[]{:S(2)}) collective-permute-start(bf16[512,128]{1,0:T(8,128)(2,1)S(1)} %convert_add_fusion.1), channel_id=1, source_target_pairs={{0,32},{16,48},{32,0},{48,16},{64,96},{80,112},{96,64},{112,80},{1... | collective-permute-start | bytes 393224 | tf_op jit(solution)/shard_map/ppermute | solution.py:56
  43.2 18.6 %collective-permute-start.13 = (bf16[96,2048]{1,0:T(8,128)(2,1)S(1)}, bf16[96,2048]{1,0:T(8,128)(2,1)S(1)}, u32[]{:S(2)}, u32[]{:S(2)}) collective-permute-start(bf16[96,2048]{1,0:T(8,128)(2,1)S(1)} %split.1), channel_id=1, source_target_pairs={{0,8},{1,9},{2,10},{3,11},{4,12},{5,13},{6,14},{7,15},{8,0},{9,1},... | collective-permute-start | bytes 1179656 | tf_op jit(solution)/shard_map/ppermute | solution.py:39
  45.4 20.1 %copy-start.7 = (f32[512,128]{1,0:T(8,128)S(1)}, f32[512,128]{1,0:T(8,128)}, u32[]{:S(2)}) copy-start(f32[512,128]{1,0:T(8,128)} %param.16) | copy-start | bytes 786436
  45.4 20.1 %copy-start.8 = (f32[512,128]{1,0:T(8,128)S(1)}, f32[512,128]{1,0:T(8,128)}, u32[]{:S(2)}) copy-start(f32[512,128]{1,0:T(8,128)} %param.15) | copy-start | bytes 786436
  53.4 5.8 %collective-permute-start.12 = (bf16[256,512]{1,0:T(8,128)(2,1)S(1)}, bf16[256,512]{1,0:T(8,128)(2,1)S(1)}, u32[]{:S(2)}, u32[]{:S(2)}) collective-permute-start(bf16[256,512]{1,0:T(8,128)(2,1)S(1)} %get-tuple-element.55), channel_id=1, source_target_pairs={{0,1},{1,0},{2,3},{3,2},{4,5},{5,4},{6,7},{7,6},{8,9},{9,8},{10,11... | collective-permute-start | bytes 786440 | tf_op jit(solution)/shard_map/ppermute | solution.py:39
  56.5 9.0 %collective-permute-start.22 = (bf16[512,128]{1,0:T(8,128)(2,1)S(1)}, bf16[512,128]{1,0:T(8,128)(2,1)S(1)}, u32[]{:S(2)}, u32[]{:S(2)}) collective-permute-start(bf16[512,128]{1,0:T(8,128)(2,1)S(1)} %convert_add_fusion), channel_id=1, source_target_pairs={{0,128},{16,144},{32,160},{48,176},{64,192},{80,208},{96,224},{112... | collective-permute-start | bytes 393224 | tf_op jit(solution)/shard_map/ppermute | solution.py:56
  57.2 10.6 %collective-permute-start.19 = (bf16[320,512]{1,0:T(8,128)(2,1)S(1)}, bf16[320,512]{1,0:T(8,128)(2,1)S(1)}, u32[]{:S(2)}, u32[]{:S(2)}) collective-permute-start(bf16[320,512]{1,0:T(8,128)(2,1)S(1)} %get-tuple-element.65), channel_id=1, source_target_pairs={{0,6},{1,7},{2,0},{3,1},{4,2},{5,3},{6,4},{7,5},{8,14},{9,15},{10,... | collective-permute-start | bytes 983048 | tf_op jit(solution)/shard_map/ppermute | solution.py:39
  58.2 10.8 %collective-permute-start.18 = (bf16[320,512]{1,0:T(8,128)(2,1)S(1)}, bf16[320,512]{1,0:T(8,128)(2,1)S(1)}, u32[]{:S(2)}, u32[]{:S(2)}) collective-permute-start(bf16[320,512]{1,0:T(8,128)(2,1)S(1)} %get-tuple-element.64), channel_id=1, source_target_pairs={{0,2},{1,3},{2,4},{3,5},{4,6},{5,7},{6,0},{7,1},{8,10},{9,11},{10,... | collective-permute-start | bytes 983048 | tf_op jit(solution)/shard_map/ppermute | solution.py:39
  61.8 9.2 %collective-permute-start.14 = (bf16[64,2048]{1,0:T(8,128)(2,1)S(1)}, bf16[64,2048]{1,0:T(8,128)(2,1)S(1)}, u32[]{:S(2)}, u32[]{:S(2)}) collective-permute-start(bf16[64,2048]{1,0:T(8,128)(2,1)S(1)} %pack.1), channel_id=1, source_target_pairs={{0,8},{1,9},{2,10},{3,11},{4,12},{5,13},{6,14},{7,15},{8,0},{9,1},... | collective-permute-start | bytes 786440 | tf_op jit(solution)/shard_map/ppermute | solution.py:39
  66.3 4.7 %copy-start.4 = (f32[512,128]{1,0:T(8,128)}, f32[512,128]{1,0:T(8,128)S(1)}, u32[]{:S(2)}) copy-start(f32[512,128]{1,0:T(8,128)S(1)} %get-tuple-element.71.glob) | copy-start | bytes 786436
  66.3 2.6 %copy-start.5 = (f32[1,512,512]{2,1,0:T(8,128)S(1)}, f32[1,512,512]{2,1,0:T(8,128)}, u32[]{:S(2)}) copy-start(f32[1,512,512]{2,1,0:T(8,128)} %param.12) | copy-start | bytes 3145732
  66.3 2.6 %copy-start.6 = (f32[1,512,512]{2,1,0:T(8,128)S(1)}, f32[1,512,512]{2,1,0:T(8,128)}, u32[]{:S(2)}) copy-start(f32[1,512,512]{2,1,0:T(8,128)} %param.13) | copy-start | bytes 3145732
  (1 other events, 0.9 us)

commit v7 on v6

--- a/solution.py
+++ b/solution.py
@@ -414,7 +414,7 @@
 
     val_own, val_x, val_pair = value_parts(toks, (after(weight_bf, g0), *blocks[1:]))
     val_back = swap_core(val_pair)
-    other_b = swap_x(after(pack(back_far, val_back, val_x), other_a))
+    other_b = swap_x(pack(back_far, val_back, val_x))
     total = replica_step(after(total, back_core), lambda i: i ^ 2)
 
     s1, s3 = relay(after(keep_above, back_x), keep_below, from_below, from_above)

time: 72.2 us -> 75.3 us (1.043)
  starting transfers between devices: 29.2 us -> 30.7 us
  local copies, waits for them, and re-layouts: 2.57 us -> 3.45 us
  waiting for transfers between devices: 28.6 us -> 29.4 us
    ppermute x4, waiting for transfers between devices: 5.38 us -> 12.1 us  [replica_step(): other = lax.ppermute(sent, 'replica', [(i, partner(i)) for i in range(16)])]
    ppermute x19, waiting for transfers between devices: 23.2 us -> 17.3 us  [fsdp_permute(): return lax.ppermute(value, 'fsdp', pairs)]
    ppermute x19, starting transfers between devices: 23.6 us -> 25.1 us  [fsdp_permute(): return lax.ppermute(value, 'fsdp', pairs)]
    unnamed x20, local copies, waits for them, and re-layouts: 2.53 us -> 3.4 us
  transfers between devices with their start and end apart: 23 -> 23, of which waited for: 7 -> 6; matrix products, arithmetic and copies ran while one was open for 1% -> 1% of each run, Pallas kernels for 9% -> 9%
where the time goes in v7:
time: 75.3 us; the launch traced here: 75.1 us
  starting transfers between devices  30.7 us (41%)
  waiting for transfers between devices  29.4 us (39%)
  Pallas kernels  8.77 us (12%)
  local copies, waits for them, and re-layouts  3.45 us (5%)
  between operations  1.76 us (2%)
  other arithmetic  1.01 us (1%)
    ppermute x19, starting transfers between devices, fsdp_permute(): return lax.ppermute(value, 'fsdp', pairs)  25.1 us
    ppermute x19, waiting for transfers between devices, fsdp_permute(): return lax.ppermute(value, 'fsdp', pairs)  17.3 us
    ppermute x4, waiting for transfers between devices, replica_step(): other = lax.ppermute(sent, 'replica', [(i, partner(i)) for i in range(16)])  12.1 us
    ppermute x4, starting transfers between devices, replica_step(): other = lax.ppermute(sent, 'replica', [(i, partner(i)) for i in range(16)])  5.62 us
    unnamed x20, local copies, waits for them, and re-layouts  3.4 us
    pallas_call x2, Pallas kernels, assemble(): pl.pallas_call(kernel, in_specs=ins, out_specs=outs if vals else outs[0],...  2.18 us
    pallas_call x1, Pallas kernels, adam(): pl.pallas_call(kernel, in_specs=[pl.BlockSpec(memory_space=pltpu.SMEM)] +...  2.03 us
  transfers between devices with their start and end apart: 23, of which 6 were waited for; matrix products, arithmetic and copies ran while one was open for 1% of the time, Pallas kernels for 9%

profile of v7, /device:TPU:64, one launch (start us, length us, event | category | flops | bytes accessed | tf_op | source)
XLA Modules:
  0.0 75.1 jit_solution(3468053653102189323)
XLA Ops:
  0.6 1.6 %copy-done = bf16[1,128,8192]{2,1,0:T(8,128)(2,1)S(1)} copy-done((bf16[1,128,8192]{2,1,0:T(8,128)(2,1)S(1)}, bf16[1,128,8192]{2,1,0:T(8,128)(2,1)}, u32[]{:S(2)}) %copy-start) | copy-done | bytes 2097176
  2.2 0.9 %copy-done.2 = bf16[1,128,512]{2,1,0:T(8,128)(2,1)S(1)} copy-done((bf16[1,128,512]{2,1,0:T(8,128)(2,1)S(1)}, bf16[1,128,512]{2,1,0:T(8,128)(2,1)}, u32[]{:S(2)}) %copy-start.2) | copy-done | bytes 131096
  3.8 0.6 collective-permute-start
  4.4 3.0 %collective-permute-start.4 = (bf16[128,2560]{1,0:T(8,128)(2,1)S(1)}, bf16[128,2560]{1,0:T(8,128)(2,1)S(1)}, u32[]{:S(2)}, u32[]{:S(2)}) collective-permute-start(bf16[128,2560]{1,0:T(8,128)(2,1)S(1)} %get-tuple-element.42), channel_id=1, source_target_pairs={{0,8},{1,9},{2,10},{3,11},{4,12},{5,13},{6,14},{7,15},{8,0},{9,1},... | collective-permute-start | bytes 1966088 | tf_op jit(solution)/shard_map/ppermute | solution.py:39
  7.5 1.7 %collective-permute-start.8 = (bf16[512,512]{1,0:T(8,128)(2,1)S(1)}, bf16[512,512]{1,0:T(8,128)(2,1)S(1)}, u32[]{:S(2)}, u32[]{:S(2)}) collective-permute-start(bf16[512,512]{1,0:T(8,128)(2,1)S(1)} %bitcast_convert_fusion.refs_0_), channel_id=1, source_target_pairs={{0,2},{1,3},{2,4},{3,5},{4,6},{5,7},{6,0},{7,1},{8,10},{9,11},{10,... | collective-permute-start | bytes 1572872 | tf_op jit(solution)/shard_map/ppermute | solution.py:39
  9.1 1.7 %collective-permute-start.7 = (bf16[512,512]{1,0:T(8,128)(2,1)S(1)}, bf16[512,512]{1,0:T(8,128)(2,1)S(1)}, u32[]{:S(2)}, u32[]{:S(2)}) collective-permute-start(bf16[512,512]{1,0:T(8,128)(2,1)S(1)} %bitcast_convert_fusion.refs_0_), channel_id=1, source_target_pairs={{0,6},{1,7},{2,0},{3,1},{4,2},{5,3},{6,4},{7,5},{8,14},{9,15},{10,... | collective-permute-start | bytes 1572872 | tf_op jit(solution)/shard_map/ppermute | solution.py:39
  10.8 4.6 %collective-permute-start.2 = (bf16[512,128]{1,0:T(8,128)(2,1)S(1)}, bf16[512,128]{1,0:T(8,128)(2,1)S(1)}, u32[]{:S(2)}, u32[]{:S(2)}) collective-permute-start(bf16[512,128]{1,0:T(8,128)(2,1)S(1)} %convert_bitcast_fusion), channel_id=1, source_target_pairs={{0,96},{16,112},{32,64},{48,80},{64,32},{80,48},{96,0},{112,16},{1... | collective-permute-start | bytes 393224 | tf_op jit(solution)/shard_map/ppermute | solution.py:56
  15.4 0.5 collective-permute-start.5
  15.9 5.4 %collective-permute-done.2 = bf16[512,128]{1,0:T(8,128)(2,1)S(1)} collective-permute-done((bf16[512,128]{1,0:T(8,128)(2,1)S(1)}, bf16[512,128]{1,0:T(8,128)(2,1)S(1)}, u32[]{:S(2)}, u32[]{:S(2)}) %collective-permute-start.2) | collective-permute-done | bytes 131104 | tf_op jit(solution)/shard_map/ppermute | solution.py:56
  21.3 0.4 collective-permute-start.3
  21.7 1.8 %collective-permute-done.4.t1 = bf16[128,2560]{1,0:T(8,128)(2,1)S(1)} collective-permute-done((bf16[128,2560]{1,0:T(8,128)(2,1)S(1)}, bf16[128,2560]{1,0:T(8,128)(2,1)S(1)}, u32[]{:S(2)}, u32[]{:S(2)}) %collective-permute-start.4) | collective-permute-done | bytes 655392 | tf_op jit(solution)/shard_map/ppermute | solution.py:39
  23.7 1.7 %collective-permute-start.10 = (bf16[256,512]{1,0:T(8,128)(2,1)S(1)}, bf16[256,512]{1,0:T(8,128)(2,1)S(1)}, u32[]{:S(2)}, u32[]{:S(2)}) collective-permute-start(bf16[256,512]{1,0:T(8,128)(2,1)S(1)} %slice.14), channel_id=1, source_target_pairs={{0,2},{1,3},{2,4},{3,5},{4,6},{5,7},{6,0},{7,1},{8,10},{9,11},{10,... | collective-permute-start | bytes 786440 | tf_op jit(solution)/shard_map/ppermute | solution.py:39
  25.3 1.7 %collective-permute-start.9 = (bf16[256,512]{1,0:T(8,128)(2,1)S(1)}, bf16[256,512]{1,0:T(8,128)(2,1)S(1)}, u32[]{:S(2)}, u32[]{:S(2)}) collective-permute-start(bf16[256,512]{1,0:T(8,128)(2,1)S(1)} %slice.13), channel_id=1, source_target_pairs={{0,6},{1,7},{2,0},{3,1},{4,2},{5,3},{6,4},{7,5},{8,14},{9,15},{10,... | collective-permute-start | bytes 786440 | tf_op jit(solution)/shard_map/ppermute | solution.py:39
  27.1 6.7 %collective-permute-done.5.t3 = bf16[128,2048]{1,0:T(8,128)(2,1)S(1)} collective-permute-done((bf16[128,2048]{1,0:T(8,128)(2,1)S(1)}, bf16[128,2048]{1,0:T(8,128)(2,1)S(1)}, u32[]{:S(2)}, u32[]{:S(2)}) %collective-permute-start.5) | collective-permute-done | bytes 524320 | tf_op jit(solution)/shard_map/ppermute | solution.py:39
  33.9 1.3 %weight_grad.1 = (f32[512,512]{1,0:T(8,128)S(1)}, bf16[448,512]{1,0:T(8,128)(2,1)S(1)}, bf16[448,512]{1,0:T(8,128)(2,1)S(1)}, f32[320,512]{1,0:T(8,128)S(1)}, f32[320,512]{1,0:T(8,128)S(1)}) custom-call(bf16[128,2048]{1,0:T(8,128)(2,1)S(1)} %get-tuple-element.48.t0, bf16[128,2560]{1,0:T(8,128)(2,1)S(1)} %collective-permute-done.4.t1, ...), custom_call_target="tpu_custom_call" | custom-call | flops 1 | bytes 1 | tf_op jit(solution)/shard_map/weight_grad/pallas_call | solution.py:236
  35.2 1.3 %input_grad.1 = (bf16[128,2048]{1,0:T(8,128)(2,1)S(1)}, bf16[128,2048]{1,0:T(8,128)(2,1)S(1)}, bf16[128,2048]{1,0:T(8,128)(2,1)S(1)}, bf16[128,2048]{1,0:T(8,128)(2,1)S(1)}) custom-call(bf16[128,512]{1,0:T(8,128)(2,1)S(1)} %bitcast.20, bf16[128,512]{1,0:T(8,128)(2,1)S(1)} %slice.12.u1, bf16[256,512]{1,0:T(8,128)(2,1)S(1)} %collective-permute-done.6.u2, ...), custom_call_target="tpu_custom_call" | custom-call | flops 1 | bytes 1 | tf_op jit(solution)/shard_map/input_grad/pallas_call | solution.py:144
  36.6 0.5 collective-permute-start.11
  37.1 3.0 %collective-permute-start.15 = (bf16[128,2048]{1,0:T(8,128)(2,1)S(1)}, bf16[128,2048]{1,0:T(8,128)(2,1)S(1)}, u32[]{:S(2)}, u32[]{:S(2)}) collective-permute-start(bf16[128,2048]{1,0:T(8,128)(2,1)S(1)} %get-tuple-element.58), channel_id=1, source_target_pairs={{0,8},{1,9},{2,10},{3,11},{4,12},{5,13},{6,14},{7,15},{8,0},{9,1},... | collective-permute-start | bytes 1572872 | tf_op jit(solution)/shard_map/ppermute | solution.py:39
  40.1 3.0 %collective-permute-start.14 = (bf16[448,512]{1,0:T(8,128)(2,1)S(1)}, bf16[448,512]{1,0:T(8,128)(2,1)S(1)}, u32[]{:S(2)}, u32[]{:S(2)}) collective-permute-start(bf16[448,512]{1,0:T(8,128)(2,1)S(1)} %get-tuple-element.56), channel_id=1, source_target_pairs={{0,6},{1,7},{2,0},{3,1},{4,2},{5,3},{6,4},{7,5},{8,14},{9,15},{10,... | collective-permute-start | bytes 1376264 | tf_op jit(solution)/shard_map/ppermute | solution.py:39
  43.2 1.2 %values.1 = (f32[128,512]{1,0:T(8,128)S(1)}, f32[128,512]{1,0:T(8,128)S(1)}, bf16[256,512]{1,0:T(8,128)(2,1)S(1)}) custom-call(bf16[128,2048]{1,0:T(8,128)(2,1)S(1)} %get-tuple-element.48.t0, bf16[128,2560]{1,0:T(8,128)(2,1)S(1)} %collective-permute-done.4.t1, bf16[128,2048]{1,0:T(8,128)(2,1)S(1)} %collective-permute-done.t2, ...), custom_call_target="tpu_custom_call" | custom-call | flops 1 | bytes 1 | tf_op jit(solution)/shard_map/values/pallas_call | solution.py:166
  44.6 8.0 %collective-permute-done.15.refs_2_ = bf16[128,2048]{1,0:T(8,128)(2,1)S(1)} collective-permute-done((bf16[128,2048]{1,0:T(8,128)(2,1)S(1)}, bf16[128,2048]{1,0:T(8,128)(2,1)S(1)}, u32[]{:S(2)}, u32[]{:S(2)}) %collective-permute-start.15) | collective-permute-done | bytes 524320 | tf_op jit(solution)/shard_map/ppermute | solution.py:39
  52.5 3.0 %collective-permute-start.22 = (bf16[96,2048]{1,0:T(8,128)(2,1)S(1)}, bf16[96,2048]{1,0:T(8,128)(2,1)S(1)}, u32[]{:S(2)}, u32[]{:S(2)}) collective-permute-start(bf16[96,2048]{1,0:T(8,128)(2,1)S(1)} %split.1), channel_id=1, source_target_pairs={{0,8},{1,9},{2,10},{3,11},{4,12},{5,13},{6,14},{7,15},{8,0},{9,1},... | collective-permute-start | bytes 1179656 | tf_op jit(solution)/shard_map/ppermute | solution.py:39
  55.6 0.8 %collective-permute-done.16.from_below = bf16[448,512]{1,0:T(8,128)(2,1)S(1)} collective-permute-done((bf16[448,512]{1,0:T(8,128)(2,1)S(1)}, bf16[448,512]{1,0:T(8,128)(2,1)S(1)}, u32[]{:S(2)}, u32[]{:S(2)}) %collective-permute-start.16) | collective-permute-done | bytes 458784 | tf_op jit(solution)/shard_map/ppermute | solution.py:39
  56.5 0.7 collective-permute-start.21
  57.2 2.3 %collective-permute-start.18 = (bf16[320,512]{1,0:T(8,128)(2,1)S(1)}, bf16[320,512]{1,0:T(8,128)(2,1)S(1)}, u32[]{:S(2)}, u32[]{:S(2)}) collective-permute-start(bf16[320,512]{1,0:T(8,128)(2,1)S(1)} %get-tuple-element.63), channel_id=1, source_target_pairs={{0,6},{1,7},{2,0},{3,1},{4,2},{5,3},{6,4},{7,5},{8,14},{9,15},{10,... | collective-permute-start | bytes 983048 | tf_op jit(solution)/shard_map/ppermute | solution.py:39
  59.5 2.1 %collective-permute-start.13 = (bf16[64,2048]{1,0:T(8,128)(2,1)S(1)}, bf16[64,2048]{1,0:T(8,128)(2,1)S(1)}, u32[]{:S(2)}, u32[]{:S(2)}) collective-permute-start(bf16[64,2048]{1,0:T(8,128)(2,1)S(1)} %pack.1), channel_id=1, source_target_pairs={{0,8},{1,9},{2,10},{3,11},{4,12},{5,13},{6,14},{7,15},{8,0},{9,1},... | collective-permute-start | bytes 786440 | tf_op jit(solution)/shard_map/ppermute | solution.py:39
  62.2 6.8 %collective-permute-done.21 = bf16[512,128]{1,0:T(8,128)(2,1)S(1)} collective-permute-done((bf16[512,128]{1,0:T(8,128)(2,1)S(1)}, bf16[512,128]{1,0:T(8,128)(2,1)S(1)}, u32[]{:S(2)}, u32[]{:S(2)}) %collective-permute-start.21) | collective-permute-done | bytes 131104 | tf_op jit(solution)/shard_map/ppermute | solution.py:56
  69.0 0.8 %multiply_subtract_fusion = (f32[512,128]{1,0:T(8,128)S(1)}, f32[512,128]{1,0:T(8,128)}) fusion(f32[512,128]{1,0:T(8,128)S(1)} %copy-done.7, bf16[512,128]{1,0:T(8,128)(2,1)S(1)} %collective-permute-done.21, bf16[512,128]{1,0:T(8,128)(2,1)S(1)} %convert_add_fusion, f32[512,128]{1,0:T(8,128)S(1)} %copy-done.8), kind=kLoop, calls=%fused_computation.1 | loop fusion | flops 655360 | bytes 1310720 | tf_op jit(solution)/shard_map/sub | solution.py:66
  69.8 1.4 %assemble.2.refs_3_ = bf16[128,8192]{1,0:T(8,128)(2,1)} custom-call(bf16[128,2048]{1,0:T(8,128)(2,1)S(1)} %get-tuple-element.68.refs_0_, bf16[128,2048]{1,0:T(8,128)(2,1)S(1)} %collective-permute-done.19.refs_1_, bf16[128,2048]{1,0:T(8,128)(2,1)S(1)} %collective-permute-done.15.refs_2_, bf16[96,2048]{1,0:T(8,128)(2,1)S(1)} %collective-permute-done.22.refs_3_), custom_call_target="tpu_custom_call" | custom-call | flops 1 | bytes 1 | tf_op jit(solution)/shard_map/assemble/pallas_call | solution.py:312
  71.2 0.5 copy-done.5
  72.1 2.0 %adam.1 = (f32[512,512]{1,0:T(8,128)}, f32[512,512]{1,0:T(8,128)}, f32[512,512]{1,0:T(8,128)}) custom-call(s32[1]{0:T(128)S(6)} %copy.18.frag, f32[512,512]{1,0:T(8,128)S(1)} %get-tuple-element.49.g0, bf16[448,512]{1,0:T(8,128)(2,1)S(1)} %collective-permute-done.14.from_above, bf16[320,512]{1,0:T(8,128)(2,1)S(1)} %collective-permute-done.17.r1, ...), custom_call_target="tpu_custom_call" | custom-call | flops 1 | bytes 1 | tf_op jit(solution)/shard_map/adam/pallas_call | solution.py:364
  74.2 0.8 %assemble.3 = (bf16[128,8192]{1,0:T(8,128)(2,1)}, bf16[128,512]{1,0:T(8,128)(2,1)}) custom-call(bf16[64,2048]{1,0:T(8,128)(2,1)S(1)} %collective-permute-done.13.refs_0_, f32[128,512]{1,0:T(8,128)S(1)} %get-tuple-element.72.refs_1_, bf16[256,512]{1,0:T(8,128)(2,1)S(1)} %collective-permute-done.12.val_back.refs_2_, ...), custom_call_target="tpu_custom_call", output_to_operand_aliasing={{0}: (3, {})} | custom-call | flops 1 | bytes 1 | tf_op jit(solution)/shard_map/assemble/pallas_call | solution.py:312
  (55 shorter events, 1.8 us)
Async XLA Ops:
  0.6 1.6 %copy-start = (bf16[1,128,8192]{2,1,0:T(8,128)(2,1)S(1)}, bf16[1,128,8192]{2,1,0:T(8,128)(2,1)}, u32[]{:S(2)}) copy-start(bf16[1,128,8192]{2,1,0:T(8,128)(2,1)} %param.9) | copy-start | bytes 6291460
  3.1 4.3 %copy-start.1 = (f32[1,512,512]{2,1,0:T(8,128)S(1)}, f32[1,512,512]{2,1,0:T(8,128)}, u32[]{:S(2)}) copy-start(f32[1,512,512]{2,1,0:T(8,128)} %param.11) | copy-start | bytes 3145732
  3.4 7.4 %copy-start.9 = (f32[1,512,128]{2,1,0:T(8,128)S(1)}, f32[1,512,128]{2,1,0:T(8,128)}, u32[]{:S(2)}) copy-start(f32[1,512,128]{2,1,0:T(8,128)} %param.14) | copy-start | bytes 786436
  3.4 7.4 %collective-permute-start.1 = (bf16[128,2048]{1,0:T(8,128)(2,1)S(1)}, bf16[128,2048]{1,0:T(8,128)(2,1)S(1)}, u32[]{:S(2)}, u32[]{:S(2)}) collective-permute-start(bf16[128,2048]{1,0:T(8,128)(2,1)S(1)} %get-tuple-element.45), channel_id=1, source_target_pairs={{0,1},{1,0},{2,3},{3,2},{4,5},{5,4},{6,7},{7,6},{8,9},{9,8},{10,11... | collective-permute-start | bytes 1572872 | tf_op jit(solution)/shard_map/ppermute | solution.py:39
  3.8 30.0 %copy-start.3 = (bf16[1,128,512]{2,1,0:T(8,128)(2,1)S(1)}, bf16[1,128,512]{2,1,0:T(8,128)(2,1)}, u32[]{:S(2)}) copy-start(bf16[1,128,512]{2,1,0:T(8,128)(2,1)} %param.10) | copy-start | bytes 393220
  3.8 7.0 %collective-permute-start = (bf16[128,2048]{1,0:T(8,128)(2,1)S(1)}, bf16[128,2048]{1,0:T(8,128)(2,1)S(1)}, u32[]{:S(2)}, u32[]{:S(2)}) collective-permute-start(bf16[128,2048]{1,0:T(8,128)(2,1)S(1)} %get-tuple-element.44), channel_id=1, source_target_pairs={{0,1},{1,0},{2,3},{3,2},{4,5},{5,4},{6,7},{7,6},{8,9},{9,8},{10,11... | collective-permute-start | bytes 1572872 | tf_op jit(solution)/shard_map/ppermute | solution.py:39
  4.4 19.1 %collective-permute-start.4 = (bf16[128,2560]{1,0:T(8,128)(2,1)S(1)}, bf16[128,2560]{1,0:T(8,128)(2,1)S(1)}, u32[]{:S(2)}, u32[]{:S(2)}) collective-permute-start(bf16[128,2560]{1,0:T(8,128)(2,1)S(1)} %get-tuple-element.42), channel_id=1, source_target_pairs={{0,8},{1,9},{2,10},{3,11},{4,12},{5,13},{6,14},{7,15},{8,0},{9,1},... | collective-permute-start | bytes 1966088 | tf_op jit(solution)/shard_map/ppermute | solution.py:39
  7.5 16.1 %collective-permute-start.8 = (bf16[512,512]{1,0:T(8,128)(2,1)S(1)}, bf16[512,512]{1,0:T(8,128)(2,1)S(1)}, u32[]{:S(2)}, u32[]{:S(2)}) collective-permute-start(bf16[512,512]{1,0:T(8,128)(2,1)S(1)} %bitcast_convert_fusion.refs_0_), channel_id=1, source_target_pairs={{0,2},{1,3},{2,4},{3,5},{4,6},{5,7},{6,0},{7,1},{8,10},{9,11},{10,... | collective-permute-start | bytes 1572872 | tf_op jit(solution)/shard_map/ppermute | solution.py:39
  9.1 16.2 %collective-permute-start.7 = (bf16[512,512]{1,0:T(8,128)(2,1)S(1)}, bf16[512,512]{1,0:T(8,128)(2,1)S(1)}, u32[]{:S(2)}, u32[]{:S(2)}) collective-permute-start(bf16[512,512]{1,0:T(8,128)(2,1)S(1)} %bitcast_convert_fusion.refs_0_), channel_id=1, source_target_pairs={{0,6},{1,7},{2,0},{3,1},{4,2},{5,3},{6,4},{7,5},{8,14},{9,15},{10,... | collective-permute-start | bytes 1572872 | tf_op jit(solution)/shard_map/ppermute | solution.py:39
  10.8 10.4 %collective-permute-start.2 = (bf16[512,128]{1,0:T(8,128)(2,1)S(1)}, bf16[512,128]{1,0:T(8,128)(2,1)S(1)}, u32[]{:S(2)}, u32[]{:S(2)}) collective-permute-start(bf16[512,128]{1,0:T(8,128)(2,1)S(1)} %convert_bitcast_fusion), channel_id=1, source_target_pairs={{0,96},{16,112},{32,64},{48,80},{64,32},{80,48},{96,0},{112,16},{1... | collective-permute-start | bytes 393224 | tf_op jit(solution)/shard_map/ppermute | solution.py:56
  15.4 18.5 %collective-permute-start.5 = (bf16[128,2048]{1,0:T(8,128)(2,1)S(1)}, bf16[128,2048]{1,0:T(8,128)(2,1)S(1)}, u32[]{:S(2)}, u32[]{:S(2)}) collective-permute-start(bf16[128,2048]{1,0:T(8,128)(2,1)S(1)} %collective-permute-done.1), channel_id=1, source_target_pairs={{0,8},{1,9},{2,10},{3,11},{4,12},{5,13},{6,14},{7,15},{8,0},{9,1},... | collective-permute-start | bytes 1572872 | tf_op jit(solution)/shard_map/ppermute | solution.py:39
  21.3 5.7 %collective-permute-start.3 = (bf16[512,128]{1,0:T(8,128)(2,1)S(1)}, bf16[512,128]{1,0:T(8,128)(2,1)S(1)}, u32[]{:S(2)}, u32[]{:S(2)}) collective-permute-start(bf16[512,128]{1,0:T(8,128)(2,1)S(1)} %add_convert_fusion), channel_id=1, source_target_pairs={{0,16},{16,0},{32,48},{48,32},{64,80},{80,64},{96,112},{112,96},{1... | collective-permute-start | bytes 393224 | tf_op jit(solution)/shard_map/ppermute | solution.py:56
  23.5 3.6 %collective-permute-start.6 = (bf16[256,512]{1,0:T(8,128)(2,1)S(1)}, bf16[256,512]{1,0:T(8,128)(2,1)S(1)}, u32[]{:S(2)}, u32[]{:S(2)}) collective-permute-start(bf16[256,512]{1,0:T(8,128)(2,1)S(1)} %pad_maximum_fusion), channel_id=1, source_target_pairs={{0,1},{1,0},{2,3},{3,2},{4,5},{5,4},{6,7},{7,6},{8,9},{9,8},{10,11... | collective-permute-start | bytes 786440 | tf_op jit(solution)/shard_map/ppermute | solution.py:39
  23.7 11.5 %collective-permute-start.10 = (bf16[256,512]{1,0:T(8,128)(2,1)S(1)}, bf16[256,512]{1,0:T(8,128)(2,1)S(1)}, u32[]{:S(2)}, u32[]{:S(2)}) collective-permute-start(bf16[256,512]{1,0:T(8,128)(2,1)S(1)} %slice.14), channel_id=1, source_target_pairs={{0,2},{1,3},{2,4},{3,5},{4,6},{5,7},{6,0},{7,1},{8,10},{9,11},{10,... | collective-permute-start | bytes 786440 | tf_op jit(solution)/shard_map/ppermute | solution.py:39
  25.3 9.9 %collective-permute-start.9 = (bf16[256,512]{1,0:T(8,128)(2,1)S(1)}, bf16[256,512]{1,0:T(8,128)(2,1)S(1)}, u32[]{:S(2)}, u32[]{:S(2)}) collective-permute-start(bf16[256,512]{1,0:T(8,128)(2,1)S(1)} %slice.13), channel_id=1, source_target_pairs={{0,6},{1,7},{2,0},{3,1},{4,2},{5,3},{6,4},{7,5},{8,14},{9,15},{10,... | collective-permute-start | bytes 786440 | tf_op jit(solution)/shard_map/ppermute | solution.py:39
  36.5 6.6 %collective-permute-start.19 = (bf16[128,2048]{1,0:T(8,128)(2,1)S(1)}, bf16[128,2048]{1,0:T(8,128)(2,1)S(1)}, u32[]{:S(2)}, u32[]{:S(2)}) collective-permute-start(bf16[128,2048]{1,0:T(8,128)(2,1)S(1)} %get-tuple-element.65), channel_id=1, source_target_pairs={{0,1},{1,0},{2,3},{3,2},{4,5},{5,4},{6,7},{7,6},{8,9},{9,8},{10,11... | collective-permute-start | bytes 1572872 | tf_op jit(solution)/shard_map/ppermute | solution.py:39
  36.6 7.8 %collective-permute-start.11 = (bf16[128,2048]{1,0:T(8,128)(2,1)S(1)}, bf16[128,2048]{1,0:T(8,128)(2,1)S(1)}, u32[]{:S(2)}, u32[]{:S(2)}) collective-permute-start(bf16[128,2048]{1,0:T(8,128)(2,1)S(1)} %get-tuple-element.52), channel_id=1, source_target_pairs={{0,1},{1,0},{2,3},{3,2},{4,5},{5,4},{6,7},{7,6},{8,9},{9,8},{10,11... | collective-permute-start | bytes 1572872 | tf_op jit(solution)/shard_map/ppermute | solution.py:39
  37.1 15.4 %collective-permute-start.15 = (bf16[128,2048]{1,0:T(8,128)(2,1)S(1)}, bf16[128,2048]{1,0:T(8,128)(2,1)S(1)}, u32[]{:S(2)}, u32[]{:S(2)}) collective-permute-start(bf16[128,2048]{1,0:T(8,128)(2,1)S(1)} %get-tuple-element.58), channel_id=1, source_target_pairs={{0,8},{1,9},{2,10},{3,11},{4,12},{5,13},{6,14},{7,15},{8,0},{9,1},... | collective-permute-start | bytes 1572872 | tf_op jit(solution)/shard_map/ppermute | solution.py:39
  40.1 15.4 %collective-permute-start.14 = (bf16[448,512]{1,0:T(8,128)(2,1)S(1)}, bf16[448,512]{1,0:T(8,128)(2,1)S(1)}, u32[]{:S(2)}, u32[]{:S(2)}) collective-permute-start(bf16[448,512]{1,0:T(8,128)(2,1)S(1)} %get-tuple-element.56), channel_id=1, source_target_pairs={{0,6},{1,7},{2,0},{3,1},{4,2},{5,3},{6,4},{7,5},{8,14},{9,15},{10,... | collective-permute-start | bytes 1376264 | tf_op jit(solution)/shard_map/ppermute | solution.py:39
  43.1 13.2 %collective-permute-start.16 = (bf16[448,512]{1,0:T(8,128)(2,1)S(1)}, bf16[448,512]{1,0:T(8,128)(2,1)S(1)}, u32[]{:S(2)}, u32[]{:S(2)}) collective-permute-start(bf16[448,512]{1,0:T(8,128)(2,1)S(1)} %get-tuple-element.61), channel_id=1, source_target_pairs={{0,2},{1,3},{2,4},{3,5},{4,6},{5,7},{6,0},{7,1},{8,10},{9,11},{10,... | collective-permute-start | bytes 1376264 | tf_op jit(solution)/shard_map/ppermute | solution.py:39
  43.2 13.3 %collective-permute-start.20 = (bf16[512,128]{1,0:T(8,128)(2,1)S(1)}, bf16[512,128]{1,0:T(8,128)(2,1)S(1)}, u32[]{:S(2)}, u32[]{:S(2)}) collective-permute-start(bf16[512,128]{1,0:T(8,128)(2,1)S(1)} %convert_add_fusion.1), channel_id=1, source_target_pairs={{0,32},{16,48},{32,0},{48,16},{64,96},{80,112},{96,64},{112,80},{1... | collective-permute-start | bytes 393224 | tf_op jit(solution)/shard_map/ppermute | solution.py:56
  44.4 15.0 %collective-permute-start.12 = (bf16[256,512]{1,0:T(8,128)(2,1)S(1)}, bf16[256,512]{1,0:T(8,128)(2,1)S(1)}, u32[]{:S(2)}, u32[]{:S(2)}) collective-permute-start(bf16[256,512]{1,0:T(8,128)(2,1)S(1)} %get-tuple-element.54), channel_id=1, source_target_pairs={{0,1},{1,0},{2,3},{3,2},{4,5},{5,4},{6,7},{7,6},{8,9},{9,8},{10,11... | collective-permute-start | bytes 786440 | tf_op jit(solution)/shard_map/ppermute | solution.py:39
  44.6 24.4 %copy-start.7 = (f32[512,128]{1,0:T(8,128)S(1)}, f32[512,128]{1,0:T(8,128)}, u32[]{:S(2)}) copy-start(f32[512,128]{1,0:T(8,128)} %param.16) | copy-start | bytes 786436
  44.6 24.4 %copy-start.8 = (f32[512,128]{1,0:T(8,128)S(1)}, f32[512,128]{1,0:T(8,128)}, u32[]{:S(2)}) copy-start(f32[512,128]{1,0:T(8,128)} %param.15) | copy-start | bytes 786436
  52.5 17.3 %collective-permute-start.22 = (bf16[96,2048]{1,0:T(8,128)(2,1)S(1)}, bf16[96,2048]{1,0:T(8,128)(2,1)S(1)}, u32[]{:S(2)}, u32[]{:S(2)}) collective-permute-start(bf16[96,2048]{1,0:T(8,128)(2,1)S(1)} %split.1), channel_id=1, source_target_pairs={{0,8},{1,9},{2,10},{3,11},{4,12},{5,13},{6,14},{7,15},{8,0},{9,1},... | collective-permute-start | bytes 1179656 | tf_op jit(solution)/shard_map/ppermute | solution.py:39
  56.5 12.5 %collective-permute-start.21 = (bf16[512,128]{1,0:T(8,128)(2,1)S(1)}, bf16[512,128]{1,0:T(8,128)(2,1)S(1)}, u32[]{:S(2)}, u32[]{:S(2)}) collective-permute-start(bf16[512,128]{1,0:T(8,128)(2,1)S(1)} %convert_add_fusion), channel_id=1, source_target_pairs={{0,128},{16,144},{32,160},{48,176},{64,192},{80,208},{96,224},{112... | collective-permute-start | bytes 393224 | tf_op jit(solution)/shard_map/ppermute | solution.py:56
  57.2 14.1 %collective-permute-start.18 = (bf16[320,512]{1,0:T(8,128)(2,1)S(1)}, bf16[320,512]{1,0:T(8,128)(2,1)S(1)}, u32[]{:S(2)}, u32[]{:S(2)}) collective-permute-start(bf16[320,512]{1,0:T(8,128)(2,1)S(1)} %get-tuple-element.63), channel_id=1, source_target_pairs={{0,6},{1,7},{2,0},{3,1},{4,2},{5,3},{6,4},{7,5},{8,14},{9,15},{10,... | collective-permute-start | bytes 983048 | tf_op jit(solution)/shard_map/ppermute | solution.py:39
  59.4 11.8 %collective-permute-start.17 = (bf16[320,512]{1,0:T(8,128)(2,1)S(1)}, bf16[320,512]{1,0:T(8,128)(2,1)S(1)}, u32[]{:S(2)}, u32[]{:S(2)}) collective-permute-start(bf16[320,512]{1,0:T(8,128)(2,1)S(1)} %get-tuple-element.62), channel_id=1, source_target_pairs={{0,2},{1,3},{2,4},{3,5},{4,6},{5,7},{6,0},{7,1},{8,10},{9,11},{10,... | collective-permute-start | bytes 983048 | tf_op jit(solution)/shard_map/ppermute | solution.py:39
  59.5 14.7 %collective-permute-start.13 = (bf16[64,2048]{1,0:T(8,128)(2,1)S(1)}, bf16[64,2048]{1,0:T(8,128)(2,1)S(1)}, u32[]{:S(2)}, u32[]{:S(2)}) collective-permute-start(bf16[64,2048]{1,0:T(8,128)(2,1)S(1)} %pack.1), channel_id=1, source_target_pairs={{0,8},{1,9},{2,10},{3,11},{4,12},{5,13},{6,14},{7,15},{8,0},{9,1},... | collective-permute-start | bytes 786440 | tf_op jit(solution)/shard_map/ppermute | solution.py:39
  69.8 4.4 %copy-start.4 = (f32[512,128]{1,0:T(8,128)}, f32[512,128]{1,0:T(8,128)S(1)}, u32[]{:S(2)}) copy-start(f32[512,128]{1,0:T(8,128)S(1)} %get-tuple-element.69.glob) | copy-start | bytes 786436
  69.8 2.0 %copy-start.5 = (f32[1,512,512]{2,1,0:T(8,128)S(1)}, f32[1,512,512]{2,1,0:T(8,128)}, u32[]{:S(2)}) copy-start(f32[1,512,512]{2,1,0:T(8,128)} %param.12) | copy-start | bytes 3145732
  69.8 2.3 %copy-start.6 = (f32[1,512,512]{2,1,0:T(8,128)S(1)}, f32[1,512,512]{2,1,0:T(8,128)}, u32[]{:S(2)}) copy-start(f32[1,512,512]{2,1,0:T(8,128)} %param.13) | copy-start | bytes 3145732
  (1 other events, 0.9 us)

commit v8 on v6

--- a/solution.py
+++ b/solution.py
@@ -210,17 +210,42 @@
     )(passed, val_back, val_x)
 
 
-def weight_grad(toks, ups):
-    def kernel(t0, t1, t2, t3, u0, u1, u2, own, to_above, to_below, keep_above, keep_below):
-        up = jnp.concatenate([u0[...], u1[...], u2[...]], axis=0)
+def token_sum(toks, ups):
+    return lax.dot_general(
+        jnp.concatenate(toks, axis=0),
+        jnp.concatenate(ups, axis=0),
+        (((0,), (0,)), ((), ())),
+        preferred_element_type=jnp.float32,
+    )
+
+
+def weight_grad_before(toks, ups):
+    def kernel(t0, t1, t2, u0, u1, u2, out):
+        y = here()[1]
+        for step in range(NY):
+            at = pl.ds(pl.multiple_of(lax.rem(y + step, NY) * ROWS, ROWS), ROWS)
+            out[step] = SCALE * token_sum(
+                [t0[:, at], t1[:, at], t2[:, at]], [u0[...], u1[...], u2[:TOK]]
+            )
+
+    return pl.pallas_call(
+        kernel,
+        in_specs=[pl.BlockSpec(memory_space=pltpu.VMEM)] * 6,
+        out_specs=pl.BlockSpec(memory_space=pltpu.VMEM),
+        out_shape=jax.ShapeDtypeStruct((NY, ROWS, F), jnp.float32),
+        cost_estimate=SMALL,
+        compiler_params=VMEM,
+        name="weight_grad_before",
+    )(*toks, *ups)
+
+
+def weight_grad(tok_far, up_pair, before):
+    def kernel(t3, u2, before, own, to_above, to_below, keep_above, keep_below):
         y = here()[1]
 
         def block(step):
             at = pl.ds(pl.multiple_of(lax.rem(y + step, NY) * ROWS, ROWS), ROWS)
-            tok = jnp.concatenate([t0[:, at], t1[:, at], t2[:, at], t3[:, at]], axis=0)
-            return SCALE * lax.dot_general(
-                tok, up, (((0,), (0,)), ((), ())), preferred_element_type=jnp.float32
-            )
+            return before[step] + SCALE * token_sum([t3[:, at]], [u2[TOK:]])
 
         grad = block(2)
         to_above[:HALF] = grad[:HALF].astype(jnp.bfloat16)
@@ -235,7 +260,7 @@
 
     return pl.pallas_call(
         kernel,
-        in_specs=[pl.BlockSpec(memory_space=pltpu.VMEM)] * 7,
+        in_specs=[pl.BlockSpec(memory_space=pltpu.VMEM)] * 3,
         out_specs=[pl.BlockSpec(memory_space=pltpu.VMEM)] * 5,
         out_shape=[shape(ROWS, F, jnp.float32)]
         + [shape(HALF + ROWS - LATER, F)] * 2
@@ -243,7 +268,7 @@
         cost_estimate=SMALL,
         compiler_params=VMEM,
         name="weight_grad",
-    )(*toks, *ups)
+    )(tok_far, up_pair, before)
 
 
 def relay(keep_above, keep_below, from_below, from_above):
@@ -403,7 +428,8 @@
     total = replica_step(total, lambda i: i ^ 1)
     up_ready, total = lax.optimization_barrier((up_own, total))
     toks = (tok_own, tok_x, tok_core, tok_far)
-    g0, to_above, to_below, keep_above, keep_below = weight_grad(toks, (up_ready, up_x, up_pair))
+    before = weight_grad_before((tok_own, tok_x, tok_core), (up_ready, up_x, up_pair))
+    g0, to_above, to_below, keep_above, keep_below = weight_grad(tok_far, up_pair, before)
     from_below, from_above = shift_y(to_above, 1), shift_y(to_below, -1)
 
     ig_own, ig_x, ig_core, ig_far = input_grad((after(up_ready, g0), up_x, up_pair), blocks)

time: 72.2 us -> 73 us (1.011)
  local copies, waits for them, and re-layouts: 2.57 us -> 3.48 us
  Pallas kernels: 8.74 us -> 9.48 us
    pallas_call x0 -> x1, Pallas kernels: none -> 1.3 us  [weight_grad_before(): pl.pallas_call(kernel, in_specs=[pl.BlockSpec(memory_space=pltpu.VMEM)] *...]
    unnamed x20, local copies, waits for them, and re-layouts: 2.53 us -> 3.43 us
where the time goes in v8:
time: 73 us; the launch traced here: 72.8 us
  starting transfers between devices  28.9 us (40%)
  waiting for transfers between devices  28.2 us (39%)
  Pallas kernels  9.48 us (13%)
  local copies, waits for them, and re-layouts  3.48 us (5%)
  between operations  1.79 us (2%)
  other arithmetic  1.01 us (1%)
    ppermute x19, starting transfers between devices, fsdp_permute(): return lax.ppermute(value, 'fsdp', pairs)  23.3 us
    ppermute x19, waiting for transfers between devices, fsdp_permute(): return lax.ppermute(value, 'fsdp', pairs)  22.7 us
    ppermute x4, starting transfers between devices, replica_step(): other = lax.ppermute(sent, 'replica', [(i, partner(i)) for i in range(16)])  5.61 us
    ppermute x4, waiting for transfers between devices, replica_step(): other = lax.ppermute(sent, 'replica', [(i, partner(i)) for i in range(16)])  5.52 us
    unnamed x20, local copies, waits for them, and re-layouts  3.43 us
    pallas_call x2, Pallas kernels, assemble(): pl.pallas_call(kernel, in_specs=ins, out_specs=outs if vals else outs[0],...  2.16 us
    pallas_call x1, Pallas kernels, adam(): pl.pallas_call(kernel, in_specs=[pl.BlockSpec(memory_space=pltpu.SMEM)] +...  2.02 us
  transfers between devices with their start and end apart: 23, of which 7 were waited for; matrix products, arithmetic and copies ran while one was open for 1% of the time, Pallas kernels for 9%

profile of v8, /device:TPU:64, one launch (start us, length us, event | category | flops | bytes accessed | tf_op | source)
XLA Modules:
  0.0 72.8 jit_solution(13906342509507917628)
XLA Ops:
  0.6 1.6 %copy-done = bf16[1,128,8192]{2,1,0:T(8,128)(2,1)S(1)} copy-done((bf16[1,128,8192]{2,1,0:T(8,128)(2,1)S(1)}, bf16[1,128,8192]{2,1,0:T(8,128)(2,1)}, u32[]{:S(2)}) %copy-start) | copy-done | bytes 2097176
  2.2 0.9 %copy-done.2 = bf16[1,128,512]{2,1,0:T(8,128)(2,1)S(1)} copy-done((bf16[1,128,512]{2,1,0:T(8,128)(2,1)S(1)}, bf16[1,128,512]{2,1,0:T(8,128)(2,1)}, u32[]{:S(2)}) %copy-start.2) | copy-done | bytes 131096
  3.8 0.5 collective-permute-start.1
  4.3 3.0 %collective-permute-start.5 = (bf16[128,2560]{1,0:T(8,128)(2,1)S(1)}, bf16[128,2560]{1,0:T(8,128)(2,1)S(1)}, u32[]{:S(2)}, u32[]{:S(2)}) collective-permute-start(bf16[128,2560]{1,0:T(8,128)(2,1)S(1)} %get-tuple-element.43), channel_id=1, source_target_pairs={{0,8},{1,9},{2,10},{3,11},{4,12},{5,13},{6,14},{7,15},{8,0},{9,1},... | collective-permute-start | bytes 1966088 | tf_op jit(solution)/shard_map/ppermute | solution.py:39
  7.4 3.1 %collective-permute-start.7 = (bf16[512,512]{1,0:T(8,128)(2,1)S(1)}, bf16[512,512]{1,0:T(8,128)(2,1)S(1)}, u32[]{:S(2)}, u32[]{:S(2)}) collective-permute-start(bf16[512,512]{1,0:T(8,128)(2,1)S(1)} %bitcast_convert_fusion.refs_0_), channel_id=1, source_target_pairs={{0,6},{1,7},{2,0},{3,1},{4,2},{5,3},{6,4},{7,5},{8,14},{9,15},{10,... | collective-permute-start | bytes 1572872 | tf_op jit(solution)/shard_map/ppermute | solution.py:39
  10.6 4.6 %collective-permute-start.2 = (bf16[512,128]{1,0:T(8,128)(2,1)S(1)}, bf16[512,128]{1,0:T(8,128)(2,1)S(1)}, u32[]{:S(2)}, u32[]{:S(2)}) collective-permute-start(bf16[512,128]{1,0:T(8,128)(2,1)S(1)} %convert_bitcast_fusion), channel_id=1, source_target_pairs={{0,96},{16,112},{32,64},{48,80},{64,32},{80,48},{96,0},{112,16},{1... | collective-permute-start | bytes 393224 | tf_op jit(solution)/shard_map/ppermute | solution.py:56
  15.1 0.5 collective-permute-start.4
  15.6 5.5 %collective-permute-done.2 = bf16[512,128]{1,0:T(8,128)(2,1)S(1)} collective-permute-done((bf16[512,128]{1,0:T(8,128)(2,1)S(1)}, bf16[512,128]{1,0:T(8,128)(2,1)S(1)}, u32[]{:S(2)}, u32[]{:S(2)}) %collective-permute-start.2) | collective-permute-done | bytes 131104 | tf_op jit(solution)/shard_map/ppermute | solution.py:56
  21.6 1.9 %collective-permute-done.5.t1 = bf16[128,2560]{1,0:T(8,128)(2,1)S(1)} collective-permute-done((bf16[128,2560]{1,0:T(8,128)(2,1)S(1)}, bf16[128,2560]{1,0:T(8,128)(2,1)S(1)}, u32[]{:S(2)}, u32[]{:S(2)}) %collective-permute-start.5) | collective-permute-done | bytes 655392 | tf_op jit(solution)/shard_map/ppermute | solution.py:39
  23.6 3.1 %collective-permute-start.9 = (bf16[256,512]{1,0:T(8,128)(2,1)S(1)}, bf16[256,512]{1,0:T(8,128)(2,1)S(1)}, u32[]{:S(2)}, u32[]{:S(2)}) collective-permute-start(bf16[256,512]{1,0:T(8,128)(2,1)S(1)} %slice.13), channel_id=1, source_target_pairs={{0,6},{1,7},{2,0},{3,1},{4,2},{5,3},{6,4},{7,5},{8,14},{9,15},{10,... | collective-permute-start | bytes 786440 | tf_op jit(solution)/shard_map/ppermute | solution.py:39
  26.9 1.3 %weight_grad_before.1.before = f32[4,512,512]{2,1,0:T(8,128)S(1)} custom-call(bf16[128,2048]{1,0:T(8,128)(2,1)S(1)} %get-tuple-element.49.t0, bf16[128,2560]{1,0:T(8,128)(2,1)S(1)} %collective-permute-done.5.t1, bf16[128,2048]{1,0:T(8,128)(2,1)S(1)} %collective-permute-done.t2, bf16[128,512]{1,0:T(8,128)(2,1)S(1)} %bitcast.19, ...), custom_call_target="tpu_custom_call" | custom-call | flops 1 | bytes 1 | tf_op jit(solution)/shard_map/weight_grad_before/pallas_call | solution.py:231
  28.2 5.6 %collective-permute-done.4.t3 = bf16[128,2048]{1,0:T(8,128)(2,1)S(1)} collective-permute-done((bf16[128,2048]{1,0:T(8,128)(2,1)S(1)}, bf16[128,2048]{1,0:T(8,128)(2,1)S(1)}, u32[]{:S(2)}, u32[]{:S(2)}) %collective-permute-start.4) | collective-permute-done | bytes 524320 | tf_op jit(solution)/shard_map/ppermute | solution.py:39
  33.8 0.7 %weight_grad.1 = (f32[512,512]{1,0:T(8,128)S(1)}, bf16[448,512]{1,0:T(8,128)(2,1)S(1)}, bf16[448,512]{1,0:T(8,128)(2,1)S(1)}, f32[320,512]{1,0:T(8,128)S(1)}, f32[320,512]{1,0:T(8,128)S(1)}) custom-call(bf16[128,2048]{1,0:T(8,128)(2,1)S(1)} %collective-permute-done.4.t3, bf16[256,512]{1,0:T(8,128)(2,1)S(1)} %collective-permute-done.6.u2, ...), custom_call_target="tpu_custom_call" | custom-call | flops 1 | bytes 1 | tf_op jit(solution)/shard_map/weight_grad/pallas_call | solution.py:261
  34.6 1.8 %collective-permute-done.10.refs_4_ = bf16[256,512]{1,0:T(8,128)(2,1)S(1)} collective-permute-done((bf16[256,512]{1,0:T(8,128)(2,1)S(1)}, bf16[256,512]{1,0:T(8,128)(2,1)S(1)}, u32[]{:S(2)}, u32[]{:S(2)}) %collective-permute-start.10) | collective-permute-done | bytes 262176 | tf_op jit(solution)/shard_map/ppermute | solution.py:39
  36.4 1.3 %input_grad.1 = (bf16[128,2048]{1,0:T(8,128)(2,1)S(1)}, bf16[128,2048]{1,0:T(8,128)(2,1)S(1)}, bf16[128,2048]{1,0:T(8,128)(2,1)S(1)}, bf16[128,2048]{1,0:T(8,128)(2,1)S(1)}) custom-call(bf16[128,512]{1,0:T(8,128)(2,1)S(1)} %bitcast.20, bf16[128,512]{1,0:T(8,128)(2,1)S(1)} %slice.12.u1, bf16[256,512]{1,0:T(8,128)(2,1)S(1)} %collective-permute-done.6.u2, ...), custom_call_target="tpu_custom_call" | custom-call | flops 1 | bytes 1 | tf_op jit(solution)/shard_map/input_grad/pallas_call | solution.py:144
  37.8 0.5 collective-permute-start.11
  38.3 3.0 %collective-permute-start.16 = (bf16[128,2048]{1,0:T(8,128)(2,1)S(1)}, bf16[128,2048]{1,0:T(8,128)(2,1)S(1)}, u32[]{:S(2)}, u32[]{:S(2)}) collective-permute-start(bf16[128,2048]{1,0:T(8,128)(2,1)S(1)} %get-tuple-element.60), channel_id=1, source_target_pairs={{0,8},{1,9},{2,10},{3,11},{4,12},{5,13},{6,14},{7,15},{8,0},{9,1},... | collective-permute-start | bytes 1572872 | tf_op jit(solution)/shard_map/ppermute | solution.py:39
  41.3 1.2 %collective-permute-start.15 = (bf16[448,512]{1,0:T(8,128)(2,1)S(1)}, bf16[448,512]{1,0:T(8,128)(2,1)S(1)}, u32[]{:S(2)}, u32[]{:S(2)}) collective-permute-start(bf16[448,512]{1,0:T(8,128)(2,1)S(1)} %get-tuple-element.58), channel_id=1, source_target_pairs={{0,6},{1,7},{2,0},{3,1},{4,2},{5,3},{6,4},{7,5},{8,14},{9,15},{10,... | collective-permute-start | bytes 1376264 | tf_op jit(solution)/shard_map/ppermute | solution.py:39
  42.5 0.8 %collective-permute-start.17 = (bf16[448,512]{1,0:T(8,128)(2,1)S(1)}, bf16[448,512]{1,0:T(8,128)(2,1)S(1)}, u32[]{:S(2)}, u32[]{:S(2)}) collective-permute-start(bf16[448,512]{1,0:T(8,128)(2,1)S(1)} %get-tuple-element.63), channel_id=1, source_target_pairs={{0,2},{1,3},{2,4},{3,5},{4,6},{5,7},{6,0},{7,1},{8,10},{9,11},{10,... | collective-permute-start | bytes 1376264 | tf_op jit(solution)/shard_map/ppermute | solution.py:39
  43.4 0.9 %collective-permute-start.13 = (bf16[96,2048]{1,0:T(8,128)(2,1)S(1)}, bf16[96,2048]{1,0:T(8,128)(2,1)S(1)}, u32[]{:S(2)}, u32[]{:S(2)}) collective-permute-start(bf16[96,2048]{1,0:T(8,128)(2,1)S(1)} %split.1), channel_id=1, source_target_pairs={{0,8},{1,9},{2,10},{3,11},{4,12},{5,13},{6,14},{7,15},{8,0},{9,1},... | collective-permute-start | bytes 1179656 | tf_op jit(solution)/shard_map/ppermute | solution.py:39
  44.3 1.2 %values.1 = (f32[128,512]{1,0:T(8,128)S(1)}, f32[128,512]{1,0:T(8,128)S(1)}, bf16[256,512]{1,0:T(8,128)(2,1)S(1)}) custom-call(bf16[128,2048]{1,0:T(8,128)(2,1)S(1)} %get-tuple-element.49.t0, bf16[128,2560]{1,0:T(8,128)(2,1)S(1)} %collective-permute-done.5.t1, bf16[128,2048]{1,0:T(8,128)(2,1)S(1)} %collective-permute-done.t2, ...), custom_call_target="tpu_custom_call" | custom-call | flops 1 | bytes 1 | tf_op jit(solution)/shard_map/values/pallas_call | solution.py:166
  45.6 9.0 %collective-permute-done.16.refs_2_ = bf16[128,2048]{1,0:T(8,128)(2,1)S(1)} collective-permute-done((bf16[128,2048]{1,0:T(8,128)(2,1)S(1)}, bf16[128,2048]{1,0:T(8,128)(2,1)S(1)}, u32[]{:S(2)}, u32[]{:S(2)}) %collective-permute-start.16) | collective-permute-done | bytes 524320 | tf_op jit(solution)/shard_map/ppermute | solution.py:39
  54.6 1.1 %collective-permute-done.17.from_below = bf16[448,512]{1,0:T(8,128)(2,1)S(1)} collective-permute-done((bf16[448,512]{1,0:T(8,128)(2,1)S(1)}, bf16[448,512]{1,0:T(8,128)(2,1)S(1)}, u32[]{:S(2)}, u32[]{:S(2)}) %collective-permute-start.17) | collective-permute-done | bytes 458784 | tf_op jit(solution)/shard_map/ppermute | solution.py:39
  55.9 0.7 collective-permute-start.22
  56.5 3.2 %collective-permute-start.19 = (bf16[320,512]{1,0:T(8,128)(2,1)S(1)}, bf16[320,512]{1,0:T(8,128)(2,1)S(1)}, u32[]{:S(2)}, u32[]{:S(2)}) collective-permute-start(bf16[320,512]{1,0:T(8,128)(2,1)S(1)} %get-tuple-element.65), channel_id=1, source_target_pairs={{0,6},{1,7},{2,0},{3,1},{4,2},{5,3},{6,4},{7,5},{8,14},{9,15},{10,... | collective-permute-start | bytes 983048 | tf_op jit(solution)/shard_map/ppermute | solution.py:39
  59.8 3.2 %collective-permute-done.13.refs_3_ = bf16[96,2048]{1,0:T(8,128)(2,1)S(1)} collective-permute-done((bf16[96,2048]{1,0:T(8,128)(2,1)S(1)}, bf16[96,2048]{1,0:T(8,128)(2,1)S(1)}, u32[]{:S(2)}, u32[]{:S(2)}) %collective-permute-start.13) | collective-permute-done | bytes 393248 | tf_op jit(solution)/shard_map/ppermute | solution.py:39
  63.0 3.0 %collective-permute-start.14 = (bf16[64,2048]{1,0:T(8,128)(2,1)S(1)}, bf16[64,2048]{1,0:T(8,128)(2,1)S(1)}, u32[]{:S(2)}, u32[]{:S(2)}) collective-permute-start(bf16[64,2048]{1,0:T(8,128)(2,1)S(1)} %pack.1), channel_id=1, source_target_pairs={{0,8},{1,9},{2,10},{3,11},{4,12},{5,13},{6,14},{7,15},{8,0},{9,1},... | collective-permute-start | bytes 786440 | tf_op jit(solution)/shard_map/ppermute | solution.py:39
  66.7 0.8 %multiply_subtract_fusion = (f32[512,128]{1,0:T(8,128)S(1)}, f32[512,128]{1,0:T(8,128)}) fusion(f32[512,128]{1,0:T(8,128)S(1)} %copy-done.7, bf16[512,128]{1,0:T(8,128)(2,1)S(1)} %collective-permute-done.22, bf16[512,128]{1,0:T(8,128)(2,1)S(1)} %convert_add_fusion, f32[512,128]{1,0:T(8,128)S(1)} %copy-done.8), kind=kLoop, calls=%fused_computation.1 | loop fusion | flops 655360 | bytes 1310720 | tf_op jit(solution)/shard_map/sub | solution.py:66
  67.5 1.4 %assemble.2.refs_3_ = bf16[128,8192]{1,0:T(8,128)(2,1)} custom-call(bf16[128,2048]{1,0:T(8,128)(2,1)S(1)} %get-tuple-element.70.refs_0_, bf16[128,2048]{1,0:T(8,128)(2,1)S(1)} %collective-permute-done.20.refs_1_, bf16[128,2048]{1,0:T(8,128)(2,1)S(1)} %collective-permute-done.16.refs_2_, bf16[96,2048]{1,0:T(8,128)(2,1)S(1)} %collective-permute-done.13.refs_3_), custom_call_target="tpu_custom_call" | custom-call | flops 1 | bytes 1 | tf_op jit(solution)/shard_map/assemble/pallas_call | solution.py:337
  68.9 0.6 copy-done.5
  69.8 2.0 %adam.1 = (f32[512,512]{1,0:T(8,128)}, f32[512,512]{1,0:T(8,128)}, f32[512,512]{1,0:T(8,128)}) custom-call(s32[1]{0:T(128)S(6)} %copy.18.frag, f32[512,512]{1,0:T(8,128)S(1)} %get-tuple-element.50.g0, bf16[448,512]{1,0:T(8,128)(2,1)S(1)} %collective-permute-done.15.from_above, bf16[320,512]{1,0:T(8,128)(2,1)S(1)} %collective-permute-done.18.r1, ...), custom_call_target="tpu_custom_call" | custom-call | flops 1 | bytes 1 | tf_op jit(solution)/shard_map/adam/pallas_call | solution.py:389
  71.9 0.8 %assemble.3 = (bf16[128,8192]{1,0:T(8,128)(2,1)}, bf16[128,512]{1,0:T(8,128)(2,1)}) custom-call(bf16[64,2048]{1,0:T(8,128)(2,1)S(1)} %collective-permute-done.14.refs_0_, f32[128,512]{1,0:T(8,128)S(1)} %get-tuple-element.74.refs_1_, bf16[256,512]{1,0:T(8,128)(2,1)S(1)} %collective-permute-done.12.val_back.refs_2_, ...), custom_call_target="tpu_custom_call", output_to_operand_aliasing={{0}: (3, {})} | custom-call | flops 1 | bytes 1 | tf_op jit(solution)/shard_map/assemble/pallas_call | solution.py:337
  (56 shorter events, 2.2 us)
Async XLA Ops:
  0.6 1.6 %copy-start = (bf16[1,128,8192]{2,1,0:T(8,128)(2,1)S(1)}, bf16[1,128,8192]{2,1,0:T(8,128)(2,1)}, u32[]{:S(2)}) copy-start(bf16[1,128,8192]{2,1,0:T(8,128)(2,1)} %param.9) | copy-start | bytes 6291460
  3.1 4.2 %copy-start.1 = (f32[1,512,512]{2,1,0:T(8,128)S(1)}, f32[1,512,512]{2,1,0:T(8,128)}, u32[]{:S(2)}) copy-start(f32[1,512,512]{2,1,0:T(8,128)} %param.11) | copy-start | bytes 3145732
  3.4 7.1 %copy-start.9 = (f32[1,512,128]{2,1,0:T(8,128)S(1)}, f32[1,512,128]{2,1,0:T(8,128)}, u32[]{:S(2)}) copy-start(f32[1,512,128]{2,1,0:T(8,128)} %param.14) | copy-start | bytes 786436
  3.7 6.8 %collective-permute-start = (bf16[128,2048]{1,0:T(8,128)(2,1)S(1)}, bf16[128,2048]{1,0:T(8,128)(2,1)S(1)}, u32[]{:S(2)}, u32[]{:S(2)}) collective-permute-start(bf16[128,2048]{1,0:T(8,128)(2,1)S(1)} %get-tuple-element.45), channel_id=1, source_target_pairs={{0,1},{1,0},{2,3},{3,2},{4,5},{5,4},{6,7},{7,6},{8,9},{9,8},{10,11... | collective-permute-start | bytes 1572872 | tf_op jit(solution)/shard_map/ppermute | solution.py:39
  3.8 23.0 %copy-start.3 = (bf16[1,128,512]{2,1,0:T(8,128)(2,1)S(1)}, bf16[1,128,512]{2,1,0:T(8,128)(2,1)}, u32[]{:S(2)}) copy-start(bf16[1,128,512]{2,1,0:T(8,128)(2,1)} %param.10) | copy-start | bytes 393220
  3.8 6.7 %collective-permute-start.1 = (bf16[128,2048]{1,0:T(8,128)(2,1)S(1)}, bf16[128,2048]{1,0:T(8,128)(2,1)S(1)}, u32[]{:S(2)}, u32[]{:S(2)}) collective-permute-start(bf16[128,2048]{1,0:T(8,128)(2,1)S(1)} %get-tuple-element.46), channel_id=1, source_target_pairs={{0,1},{1,0},{2,3},{3,2},{4,5},{5,4},{6,7},{7,6},{8,9},{9,8},{10,11... | collective-permute-start | bytes 1572872 | tf_op jit(solution)/shard_map/ppermute | solution.py:39
  4.3 19.1 %collective-permute-start.5 = (bf16[128,2560]{1,0:T(8,128)(2,1)S(1)}, bf16[128,2560]{1,0:T(8,128)(2,1)S(1)}, u32[]{:S(2)}, u32[]{:S(2)}) collective-permute-start(bf16[128,2560]{1,0:T(8,128)(2,1)S(1)} %get-tuple-element.43), channel_id=1, source_target_pairs={{0,8},{1,9},{2,10},{3,11},{4,12},{5,13},{6,14},{7,15},{8,0},{9,1},... | collective-permute-start | bytes 1966088 | tf_op jit(solution)/shard_map/ppermute | solution.py:39
  7.4 16.1 %collective-permute-start.7 = (bf16[512,512]{1,0:T(8,128)(2,1)S(1)}, bf16[512,512]{1,0:T(8,128)(2,1)S(1)}, u32[]{:S(2)}, u32[]{:S(2)}) collective-permute-start(bf16[512,512]{1,0:T(8,128)(2,1)S(1)} %bitcast_convert_fusion.refs_0_), channel_id=1, source_target_pairs={{0,6},{1,7},{2,0},{3,1},{4,2},{5,3},{6,4},{7,5},{8,14},{9,15},{10,... | collective-permute-start | bytes 1572872 | tf_op jit(solution)/shard_map/ppermute | solution.py:39
  10.5 16.2 %collective-permute-start.8 = (bf16[512,512]{1,0:T(8,128)(2,1)S(1)}, bf16[512,512]{1,0:T(8,128)(2,1)S(1)}, u32[]{:S(2)}, u32[]{:S(2)}) collective-permute-start(bf16[512,512]{1,0:T(8,128)(2,1)S(1)} %bitcast_convert_fusion.refs_0_), channel_id=1, source_target_pairs={{0,2},{1,3},{2,4},{3,5},{4,6},{5,7},{6,0},{7,1},{8,10},{9,11},{10,... | collective-permute-start | bytes 1572872 | tf_op jit(solution)/shard_map/ppermute | solution.py:39
  10.6 10.6 %collective-permute-start.2 = (bf16[512,128]{1,0:T(8,128)(2,1)S(1)}, bf16[512,128]{1,0:T(8,128)(2,1)S(1)}, u32[]{:S(2)}, u32[]{:S(2)}) collective-permute-start(bf16[512,128]{1,0:T(8,128)(2,1)S(1)} %convert_bitcast_fusion), channel_id=1, source_target_pairs={{0,96},{16,112},{32,64},{48,80},{64,32},{80,48},{96,0},{112,16},{1... | collective-permute-start | bytes 393224 | tf_op jit(solution)/shard_map/ppermute | solution.py:56
  15.1 18.7 %collective-permute-start.4 = (bf16[128,2048]{1,0:T(8,128)(2,1)S(1)}, bf16[128,2048]{1,0:T(8,128)(2,1)S(1)}, u32[]{:S(2)}, u32[]{:S(2)}) collective-permute-start(bf16[128,2048]{1,0:T(8,128)(2,1)S(1)} %collective-permute-done.1), channel_id=1, source_target_pairs={{0,8},{1,9},{2,10},{3,11},{4,12},{5,13},{6,14},{7,15},{8,0},{9,1},... | collective-permute-start | bytes 1572872 | tf_op jit(solution)/shard_map/ppermute | solution.py:39
  21.2 5.6 %collective-permute-start.3 = (bf16[512,128]{1,0:T(8,128)(2,1)S(1)}, bf16[512,128]{1,0:T(8,128)(2,1)S(1)}, u32[]{:S(2)}, u32[]{:S(2)}) collective-permute-start(bf16[512,128]{1,0:T(8,128)(2,1)S(1)} %add_convert_fusion), channel_id=1, source_target_pairs={{0,16},{16,0},{32,48},{48,32},{64,80},{80,64},{96,112},{112,96},{1... | collective-permute-start | bytes 393224 | tf_op jit(solution)/shard_map/ppermute | solution.py:56
  23.5 3.4 %collective-permute-start.6 = (bf16[256,512]{1,0:T(8,128)(2,1)S(1)}, bf16[256,512]{1,0:T(8,128)(2,1)S(1)}, u32[]{:S(2)}, u32[]{:S(2)}) collective-permute-start(bf16[256,512]{1,0:T(8,128)(2,1)S(1)} %pad_maximum_fusion), channel_id=1, source_target_pairs={{0,1},{1,0},{2,3},{3,2},{4,5},{5,4},{6,7},{7,6},{8,9},{9,8},{10,11... | collective-permute-start | bytes 786440 | tf_op jit(solution)/shard_map/ppermute | solution.py:39
  23.6 11.0 %collective-permute-start.9 = (bf16[256,512]{1,0:T(8,128)(2,1)S(1)}, bf16[256,512]{1,0:T(8,128)(2,1)S(1)}, u32[]{:S(2)}, u32[]{:S(2)}) collective-permute-start(bf16[256,512]{1,0:T(8,128)(2,1)S(1)} %slice.13), channel_id=1, source_target_pairs={{0,6},{1,7},{2,0},{3,1},{4,2},{5,3},{6,4},{7,5},{8,14},{9,15},{10,... | collective-permute-start | bytes 786440 | tf_op jit(solution)/shard_map/ppermute | solution.py:39
  26.7 9.7 %collective-permute-start.10 = (bf16[256,512]{1,0:T(8,128)(2,1)S(1)}, bf16[256,512]{1,0:T(8,128)(2,1)S(1)}, u32[]{:S(2)}, u32[]{:S(2)}) collective-permute-start(bf16[256,512]{1,0:T(8,128)(2,1)S(1)} %slice.14), channel_id=1, source_target_pairs={{0,2},{1,3},{2,4},{3,5},{4,6},{5,7},{6,0},{7,1},{8,10},{9,11},{10,... | collective-permute-start | bytes 786440 | tf_op jit(solution)/shard_map/ppermute | solution.py:39
  37.7 5.7 %collective-permute-start.20 = (bf16[128,2048]{1,0:T(8,128)(2,1)S(1)}, bf16[128,2048]{1,0:T(8,128)(2,1)S(1)}, u32[]{:S(2)}, u32[]{:S(2)}) collective-permute-start(bf16[128,2048]{1,0:T(8,128)(2,1)S(1)} %get-tuple-element.67), channel_id=1, source_target_pairs={{0,1},{1,0},{2,3},{3,2},{4,5},{5,4},{6,7},{7,6},{8,9},{9,8},{10,11... | collective-permute-start | bytes 1572872 | tf_op jit(solution)/shard_map/ppermute | solution.py:39
  37.8 5.6 %collective-permute-start.11 = (bf16[128,2048]{1,0:T(8,128)(2,1)S(1)}, bf16[128,2048]{1,0:T(8,128)(2,1)S(1)}, u32[]{:S(2)}, u32[]{:S(2)}) collective-permute-start(bf16[128,2048]{1,0:T(8,128)(2,1)S(1)} %get-tuple-element.53), channel_id=1, source_target_pairs={{0,1},{1,0},{2,3},{3,2},{4,5},{5,4},{6,7},{7,6},{8,9},{9,8},{10,11... | collective-permute-start | bytes 1572872 | tf_op jit(solution)/shard_map/ppermute | solution.py:39
  38.3 16.3 %collective-permute-start.16 = (bf16[128,2048]{1,0:T(8,128)(2,1)S(1)}, bf16[128,2048]{1,0:T(8,128)(2,1)S(1)}, u32[]{:S(2)}, u32[]{:S(2)}) collective-permute-start(bf16[128,2048]{1,0:T(8,128)(2,1)S(1)} %get-tuple-element.60), channel_id=1, source_target_pairs={{0,8},{1,9},{2,10},{3,11},{4,12},{5,13},{6,14},{7,15},{8,0},{9,1},... | collective-permute-start | bytes 1572872 | tf_op jit(solution)/shard_map/ppermute | solution.py:39
  41.3 13.3 %collective-permute-start.15 = (bf16[448,512]{1,0:T(8,128)(2,1)S(1)}, bf16[448,512]{1,0:T(8,128)(2,1)S(1)}, u32[]{:S(2)}, u32[]{:S(2)}) collective-permute-start(bf16[448,512]{1,0:T(8,128)(2,1)S(1)} %get-tuple-element.58), channel_id=1, source_target_pairs={{0,6},{1,7},{2,0},{3,1},{4,2},{5,3},{6,4},{7,5},{8,14},{9,15},{10,... | collective-permute-start | bytes 1376264 | tf_op jit(solution)/shard_map/ppermute | solution.py:39
  42.5 13.2 %collective-permute-start.17 = (bf16[448,512]{1,0:T(8,128)(2,1)S(1)}, bf16[448,512]{1,0:T(8,128)(2,1)S(1)}, u32[]{:S(2)}, u32[]{:S(2)}) collective-permute-start(bf16[448,512]{1,0:T(8,128)(2,1)S(1)} %get-tuple-element.63), channel_id=1, source_target_pairs={{0,2},{1,3},{2,4},{3,5},{4,6},{5,7},{6,0},{7,1},{8,10},{9,11},{10,... | collective-permute-start | bytes 1376264 | tf_op jit(solution)/shard_map/ppermute | solution.py:39
  43.4 12.4 %collective-permute-start.21 = (bf16[512,128]{1,0:T(8,128)(2,1)S(1)}, bf16[512,128]{1,0:T(8,128)(2,1)S(1)}, u32[]{:S(2)}, u32[]{:S(2)}) collective-permute-start(bf16[512,128]{1,0:T(8,128)(2,1)S(1)} %convert_add_fusion.1), channel_id=1, source_target_pairs={{0,32},{16,48},{32,0},{48,16},{64,96},{80,112},{96,64},{112,80},{1... | collective-permute-start | bytes 393224 | tf_op jit(solution)/shard_map/ppermute | solution.py:56
  43.4 19.6 %collective-permute-start.13 = (bf16[96,2048]{1,0:T(8,128)(2,1)S(1)}, bf16[96,2048]{1,0:T(8,128)(2,1)S(1)}, u32[]{:S(2)}, u32[]{:S(2)}) collective-permute-start(bf16[96,2048]{1,0:T(8,128)(2,1)S(1)} %split.1), channel_id=1, source_target_pairs={{0,8},{1,9},{2,10},{3,11},{4,12},{5,13},{6,14},{7,15},{8,0},{9,1},... | collective-permute-start | bytes 1179656 | tf_op jit(solution)/shard_map/ppermute | solution.py:39
  45.5 21.2 %copy-start.7 = (f32[512,128]{1,0:T(8,128)S(1)}, f32[512,128]{1,0:T(8,128)}, u32[]{:S(2)}) copy-start(f32[512,128]{1,0:T(8,128)} %param.16) | copy-start | bytes 786436
  45.5 21.2 %copy-start.8 = (f32[512,128]{1,0:T(8,128)S(1)}, f32[512,128]{1,0:T(8,128)}, u32[]{:S(2)}) copy-start(f32[512,128]{1,0:T(8,128)} %param.15) | copy-start | bytes 786436
  54.6 5.2 %collective-permute-start.12 = (bf16[256,512]{1,0:T(8,128)(2,1)S(1)}, bf16[256,512]{1,0:T(8,128)(2,1)S(1)}, u32[]{:S(2)}, u32[]{:S(2)}) collective-permute-start(bf16[256,512]{1,0:T(8,128)(2,1)S(1)} %get-tuple-element.55), channel_id=1, source_target_pairs={{0,1},{1,0},{2,3},{3,2},{4,5},{5,4},{6,7},{7,6},{8,9},{9,8},{10,11... | collective-permute-start | bytes 786440 | tf_op jit(solution)/shard_map/ppermute | solution.py:39
  55.9 10.8 %collective-permute-start.22 = (bf16[512,128]{1,0:T(8,128)(2,1)S(1)}, bf16[512,128]{1,0:T(8,128)(2,1)S(1)}, u32[]{:S(2)}, u32[]{:S(2)}) collective-permute-start(bf16[512,128]{1,0:T(8,128)(2,1)S(1)} %convert_add_fusion), channel_id=1, source_target_pairs={{0,128},{16,144},{32,160},{48,176},{64,192},{80,208},{96,224},{112... | collective-permute-start | bytes 393224 | tf_op jit(solution)/shard_map/ppermute | solution.py:56
  56.5 12.4 %collective-permute-start.18 = (bf16[320,512]{1,0:T(8,128)(2,1)S(1)}, bf16[320,512]{1,0:T(8,128)(2,1)S(1)}, u32[]{:S(2)}, u32[]{:S(2)}) collective-permute-start(bf16[320,512]{1,0:T(8,128)(2,1)S(1)} %get-tuple-element.64), channel_id=1, source_target_pairs={{0,2},{1,3},{2,4},{3,5},{4,6},{5,7},{6,0},{7,1},{8,10},{9,11},{10,... | collective-permute-start | bytes 983048 | tf_op jit(solution)/shard_map/ppermute | solution.py:39
  56.5 12.4 %collective-permute-start.19 = (bf16[320,512]{1,0:T(8,128)(2,1)S(1)}, bf16[320,512]{1,0:T(8,128)(2,1)S(1)}, u32[]{:S(2)}, u32[]{:S(2)}) collective-permute-start(bf16[320,512]{1,0:T(8,128)(2,1)S(1)} %get-tuple-element.65), channel_id=1, source_target_pairs={{0,6},{1,7},{2,0},{3,1},{4,2},{5,3},{6,4},{7,5},{8,14},{9,15},{10,... | collective-permute-start | bytes 983048 | tf_op jit(solution)/shard_map/ppermute | solution.py:39
  63.0 8.9 %collective-permute-start.14 = (bf16[64,2048]{1,0:T(8,128)(2,1)S(1)}, bf16[64,2048]{1,0:T(8,128)(2,1)S(1)}, u32[]{:S(2)}, u32[]{:S(2)}) collective-permute-start(bf16[64,2048]{1,0:T(8,128)(2,1)S(1)} %pack.1), channel_id=1, source_target_pairs={{0,8},{1,9},{2,10},{3,11},{4,12},{5,13},{6,14},{7,15},{8,0},{9,1},... | collective-permute-start | bytes 786440 | tf_op jit(solution)/shard_map/ppermute | solution.py:39
  67.5 4.4 %copy-start.4 = (f32[512,128]{1,0:T(8,128)}, f32[512,128]{1,0:T(8,128)S(1)}, u32[]{:S(2)}) copy-start(f32[512,128]{1,0:T(8,128)S(1)} %get-tuple-element.71.glob) | copy-start | bytes 786436
  67.5 2.0 %copy-start.5 = (f32[1,512,512]{2,1,0:T(8,128)S(1)}, f32[1,512,512]{2,1,0:T(8,128)}, u32[]{:S(2)}) copy-start(f32[1,512,512]{2,1,0:T(8,128)} %param.12) | copy-start | bytes 3145732
  67.5 2.3 %copy-start.6 = (f32[1,512,512]{2,1,0:T(8,128)S(1)}, f32[1,512,512]{2,1,0:T(8,128)}, u32[]{:S(2)}) copy-start(f32[1,512,512]{2,1,0:T(8,128)} %param.13) | copy-start | bytes 3145732
  (1 other events, 0.9 us)

commit v9 on v6

--- a/solution.py
+++ b/solution.py
@@ -123,33 +123,39 @@
     )(tokens, up)
 
 
-def places(blocks):
+PLACES = ((0, 0), (1, 0), (3, 0), (2, 0), (2, HALF))
+
+
+def places(blocks, where=PLACES):
     y = here()[1]
-    for (step, start), block in zip(((0, 0), (1, 0), (3, 0), (2, 0), (2, HALF)), blocks, strict=True):
+    for (step, start), block in zip(where, blocks, strict=True):
         at = pl.multiple_of(lax.rem(y + step, NY) * ROWS + start, HALF)
         yield pl.ds(at, block.shape[0]), block
 
 
-def input_grad(ups, blocks):
+def input_grad(ups, blocks, where, before=()):
+    n = len(blocks)
+
     def kernel(u0, u1, u2, *refs):
         up = jnp.concatenate([u0[...], u1[...], u2[...]], axis=0)
-        for at, block in places(refs[:5]):
+        for at, block in places(refs[:n], where):
             grad = lax.dot_general(
                 up, block[...], (((1,), (1,)), ((), ())), preferred_element_type=jnp.float32
             )
             grad = (grad * SCALE).astype(jnp.bfloat16)
-            for k, out in enumerate(refs[5:]):
+            for k, out in enumerate(refs[-4:]):
                 out[:, at] = grad[k * TOK : (k + 1) * TOK]
 
     return pl.pallas_call(
         kernel,
-        in_specs=[pl.BlockSpec(memory_space=pltpu.VMEM)] * 8,
+        in_specs=[pl.BlockSpec(memory_space=pltpu.VMEM)] * (3 + n + len(before)),
         out_specs=[pl.BlockSpec(memory_space=pltpu.VMEM)] * 4,
         out_shape=[shape(TOK, PIECE)] * 4,
+        input_output_aliases={3 + n + k: k for k in range(len(before))},
         cost_estimate=SMALL,
         compiler_params=VMEM,
         name="input_grad",
-    )(*ups, *blocks)
+    )(*ups, *blocks, *before)
 
 
 def value_parts(toks, blocks):
@@ -406,7 +412,10 @@
     g0, to_above, to_below, keep_above, keep_below = weight_grad(toks, (up_ready, up_x, up_pair))
     from_below, from_above = shift_y(to_above, 1), shift_y(to_below, -1)
 
-    ig_own, ig_x, ig_core, ig_far = input_grad((after(up_ready, g0), up_x, up_pair), blocks)
+    before = input_grad((up_ready, up_x, up_pair), blocks[:3], PLACES[:3])
+    ig_own, ig_x, ig_core, ig_far = input_grad(
+        (after(up_ready, g0), up_x, up_pair), blocks[3:], PLACES[3:], before
+    )
     back_x = swap_x(ig_x)
     back_far = swap_core(ig_far)
     back_core = swap_core(ig_core)

time: 72.2 us -> 71.3 us (0.988)
  waiting for transfers between devices: 28.6 us -> 27.5 us
    ppermute x19, waiting for transfers between devices: 23.2 us -> 22.2 us  [fsdp_permute(): return lax.ppermute(value, 'fsdp', pairs)]
    pallas_call x1 -> x2, Pallas kernels: 1.29 us -> 1.49 us  [input_grad(): pl.pallas_call(kernel, in_specs=[pl.BlockSpec(memory_space=pltpu.VMEM)] *...]
  transfers between devices with their start and end apart: 23 -> 23, of which waited for: 7 -> 7; matrix products, arithmetic and copies ran while one was open for 1% -> 1% of each run, Pallas kernels for 9% -> 10%
where the time goes in v9:
time: 71.3 us; the launch traced here: 71.1 us
  starting transfers between devices  29.2 us (41%)
  waiting for transfers between devices  27.5 us (39%)
  Pallas kernels  8.95 us (13%)
  local copies, waits for them, and re-layouts  2.57 us (4%)
  between operations  1.78 us (2%)
  other arithmetic  1.01 us (1%)
    ppermute x19, starting transfers between devices, fsdp_permute(): return lax.ppermute(value, 'fsdp', pairs)  23.6 us
    ppermute x19, waiting for transfers between devices, fsdp_permute(): return lax.ppermute(value, 'fsdp', pairs)  22.2 us
    ppermute x4, starting transfers between devices, replica_step(): other = lax.ppermute(sent, 'replica', [(i, partner(i)) for i in range(16)])  5.62 us
    ppermute x4, waiting for transfers between devices, replica_step(): other = lax.ppermute(sent, 'replica', [(i, partner(i)) for i in range(16)])  5.38 us
    unnamed x20, local copies, waits for them, and re-layouts  2.53 us
    pallas_call x2, Pallas kernels, assemble(): pl.pallas_call(kernel, in_specs=ins, out_specs=outs if vals else outs[0],...  2.16 us
    pallas_call x1, Pallas kernels, adam(): pl.pallas_call(kernel, in_specs=[pl.BlockSpec(memory_space=pltpu.SMEM)] +...  2.03 us
    pallas_call x2, Pallas kernels, input_grad(): pl.pallas_call(kernel, in_specs=[pl.BlockSpec(memory_space=pltpu.VMEM)] *...  1.49 us
  transfers between devices with their start and end apart: 23, of which 7 were waited for; matrix products, arithmetic and copies ran while one was open for 1% of the time, Pallas kernels for 10%

profile of v9, /device:TPU:64, one launch (start us, length us, event | category | flops | bytes accessed | tf_op | source)
XLA Modules:
  0.0 71.1 jit_solution(16031999621362048609)
XLA Ops:
  0.6 1.6 %copy-done = bf16[1,128,8192]{2,1,0:T(8,128)(2,1)S(1)} copy-done((bf16[1,128,8192]{2,1,0:T(8,128)(2,1)S(1)}, bf16[1,128,8192]{2,1,0:T(8,128)(2,1)}, u32[]{:S(2)}) %copy-start) | copy-done | bytes 2097176
  2.2 0.9 %copy-done.1 = bf16[1,128,512]{2,1,0:T(8,128)(2,1)S(1)} copy-done((bf16[1,128,512]{2,1,0:T(8,128)(2,1)S(1)}, bf16[1,128,512]{2,1,0:T(8,128)(2,1)}, u32[]{:S(2)}) %copy-start.1) | copy-done | bytes 131096
  3.8 0.6 collective-permute-start
  4.4 3.0 %collective-permute-start.4 = (bf16[128,2560]{1,0:T(8,128)(2,1)S(1)}, bf16[128,2560]{1,0:T(8,128)(2,1)S(1)}, u32[]{:S(2)}, u32[]{:S(2)}) collective-permute-start(bf16[128,2560]{1,0:T(8,128)(2,1)S(1)} %get-tuple-element.47), channel_id=1, source_target_pairs={{0,8},{1,9},{2,10},{3,11},{4,12},{5,13},{6,14},{7,15},{8,0},{9,1},... | collective-permute-start | bytes 1966088 | tf_op jit(solution)/shard_map/ppermute | solution.py:39
  7.5 1.7 %collective-permute-start.9 = (bf16[512,512]{1,0:T(8,128)(2,1)S(1)}, bf16[512,512]{1,0:T(8,128)(2,1)S(1)}, u32[]{:S(2)}, u32[]{:S(2)}) collective-permute-start(bf16[512,512]{1,0:T(8,128)(2,1)S(1)} %bitcast_convert_fusion.refs_0_), channel_id=1, source_target_pairs={{0,2},{1,3},{2,4},{3,5},{4,6},{5,7},{6,0},{7,1},{8,10},{9,11},{10,... | collective-permute-start | bytes 1572872 | tf_op jit(solution)/shard_map/ppermute | solution.py:39
  9.1 1.7 %collective-permute-start.7 = (bf16[512,512]{1,0:T(8,128)(2,1)S(1)}, bf16[512,512]{1,0:T(8,128)(2,1)S(1)}, u32[]{:S(2)}, u32[]{:S(2)}) collective-permute-start(bf16[512,512]{1,0:T(8,128)(2,1)S(1)} %bitcast_convert_fusion.refs_0_), channel_id=1, source_target_pairs={{0,6},{1,7},{2,0},{3,1},{4,2},{5,3},{6,4},{7,5},{8,14},{9,15},{10,... | collective-permute-start | bytes 1572872 | tf_op jit(solution)/shard_map/ppermute | solution.py:39
  10.8 4.6 %collective-permute-start.2 = (bf16[512,128]{1,0:T(8,128)(2,1)S(1)}, bf16[512,128]{1,0:T(8,128)(2,1)S(1)}, u32[]{:S(2)}, u32[]{:S(2)}) collective-permute-start(bf16[512,128]{1,0:T(8,128)(2,1)S(1)} %convert_bitcast_fusion), channel_id=1, source_target_pairs={{0,96},{16,112},{32,64},{48,80},{64,32},{80,48},{96,0},{112,16},{1... | collective-permute-start | bytes 393224 | tf_op jit(solution)/shard_map/ppermute | solution.py:56
  15.4 0.5 collective-permute-start.5
  15.9 5.4 %collective-permute-done.2 = bf16[512,128]{1,0:T(8,128)(2,1)S(1)} collective-permute-done((bf16[512,128]{1,0:T(8,128)(2,1)S(1)}, bf16[512,128]{1,0:T(8,128)(2,1)S(1)}, u32[]{:S(2)}, u32[]{:S(2)}) %collective-permute-start.2) | collective-permute-done | bytes 131104 | tf_op jit(solution)/shard_map/ppermute | solution.py:56
  21.7 1.8 %collective-permute-done.4.t1 = bf16[128,2560]{1,0:T(8,128)(2,1)S(1)} collective-permute-done((bf16[128,2560]{1,0:T(8,128)(2,1)S(1)}, bf16[128,2560]{1,0:T(8,128)(2,1)S(1)}, u32[]{:S(2)}, u32[]{:S(2)}) %collective-permute-start.4) | collective-permute-done | bytes 655392 | tf_op jit(solution)/shard_map/ppermute | solution.py:39
  23.7 1.7 %collective-permute-start.10 = (bf16[256,512]{1,0:T(8,128)(2,1)S(1)}, bf16[256,512]{1,0:T(8,128)(2,1)S(1)}, u32[]{:S(2)}, u32[]{:S(2)}) collective-permute-start(bf16[256,512]{1,0:T(8,128)(2,1)S(1)} %slice.14), channel_id=1, source_target_pairs={{0,2},{1,3},{2,4},{3,5},{4,6},{5,7},{6,0},{7,1},{8,10},{9,11},{10,... | collective-permute-start | bytes 786440 | tf_op jit(solution)/shard_map/ppermute | solution.py:39
  25.3 1.7 %collective-permute-start.8 = (bf16[256,512]{1,0:T(8,128)(2,1)S(1)}, bf16[256,512]{1,0:T(8,128)(2,1)S(1)}, u32[]{:S(2)}, u32[]{:S(2)}) collective-permute-start(bf16[256,512]{1,0:T(8,128)(2,1)S(1)} %slice.13), channel_id=1, source_target_pairs={{0,6},{1,7},{2,0},{3,1},{4,2},{5,3},{6,4},{7,5},{8,14},{9,15},{10,... | collective-permute-start | bytes 786440 | tf_op jit(solution)/shard_map/ppermute | solution.py:39
  27.1 1.0 %input_grad.2 = (bf16[128,2048]{1,0:T(8,128)(2,1)S(1)}, bf16[128,2048]{1,0:T(8,128)(2,1)S(1)}, bf16[128,2048]{1,0:T(8,128)(2,1)S(1)}, bf16[128,2048]{1,0:T(8,128)(2,1)S(1)}) custom-call(bf16[128,512]{1,0:T(8,128)(2,1)S(1)} %bitcast.18, bf16[128,512]{1,0:T(8,128)(2,1)S(1)} %slice.12.u1, bf16[256,512]{1,0:T(8,128)(2,1)S(1)} %collective-permute-done.6.u2, ...), custom_call_target="tpu_custom_call" | custom-call | flops 1 | bytes 1 | tf_op jit(solution)/shard_map/input_grad/pallas_call | solution.py:149
  28.2 5.7 %collective-permute-done.5.t3 = bf16[128,2048]{1,0:T(8,128)(2,1)S(1)} collective-permute-done((bf16[128,2048]{1,0:T(8,128)(2,1)S(1)}, bf16[128,2048]{1,0:T(8,128)(2,1)S(1)}, u32[]{:S(2)}, u32[]{:S(2)}) %collective-permute-start.5) | collective-permute-done | bytes 524320 | tf_op jit(solution)/shard_map/ppermute | solution.py:39
  33.9 1.3 %weight_grad.1 = (f32[512,512]{1,0:T(8,128)S(1)}, bf16[448,512]{1,0:T(8,128)(2,1)S(1)}, bf16[448,512]{1,0:T(8,128)(2,1)S(1)}, f32[320,512]{1,0:T(8,128)S(1)}, f32[320,512]{1,0:T(8,128)S(1)}) custom-call(bf16[128,2048]{1,0:T(8,128)(2,1)S(1)} %get-tuple-element.53.t0, bf16[128,2560]{1,0:T(8,128)(2,1)S(1)} %collective-permute-done.4.t1, ...), custom_call_target="tpu_custom_call" | custom-call | flops 1 | bytes 1 | tf_op jit(solution)/shard_map/weight_grad/pallas_call | solution.py:242
  35.8 0.5 collective-permute-start.11
  36.3 3.0 %collective-permute-start.16 = (bf16[128,2048]{1,0:T(8,128)(2,1)S(1)}, bf16[128,2048]{1,0:T(8,128)(2,1)S(1)}, u32[]{:S(2)}, u32[]{:S(2)}) collective-permute-start(bf16[128,2048]{1,0:T(8,128)(2,1)S(1)} %get-tuple-element.68), channel_id=1, source_target_pairs={{0,8},{1,9},{2,10},{3,11},{4,12},{5,13},{6,14},{7,15},{8,0},{9,1},... | collective-permute-start | bytes 1572872 | tf_op jit(solution)/shard_map/ppermute | solution.py:39
  39.3 3.0 %collective-permute-start.15 = (bf16[448,512]{1,0:T(8,128)(2,1)S(1)}, bf16[448,512]{1,0:T(8,128)(2,1)S(1)}, u32[]{:S(2)}, u32[]{:S(2)}) collective-permute-start(bf16[448,512]{1,0:T(8,128)(2,1)S(1)} %get-tuple-element.66), channel_id=1, source_target_pairs={{0,6},{1,7},{2,0},{3,1},{4,2},{5,3},{6,4},{7,5},{8,14},{9,15},{10,... | collective-permute-start | bytes 1376264 | tf_op jit(solution)/shard_map/ppermute | solution.py:39
  42.4 1.0 %collective-permute-start.13 = (bf16[96,2048]{1,0:T(8,128)(2,1)S(1)}, bf16[96,2048]{1,0:T(8,128)(2,1)S(1)}, u32[]{:S(2)}, u32[]{:S(2)}) collective-permute-start(bf16[96,2048]{1,0:T(8,128)(2,1)S(1)} %split.1), channel_id=1, source_target_pairs={{0,8},{1,9},{2,10},{3,11},{4,12},{5,13},{6,14},{7,15},{8,0},{9,1},... | collective-permute-start | bytes 1179656 | tf_op jit(solution)/shard_map/ppermute | solution.py:39
  43.4 1.2 %values.1 = (f32[128,512]{1,0:T(8,128)S(1)}, f32[128,512]{1,0:T(8,128)S(1)}, bf16[256,512]{1,0:T(8,128)(2,1)S(1)}) custom-call(bf16[128,2048]{1,0:T(8,128)(2,1)S(1)} %get-tuple-element.53.t0, bf16[128,2560]{1,0:T(8,128)(2,1)S(1)} %collective-permute-done.4.t1, bf16[128,2048]{1,0:T(8,128)(2,1)S(1)} %collective-permute-done.t2, ...), custom_call_target="tpu_custom_call" | custom-call | flops 1 | bytes 1 | tf_op jit(solution)/shard_map/values/pallas_call | solution.py:172
  44.6 7.9 %collective-permute-done.16.refs_2_ = bf16[128,2048]{1,0:T(8,128)(2,1)S(1)} collective-permute-done((bf16[128,2048]{1,0:T(8,128)(2,1)S(1)}, bf16[128,2048]{1,0:T(8,128)(2,1)S(1)}, u32[]{:S(2)}, u32[]{:S(2)}) %collective-permute-start.16) | collective-permute-done | bytes 524320 | tf_op jit(solution)/shard_map/ppermute | solution.py:39
  52.6 2.9 %collective-permute-done.17.from_below = bf16[448,512]{1,0:T(8,128)(2,1)S(1)} collective-permute-done((bf16[448,512]{1,0:T(8,128)(2,1)S(1)}, bf16[448,512]{1,0:T(8,128)(2,1)S(1)}, u32[]{:S(2)}, u32[]{:S(2)}) %collective-permute-start.17) | collective-permute-done | bytes 458784 | tf_op jit(solution)/shard_map/ppermute | solution.py:39
  55.7 0.7 collective-permute-start.22
  56.3 1.0 %collective-permute-start.19 = (bf16[320,512]{1,0:T(8,128)(2,1)S(1)}, bf16[320,512]{1,0:T(8,128)(2,1)S(1)}, u32[]{:S(2)}, u32[]{:S(2)}) collective-permute-start(bf16[320,512]{1,0:T(8,128)(2,1)S(1)} %get-tuple-element.73), channel_id=1, source_target_pairs={{0,6},{1,7},{2,0},{3,1},{4,2},{5,3},{6,4},{7,5},{8,14},{9,15},{10,... | collective-permute-start | bytes 983048 | tf_op jit(solution)/shard_map/ppermute | solution.py:39
  57.3 1.0 %collective-permute-start.18 = (bf16[320,512]{1,0:T(8,128)(2,1)S(1)}, bf16[320,512]{1,0:T(8,128)(2,1)S(1)}, u32[]{:S(2)}, u32[]{:S(2)}) collective-permute-start(bf16[320,512]{1,0:T(8,128)(2,1)S(1)} %get-tuple-element.72), channel_id=1, source_target_pairs={{0,2},{1,3},{2,4},{3,5},{4,6},{5,7},{6,0},{7,1},{8,10},{9,11},{10,... | collective-permute-start | bytes 983048 | tf_op jit(solution)/shard_map/ppermute | solution.py:39
  58.4 2.6 %collective-permute-done.13.refs_3_ = bf16[96,2048]{1,0:T(8,128)(2,1)S(1)} collective-permute-done((bf16[96,2048]{1,0:T(8,128)(2,1)S(1)}, bf16[96,2048]{1,0:T(8,128)(2,1)S(1)}, u32[]{:S(2)}, u32[]{:S(2)}) %collective-permute-start.13) | collective-permute-done | bytes 393248 | tf_op jit(solution)/shard_map/ppermute | solution.py:39
  61.0 3.0 %collective-permute-start.14 = (bf16[64,2048]{1,0:T(8,128)(2,1)S(1)}, bf16[64,2048]{1,0:T(8,128)(2,1)S(1)}, u32[]{:S(2)}, u32[]{:S(2)}) collective-permute-start(bf16[64,2048]{1,0:T(8,128)(2,1)S(1)} %pack.1), channel_id=1, source_target_pairs={{0,8},{1,9},{2,10},{3,11},{4,12},{5,13},{6,14},{7,15},{8,0},{9,1},... | collective-permute-start | bytes 786440 | tf_op jit(solution)/shard_map/ppermute | solution.py:39
  64.7 0.8 %multiply_subtract_fusion = (f32[512,128]{1,0:T(8,128)S(1)}, f32[512,128]{1,0:T(8,128)}) fusion(f32[512,128]{1,0:T(8,128)S(1)} %copy-done.7, bf16[512,128]{1,0:T(8,128)(2,1)S(1)} %collective-permute-done.22, bf16[512,128]{1,0:T(8,128)(2,1)S(1)} %convert_add_fusion, f32[512,128]{1,0:T(8,128)S(1)} %copy-done.8), kind=kLoop, calls=%fused_computation.1 | loop fusion | flops 655360 | bytes 1310720 | tf_op jit(solution)/shard_map/sub | solution.py:66
  65.5 1.4 %assemble.2.refs_3_ = bf16[128,8192]{1,0:T(8,128)(2,1)} custom-call(bf16[128,2048]{1,0:T(8,128)(2,1)S(1)} %get-tuple-element.78.refs_0_, bf16[128,2048]{1,0:T(8,128)(2,1)S(1)} %collective-permute-done.20.refs_1_, bf16[128,2048]{1,0:T(8,128)(2,1)S(1)} %collective-permute-done.16.refs_2_, bf16[96,2048]{1,0:T(8,128)(2,1)S(1)} %collective-permute-done.13.refs_3_), custom_call_target="tpu_custom_call" | custom-call | flops 1 | bytes 1 | tf_op jit(solution)/shard_map/assemble/pallas_call | solution.py:318
  66.9 1.2 %collective-permute-done.18.r1 = bf16[320,512]{1,0:T(8,128)(2,1)S(1)} collective-permute-done((bf16[320,512]{1,0:T(8,128)(2,1)S(1)}, bf16[320,512]{1,0:T(8,128)(2,1)S(1)}, u32[]{:S(2)}, u32[]{:S(2)}) %collective-permute-start.18) | collective-permute-done | bytes 327712 | tf_op jit(solution)/shard_map/ppermute | solution.py:39
  68.1 2.0 %adam.1 = (f32[512,512]{1,0:T(8,128)}, f32[512,512]{1,0:T(8,128)}, f32[512,512]{1,0:T(8,128)}) custom-call(s32[1]{0:T(128)S(6)} %copy.26.frag, f32[512,512]{1,0:T(8,128)S(1)} %get-tuple-element.54.g0, bf16[448,512]{1,0:T(8,128)(2,1)S(1)} %collective-permute-done.15.from_above, bf16[320,512]{1,0:T(8,128)(2,1)S(1)} %collective-permute-done.18.r1, ...), custom_call_target="tpu_custom_call" | custom-call | flops 1 | bytes 1 | tf_op jit(solution)/shard_map/adam/pallas_call | solution.py:370
  70.2 0.8 %assemble.3 = (bf16[128,8192]{1,0:T(8,128)(2,1)}, bf16[128,512]{1,0:T(8,128)(2,1)}) custom-call(bf16[64,2048]{1,0:T(8,128)(2,1)S(1)} %collective-permute-done.14.refs_0_, f32[128,512]{1,0:T(8,128)S(1)} %get-tuple-element.82.refs_1_, bf16[256,512]{1,0:T(8,128)(2,1)S(1)} %collective-permute-done.12.val_back.refs_2_, ...), custom_call_target="tpu_custom_call", output_to_operand_aliasing={{0}: (3, {})} | custom-call | flops 1 | bytes 1 | tf_op jit(solution)/shard_map/assemble/pallas_call | solution.py:318
  (56 shorter events, 2.2 us)
Async XLA Ops:
  0.6 1.6 %copy-start = (bf16[1,128,8192]{2,1,0:T(8,128)(2,1)S(1)}, bf16[1,128,8192]{2,1,0:T(8,128)(2,1)}, u32[]{:S(2)}) copy-start(bf16[1,128,8192]{2,1,0:T(8,128)(2,1)} %param.9) | copy-start | bytes 6291460
  3.1 4.3 %copy-start.3 = (f32[1,512,512]{2,1,0:T(8,128)S(1)}, f32[1,512,512]{2,1,0:T(8,128)}, u32[]{:S(2)}) copy-start(f32[1,512,512]{2,1,0:T(8,128)} %param.11) | copy-start | bytes 3145732
  3.4 7.4 %copy-start.9 = (f32[1,512,128]{2,1,0:T(8,128)S(1)}, f32[1,512,128]{2,1,0:T(8,128)}, u32[]{:S(2)}) copy-start(f32[1,512,128]{2,1,0:T(8,128)} %param.14) | copy-start | bytes 786436
  3.4 7.4 %collective-permute-start.1 = (bf16[128,2048]{1,0:T(8,128)(2,1)S(1)}, bf16[128,2048]{1,0:T(8,128)(2,1)S(1)}, u32[]{:S(2)}, u32[]{:S(2)}) collective-permute-start(bf16[128,2048]{1,0:T(8,128)(2,1)S(1)} %get-tuple-element.50), channel_id=1, source_target_pairs={{0,1},{1,0},{2,3},{3,2},{4,5},{5,4},{6,7},{7,6},{8,9},{9,8},{10,11... | collective-permute-start | bytes 1572872 | tf_op jit(solution)/shard_map/ppermute | solution.py:39
  3.8 23.3 %copy-start.2 = (bf16[1,128,512]{2,1,0:T(8,128)(2,1)S(1)}, bf16[1,128,512]{2,1,0:T(8,128)(2,1)}, u32[]{:S(2)}) copy-start(bf16[1,128,512]{2,1,0:T(8,128)(2,1)} %param.10) | copy-start | bytes 393220
  3.8 7.0 %collective-permute-start = (bf16[128,2048]{1,0:T(8,128)(2,1)S(1)}, bf16[128,2048]{1,0:T(8,128)(2,1)S(1)}, u32[]{:S(2)}, u32[]{:S(2)}) collective-permute-start(bf16[128,2048]{1,0:T(8,128)(2,1)S(1)} %get-tuple-element.49), channel_id=1, source_target_pairs={{0,1},{1,0},{2,3},{3,2},{4,5},{5,4},{6,7},{7,6},{8,9},{9,8},{10,11... | collective-permute-start | bytes 1572872 | tf_op jit(solution)/shard_map/ppermute | solution.py:39
  4.4 19.1 %collective-permute-start.4 = (bf16[128,2560]{1,0:T(8,128)(2,1)S(1)}, bf16[128,2560]{1,0:T(8,128)(2,1)S(1)}, u32[]{:S(2)}, u32[]{:S(2)}) collective-permute-start(bf16[128,2560]{1,0:T(8,128)(2,1)S(1)} %get-tuple-element.47), channel_id=1, source_target_pairs={{0,8},{1,9},{2,10},{3,11},{4,12},{5,13},{6,14},{7,15},{8,0},{9,1},... | collective-permute-start | bytes 1966088 | tf_op jit(solution)/shard_map/ppermute | solution.py:39
  7.5 16.1 %collective-permute-start.9 = (bf16[512,512]{1,0:T(8,128)(2,1)S(1)}, bf16[512,512]{1,0:T(8,128)(2,1)S(1)}, u32[]{:S(2)}, u32[]{:S(2)}) collective-permute-start(bf16[512,512]{1,0:T(8,128)(2,1)S(1)} %bitcast_convert_fusion.refs_0_), channel_id=1, source_target_pairs={{0,2},{1,3},{2,4},{3,5},{4,6},{5,7},{6,0},{7,1},{8,10},{9,11},{10,... | collective-permute-start | bytes 1572872 | tf_op jit(solution)/shard_map/ppermute | solution.py:39
  9.1 16.2 %collective-permute-start.7 = (bf16[512,512]{1,0:T(8,128)(2,1)S(1)}, bf16[512,512]{1,0:T(8,128)(2,1)S(1)}, u32[]{:S(2)}, u32[]{:S(2)}) collective-permute-start(bf16[512,512]{1,0:T(8,128)(2,1)S(1)} %bitcast_convert_fusion.refs_0_), channel_id=1, source_target_pairs={{0,6},{1,7},{2,0},{3,1},{4,2},{5,3},{6,4},{7,5},{8,14},{9,15},{10,... | collective-permute-start | bytes 1572872 | tf_op jit(solution)/shard_map/ppermute | solution.py:39
  10.8 10.4 %collective-permute-start.2 = (bf16[512,128]{1,0:T(8,128)(2,1)S(1)}, bf16[512,128]{1,0:T(8,128)(2,1)S(1)}, u32[]{:S(2)}, u32[]{:S(2)}) collective-permute-start(bf16[512,128]{1,0:T(8,128)(2,1)S(1)} %convert_bitcast_fusion), channel_id=1, source_target_pairs={{0,96},{16,112},{32,64},{48,80},{64,32},{80,48},{96,0},{112,16},{1... | collective-permute-start | bytes 393224 | tf_op jit(solution)/shard_map/ppermute | solution.py:56
  15.4 18.5 %collective-permute-start.5 = (bf16[128,2048]{1,0:T(8,128)(2,1)S(1)}, bf16[128,2048]{1,0:T(8,128)(2,1)S(1)}, u32[]{:S(2)}, u32[]{:S(2)}) collective-permute-start(bf16[128,2048]{1,0:T(8,128)(2,1)S(1)} %collective-permute-done.1), channel_id=1, source_target_pairs={{0,8},{1,9},{2,10},{3,11},{4,12},{5,13},{6,14},{7,15},{8,0},{9,1},... | collective-permute-start | bytes 1572872 | tf_op jit(solution)/shard_map/ppermute | solution.py:39
  21.3 5.7 %collective-permute-start.3 = (bf16[512,128]{1,0:T(8,128)(2,1)S(1)}, bf16[512,128]{1,0:T(8,128)(2,1)S(1)}, u32[]{:S(2)}, u32[]{:S(2)}) collective-permute-start(bf16[512,128]{1,0:T(8,128)(2,1)S(1)} %add_convert_fusion), channel_id=1, source_target_pairs={{0,16},{16,0},{32,48},{48,32},{64,80},{80,64},{96,112},{112,96},{1... | collective-permute-start | bytes 393224 | tf_op jit(solution)/shard_map/ppermute | solution.py:56
  23.5 3.6 %collective-permute-start.6 = (bf16[256,512]{1,0:T(8,128)(2,1)S(1)}, bf16[256,512]{1,0:T(8,128)(2,1)S(1)}, u32[]{:S(2)}, u32[]{:S(2)}) collective-permute-start(bf16[256,512]{1,0:T(8,128)(2,1)S(1)} %pad_maximum_fusion), channel_id=1, source_target_pairs={{0,1},{1,0},{2,3},{3,2},{4,5},{5,4},{6,7},{7,6},{8,9},{9,8},{10,11... | collective-permute-start | bytes 786440 | tf_op jit(solution)/shard_map/ppermute | solution.py:39
  23.7 11.5 %collective-permute-start.10 = (bf16[256,512]{1,0:T(8,128)(2,1)S(1)}, bf16[256,512]{1,0:T(8,128)(2,1)S(1)}, u32[]{:S(2)}, u32[]{:S(2)}) collective-permute-start(bf16[256,512]{1,0:T(8,128)(2,1)S(1)} %slice.14), channel_id=1, source_target_pairs={{0,2},{1,3},{2,4},{3,5},{4,6},{5,7},{6,0},{7,1},{8,10},{9,11},{10,... | collective-permute-start | bytes 786440 | tf_op jit(solution)/shard_map/ppermute | solution.py:39
  25.3 9.9 %collective-permute-start.8 = (bf16[256,512]{1,0:T(8,128)(2,1)S(1)}, bf16[256,512]{1,0:T(8,128)(2,1)S(1)}, u32[]{:S(2)}, u32[]{:S(2)}) collective-permute-start(bf16[256,512]{1,0:T(8,128)(2,1)S(1)} %slice.13), channel_id=1, source_target_pairs={{0,6},{1,7},{2,0},{3,1},{4,2},{5,3},{6,4},{7,5},{8,14},{9,15},{10,... | collective-permute-start | bytes 786440 | tf_op jit(solution)/shard_map/ppermute | solution.py:39
  35.7 6.6 %collective-permute-start.20 = (bf16[128,2048]{1,0:T(8,128)(2,1)S(1)}, bf16[128,2048]{1,0:T(8,128)(2,1)S(1)}, u32[]{:S(2)}, u32[]{:S(2)}) collective-permute-start(bf16[128,2048]{1,0:T(8,128)(2,1)S(1)} %get-tuple-element.75), channel_id=1, source_target_pairs={{0,1},{1,0},{2,3},{3,2},{4,5},{5,4},{6,7},{7,6},{8,9},{9,8},{10,11... | collective-permute-start | bytes 1572872 | tf_op jit(solution)/shard_map/ppermute | solution.py:39
  35.8 6.6 %collective-permute-start.11 = (bf16[128,2048]{1,0:T(8,128)(2,1)S(1)}, bf16[128,2048]{1,0:T(8,128)(2,1)S(1)}, u32[]{:S(2)}, u32[]{:S(2)}) collective-permute-start(bf16[128,2048]{1,0:T(8,128)(2,1)S(1)} %get-tuple-element.61), channel_id=1, source_target_pairs={{0,1},{1,0},{2,3},{3,2},{4,5},{5,4},{6,7},{7,6},{8,9},{9,8},{10,11... | collective-permute-start | bytes 1572872 | tf_op jit(solution)/shard_map/ppermute | solution.py:39
  36.3 16.3 %collective-permute-start.16 = (bf16[128,2048]{1,0:T(8,128)(2,1)S(1)}, bf16[128,2048]{1,0:T(8,128)(2,1)S(1)}, u32[]{:S(2)}, u32[]{:S(2)}) collective-permute-start(bf16[128,2048]{1,0:T(8,128)(2,1)S(1)} %get-tuple-element.68), channel_id=1, source_target_pairs={{0,8},{1,9},{2,10},{3,11},{4,12},{5,13},{6,14},{7,15},{8,0},{9,1},... | collective-permute-start | bytes 1572872 | tf_op jit(solution)/shard_map/ppermute | solution.py:39
  39.3 13.3 %collective-permute-start.15 = (bf16[448,512]{1,0:T(8,128)(2,1)S(1)}, bf16[448,512]{1,0:T(8,128)(2,1)S(1)}, u32[]{:S(2)}, u32[]{:S(2)}) collective-permute-start(bf16[448,512]{1,0:T(8,128)(2,1)S(1)} %get-tuple-element.66), channel_id=1, source_target_pairs={{0,6},{1,7},{2,0},{3,1},{4,2},{5,3},{6,4},{7,5},{8,14},{9,15},{10,... | collective-permute-start | bytes 1376264 | tf_op jit(solution)/shard_map/ppermute | solution.py:39
  42.3 13.2 %collective-permute-start.17 = (bf16[448,512]{1,0:T(8,128)(2,1)S(1)}, bf16[448,512]{1,0:T(8,128)(2,1)S(1)}, u32[]{:S(2)}, u32[]{:S(2)}) collective-permute-start(bf16[448,512]{1,0:T(8,128)(2,1)S(1)} %get-tuple-element.71), channel_id=1, source_target_pairs={{0,2},{1,3},{2,4},{3,5},{4,6},{5,7},{6,0},{7,1},{8,10},{9,11},{10,... | collective-permute-start | bytes 1376264 | tf_op jit(solution)/shard_map/ppermute | solution.py:39
  42.3 13.3 %collective-permute-start.21 = (bf16[512,128]{1,0:T(8,128)(2,1)S(1)}, bf16[512,128]{1,0:T(8,128)(2,1)S(1)}, u32[]{:S(2)}, u32[]{:S(2)}) collective-permute-start(bf16[512,128]{1,0:T(8,128)(2,1)S(1)} %convert_add_fusion.1), channel_id=1, source_target_pairs={{0,32},{16,48},{32,0},{48,16},{64,96},{80,112},{96,64},{112,80},{1... | collective-permute-start | bytes 393224 | tf_op jit(solution)/shard_map/ppermute | solution.py:56
  42.4 18.6 %collective-permute-start.13 = (bf16[96,2048]{1,0:T(8,128)(2,1)S(1)}, bf16[96,2048]{1,0:T(8,128)(2,1)S(1)}, u32[]{:S(2)}, u32[]{:S(2)}) collective-permute-start(bf16[96,2048]{1,0:T(8,128)(2,1)S(1)} %split.1), channel_id=1, source_target_pairs={{0,8},{1,9},{2,10},{3,11},{4,12},{5,13},{6,14},{7,15},{8,0},{9,1},... | collective-permute-start | bytes 1179656 | tf_op jit(solution)/shard_map/ppermute | solution.py:39
  44.6 20.1 %copy-start.7 = (f32[512,128]{1,0:T(8,128)S(1)}, f32[512,128]{1,0:T(8,128)}, u32[]{:S(2)}) copy-start(f32[512,128]{1,0:T(8,128)} %param.16) | copy-start | bytes 786436
  44.6 20.1 %copy-start.8 = (f32[512,128]{1,0:T(8,128)S(1)}, f32[512,128]{1,0:T(8,128)}, u32[]{:S(2)}) copy-start(f32[512,128]{1,0:T(8,128)} %param.15) | copy-start | bytes 786436
  52.6 5.8 %collective-permute-start.12 = (bf16[256,512]{1,0:T(8,128)(2,1)S(1)}, bf16[256,512]{1,0:T(8,128)(2,1)S(1)}, u32[]{:S(2)}, u32[]{:S(2)}) collective-permute-start(bf16[256,512]{1,0:T(8,128)(2,1)S(1)} %get-tuple-element.63), channel_id=1, source_target_pairs={{0,1},{1,0},{2,3},{3,2},{4,5},{5,4},{6,7},{7,6},{8,9},{9,8},{10,11... | collective-permute-start | bytes 786440 | tf_op jit(solution)/shard_map/ppermute | solution.py:39
  55.7 9.0 %collective-permute-start.22 = (bf16[512,128]{1,0:T(8,128)(2,1)S(1)}, bf16[512,128]{1,0:T(8,128)(2,1)S(1)}, u32[]{:S(2)}, u32[]{:S(2)}) collective-permute-start(bf16[512,128]{1,0:T(8,128)(2,1)S(1)} %convert_add_fusion), channel_id=1, source_target_pairs={{0,128},{16,144},{32,160},{48,176},{64,192},{80,208},{96,224},{112... | collective-permute-start | bytes 393224 | tf_op jit(solution)/shard_map/ppermute | solution.py:56
  56.3 10.6 %collective-permute-start.19 = (bf16[320,512]{1,0:T(8,128)(2,1)S(1)}, bf16[320,512]{1,0:T(8,128)(2,1)S(1)}, u32[]{:S(2)}, u32[]{:S(2)}) collective-permute-start(bf16[320,512]{1,0:T(8,128)(2,1)S(1)} %get-tuple-element.73), channel_id=1, source_target_pairs={{0,6},{1,7},{2,0},{3,1},{4,2},{5,3},{6,4},{7,5},{8,14},{9,15},{10,... | collective-permute-start | bytes 983048 | tf_op jit(solution)/shard_map/ppermute | solution.py:39
  57.3 10.8 %collective-permute-start.18 = (bf16[320,512]{1,0:T(8,128)(2,1)S(1)}, bf16[320,512]{1,0:T(8,128)(2,1)S(1)}, u32[]{:S(2)}, u32[]{:S(2)}) collective-permute-start(bf16[320,512]{1,0:T(8,128)(2,1)S(1)} %get-tuple-element.72), channel_id=1, source_target_pairs={{0,2},{1,3},{2,4},{3,5},{4,6},{5,7},{6,0},{7,1},{8,10},{9,11},{10,... | collective-permute-start | bytes 983048 | tf_op jit(solution)/shard_map/ppermute | solution.py:39
  61.0 9.2 %collective-permute-start.14 = (bf16[64,2048]{1,0:T(8,128)(2,1)S(1)}, bf16[64,2048]{1,0:T(8,128)(2,1)S(1)}, u32[]{:S(2)}, u32[]{:S(2)}) collective-permute-start(bf16[64,2048]{1,0:T(8,128)(2,1)S(1)} %pack.1), channel_id=1, source_target_pairs={{0,8},{1,9},{2,10},{3,11},{4,12},{5,13},{6,14},{7,15},{8,0},{9,1},... | collective-permute-start | bytes 786440 | tf_op jit(solution)/shard_map/ppermute | solution.py:39
  65.5 4.7 %copy-start.4 = (f32[512,128]{1,0:T(8,128)}, f32[512,128]{1,0:T(8,128)S(1)}, u32[]{:S(2)}) copy-start(f32[512,128]{1,0:T(8,128)S(1)} %get-tuple-element.79.glob) | copy-start | bytes 786436
  65.5 2.6 %copy-start.5 = (f32[1,512,512]{2,1,0:T(8,128)S(1)}, f32[1,512,512]{2,1,0:T(8,128)}, u32[]{:S(2)}) copy-start(f32[1,512,512]{2,1,0:T(8,128)} %param.12) | copy-start | bytes 3145732
  65.5 2.6 %copy-start.6 = (f32[1,512,512]{2,1,0:T(8,128)S(1)}, f32[1,512,512]{2,1,0:T(8,128)}, u32[]{:S(2)}) copy-start(f32[1,512,512]{2,1,0:T(8,128)} %param.13) | copy-start | bytes 3145732
  (1 other events, 0.9 us)
